TPU v7x, 32 devices: a whole 2x2x4 slice. The times are simulated.
32 devices in a mesh: org: 8 (over z, y), dst: 4 (over x, core).
Axes of the slice: x: 2, y: 2, z: 4, core: 2. Of those that a mesh axis runs over, the one named last changes fastest.
Arguments:
- od_cells: bfloat16 [16384, 128, 128], P('org', 'dst'), may hold values from -100 to 100
- anchor_edges: int32 [16384, 4], P('org'), may hold values from 0 to 255, all different within a row
- edge_weight: float32 [256], replicated, may hold values from 0.5 to 4
- mixing: bfloat16 [128, 128], replicated, may hold values from -0.5 to 0.5
- dst_edges: int32 [128, 3], replicated, may hold values from 0 to 127, all different within a row
- dst_weight: float32 [128], replicated, may hold values from 0.5 to 4
- out_bias: float32 [128], replicated, may hold values from -1.2 to 1.2
Outputs:
- layer_out: bfloat16 [16384, 128, 128], P(('org', 'dst'))
Inputs may be any that keep to these rules, and one draw needn't show every extreme that they name: `anchor_edges`: each anchor zone lists 4 different corridors, and every corridor is listed by at least one anchor zone. `dst_edges`: each destination zone lists 3 different hyperedges, and every hyperedge is listed by at least one destination zone.
All inputs are finite; a program needn't handle non-finite values.
Results may differ from a plain program's by a relative error of at most 0.0066.
Values may be sent and summed in bfloat16 or wider, within the bound.
No kernel may reach another device: no remote copies, remote signals or barrier semaphores. Data moves between devices by JAX's collectives and lax.ppermute only.
A program may use at most 128 MiB of HBM per device.

v0:
```python
import jax
import jax.numpy as jnp
from jax import lax
from jax.sharding import PartitionSpec as P


def corridor_table(edge_ids, edge_count):
    columns = jnp.arange(edge_count, dtype=jnp.int32)
    return jnp.sum((edge_ids[:, :, None] == columns[None, None, :]).astype(jnp.float32), axis=1)


def anchor_root(member, edge_weight):
    return lax.rsqrt(jnp.sum(member * edge_weight[None, :], axis=1))


def dest_operator(dst_edges, dst_weight):
    dst_member = corridor_table(dst_edges, dst_weight.shape[0])
    dst_degree = jnp.sum(dst_member * dst_weight[None, :], axis=1)
    edge_sizes = jnp.sum(dst_member, axis=0)
    left_factor = dst_member * lax.rsqrt(dst_degree)[:, None]
    right_factor = left_factor * (dst_weight / edge_sizes)[None, :]
    result = jnp.dot(right_factor, left_factor.T, precision=lax.Precision.HIGHEST)
    return result.astype(jnp.bfloat16)


def back_mix(member_rows, root_rows, totals, mixing):
    spread = jnp.einsum("re,ekc->rkc", member_rows, totals, preferred_element_type=jnp.float32)
    first_layer = (spread * root_rows[:, None, None]).astype(jnp.bfloat16)
    mixed_rows = jnp.einsum("rkc,cf->rkf", first_layer, mixing, preferred_element_type=jnp.float32)
    return mixed_rows.astype(jnp.bfloat16)


def dest_conv(dst_matrix, mixed_rows):
    return jnp.einsum("de,oec->odc", dst_matrix, mixed_rows, preferred_element_type=jnp.float32)


def shards(od_cells, anchor_edges, edge_weight, mixing, dst_edges, dst_weight, out_bias):
    edge_count = edge_weight.shape[0]
    member = corridor_table(anchor_edges, edge_count)
    inverse_root = anchor_root(member, edge_weight)
    member_hot = member.astype(jnp.bfloat16)
    weighted = member_hot * inverse_root.astype(jnp.bfloat16)[:, None]
    partial_sums = jnp.einsum("oe,odc->edc", weighted, od_cells, preferred_element_type=jnp.float32)
    local_counts = jnp.sum(member, axis=0)
    whole_sums, whole_counts = lax.psum((partial_sums, local_counts), "org")
    totals = (whole_sums * (edge_weight / whole_counts)[:, None, None]).astype(jnp.bfloat16)
    dst_matrix = dest_operator(dst_edges, dst_weight)
    mixed_rows = back_mix(member_hot, inverse_root, totals, mixing)
    convolved = dest_conv(
        dst_matrix, lax.all_to_all(mixed_rows, "dst", split_axis=0, concat_axis=1, tiled=True)
    )
    return jnp.maximum(convolved + out_bias[None, None, :], 0.0).astype(jnp.bfloat16)


def solution(mesh):
    in_specs = (P("org", "dst", None), P("org", None), P(), P(), P(), P(), P())
    out_specs = P(("org", "dst"), None, None)
    return jax.shard_map(shards, mesh=mesh, in_specs=in_specs, out_specs=out_specs, check_vma=False)
```

profile of v0, /device:TPU:13, one launch (start us, length us, event | category | flops | bytes accessed | tf_op | source)
XLA Modules:
  0.0 465.9 jit_solution(12960962080524107790)
XLA Ops:
  6.5 0.0 copy-start
  6.5 0.0 all-reduce.2.cloned.1.call-start
  6.5 4.1 convert_reduce_fusion
  10.7 1.0 multiply_reduce_fusion
  11.7 0.0 copy-start.2
  11.7 14.7 %fusion.1 = f32[256,32,128]{2,0,1:T(8,128)} fusion(bf16[2048,32,128]{2,1,0:T(8,128)(2,1)} %param.7, bf16[2048]{0:T(1024)(128)(2,1)S(1)} %get-tuple-element.9, f32[2048,256]{1,0:T(8,128)S(1)} %get-tuple-element.6), kind=kOutput, calls=%fused_computation.3 | convolution fusion | flops 4297588736 | bytes 23072768 | tf_op jit(solution)/shard_map/oe,odc->edc/dot_general | solution.py:43
  26.5 0.0 all-reduce.2.cloned.1.call-update
  26.5 12.9 %psum.15 = f32[256]{0:T(256)S(1)} all-reduce(f32[256]{0:T(256)S(1)} %get-tuple-element.5), channel_id=1, replica_groups=mesh['org'=8,'dst'=4] {'org'}, use_global_device_ids=true, to_apply=%region_4.0 | all-reduce | flops 256 | bytes 2048 | tf_op jit(solution)/shard_map/psum | solution.py:45
  39.3 0.0 copy-done.2
  39.4 143.1 %all-reduce.2.cloned.1.call-done = f32[256,32,128]{2,0,1:T(8,128)} async-done(((f32[256,32,128]{2,0,1:T(8,128)}), f32[256,32,128]{2,0,1:T(8,128)}) %all-reduce.2.cloned.1.call-update) | async-done | bytes 4194320 | tf_op jit(solution)/shard_map/psum | solution.py:45
  182.4 0.0 copy-done
  182.4 13.9 %convolution_convert_fusion = bf16[2048,32,128]{2,0,1:T(8,128)(2,1)} fusion(f32[2048]{0:T(1024)S(1)} %get-tuple-element.10, f32[256,32,128]{2,0,1:T(8,128)} %all-reduce.2.cloned.1.call-done, f32[256]{0:T(256)S(1)} %div.6, f32[2048,256]{1,0:T(8,128)S(1)} %get-tuple-element.6, bf16[128,128]{1,0:T(8,128)(2,1)S(1)} %copy-done), kind=kOutput, calls=%fused_computation.5 | convolution fusion | flops 6470238208 | bytes 23110656 | tf_op jit(solution)/shard_map/rkc,cf->rkf/dot_general | solution.py:29
  196.3 18.6 %copy.34 = bf16[2048,32,128]{2,1,0:T(8,128)(2,1)} copy(bf16[2048,32,128]{2,0,1:T(8,128)(2,1)} %convolution_convert_fusion) | data formatting | bytes 33554432 | tf_op jit(solution)/shard_map/convert_element_type | solution.py:30
  214.9 0.0 copy-start.4
  214.9 0.0 copy-start.5
  214.9 7.9 %all-to-all-start = ((bf16[2048,32,128]{2,1,0:T(8,128)(2,1)}), bf16[2048,32,128]{2,1,0:T(8,128)(2,1)}, u32[]{:S(2)}, u32[]{:S(2)}) async-start(bf16[2048,32,128]{2,1,0:T(8,128)(2,1)} %copy.34), calls=%async_computation | async-start | bytes 33554432 | tf_op jit(solution)/shard_map/all_to_all | solution.py:50
  222.8 0.0 copy-done.4
  222.8 0.1 convert_reduce_fusion.2
  223.0 0.0 copy-done.5
  223.0 0.1 multiply_reduce_fusion.1
  223.1 0.3 fusion.5
  223.4 181.6 %all-to-all-done = bf16[2048,32,128]{2,1,0:T(8,128)(2,1)} async-done(((bf16[2048,32,128]{2,1,0:T(8,128)(2,1)}), bf16[2048,32,128]{2,1,0:T(8,128)(2,1)}, u32[]{:S(2)}, u32[]{:S(2)}) %all-to-all-start) | async-done | bytes 16777248 | tf_op jit(solution)/shard_map/all_to_all | solution.py:50
  405.1 0.0 copy-start.3
  405.1 15.6 %copy.35 = bf16[512,4,32,128]{3,2,1,0:T(8,128)(2,1)} copy(bf16[512,4,32,128]{3,2,0,1:T(8,128)(2,1)} %bitcast.4) | data formatting | bytes 33554432 | tf_op jit(solution)/shard_map/all_to_all | solution.py:50
  420.6 0.0 copy-done.3
  420.6 0.0 copy-start.1
  420.6 16.1 %fusion = bf16[512,128,128]{1,2,0:T(8,128)(2,1)} fusion(f32[128]{0:T(128)S(1)} %copy-done.3, bf16[512,128,128]{2,1,0:T(8,128)(2,1)} %bitcast.20, bf16[128,128,1]{1,0,2:T(8,128)(2,1)S(1)} %fusion.5), kind=kOutput, calls=%fused_computation.2 | convolution fusion | flops 2172649472 | bytes 33587712 | tf_op jit(solution)/shard_map/de,oec->odc/dot_general | solution.py:34
  436.7 22.4 %copy.37 = bf16[512,128,128]{2,1,0:T(8,128)(2,1)} copy(bf16[512,128,128]{1,2,0:T(8,128)(2,1)} %fusion) | data formatting | bytes 33554432 | tf_op jit(solution)/shard_map/convert_element_type | solution.py:52
  459.1 0.0 copy-done.1
  (4 shorter events, 0.0 us)
Async XLA Ops:
  6.5 175.9 %copy-start = (bf16[128,128]{1,0:T(8,128)(2,1)S(1)}, bf16[128,128]{1,0:T(8,128)(2,1)}, u32[]{:S(2)}) copy-start(bf16[128,128]{1,0:T(8,128)(2,1)} %param.10) | copy-start | bytes 98308
  6.5 175.9 %all-reduce.2.cloned.1.call-start = ((), (), s32[]{:S(2)}) async-start(), calls=%async_computation.1 | async-start | bytes 8388608 | tf_op jit(solution)/shard_map/psum | solution.py:45
  11.7 27.6 %copy-start.2 = (f32[256]{0:T(256)S(1)}, f32[256]{0:T(256)}, u32[]{:S(2)}) copy-start(f32[256]{0:T(256)} %param.9) | copy-start | bytes 3076
  214.9 7.9 %copy-start.4 = (s32[128,3]{0,1:T(4,128)S(1)}, s32[128,3]{0,1:T(4,128)}, u32[]{:S(2)}) copy-start(s32[128,3]{0,1:T(4,128)} %param.11) | copy-start | bytes 4612
  214.9 8.0 %copy-start.5 = (f32[128]{0:T(128)S(1)}, f32[128]{0:T(128)}, u32[]{:S(2)}) copy-start(f32[128]{0:T(128)} %param.12) | copy-start | bytes 1540
  214.9 190.1 %all-to-all-start = ((bf16[2048,32,128]{2,1,0:T(8,128)(2,1)}), bf16[2048,32,128]{2,1,0:T(8,128)(2,1)}, u32[]{:S(2)}, u32[]{:S(2)}) async-start(bf16[2048,32,128]{2,1,0:T(8,128)(2,1)} %copy.34), calls=%async_computation | async-start | bytes 33554432 | tf_op jit(solution)/shard_map/all_to_all | solution.py:50
  405.1 15.6 %copy-start.3 = (f32[128]{0:T(128)S(1)}, f32[128]{0:T(128)}, u32[]{:S(2)}) copy-start(f32[128]{0:T(128)} %param.13) | copy-start | bytes 1540
  420.6 38.5 %copy-start.1 = (bf16[128,128]{1,0:T(8,128)(2,1)S(1)}, bf16[128,128]{1,0:T(8,128)(2,1)}, u32[]{:S(2)}) copy-start(bf16[128,128]{1,0:T(8,128)(2,1)} %param.10) | copy-start | bytes 98308
Sparse Core Ops, SparseCore 0:
  26.6 155.7 all-reduce.1
where the time goes:
time: 471 us; the launch traced here: 466 us
  waiting for transfers between devices  325 us (69%)
  local copies, waits for them, and re-layouts  56.5 us (12%)
  matrix products  45.1 us (10%)
  between operations  13.4 us (3%)
  blocking collectives  12.9 us (3%)
  starting transfers between devices  7.91 us (2%)
  other arithmetic  5.41 us (1%)
    all_to_all x1, waiting for transfers between devices, shards(): lax.all_to_all(mixed_rows, 'dst', split_axis=0, concat_axis=1, tiled=True)  182 us
    psum x1, waiting for transfers between devices, shards(): whole_sums, whole_counts = lax.psum((partial_sums, local_counts), 'org')  143 us
    convert_element_type x1, local copies, waits for them, and re-layouts, shards(): jnp.maximum(convolved + out_bias[None, None, :], 0.0).astype(jnp.bfloat16)  22.4 us
    convert_element_type x1, local copies, waits for them, and re-layouts, back_mix(): return mixed_rows.astype(jnp.bfloat16)  18.6 us
    dot_general x1, matrix products, dest_conv(): jnp.einsum('de,oec->odc', dst_matrix, mixed_rows, preferred_element_type=...  16.1 us
    all_to_all x1, local copies, waits for them, and re-layouts, shards(): lax.all_to_all(mixed_rows, 'dst', split_axis=0, concat_axis=1, tiled=True)  15.6 us
    dot_general x1, matrix products, shards(): jnp.einsum('oe,odc->edc', weighted, od_cells, preferred_element_type=jnp....  14.7 us
    dot_general x1, matrix products, back_mix(): jnp.einsum('rkc,cf->rkf', first_layer, mixing, preferred_element_type=jnp...  13.9 us
  transfers between devices with their start and end apart: 2, of which 2 were waited for; matrix products, arithmetic and copies ran while one was open for 0% of the time, Pallas kernels for 0%

commit v1 on v0

v1 whole, which is shorter than its diff:
```python
import jax
import jax.numpy as jnp
from jax import lax
from jax.sharding import PartitionSpec as P


def corridor_table(edge_ids, edge_count):
    columns = jnp.arange(edge_count, dtype=jnp.int32)
    return jnp.sum((edge_ids[:, :, None] == columns[None, None, :]).astype(jnp.float32), axis=1)


def dest_operator(dst_edges, dst_weight):
    dst_member = corridor_table(dst_edges, dst_weight.shape[0])
    dst_degree = jnp.sum(dst_member * dst_weight[None, :], axis=1)
    edge_sizes = jnp.sum(dst_member, axis=0)
    left_factor = dst_member * lax.rsqrt(dst_degree)[:, None]
    right_factor = left_factor * (dst_weight / edge_sizes)[None, :]
    result = jnp.dot(right_factor, left_factor.T, precision=lax.Precision.HIGHEST)
    return result.astype(jnp.bfloat16)


def shards(od_cells, anchor_edges, edge_weight, mixing, dst_edges, dst_weight, out_bias):
    edge_count = edge_weight.shape[0]
    n_org = lax.axis_size("org")
    n_dst = lax.axis_size("dst")
    member = corridor_table(anchor_edges, edge_count)
    inverse_root = lax.rsqrt(jnp.sum(member * edge_weight[None, :], axis=1))
    member_hot = member.astype(jnp.bfloat16)
    weighted = member_hot * inverse_root.astype(jnp.bfloat16)[:, None]
    whole_counts = lax.psum(jnp.sum(member, axis=0), "org")
    partial_sums = jnp.einsum("oe,odc->edc", weighted, od_cells, preferred_element_type=jnp.float32)
    own = edge_count // n_org
    parts = partial_sums.astype(jnp.bfloat16).reshape((n_org, own) + partial_sums.shape[1:])
    parts = lax.all_to_all(parts, "org", split_axis=0, concat_axis=0, tiled=True)
    sums = jnp.sum(parts.astype(jnp.float32), axis=0)
    first = lax.axis_index("org") * own
    scale = lax.dynamic_slice_in_dim(edge_weight / whole_counts, first, own, 0)
    totals = (sums * scale[:, None, None]).astype(jnp.bfloat16)
    mixed = jnp.einsum("ekc,cf->ekf", totals, mixing, preferred_element_type=jnp.float32).astype(jnp.bfloat16)
    mixed = lax.all_to_all(mixed, "dst", split_axis=0, concat_axis=1, tiled=True)
    dst_matrix = dest_operator(dst_edges, dst_weight)
    table = jnp.einsum("dk,ekc->edc", dst_matrix, mixed, preferred_element_type=jnp.float32).astype(jnp.bfloat16)
    table = lax.all_gather(table, ("org", "dst"), axis=0, tiled=True)
    rows = anchor_edges.shape[0] // n_dst
    start = lax.axis_index("dst") * rows
    own_member = lax.dynamic_slice_in_dim(member_hot, start, rows, 0)
    own_root = lax.dynamic_slice_in_dim(inverse_root, start, rows, 0)
    spread = jnp.einsum("re,edc->rdc", own_member, table, preferred_element_type=jnp.float32)
    result = spread * own_root[:, None, None] + out_bias[None, None, :]
    return jnp.maximum(result, 0.0).astype(jnp.bfloat16)


def solution(mesh):
    in_specs = (P("org", "dst", None), P("org", None), P(), P(), P(), P(), P())
    out_specs = P(("org", "dst"), None, None)
    return jax.shard_map(shards, mesh=mesh, in_specs=in_specs, out_specs=out_specs, check_vma=False)
```

time: 471 us -> 225 us (0.48)
  waiting for transfers between devices: 325 us -> 82 us
  blocking collectives: 12.9 us -> 53 us
  local copies, waits for them, and re-layouts: 56.5 us -> 21.4 us
  matrix products: 45.1 us -> 35 us
    all_to_all x1 -> x2, waiting for transfers between devices: 182 us -> 4.7 us  [the longest x1 4.7 us: shards(): lax.all_to_all(mixed, 'dst', split_axis=0, concat_axis=1, tiled=True)]
    psum x1 -> x0, waiting for transfers between devices: 143 us -> none  [shards(): whole_sums, whole_counts = lax.psum((partial_sums, local_counts), 'org')]
    all_gather x0 -> x1, waiting for transfers between devices: none -> 77.2 us  [shards(): table = lax.all_gather(table, ('org', 'dst'), axis=0, tiled=True)]
    psum x1, blocking collectives: 12.9 us -> 53 us  [shards(): whole_counts = lax.psum(jnp.sum(member, axis=0), 'org')]
    convert_element_type x2, local copies, waits for them, and re-layouts: 41 us -> 19.5 us  [the longest x1 18.6 us: shards(): return jnp.maximum(result, 0.0).astype(jnp.bfloat16)]
    all_to_all x1, local copies, waits for them, and re-layouts: 15.6 us -> 0.02 us  [shards(): lax.all_to_all(mixed, 'dst', split_axis=0, concat_axis=1, tiled=True)]
    dot_general x2 -> x3, matrix products: 30 us -> 21.4 us  [the longest x1 20.2 us: shards(): jnp.einsum('re,edc->rdc', own_member, table, preferred_element_type=jnp.f...]
    all_to_all x1 -> x2, starting transfers between devices: 7.9 us -> 12.4 us  [the longest x1 6.77 us: shards(): lax.all_to_all(mixed, 'dst', split_axis=0, concat_axis=1, tiled=True)]
  transfers between devices with their start and end apart: 2 -> 3, of which waited for: 2 -> 2; matrix products, arithmetic and copies ran while one was open for 0% -> 0% of each run, Pallas kernels for 0% -> 0%
where the time goes in v1:
time: 225 us; the launch traced here: 223 us
  waiting for transfers between devices  82 us (36%)
  blocking collectives  53 us (24%)
  matrix products  35 us (16%)
  local copies, waits for them, and re-layouts  21.4 us (10%)
  between operations  13.5 us (6%)
  starting transfers between devices  12.4 us (6%)
  other arithmetic  5.88 us (3%)
    all_gather x1, waiting for transfers between devices, shards(): table = lax.all_gather(table, ('org', 'dst'), axis=0, tiled=True)  77.2 us
    psum x1, blocking collectives, shards(): whole_counts = lax.psum(jnp.sum(member, axis=0), 'org')  53 us
    dot_general x1, matrix products, shards(): jnp.einsum('re,edc->rdc', own_member, table, preferred_element_type=jnp.f...  20.2 us
    convert_element_type x1, local copies, waits for them, and re-layouts, shards(): return jnp.maximum(result, 0.0).astype(jnp.bfloat16)  18.6 us
    dot_general x1, matrix products, shards(): jnp.einsum('oe,odc->edc', weighted, od_cells, preferred_element_type=jnp....  13.3 us
    all_to_all x1, starting transfers between devices, shards(): lax.all_to_all(mixed, 'dst', split_axis=0, concat_axis=1, tiled=True)  6.77 us
    all_to_all x1, starting transfers between devices, shards(): lax.all_to_all(parts, 'org', split_axis=0, concat_axis=0, tiled=True)  5.66 us
    all_to_all x1, waiting for transfers between devices, shards(): lax.all_to_all(mixed, 'dst', split_axis=0, concat_axis=1, tiled=True)  4.7 us
  transfers between devices with their start and end apart: 3, of which 2 were waited for; matrix products, arithmetic and copies ran while one was open for 0% of the time, Pallas kernels for 0%

profile of v1, /device:TPU:13, one launch (start us, length us, event | category | flops | bytes accessed | tf_op | source)
XLA Modules:
  0.0 223.3 jit_solution(10060354081713574057)
XLA Ops:
  6.5 0.0 copy-start
  6.5 4.1 %convert_reduce_fusion = (f32[256]{0:T(256)S(1)}, f32[2048,256]{1,0:T(8,128)S(1)}) fusion(s32[2048,4]{0,1:T(4,128)} %param.8), kind=kLoop, calls=%fused_computation.3 | loop fusion | flops 7864064 | bytes 2130944 | tf_op jit(solution)/shard_map/reduce_sum | solution.py:30
  10.7 1.1 fusion.20
  11.8 13.3 %fusion.3 = bf16[256,32,128]{2,0,1:T(8,128)(2,1)S(1)} fusion(bf16[2048,32,128]{2,1,0:T(8,128)(2,1)} %param.7, bf16[2048,256]{1,0:T(8,128)(2,1)S(1)} %get-tuple-element.9, bf16[2048]{0:T(1024)(128)(2,1)S(1)} %get-tuple-element.11), kind=kOutput, calls=%fused_computation.9 | convolution fusion | flops 4298113024 | bytes 19927040 | tf_op jit(solution)/shard_map/oe,odc->edc/dot_general | solution.py:31
  25.1 0.0 copy-start.1
  25.1 0.0 copy-start.2
  25.1 0.0 copy-start.3
  25.1 0.0 copy-start.4
  25.1 1.8 copy.44
  26.9 5.7 %all-to-all-start = ((bf16[8,32,32,128]{3,1,2,0:T(8,128)(2,1)}), bf16[8,32,32,128]{3,1,2,0:T(8,128)(2,1)S(1)}, u32[]{:S(2)}, u32[]{:S(2)}) async-start(bf16[8,32,32,128]{3,1,2,0:T(8,128)(2,1)} %copy.44), calls=%async_computation | async-start | bytes 4194304 | tf_op jit(solution)/shard_map/all_to_all | solution.py:34
  32.5 53.0 %psum.7 = f32[256]{0:T(256)S(1)} all-reduce(f32[256]{0:T(256)S(1)} %get-tuple-element.5), channel_id=1, replica_groups=mesh['org'=8,'dst'=4] {'org'}, use_global_device_ids=true, to_apply=%region_4.0 | all-reduce | flops 256 | bytes 2048 | tf_op jit(solution)/shard_map/psum | solution.py:30
  85.6 0.0 copy-done.1
  85.6 0.0 copy-done.2
  85.6 0.1 convert_reduce_fusion.3
  85.7 0.0 copy-done.3
  85.7 0.1 dynamic_slice.10
  85.8 0.0 all-to-all-done
  85.8 0.3 convert_reduce_fusion.2
  86.1 0.1 multiply_convert_fusion
  86.2 0.0 copy-done
  86.2 0.9 convolution_convert_fusion.1
  87.2 6.8 %all-to-all-start.1 = ((bf16[32,32,128]{2,1,0:T(8,128)(2,1)}), bf16[32,32,128]{2,1,0:T(8,128)(2,1)S(1)}, u32[]{:S(2)}, u32[]{:S(2)}) async-start(bf16[32,32,128]{2,1,0:T(8,128)(2,1)} %convolution_convert_fusion.1), calls=%async_computation.1 | async-start | bytes 524288 | tf_op jit(solution)/shard_map/all_to_all | solution.py:40
  93.9 0.0 all-gather.2.cloned.1.call-start
  93.9 0.1 multiply_reduce_fusion.1
  94.1 0.4 fusion.7
  94.4 4.7 %all-to-all-done.1 = bf16[32,32,128]{2,1,0:T(8,128)(2,1)S(1)} async-done(((bf16[32,32,128]{2,1,0:T(8,128)(2,1)}), bf16[32,32,128]{2,1,0:T(8,128)(2,1)S(1)}, u32[]{:S(2)}, u32[]{:S(2)}) %all-to-all-start.1) | async-done | bytes 262176 | tf_op jit(solution)/shard_map/all_to_all | solution.py:40
  99.1 0.3 fusion.6
  99.4 0.9 copy.49
  100.3 0.0 all-gather.2.cloned.1.call-update
  100.3 0.1 dynamic_slice.11
  100.4 77.2 %all-gather.2.cloned.1.call-done = bf16[256,128,128]{2,1,0:T(8,128)(2,1)} async-done(((bf16[8,128,128]{2,1,0:T(8,128)(2,1)}), bf16[256,128,128]{2,1,0:T(8,128)(2,1)}) %all-gather.2.cloned.1.call-update) | async-done | bytes 8388624 | tf_op jit(solution)/shard_map/all_gather | solution.py:43
  177.6 0.0 copy-done.4
  177.6 20.2 %maximum_convert_fusion = bf16[512,128,128]{2,0,1:T(8,128)(2,1)} fusion(f32[128]{0:T(128)S(1)} %copy-done.4, f32[512]{0:T(512)S(1)} %dynamic_slice.11, bf16[256,128,128]{2,1,0:T(8,128)(2,1)} %all-gather.2.cloned.1.call-done, bf16[2048,256]{1,0:T(8,128)(2,1)S(1)} %get-tuple-element.9, s32[]{:T(128)S(6)} %select_n.7), kind=kOutput, calls=%fused_computation | convolution fusion | flops 4328521728 | bytes 25430532 | tf_op jit(solution)/shard_map/re,edc->rdc/dot_general | solution.py:48
  197.8 18.6 %copy.51 = bf16[512,128,128]{2,1,0:T(8,128)(2,1)} copy(bf16[512,128,128]{2,0,1:T(8,128)(2,1)} %maximum_convert_fusion) | data formatting | bytes 33554432 | tf_op jit(solution)/shard_map/convert_element_type | solution.py:50
  (5 shorter events, 0.0 us)
Async XLA Ops:
  6.5 79.7 %copy-start = (bf16[128,128]{1,0:T(8,128)(2,1)S(1)}, bf16[128,128]{1,0:T(8,128)(2,1)}, u32[]{:S(2)}) copy-start(bf16[128,128]{1,0:T(8,128)(2,1)} %param.10) | copy-start | bytes 98308
  25.1 60.5 %copy-start.1 = (f32[256]{0:T(256)S(1)}, f32[256]{0:T(256)}, u32[]{:S(2)}) copy-start(f32[256]{0:T(256)} %param.9) | copy-start | bytes 3076
  25.1 60.5 %copy-start.2 = (s32[128,3]{0,1:T(4,128)S(1)}, s32[128,3]{0,1:T(4,128)}, u32[]{:S(2)}) copy-start(s32[128,3]{0,1:T(4,128)} %param.11) | copy-start | bytes 4612
  25.1 60.6 %copy-start.3 = (f32[128]{0:T(128)S(1)}, f32[128]{0:T(128)}, u32[]{:S(2)}) copy-start(f32[128]{0:T(128)} %param.12) | copy-start | bytes 1540
  25.1 152.5 %copy-start.4 = (f32[128]{0:T(128)S(1)}, f32[128]{0:T(128)}, u32[]{:S(2)}) copy-start(f32[128]{0:T(128)} %param.13) | copy-start | bytes 1540
  26.9 58.9 %all-to-all-start = ((bf16[8,32,32,128]{3,1,2,0:T(8,128)(2,1)}), bf16[8,32,32,128]{3,1,2,0:T(8,128)(2,1)S(1)}, u32[]{:S(2)}, u32[]{:S(2)}) async-start(bf16[8,32,32,128]{3,1,2,0:T(8,128)(2,1)} %copy.44), calls=%async_computation | async-start | bytes 4194304 | tf_op jit(solution)/shard_map/all_to_all | solution.py:34
  87.2 11.9 %all-to-all-start.1 = ((bf16[32,32,128]{2,1,0:T(8,128)(2,1)}), bf16[32,32,128]{2,1,0:T(8,128)(2,1)S(1)}, u32[]{:S(2)}, u32[]{:S(2)}) async-start(bf16[32,32,128]{2,1,0:T(8,128)(2,1)} %convolution_convert_fusion.1), calls=%async_computation.1 | async-start | bytes 524288 | tf_op jit(solution)/shard_map/all_to_all | solution.py:40
  93.9 83.7 %all-gather.2.cloned.1.call-start = ((), (), s32[]{:S(2)}) async-start(), calls=%async_computation.2 | async-start | bytes 8650752 | tf_op jit(solution)/shard_map/all_gather | solution.py:43
Sparse Core Ops, SparseCore 0:
  100.4 77.1 all-gather.1

commit v2 on v1

v2 whole, which is shorter than its diff:
```python
import functools

import jax
import jax.numpy as jnp
from jax import lax
from jax.experimental import pallas as pl
from jax.experimental.pallas import tpu as pltpu
from jax.sharding import Mesh, PartitionSpec as P

BF16 = jnp.bfloat16
F32 = jnp.float32
COUNT_BASE = 128.0
HEAD = 16


def corridor_table(edge_ids, edge_count):
    columns = jnp.arange(edge_count, dtype=jnp.int32)
    return jnp.sum((edge_ids[:, :, None] == columns[None, None, :]).astype(F32), axis=1)


def dest_operator(dst_edges, dst_weight):
    dst_member = corridor_table(dst_edges, dst_weight.shape[0])
    dst_degree = jnp.sum(dst_member * dst_weight[None, :], axis=1)
    edge_sizes = jnp.sum(dst_member, axis=0)
    left_factor = dst_member * lax.rsqrt(dst_degree)[:, None]
    right_factor = left_factor * (dst_weight / edge_sizes)[None, :]
    result = jnp.dot(right_factor, left_factor.T, precision=lax.Precision.HIGHEST)
    return result.astype(BF16)


def gather_kernel(own, edges_ref, weight_ref, cells_ref, out_ref, root_ref, wide_ref, total_ref, count_ref):
    step = pl.program_id(0)
    last = pl.num_programs(0) - 1
    rows, zones, lanes = cells_ref.shape
    edges = weight_ref.shape[0]

    @pl.when(step == 0)
    def _():
        total_ref[...] = jnp.zeros_like(total_ref)
        count_ref[...] = jnp.zeros_like(count_ref)

    columns = lax.broadcasted_iota(jnp.int32, (edges, rows), 0)
    ids = edges_ref[...]
    member = columns == ids[0:1, :]
    for j in range(1, ids.shape[0]):
        member = jnp.logical_or(member, columns == ids[j : j + 1, :])
    root = lax.rsqrt(jnp.sum(jnp.where(member, weight_ref[...], 0.0), axis=0, keepdims=True))
    root_ref[...] = root
    rounded = root.astype(BF16).astype(F32)
    weighted = jnp.where(member, rounded, 0.0).astype(BF16)
    hot = jnp.where(member, 1.0, 0.0).astype(BF16)
    count_ref[...] += jnp.dot(hot, jnp.ones((rows, lanes), BF16), preferred_element_type=F32)

    part = min(rows, 16)

    def widen(i, carry):
        piece = cells_ref[pl.ds(i * part, part)].astype(F32)
        wide_ref[pl.ds(i * part * zones, part * zones), :] = piece.reshape(part * zones, lanes)
        return carry

    lax.fori_loop(0, rows // part, widen, 0)
    for pair in range(zones // 2):
        left = wide_ref[pl.ds(2 * pair, rows, stride=zones), :].astype(BF16)
        right = wide_ref[pl.ds(2 * pair + 1, rows, stride=zones), :].astype(BF16)
        both = jnp.concatenate([left, right], axis=1)
        total_ref[pair] += jnp.dot(weighted, both, preferred_element_type=F32)

    @pl.when(step == last)
    def _():
        for d in range(zones):
            column = total_ref[d // 2, :, (d % 2) * lanes : (d % 2 + 1) * lanes]
            wide_ref[pl.ds(d, edges, stride=zones), :] = column
        counts = count_ref[...]
        high = jnp.floor(counts * (1.0 / COUNT_BASE))
        low = counts - high * COUNT_BASE
        for block in range(edges // own):
            first = block * own
            data = wide_ref[first * zones : (first + own) * zones, :].astype(BF16)
            out_ref[block, HEAD : HEAD + own * zones, :] = data
            pad = jnp.zeros((HEAD // 2 - own, lanes), F32) if own < HEAD // 2 else None
            head = [high[first : first + own], low[first : first + own]]
            if pad is not None:
                head = [head[0], pad, head[1], pad]
            out_ref[block, 0:HEAD, :] = jnp.concatenate(head, axis=0).astype(BF16)


def partial_sums(cells, edges_t, edge_weight, own):
    anchors, zones, lanes = cells.shape
    edges = edge_weight.shape[0]
    rows = min(512, anchors)
    blocks = edges // own
    wide = max(rows, edges) * zones
    return pl.pallas_call(
        functools.partial(gather_kernel, own),
        grid=(anchors // rows,),
        in_specs=[
            pl.BlockSpec((edges_t.shape[0], rows), lambda i: (0, i)),
            pl.BlockSpec((edges, 1), lambda i: (0, 0)),
            pl.BlockSpec((rows, zones, lanes), lambda i: (i, 0, 0)),
        ],
        out_specs=[
            pl.BlockSpec((blocks, HEAD + own * zones, lanes), lambda i: (0, 0, 0)),
            pl.BlockSpec((1, rows), lambda i: (0, i)),
        ],
        out_shape=[
            jax.ShapeDtypeStruct((blocks, HEAD + own * zones, lanes), BF16),
            jax.ShapeDtypeStruct((1, anchors), F32),
        ],
        scratch_shapes=[
            pltpu.VMEM((wide, lanes), F32),
            pltpu.VMEM((zones // 2, edges, 2 * lanes), F32),
            pltpu.VMEM((edges, lanes), F32),
        ],
        compiler_params=pltpu.CompilerParams(vmem_limit_bytes=48 * 1024 * 1024),
        cost_estimate=pl.CostEstimate(
            flops=2 * anchors * edges * zones * lanes, bytes_accessed=2 * anchors * zones * lanes, transcendentals=0
        ),
    )(edges_t, edge_weight[:, None], cells)


def table_kernel(own, n_org, n_dst, parts_ref, weight_ref, mixing_ref, matrix_ref, out_ref):
    lanes = parts_ref.shape[2]
    zones = (parts_ref.shape[1] - HEAD) // own
    head = parts_ref[0, 0:HEAD, :].astype(F32)
    for j in range(1, n_org):
        head = head + parts_ref[j * n_dst, 0:HEAD, :].astype(F32)
    half = HEAD // 2
    counts = head[0:half] * COUNT_BASE + head[half:HEAD]
    for e in range(own):
        scale = weight_ref[e : e + 1, :] / counts[e : e + 1, :]
        pieces = []
        for k in range(n_dst):
            at = slice(HEAD + e * zones, HEAD + (e + 1) * zones)
            total = parts_ref[k, at, :].astype(F32)
            for j in range(1, n_org):
                total = total + parts_ref[j * n_dst + k, at, :].astype(F32)
            pieces.append(total * scale)
        totals = jnp.concatenate(pieces, axis=0).astype(BF16)
        mixed = jnp.dot(totals, mixing_ref[...], preferred_element_type=F32)
        high = mixed.astype(BF16)
        low = (mixed - high.astype(F32)).astype(BF16)
        both = jnp.dot(matrix_ref[...], jnp.concatenate([high, low], axis=1), preferred_element_type=F32)
        out_ref[e] = (both[:, 0:lanes] + both[:, lanes : 2 * lanes]).astype(BF16)


def table_rows(parts, weight_rows, mixing, matrix, own, n_org, n_dst):
    zones = matrix.shape[0]
    lanes = parts.shape[2]
    whole = pl.BlockSpec(memory_space=pltpu.VMEM)
    return pl.pallas_call(
        functools.partial(table_kernel, own, n_org, n_dst),
        in_specs=[whole] * 4,
        out_specs=whole,
        out_shape=jax.ShapeDtypeStruct((own, zones, lanes), BF16),
        compiler_params=pltpu.CompilerParams(vmem_limit_bytes=32 * 1024 * 1024),
        cost_estimate=pl.CostEstimate(flops=8 * own * zones * lanes * lanes, bytes_accessed=parts.size * 2, transcendentals=0),
    )(parts, weight_rows, mixing, matrix)


def spread_kernel(places_ref, root_ref, near_ref, far_ref, bias_ref, out_ref, table_ref, sems):
    step = pl.program_id(0)
    rows, zones, lanes = out_ref.shape
    half = near_ref.shape[0]

    @pl.when(step == 0)
    def _():
        first = pltpu.make_async_copy(near_ref, table_ref.at[pl.ds(0, half)], sems.at[0])
        second = pltpu.make_async_copy(far_ref, table_ref.at[pl.ds(half, half)], sems.at[1])
        first.start()
        second.start()
        first.wait()
        second.wait()

    bias = bias_ref[...]
    count = places_ref.shape[0]

    def one(i, carry):
        at = step * rows + i
        scale = root_ref[0, at]
        total = table_ref[places_ref[0, at]].astype(F32)
        for j in range(1, count):
            total = total + table_ref[places_ref[j, at]].astype(F32)
        out_ref[i] = jnp.maximum(total * scale + bias, 0.0).astype(BF16)
        return carry

    lax.fori_loop(0, rows, one, 0)


def spread(places, root, near, far, bias):
    anchors = places.shape[1]
    half, zones, lanes = near.shape
    rows = min(32, anchors)
    return pl.pallas_call(
        spread_kernel,
        grid=(anchors // rows,),
        in_specs=[
            pl.BlockSpec(memory_space=pltpu.SMEM),
            pl.BlockSpec(memory_space=pltpu.SMEM),
            pl.BlockSpec(memory_space=pl.ANY),
            pl.BlockSpec(memory_space=pl.ANY),
            pl.BlockSpec((1, lanes), lambda i: (0, 0)),
        ],
        out_specs=pl.BlockSpec((rows, zones, lanes), lambda i: (i, 0, 0)),
        out_shape=jax.ShapeDtypeStruct((anchors, zones, lanes), BF16),
        scratch_shapes=[pltpu.VMEM((2 * half, zones, lanes), BF16), pltpu.SemaphoreType.DMA((2,))],
        compiler_params=pltpu.CompilerParams(vmem_limit_bytes=32 * 1024 * 1024),
        cost_estimate=pl.CostEstimate(
            flops=8 * anchors * zones * lanes, bytes_accessed=2 * (anchors + 2 * half) * zones * lanes, transcendentals=0
        ),
    )(places, root, near, far, bias)


def shards(od_cells, anchor_edges, edge_weight, mixing, dst_edges, dst_weight, out_bias):
    n_org = lax.axis_size("org")
    n_core = lax.axis_size("core")
    n_dst = lax.axis_size("far") * n_core
    own = edge_weight.shape[0] // (n_org * n_dst)
    everyone = ("org", "far", "core")
    edges_t = anchor_edges.T
    parts, roots = partial_sums(od_cells, edges_t, edge_weight, own)
    parts = lax.all_to_all(parts, everyone, split_axis=0, concat_axis=0, tiled=True)
    own_weight = lax.dynamic_slice_in_dim(edge_weight, lax.axis_index(everyone) * own, own, 0)
    weight_rows = jnp.broadcast_to(own_weight[:, None], (own, parts.shape[2]))
    matrix = dest_operator(dst_edges, dst_weight)
    block = table_rows(parts, weight_rows, mixing, matrix, own, n_org, n_dst)
    near = lax.all_gather(block, ("org", "far"), axis=0, tiled=True)
    far = lax.ppermute(near, "core", [(c, (c + 1) % n_core) for c in range(n_core)])
    rows = anchor_edges.shape[0] // n_dst
    start = lax.axis_index(("far", "core")) * rows
    ids = lax.dynamic_slice_in_dim(edges_t, start, rows, 1)
    holder = ids // own
    places = (holder // n_core) * own + ids % own
    places = places + jnp.where(holder % n_core == lax.axis_index("core"), 0, near.shape[0])
    own_root = lax.dynamic_slice_in_dim(roots, start, rows, 1)
    return spread(places, own_root, near, far, out_bias[None, :])


def solution(mesh):
    n_org, n_dst = mesh.devices.shape
    fine = Mesh(mesh.devices.reshape(n_org, n_dst // 2, 2), ("org", "far", "core"))
    dst = ("far", "core")
    in_specs = (P("org", dst, None), P("org", None), P(), P(), P(), P(), P())
    out_specs = P(("org",) + dst, None, None)
    return jax.shard_map(shards, mesh=fine, in_specs=in_specs, out_specs=out_specs, check_vma=False)
```

time: 225 us -> 218 us (0.969)
  Pallas kernels: 0 us -> 56.6 us
  blocking collectives: 53 us -> 0 us
  waiting for transfers between devices: 82 us -> 131 us
  matrix products: 35 us -> 0.35 us
  local copies, waits for them, and re-layouts: 21.4 us -> 5.28 us
  other arithmetic: 5.88 us -> 0.98 us
  starting transfers between devices: 12.4 us -> 8.17 us
    pallas_call x0 -> x3, Pallas kernels: none -> 56.6 us  [the longest x1 32.3 us: partial_sums(): pl.pallas_call(functools.partial(gather_kernel, own), grid=(anchors // ro...]
    psum x1 -> x0, blocking collectives: 53 us -> none  [shards(): whole_counts = lax.psum(jnp.sum(member, axis=0), 'org')]
    all_to_all x2 -> x1, waiting for transfers between devices: 4.7 us -> 47.6 us  [shards(): lax.all_to_all(parts, everyone, split_axis=0, concat_axis=0, tiled=True)]
    dot_general x4 -> x0, matrix products: 34.7 us -> none  [the longest x1 20.2 us: shards(): jnp.einsum('re,edc->rdc', own_member, table, preferred_element_type=jnp.f...]
    convert_element_type x2 -> x0, local copies, waits for them, and re-layouts: 19.5 us -> none  [the longest x1 18.6 us: shards(): return jnp.maximum(result, 0.0).astype(jnp.bfloat16)]
    ppermute x0 -> x1, waiting for transfers between devices: none -> 6.39 us  [shards(): lax.ppermute(near, 'core', [(c, (c + 1) % n_core) for c in range(n_core)])]
    all_to_all x2 -> x1, starting transfers between devices: 12.4 us -> 6.3 us  [shards(): lax.all_to_all(parts, everyone, split_axis=0, concat_axis=0, tiled=True)]
    reduce_sum x2 -> x0, other arithmetic: 4.43 us -> none  [the longest x1 4.14 us: shards(): whole_counts = lax.psum(jnp.sum(member, axis=0), 'org')]
  transfers between devices with their start and end apart: 3 -> 3, of which waited for: 2 -> 3; matrix products, arithmetic and copies ran while one was open for 0% -> 1% of each run, Pallas kernels for 0% -> 0%
where the time goes in v2:
time: 218 us; the launch traced here: 216 us
  waiting for transfers between devices  131 us (60%)
  Pallas kernels  56.6 us (26%)
  between operations  13.5 us (6%)
  starting transfers between devices  8.17 us (4%)
  local copies, waits for them, and re-layouts  5.28 us (2%)
    all_gather x1, waiting for transfers between devices, shards(): near = lax.all_gather(block, ('org', 'far'), axis=0, tiled=True)  77.2 us
    all_to_all x1, waiting for transfers between devices, shards(): lax.all_to_all(parts, everyone, split_axis=0, concat_axis=0, tiled=True)  47.6 us
    pallas_call x1, Pallas kernels, partial_sums(): pl.pallas_call(functools.partial(gather_kernel, own), grid=(anchors // ro...  32.3 us
    pallas_call x1, Pallas kernels, spread(): pl.pallas_call(spread_kernel, grid=(anchors // rows,), in_specs=[pl.Block...  22.7 us
    ppermute x1, waiting for transfers between devices, shards(): lax.ppermute(near, 'core', [(c, (c + 1) % n_core) for c in range(n_core)])  6.39 us
    all_to_all x1, starting transfers between devices, shards(): lax.all_to_all(parts, everyone, split_axis=0, concat_axis=0, tiled=True)  6.3 us
  transfers between devices with their start and end apart: 3, of which 3 were waited for; matrix products, arithmetic and copies ran while one was open for 1% of the time, Pallas kernels for 0%

profile of v2, /device:TPU:13, one launch (start us, length us, event | category | flops | bytes accessed | tf_op | source)
XLA Modules:
  0.0 216.1 jit_solution(6172263730686866230)
XLA Ops:
  6.5 0.8 copy.13.weight_ref
  7.3 0.0 copy-start.2
  7.4 0.8 copy-done.2
  8.1 32.3 %shard_map.73 = (bf16[32,272,128]{2,1,0:T(8,128)(2,1)S(1)}, f32[1,2048]{1,0:T(1,128)S(1)}) custom-call(s32[4,2048]{1,0:T(4,128)S(1)} %bitcast.21, f32[256,1]{1,0:T(8,128)S(1)} %copy.13.weight_ref, bf16[2048,32,128]{2,1,0:T(8,128)(2,1)} %cells_ref.1), custom_call_target="tpu_custom_call" | custom-call | flops 4294967296 | bytes 16777216 | tf_op jit(solution)/shard_map/pallas_call | solution.py:93
  40.4 0.0 copy-start.1
  40.4 1.4 copy-done.1
  41.8 0.0 copy-start.6
  41.8 0.0 copy-start.5
  41.8 0.0 copy-start.7
  41.8 0.0 copy-start.3
  41.8 0.0 copy-start.4
  41.8 6.3 %all-to-all-start = ((bf16[32,272,128]{2,1,0:T(8,128)(2,1)}), bf16[32,272,128]{2,1,0:T(8,128)(2,1)S(1)}, u32[]{:S(2)}, u32[]{:S(2)}) async-start(bf16[32,272,128]{2,1,0:T(8,128)(2,1)} %copy-done.1), calls=%async_computation | async-start | bytes 4456448 | tf_op jit(solution)/shard_map/all_to_all | solution.py:221
  48.1 0.0 all-gather.2.cloned.1.call-start
  48.2 0.0 copy-done.6
  48.2 0.1 dynamic_slice.11
  48.3 0.0 copy-done.5
  48.3 0.1 convert_reduce_fusion
  48.4 0.0 copy-done.7
  48.4 0.1 multiply_reduce_fusion
  48.5 0.3 convolution_convert_fusion.matrix_ref
  48.9 47.6 %all-to-all-done.parts_ref = bf16[32,272,128]{2,1,0:T(8,128)(2,1)S(1)} async-done(((bf16[32,272,128]{2,1,0:T(8,128)(2,1)}), bf16[32,272,128]{2,1,0:T(8,128)(2,1)S(1)}, u32[]{:S(2)}, u32[]{:S(2)}) %all-to-all-start) | async-done | bytes 2228256 | tf_op jit(solution)/shard_map/all_to_all | solution.py:221
  96.5 0.1 broadcast_in_dim.14.weight_ref
  96.6 0.0 copy-done.3
  96.6 1.6 shard_map.74
  98.2 0.0 all-gather.2.cloned.1.call-update
  98.2 77.2 %all-gather.2.cloned.1.call-done.near_ref = bf16[128,128,128]{2,1,0:T(8,128)(2,1)} async-done(((bf16[8,128,128]{2,1,0:T(8,128)(2,1)}), bf16[128,128,128]{2,1,0:T(8,128)(2,1)}) %all-gather.2.cloned.1.call-update) | async-done | bytes 4194320 | tf_op jit(solution)/shard_map/all_gather | solution.py:226
  175.5 1.8 collective-permute-start
  177.3 0.7 fusion.6.places_ref
  178.0 6.4 %collective-permute-done.far_ref = bf16[128,128,128]{2,1,0:T(8,128)(2,1)} collective-permute-done((bf16[128,128,128]{2,1,0:T(8,128)(2,1)}, bf16[128,128,128]{2,1,0:T(8,128)(2,1)}, u32[]{:S(2)}, u32[]{:S(2)}) %collective-permute-start) | collective-permute-done | bytes 4194336 | tf_op jit(solution)/shard_map/ppermute | solution.py:227
  184.4 0.0 copy-done.4
  184.4 0.0 copy-start
  184.4 2.2 %copy-done = bf16[128,128,128]{2,1,0:T(8,128)(2,1)S(1)} copy-done((bf16[128,128,128]{2,1,0:T(8,128)(2,1)S(1)}, bf16[128,128,128]{2,1,0:T(8,128)(2,1)}, u32[]{:S(2)}) %copy-start) | copy-done | bytes 4194328
  186.6 22.7 %shard_map.75 = bf16[512,128,128]{2,1,0:T(8,128)(2,1)} custom-call(s32[4,512]{1,0:T(4,128)S(1)} %fusion.6.places_ref, f32[1,512]{1,0:T(1,128)S(1)} %constant_dynamic-slice_fusion.root_ref, bf16[128,128,128]{2,1,0:T(8,128)(2,1)S(1)} %copy-done, bf16[128,128,128]{2,1,0:T(8,128)(2,1)} %collective-permute-done.far_ref, f32[1,128]{1,0:T(1,128)S(1)} %bitcast.22), custom_call_target="tpu_custom_call" | custom-call | flops 67108864 | bytes 25165824 | tf_op jit(solution)/shard_map/pallas_call | solution.py:193
  (3 shorter events, 0.0 us)
Async XLA Ops:
  7.3 0.8 copy-start.2
  40.4 1.4 copy-start.1
  41.8 6.4 %copy-start.6 = (f32[256]{0:T(256)S(1)}, f32[256]{0:T(256)}, u32[]{:S(2)}) copy-start(f32[256]{0:T(256)} %param.9) | copy-start | bytes 3076
  41.8 6.5 %copy-start.5 = (s32[128,3]{0,1:T(4,128)S(1)}, s32[128,3]{0,1:T(4,128)}, u32[]{:S(2)}) copy-start(s32[128,3]{0,1:T(4,128)} %param.11) | copy-start | bytes 4612
  41.8 6.6 %copy-start.7 = (f32[128]{0:T(128)S(1)}, f32[128]{0:T(128)}, u32[]{:S(2)}) copy-start(f32[128]{0:T(128)} %param.12) | copy-start | bytes 1540
  41.8 54.8 %copy-start.3 = (bf16[128,128]{1,0:T(8,128)(2,1)S(1)}, bf16[128,128]{1,0:T(8,128)(2,1)}, u32[]{:S(2)}) copy-start(bf16[128,128]{1,0:T(8,128)(2,1)} %mixing_ref.1) | copy-start | bytes 98308
  41.8 142.6 %copy-start.4 = (f32[128]{0:T(128)S(1)}, f32[128]{0:T(128)}, u32[]{:S(2)}) copy-start(f32[128]{0:T(128)} %param.13) | copy-start | bytes 1540
  41.8 54.7 %all-to-all-start = ((bf16[32,272,128]{2,1,0:T(8,128)(2,1)}), bf16[32,272,128]{2,1,0:T(8,128)(2,1)S(1)}, u32[]{:S(2)}, u32[]{:S(2)}) async-start(bf16[32,272,128]{2,1,0:T(8,128)(2,1)} %copy-done.1), calls=%async_computation | async-start | bytes 4456448 | tf_op jit(solution)/shard_map/all_to_all | solution.py:221
  48.1 127.4 %all-gather.2.cloned.1.call-start = ((), (), s32[]{:S(2)}) async-start(), calls=%async_computation.1 | async-start | bytes 4456448 | tf_op jit(solution)/shard_map/all_gather | solution.py:226
  175.5 9.0 %collective-permute-start = (bf16[128,128,128]{2,1,0:T(8,128)(2,1)}, bf16[128,128,128]{2,1,0:T(8,128)(2,1)}, u32[]{:S(2)}, u32[]{:S(2)}) collective-permute-start(bf16[128,128,128]{2,1,0:T(8,128)(2,1)} %all-gather.2.cloned.1.call-done.near_ref), channel_id=1, source_target_pairs={{0,1},{1,0},{2,3},{3,2},{4,5},{5,4},{6,7},{7,6},{8,9},{9,8},{10,11... | collective-permute-start | bytes 12582920 | tf_op jit(solution)/shard_map/ppermute | solution.py:227
  184.4 2.2 %copy-start = (bf16[128,128,128]{2,1,0:T(8,128)(2,1)S(1)}, bf16[128,128,128]{2,1,0:T(8,128)(2,1)}, u32[]{:S(2)}) copy-start(bf16[128,128,128]{2,1,0:T(8,128)(2,1)} %all-gather.2.cloned.1.call-done.near_ref) | copy-start | bytes 12582916
Sparse Core Ops, SparseCore 0:
  98.4 77.0 all-gather.1

commit v3 on v2

v3 whole, which is shorter than its diff:
```python
import functools

import jax
import jax.numpy as jnp
from jax import lax
from jax.experimental import pallas as pl
from jax.experimental.pallas import tpu as pltpu
from jax.sharding import Mesh, PartitionSpec as P

BF16 = jnp.bfloat16
F32 = jnp.float32
COUNT_BASE = 128.0
HEAD = 16


def corridor_table(edge_ids, edge_count):
    columns = jnp.arange(edge_count, dtype=jnp.int32)
    return jnp.sum((edge_ids[:, :, None] == columns[None, None, :]).astype(F32), axis=1)


def dest_operator(dst_edges, dst_weight):
    dst_member = corridor_table(dst_edges, dst_weight.shape[0])
    dst_degree = jnp.sum(dst_member * dst_weight[None, :], axis=1)
    edge_sizes = jnp.sum(dst_member, axis=0)
    left_factor = dst_member * lax.rsqrt(dst_degree)[:, None]
    right_factor = left_factor * (dst_weight / edge_sizes)[None, :]
    result = jnp.dot(right_factor, left_factor.T, precision=lax.Precision.HIGHEST)
    return result.astype(BF16)


def gather_kernel(own, group, pitch, edges_ref, weight_ref, cells_ref, out_ref, root_ref, wide_ref, total_ref, count_ref):
    step = pl.program_id(0)
    last = pl.num_programs(0) - 1
    rows, zones, lanes = cells_ref.shape
    edges = total_ref.shape[1]

    @pl.when(step == 0)
    def _():
        total_ref[...] = jnp.zeros_like(total_ref)
        count_ref[...] = jnp.zeros_like(count_ref)

    columns = lax.broadcasted_iota(jnp.int32, (edges, rows), 0)
    ids = edges_ref[...]
    member = columns == ids[0:1, :]
    for j in range(1, ids.shape[0]):
        member = jnp.logical_or(member, columns == ids[j : j + 1, :])
    upright = jnp.transpose(jnp.broadcast_to(weight_ref[...], (lanes, edges)))
    upright = jnp.concatenate([upright] * (rows // lanes), axis=1)
    root = lax.rsqrt(jnp.sum(jnp.where(member, upright, 0.0), axis=0, keepdims=True))
    root_ref[...] = root
    rounded = root.astype(BF16).astype(F32)
    weighted = jnp.where(member, rounded, 0.0).astype(BF16)
    hot = jnp.where(member, 1.0, 0.0).astype(BF16)
    count_ref[...] += jnp.dot(hot, jnp.ones((rows, lanes), BF16), preferred_element_type=F32)

    part = 32
    groups = zones // group
    pairs = group // 2

    def widen(g, first):
        piece = cells_ref[pl.ds(first, part), g * group : (g + 1) * group, :].astype(F32)
        for i in range(part):
            wide_ref[g, pl.ds(pl.multiple_of((first + i) * pitch, 8), group), :] = piece[i]

    def widen_first(i, carry):
        widen(0, i * part)
        return carry

    lax.fori_loop(0, rows // part, widen_first, 0)
    share = rows // part // pairs
    for g in range(groups):
        for pair in range(pairs):
            if g + 1 < groups:
                for i in range(share):
                    widen(g + 1, (pair * share + i) * part)
            left = wide_ref[g, pl.ds(2 * pair, rows, stride=pitch), :].astype(BF16)
            right = wide_ref[g, pl.ds(2 * pair + 1, rows, stride=pitch), :].astype(BF16)
            both = jnp.concatenate([left, right], axis=1)
            total_ref[g * pairs + pair] += jnp.dot(weighted, both, preferred_element_type=F32)

    @pl.when(step == last)
    def _():
        counts = count_ref[...]
        high = jnp.floor(counts * (1.0 / COUNT_BASE))
        low = counts - high * COUNT_BASE
        for block in range(edges // own):
            at = slice(block * own, (block + 1) * own)
            head = [high[at], low[at]]
            if own < HEAD // 2:
                pad = jnp.zeros((HEAD // 2 - own, lanes), F32)
                head = [head[0], pad, head[1], pad]
            out_ref[block, 0:HEAD, :] = jnp.concatenate(head, axis=0).astype(BF16)
            data = []
            for d in range(zones):
                data.append(total_ref[d // 2, at, (d % 2) * lanes : (d % 2 + 1) * lanes])
            out_ref[block, HEAD : HEAD + own * zones, :] = jnp.concatenate(data, axis=0).astype(BF16)


def partial_sums(cells, edges_t, edge_weight, own):
    anchors, zones, lanes = cells.shape
    edges = edge_weight.shape[0]
    rows = min(512, anchors)
    blocks = edges // own
    group = min(zones, 16)
    pitch = group + 8
    return pl.pallas_call(
        functools.partial(gather_kernel, own, group, pitch),
        grid=(anchors // rows,),
        in_specs=[
            pl.BlockSpec((edges_t.shape[0], rows), lambda i: (0, i)),
            pl.BlockSpec((1, edges), lambda i: (0, 0)),
            pl.BlockSpec((rows, zones, lanes), lambda i: (i, 0, 0)),
        ],
        out_specs=[
            pl.BlockSpec((blocks, HEAD + own * zones, lanes), lambda i: (0, 0, 0)),
            pl.BlockSpec((1, rows), lambda i: (0, i)),
        ],
        out_shape=[
            jax.ShapeDtypeStruct((blocks, HEAD + own * zones, lanes), BF16),
            jax.ShapeDtypeStruct((1, anchors), F32),
        ],
        scratch_shapes=[
            pltpu.VMEM((zones // group, rows * pitch, lanes), F32),
            pltpu.VMEM((zones // 2, edges, 2 * lanes), F32),
            pltpu.VMEM((edges, lanes), F32),
        ],
        compiler_params=pltpu.CompilerParams(vmem_limit_bytes=48 * 1024 * 1024),
        cost_estimate=pl.CostEstimate(
            flops=2 * anchors * edges * zones * lanes, bytes_accessed=2 * anchors * zones * lanes, transcendentals=0
        ),
    )(edges_t, edge_weight[None, :], cells)


def table_kernel(own, n_org, n_dst, parts_ref, weight_ref, mixing_ref, matrix_ref, keep_ref, give_ref, mixed_ref):
    lanes = parts_ref.shape[2]
    rows = parts_ref.shape[1] - HEAD
    zones = rows // own
    head = parts_ref[0, 0:HEAD, :].astype(F32)
    for j in range(1, n_org):
        head = head + parts_ref[j * n_dst, 0:HEAD, :].astype(F32)
    half = HEAD // 2
    counts = head[0:half] * COUNT_BASE + head[half:HEAD]
    scale = jnp.concatenate([weight_ref[...] / counts[0:own]] * zones, axis=0)
    for k in range(n_dst):
        total = parts_ref[k, HEAD:, :].astype(F32)
        for j in range(1, n_org):
            total = total + parts_ref[j * n_dst + k, HEAD:, :].astype(F32)
        totals = (total * scale).astype(BF16)
        mixed_ref[k * rows : (k + 1) * rows, :] = jnp.dot(totals, mixing_ref[...], preferred_element_type=F32)
    whole = n_dst * zones
    for e in range(own):
        mixed = mixed_ref[pl.ds(e, whole, stride=own), :] if own > 1 else mixed_ref[...]
        high = mixed.astype(BF16)
        low = (mixed - high.astype(F32)).astype(BF16)
        both = jnp.dot(matrix_ref[...], jnp.concatenate([high, low], axis=1), preferred_element_type=F32)
        result = (both[:, 0:lanes] + both[:, lanes : 2 * lanes]).astype(BF16)
        keep_ref[e] = result[0 : whole // 2]
        give_ref[e] = result[whole // 2 :]


def table_rows(parts, weight_rows, mixing, matrix, own, n_org, n_dst):
    zones = matrix.shape[0]
    lanes = parts.shape[2]
    whole = pl.BlockSpec(memory_space=pltpu.VMEM)
    half = jax.ShapeDtypeStruct((own, zones // 2, lanes), BF16)
    return pl.pallas_call(
        functools.partial(table_kernel, own, n_org, n_dst),
        in_specs=[whole] * 4,
        out_specs=[whole] * 2,
        out_shape=[half, half],
        scratch_shapes=[pltpu.VMEM((zones * own, lanes), F32)],
        compiler_params=pltpu.CompilerParams(vmem_limit_bytes=32 * 1024 * 1024),
        cost_estimate=pl.CostEstimate(flops=8 * own * zones * lanes * lanes, bytes_accessed=parts.size * 2, transcendentals=0),
    )(parts, weight_rows, mixing, matrix)


def spread_kernel(n_long, n_short, half_ref, long_at_ref, short_at_ref, root_ref, bias_ref, *refs):
    longs = refs[:n_long]
    shorts = refs[n_long : n_long + n_short]
    out_ref, long_ref, short_ref, sems = refs[-4:]
    step = pl.program_id(0)
    rows, zones, lanes = out_ref.shape

    @pl.when(step == 0)
    def _():
        copies = []
        for table, sources in ((long_ref, longs), (short_ref, shorts)):
            size = sources[0].shape[0]
            for i, source in enumerate(sources):
                copies.append(pltpu.make_async_copy(source, table.at[pl.ds(i * size, size)], sems.at[len(copies)]))
        for copy in copies:
            copy.start()
        for copy in copies:
            copy.wait()

    bias = bias_ref[...]
    count = long_at_ref.shape[0]
    tile = 16

    def one(i, carry):
        at = step * rows + i
        scale = root_ref[0, at]
        start = 0
        for table, places in ((long_ref, long_at_ref), (short_ref, short_at_ref)):
            spots = [places[j, at] for j in range(count)]
            for first in range(0, table.shape[1], tile):
                total = table[spots[0], first : first + tile, :].astype(F32)
                for spot in spots[1:]:
                    total = total + table[spot, first : first + tile, :].astype(F32)
                value = jnp.maximum(total * scale + bias, 0.0).astype(BF16)
                out_ref[i, start : start + tile, :] = value
                start += tile
        return carry

    lax.fori_loop(0, rows, one, 0, unroll=4)


def spread(half, long_at, short_at, root, bias, longs, shorts, before=None):
    anchors = long_at.shape[1]
    lanes = bias.shape[1]
    zones = longs[0].shape[1] + shorts[0].shape[1]
    rows = min(32, anchors)
    smem = pl.BlockSpec(memory_space=pltpu.SMEM)
    anywhere = pl.BlockSpec(memory_space=pl.ANY)
    tables = [pltpu.VMEM((len(pieces) * pieces[0].shape[0],) + pieces[0].shape[1:], BF16) for pieces in (longs, shorts)]
    operands = [half, long_at, short_at, root, bias] + longs + shorts
    specs = [smem, smem, smem, pl.BlockSpec((1, lanes), lambda i, h: (0, 0))] + [anywhere] * len(longs + shorts)
    aliases = {}
    if before is not None:
        aliases = {len(operands): 0}
        operands.append(before)
        specs.append(anywhere)
    return pl.pallas_call(
        functools.partial(spread_kernel, len(longs), len(shorts)),
        grid_spec=pltpu.PrefetchScalarGridSpec(
            num_scalar_prefetch=1,
            grid=(anchors // rows,),
            in_specs=specs,
            out_specs=pl.BlockSpec((rows, zones, lanes), lambda i, h: (i, h[0], 0)),
            scratch_shapes=tables + [pltpu.SemaphoreType.DMA((len(longs) + len(shorts),))],
        ),
        out_shape=jax.ShapeDtypeStruct((anchors, 2 * zones, lanes), BF16),
        input_output_aliases=aliases,
        compiler_params=pltpu.CompilerParams(vmem_limit_bytes=24 * 1024 * 1024),
        cost_estimate=pl.CostEstimate(
            flops=8 * anchors * zones * lanes, bytes_accessed=2 * anchors * zones * lanes, transcendentals=0
        ),
    )(*operands)


LINE = ("slow", "rest")
SQUARE = ("mid", "near", "core")


def shifted(x, amount):
    size = lax.axis_size(LINE)
    return lax.ppermute(x, LINE, [(i, (i + amount) % size) for i in range(size)])


def crossed(x, turn):
    pairs = []
    for device in range(8):
        core = device % 2
        pairs.append((device, device ^ (2 if core == turn else 4)))
    return lax.ppermute(x, SQUARE, pairs)


def swapped(x):
    return lax.ppermute(x, "core", [(0, 1), (1, 0)])


def gather_table(keep, give):
    size = lax.axis_size(LINE)
    block = jnp.concatenate([keep, swapped(give)], axis=0)
    split = block.shape[1] * 3 // 4
    long, short = block[:, :split], block[:, split:]
    line = [long] + [shifted(long, k) for k in range(1, size)]
    short = jnp.concatenate([short, crossed(short, 0)], axis=0)
    short = jnp.concatenate([short, crossed(short, 1)], axis=0)
    long = jnp.concatenate(line, axis=0)
    first = crossed(long, 0)
    second = crossed(long, 1)
    both = crossed(first, 1)
    shorts = [short] + [shifted(short, k) for k in range(1, size)]
    return [long, first, second, both], shorts


def places_of(ids, core, own):
    rest, size = lax.axis_size("rest"), lax.axis_size(LINE)
    owner = ids // own
    slot = jnp.where(owner % 2 == core, 0, own) + ids % own
    near = jnp.bitwise_xor(owner // 2 % 2, lax.axis_index("near"))
    mid = jnp.bitwise_xor(owner // (4 * rest) % 2, lax.axis_index("mid"))
    line = owner // (8 * rest) * rest + owner // 4 % rest
    line = lax.rem(lax.axis_index(LINE) - line + size, size)
    square = jnp.where(core == 0, 2 * mid + near, 2 * near + mid)
    return (square * size + line) * (2 * own) + slot, (line * 4 + square) * (2 * own) + slot


def shards(od_cells, anchor_edges, edge_weight, mixing, dst_edges, dst_weight, out_bias):
    n_org = lax.axis_size("slow") * lax.axis_size("mid")
    n_dst = lax.axis_size("rest") * lax.axis_size("near") * lax.axis_size("core")
    own = edge_weight.shape[0] // (n_org * n_dst)
    everyone = ("slow", "mid", "rest", "near", "core")
    core = lax.axis_index("core")
    edges_t = anchor_edges.T
    parts, roots = partial_sums(od_cells, edges_t, edge_weight, own)
    parts = lax.all_to_all(parts, everyone, split_axis=0, concat_axis=0, tiled=True)
    own_weight = lax.dynamic_slice_in_dim(edge_weight, lax.axis_index(everyone) * own, own, 0)
    weight_rows = jnp.broadcast_to(own_weight[:, None], (own, parts.shape[2]))
    matrix = dest_operator(dst_edges, dst_weight)
    half = matrix.shape[0] // 2
    matrix = jnp.where(core == 0, matrix, jnp.concatenate([matrix[half:], matrix[:half]], axis=0))
    keep, give = table_rows(parts, weight_rows, mixing, matrix, own, n_org, n_dst)
    longs, shorts = gather_table(keep, give)
    rows = anchor_edges.shape[0] // n_dst
    start = lax.axis_index(("rest", "near", "core")) * rows
    ids = lax.dynamic_slice_in_dim(edges_t, start, rows, 1)
    own_root = lax.dynamic_slice_in_dim(roots, start, rows, 1)
    bias = out_bias[None, :]
    other = 1 - core
    result = spread(core[None], *places_of(ids, core, own), own_root, bias, longs, shorts)
    longs, shorts = [swapped(x) for x in longs], [swapped(x) for x in shorts]
    return spread(other[None], *places_of(ids, other, own), own_root, bias, longs, shorts, result)


def solution(mesh):
    n_org, n_dst = mesh.devices.shape
    fine = Mesh(mesh.devices.reshape(n_org // 2, 2, n_dst // 4, 2, 2), ("slow", "mid", "rest", "near", "core"))
    org, dst = ("slow", "mid"), ("rest", "near", "core")
    in_specs = (P(org, dst, None), P(org, None), P(), P(), P(), P(), P())
    out_specs = P(org + dst, None, None)
    return jax.shard_map(shards, mesh=fine, in_specs=in_specs, out_specs=out_specs, check_vma=False)
```

time: 218 us -> 190 us (0.87)
  the two profiles are of different devices: /device:TPU:13 before, /device:TPU:0 now
where the time goes in v3:
time: 190 us; the launch traced here: 189 us
  waiting for transfers between devices  118 us (62%)
  Pallas kernels  41.8 us (22%)
  starting transfers between devices  21.9 us (12%)
  local copies, waits for them, and re-layouts  6.42 us (3%)
    all_to_all x1, waiting for transfers between devices, shards(): lax.all_to_all(parts, everyone, split_axis=0, concat_axis=0, tiled=True)  51 us
    ppermute x6, waiting for transfers between devices, shifted(): lax.ppermute(x, LINE, [(i, (i + amount) % size) for i in range(size)])  34.9 us
    ppermute x5, waiting for transfers between devices, crossed(): return lax.ppermute(x, SQUARE, pairs)  28.6 us
    pallas_call x2, Pallas kernels, spread(): pl.pallas_call(functools.partial(spread_kernel, len(longs), len(shorts)),...  26.4 us
    pallas_call x1, Pallas kernels, partial_sums(): pl.pallas_call(functools.partial(gather_kernel, own, group, pitch), grid=...  14.8 us
    ppermute x6, starting transfers between devices, shifted(): lax.ppermute(x, LINE, [(i, (i + amount) % size) for i in range(size)])  7.73 us
    all_to_all x1, starting transfers between devices, shards(): lax.all_to_all(parts, everyone, split_axis=0, concat_axis=0, tiled=True)  7.27 us
    unnamed x33, local copies, waits for them, and re-layouts  6.22 us
  transfers between devices with their start and end apart: 21, of which 10 were waited for; matrix products, arithmetic and copies ran while one was open for 0% of the time, Pallas kernels for 7%

profile of v3, /device:TPU:0, one launch (start us, length us, event | category | flops | bytes accessed | tf_op | source)
XLA Modules:
  0.0 189.4 jit_solution(15044693951851932384)
XLA Ops:
  0.0 0.8 copy-done.9
  0.8 0.7 copy-done.13
  1.5 14.8 %shard_map.73 = (bf16[32,272,128]{2,1,0:T(8,128)(2,1)S(1)}, f32[1,2048]{1,0:T(1,128)S(1)}) custom-call(s32[4,2048]{1,0:T(4,128)S(1)} %bitcast.31, f32[1,256]{1,0:T(1,128)S(1)} %bitcast.34, bf16[2048,32,128]{2,1,0:T(8,128)(2,1)} %cells_ref.1), custom_call_target="tpu_custom_call" | custom-call | flops 4294967296 | bytes 16777216 | tf_op jit(solution)/shard_map/pallas_call | solution.py:106
  16.3 0.0 copy-start
  16.3 1.4 copy-done
  17.6 7.3 %all-to-all-start = ((bf16[32,272,128]{2,1,0:T(8,128)(2,1)}), bf16[32,272,128]{2,1,0:T(8,128)(2,1)S(1)}, u32[]{:S(2)}, u32[]{:S(2)}) async-start(bf16[32,272,128]{2,1,0:T(8,128)(2,1)} %copy-done), calls=%async_computation | async-start | bytes 4456448 | tf_op jit(solution)/shard_map/all_to_all | solution.py:308
  24.9 0.1 dynamic_slice.11
  25.0 0.1 convert_reduce_fusion
  25.2 0.1 multiply_reduce_fusion
  25.3 0.3 convolution_convert_fusion
  25.7 51.0 %all-to-all-done.parts_ref = bf16[32,272,128]{2,1,0:T(8,128)(2,1)S(1)} async-done(((bf16[32,272,128]{2,1,0:T(8,128)(2,1)}), bf16[32,272,128]{2,1,0:T(8,128)(2,1)S(1)}, u32[]{:S(2)}, u32[]{:S(2)}) %all-to-all-start) | async-done | bytes 2228256 | tf_op jit(solution)/shard_map/all_to_all | solution.py:308
  76.6 0.1 broadcast_in_dim.32.weight_ref
  76.7 0.7 shard_map.74
  77.4 0.1 collective-permute-start
  77.5 1.3 collective-permute-done
  78.9 1.8 collective-permute-start.3
  80.6 1.1 collective-permute-start.1
  81.7 5.2 %collective-permute-done.3 = bf16[16,48,128]{2,1,0:T(8,128)(2,1)S(1)} collective-permute-done((bf16[16,48,128]{2,1,0:T(8,128)(2,1)S(1)}, bf16[16,48,128]{2,1,0:T(8,128)(2,1)S(1)}, u32[]{:S(2)}, u32[]{:S(2)}) %collective-permute-start.3) | collective-permute-done | bytes 196640 | tf_op jit(solution)/shard_map/ppermute | solution.py:257
  86.9 10.9 %collective-permute-done.2 = bf16[16,48,128]{2,1,0:T(8,128)(2,1)S(1)} collective-permute-done((bf16[16,48,128]{2,1,0:T(8,128)(2,1)S(1)}, bf16[16,48,128]{2,1,0:T(8,128)(2,1)S(1)}, u32[]{:S(2)}, u32[]{:S(2)}) %collective-permute-start.2) | collective-permute-done | bytes 196640 | tf_op jit(solution)/shard_map/ppermute | solution.py:257
  97.9 0.1 pad_maximum_fusion.refs_0_
  98.0 1.6 collective-permute-start.5
  99.5 0.6 collective-permute-start.11
  100.1 0.9 collective-permute-start.7
  101.0 17.3 %collective-permute-done.5.refs_1_ = bf16[64,48,128]{2,1,0:T(8,128)(2,1)S(1)} collective-permute-done((bf16[64,48,128]{2,1,0:T(8,128)(2,1)S(1)}, bf16[64,48,128]{2,1,0:T(8,128)(2,1)S(1)}, u32[]{:S(2)}, u32[]{:S(2)}) %collective-permute-start.5) | collective-permute-done | bytes 786464 | tf_op jit(solution)/shard_map/ppermute | solution.py:265
  118.3 1.0 collective-permute-start.9
  119.3 0.4 collective-permute-done.11
  119.8 1.1 collective-permute-start.12
  120.8 10.9 %collective-permute-done.12 = bf16[32,16,128]{2,1,0:T(8,128)(2,1)S(1)} collective-permute-done((bf16[32,16,128]{2,1,0:T(8,128)(2,1)S(1)}, bf16[32,16,128]{2,1,0:T(8,128)(2,1)S(1)}, u32[]{:S(2)}, u32[]{:S(2)}) %collective-permute-start.12) | collective-permute-done | bytes 131104 | tf_op jit(solution)/shard_map/ppermute | solution.py:265
  131.8 0.1 collective-permute-start.18
  131.9 2.8 %collective-permute-start.16 = (bf16[64,16,128]{2,1,0:T(8,128)(2,1)S(1)}, bf16[64,16,128]{2,1,0:T(8,128)(2,1)S(1)}, u32[]{:S(2)}, u32[]{:S(2)}) collective-permute-start(bf16[64,16,128]{2,1,0:T(8,128)(2,1)S(1)} %pad_maximum_fusion.1.refs_4_), channel_id=1, source_target_pairs={{0,16},{8,24},{16,0},{24,8},{1,17},{9,25},{17,1},{25,9},{2,18},{10... | collective-permute-start | bytes 786440 | tf_op jit(solution)/shard_map/ppermute | solution.py:257
  134.7 1.9 %collective-permute-start.14 = (bf16[64,16,128]{2,1,0:T(8,128)(2,1)S(1)}, bf16[64,16,128]{2,1,0:T(8,128)(2,1)S(1)}, u32[]{:S(2)}, u32[]{:S(2)}) collective-permute-start(bf16[64,16,128]{2,1,0:T(8,128)(2,1)S(1)} %pad_maximum_fusion.1.refs_4_), channel_id=1, source_target_pairs={{0,8},{8,16},{16,24},{24,0},{1,9},{9,17},{17,25},{25,1},{2,10},{10... | collective-permute-start | bytes 786440 | tf_op jit(solution)/shard_map/ppermute | solution.py:257
  136.6 3.0 %collective-permute-done.18.refs_7_ = bf16[64,16,128]{2,1,0:T(8,128)(2,1)} collective-permute-done((bf16[64,16,128]{2,1,0:T(8,128)(2,1)S(1)}, bf16[64,16,128]{2,1,0:T(8,128)(2,1)}, u32[]{:S(2)}, u32[]{:S(2)}) %collective-permute-start.18) | collective-permute-done | bytes 262176 | tf_op jit(solution)/shard_map/ppermute | solution.py:257
  139.6 15.7 %collective-permute-done.16.refs_6_ = bf16[64,16,128]{2,1,0:T(8,128)(2,1)S(1)} collective-permute-done((bf16[64,16,128]{2,1,0:T(8,128)(2,1)S(1)}, bf16[64,16,128]{2,1,0:T(8,128)(2,1)S(1)}, u32[]{:S(2)}, u32[]{:S(2)}) %collective-permute-start.16) | collective-permute-done | bytes 262176 | tf_op jit(solution)/shard_map/ppermute | solution.py:257
  155.4 0.5 collective-permute-start.4
  155.9 0.7 copy-done.5
  156.6 0.1 collective-permute-start.6
  156.7 0.4 collective-permute-start.8
  157.1 0.1 collective-permute-start.10
  157.3 0.4 collective-permute-start.17
  157.7 0.1 multiply_add_fusion
  157.8 2.3 %collective-permute-done.17.refs_6_ = bf16[64,16,128]{2,1,0:T(8,128)(2,1)S(1)} collective-permute-done((bf16[64,16,128]{2,1,0:T(8,128)(2,1)}, bf16[64,16,128]{2,1,0:T(8,128)(2,1)S(1)}, u32[]{:S(2)}, u32[]{:S(2)}) %collective-permute-start.17) | collective-permute-done | bytes 262176 | tf_op jit(solution)/shard_map/ppermute | solution.py:269
  160.1 0.7 copy-done.7
  160.8 0.1 collective-permute-start.15
  161.0 0.0 copy-start.2
  161.0 0.9 copy-done.2
  162.0 0.9 copy-done.4
  162.9 12.8 %shard_map.75.refs_8_ = bf16[512,128,128]{2,1,0:T(8,128)(2,1)} custom-call(s32[1]{0:T(128)} %bitcast.5.half_ref, s32[4,512]{1,0:T(4,128)S(1)} %get-tuple-element.21.long_at_ref, s32[4,512]{1,0:T(4,128)S(1)} %get-tuple-element.15.short_at_ref, f32[1,512]{1,0:T(1,128)S(1)} %constant_dynamic-slice_fusion.root_ref, f32[1,128]{1,0:T(1,128)S(1)} %bitcast.32, ...), custom_call_target="tpu_custom_call" | custom-call | flops 33554432 | bytes 8388608 | tf_op jit(solution)/shard_map/pallas_call | solution.py:233
  175.8 13.6 %shard_map.76 = bf16[512,128,128]{2,1,0:T(8,128)(2,1)} custom-call(s32[1]{0:T(128)} %bitcast.half_ref, s32[4,512]{1,0:T(4,128)S(1)} %get-tuple-element.23.long_at_ref, s32[4,512]{1,0:T(4,128)S(1)} %get-tuple-element.22.short_at_ref, f32[1,512]{1,0:T(1,128)S(1)} %constant_dynamic-slice_fusion.root_ref, ...), custom_call_target="tpu_custom_call", output_to_operand_aliasing={{}: (13, {})} | custom-call | flops 33554432 | bytes 8388608 | tf_op jit(solution)/shard_map/pallas_call | solution.py:233
  (50 shorter events, 0.3 us)
Async XLA Ops:
  0.0 25.0 %copy-start.14 = (s32[128,3]{0,1:T(4,128)S(1)}, s32[128,3]{0,1:T(4,128)}, u32[]{:S(2)}) copy-start(s32[128,3]{0,1:T(4,128)} %param.11) | copy-start | bytes 4612
  0.0 25.1 %copy-start.15 = (f32[128]{0:T(128)S(1)}, f32[128]{0:T(128)}, u32[]{:S(2)}) copy-start(f32[128]{0:T(128)} %param.12) | copy-start | bytes 1540
  0.0 161.0 %copy-start.12 = (f32[128]{0:T(128)S(1)}, f32[128]{0:T(128)}, u32[]{:S(2)}) copy-start(f32[128]{0:T(128)} %param.13) | copy-start | bytes 1540
  0.0 0.8 copy-start.9
  0.8 0.7 copy-start.13
  1.5 75.2 %copy-start.11 = (bf16[128,128]{1,0:T(8,128)(2,1)S(1)}, bf16[128,128]{1,0:T(8,128)(2,1)}, u32[]{:S(2)}) copy-start(bf16[128,128]{1,0:T(8,128)(2,1)} %mixing_ref.1) | copy-start | bytes 98308
  1.5 156.2 %copy-start.10 = (s32[2048,4]{0,1:T(4,128)S(1)}, s32[2048,4]{0,1:T(4,128)}, u32[]{:S(2)}) copy-start(s32[2048,4]{0,1:T(4,128)} %param.8) | copy-start | bytes 98308
  16.3 1.4 copy-start
  17.6 59.0 %all-to-all-start = ((bf16[32,272,128]{2,1,0:T(8,128)(2,1)}), bf16[32,272,128]{2,1,0:T(8,128)(2,1)S(1)}, u32[]{:S(2)}, u32[]{:S(2)}) async-start(bf16[32,272,128]{2,1,0:T(8,128)(2,1)} %copy-done), calls=%async_computation | async-start | bytes 4456448 | tf_op jit(solution)/shard_map/all_to_all | solution.py:308
  77.4 1.4 collective-permute-start
  78.9 8.1 %collective-permute-start.3 = (bf16[16,48,128]{2,1,0:T(8,128)(2,1)S(1)}, bf16[16,48,128]{2,1,0:T(8,128)(2,1)S(1)}, u32[]{:S(2)}, u32[]{:S(2)}) collective-permute-start(bf16[16,48,128]{2,1,0:T(8,128)(2,1)S(1)} %slice.18), channel_id=1, source_target_pairs={{0,24},{8,0},{16,8},{24,16},{1,25},{9,1},{17,9},{25,17},{2,26},{10... | collective-permute-start | bytes 589832 | tf_op jit(solution)/shard_map/ppermute | solution.py:257
  80.6 17.2 %collective-permute-start.2 = (bf16[16,48,128]{2,1,0:T(8,128)(2,1)S(1)}, bf16[16,48,128]{2,1,0:T(8,128)(2,1)S(1)}, u32[]{:S(2)}, u32[]{:S(2)}) collective-permute-start(bf16[16,48,128]{2,1,0:T(8,128)(2,1)S(1)} %slice.18), channel_id=1, source_target_pairs={{0,16},{8,24},{16,0},{24,8},{1,17},{9,25},{17,1},{25,9},{2,18},{10... | collective-permute-start | bytes 589832 | tf_op jit(solution)/shard_map/ppermute | solution.py:257
  80.6 17.2 %collective-permute-start.1 = (bf16[16,48,128]{2,1,0:T(8,128)(2,1)S(1)}, bf16[16,48,128]{2,1,0:T(8,128)(2,1)S(1)}, u32[]{:S(2)}, u32[]{:S(2)}) collective-permute-start(bf16[16,48,128]{2,1,0:T(8,128)(2,1)S(1)} %slice.18), channel_id=1, source_target_pairs={{0,8},{8,16},{16,24},{24,0},{1,9},{9,17},{17,25},{25,1},{2,10},{10... | collective-permute-start | bytes 589832 | tf_op jit(solution)/shard_map/ppermute | solution.py:257
  98.0 20.4 %collective-permute-start.5 = (bf16[64,48,128]{2,1,0:T(8,128)(2,1)S(1)}, bf16[64,48,128]{2,1,0:T(8,128)(2,1)S(1)}, u32[]{:S(2)}, u32[]{:S(2)}) collective-permute-start(bf16[64,48,128]{2,1,0:T(8,128)(2,1)S(1)} %pad_maximum_fusion.refs_0_), channel_id=1, source_target_pairs={{0,2},{1,5},{2,0},{3,7},{4,6},{5,1},{6,4},{7,3},{8,10},{9,13},{10,... | collective-permute-start | bytes 2359304 | tf_op jit(solution)/shard_map/ppermute | solution.py:265
  99.5 20.2 %collective-permute-start.11 = (bf16[16,16,128]{2,1,0:T(8,128)(2,1)S(1)}, bf16[16,16,128]{2,1,0:T(8,128)(2,1)S(1)}, u32[]{:S(2)}, u32[]{:S(2)}) collective-permute-start(bf16[16,16,128]{2,1,0:T(8,128)(2,1)S(1)} %slice.19), channel_id=1, source_target_pairs={{0,2},{1,5},{2,0},{3,7},{4,6},{5,1},{6,4},{7,3},{8,10},{9,13},{10,... | collective-permute-start | bytes 196616 | tf_op jit(solution)/shard_map/ppermute | solution.py:265
  100.1 56.5 %collective-permute-start.7 = (bf16[64,48,128]{2,1,0:T(8,128)(2,1)S(1)}, bf16[64,48,128]{2,1,0:T(8,128)(2,1)S(1)}, u32[]{:S(2)}, u32[]{:S(2)}) collective-permute-start(bf16[64,48,128]{2,1,0:T(8,128)(2,1)S(1)} %pad_maximum_fusion.refs_0_), channel_id=1, source_target_pairs={{0,4},{1,3},{2,6},{3,1},{4,0},{5,7},{6,2},{7,5},{8,12},{9,11},{10,... | collective-permute-start | bytes 2359304 | tf_op jit(solution)/shard_map/ppermute | solution.py:265
  118.3 38.8 %collective-permute-start.9 = (bf16[64,48,128]{2,1,0:T(8,128)(2,1)S(1)}, bf16[64,48,128]{2,1,0:T(8,128)(2,1)S(1)}, u32[]{:S(2)}, u32[]{:S(2)}) collective-permute-start(bf16[64,48,128]{2,1,0:T(8,128)(2,1)S(1)} %collective-permute-done.5.refs_1_), channel_id=1, source_target_pairs={{0,4},{1,3},{2,6},{3,1},{4,0},{5,7},{6,2},{7,5},{8,12},{9,11},{10,... | collective-permute-start | bytes 2359304 | tf_op jit(solution)/shard_map/ppermute | solution.py:265
  119.8 12.0 %collective-permute-start.12 = (bf16[32,16,128]{2,1,0:T(8,128)(2,1)S(1)}, bf16[32,16,128]{2,1,0:T(8,128)(2,1)S(1)}, u32[]{:S(2)}, u32[]{:S(2)}) collective-permute-start(bf16[32,16,128]{2,1,0:T(8,128)(2,1)S(1)} %pad_maximum_fusion.2), channel_id=1, source_target_pairs={{0,4},{1,3},{2,6},{3,1},{4,0},{5,7},{6,2},{7,5},{8,12},{9,11},{10,... | collective-permute-start | bytes 393224 | tf_op jit(solution)/shard_map/ppermute | solution.py:265
  131.8 7.8 %collective-permute-start.18 = (bf16[64,16,128]{2,1,0:T(8,128)(2,1)S(1)}, bf16[64,16,128]{2,1,0:T(8,128)(2,1)}, u32[]{:S(2)}, u32[]{:S(2)}) collective-permute-start(bf16[64,16,128]{2,1,0:T(8,128)(2,1)S(1)} %pad_maximum_fusion.1.refs_4_), channel_id=1, source_target_pairs={{0,24},{8,0},{16,8},{24,16},{1,25},{9,1},{17,9},{25,17},{2,26},{10... | collective-permute-start | bytes 786440 | tf_op jit(solution)/shard_map/ppermute | solution.py:257
  131.9 23.4 %collective-permute-start.16 = (bf16[64,16,128]{2,1,0:T(8,128)(2,1)S(1)}, bf16[64,16,128]{2,1,0:T(8,128)(2,1)S(1)}, u32[]{:S(2)}, u32[]{:S(2)}) collective-permute-start(bf16[64,16,128]{2,1,0:T(8,128)(2,1)S(1)} %pad_maximum_fusion.1.refs_4_), channel_id=1, source_target_pairs={{0,16},{8,24},{16,0},{24,8},{1,17},{9,25},{17,1},{25,9},{2,18},{10... | collective-permute-start | bytes 786440 | tf_op jit(solution)/shard_map/ppermute | solution.py:257
  134.7 20.7 %collective-permute-start.14 = (bf16[64,16,128]{2,1,0:T(8,128)(2,1)S(1)}, bf16[64,16,128]{2,1,0:T(8,128)(2,1)S(1)}, u32[]{:S(2)}, u32[]{:S(2)}) collective-permute-start(bf16[64,16,128]{2,1,0:T(8,128)(2,1)S(1)} %pad_maximum_fusion.1.refs_4_), channel_id=1, source_target_pairs={{0,8},{8,16},{16,24},{24,0},{1,9},{9,17},{17,25},{25,1},{2,10},{10... | collective-permute-start | bytes 786440 | tf_op jit(solution)/shard_map/ppermute | solution.py:257
  139.6 16.3 %collective-permute-start.13 = (bf16[64,16,128]{2,1,0:T(8,128)(2,1)S(1)}, bf16[64,16,128]{2,1,0:T(8,128)(2,1)S(1)}, u32[]{:S(2)}, u32[]{:S(2)}) collective-permute-start(bf16[64,16,128]{2,1,0:T(8,128)(2,1)S(1)} %pad_maximum_fusion.1.refs_4_), channel_id=1, source_target_pairs={{0,1},{1,0},{2,3},{3,2},{4,5},{5,4},{6,7},{7,6},{8,9},{9,8},{10,11... | collective-permute-start | bytes 786440 | tf_op jit(solution)/shard_map/ppermute | solution.py:269
  155.3 1.8 copy-start.1
  155.3 1.9 %collective-permute-start.19 = (bf16[64,16,128]{2,1,0:T(8,128)(2,1)}, bf16[64,16,128]{2,1,0:T(8,128)(2,1)}, u32[]{:S(2)}, u32[]{:S(2)}) collective-permute-start(bf16[64,16,128]{2,1,0:T(8,128)(2,1)} %collective-permute-done.18.refs_7_), channel_id=1, source_target_pairs={{0,1},{1,0},{2,3},{3,2},{4,5},{5,4},{6,7},{7,6},{8,9},{9,8},{10,11... | collective-permute-start | bytes 786440 | tf_op jit(solution)/shard_map/ppermute | solution.py:269
  155.4 1.8 copy-start.3
  155.4 20.4 %collective-permute-start.4 = (bf16[64,48,128]{2,1,0:T(8,128)(2,1)S(1)}, bf16[64,48,128]{2,1,0:T(8,128)(2,1)}, u32[]{:S(2)}, u32[]{:S(2)}) collective-permute-start(bf16[64,48,128]{2,1,0:T(8,128)(2,1)S(1)} %pad_maximum_fusion.refs_0_), channel_id=1, source_target_pairs={{0,1},{1,0},{2,3},{3,2},{4,5},{5,4},{6,7},{7,6},{8,9},{9,8},{10,11... | collective-permute-start | bytes 2359304 | tf_op jit(solution)/shard_map/ppermute | solution.py:269
  155.9 0.7 copy-start.5
  156.6 19.2 %collective-permute-start.6 = (bf16[64,48,128]{2,1,0:T(8,128)(2,1)S(1)}, bf16[64,48,128]{2,1,0:T(8,128)(2,1)}, u32[]{:S(2)}, u32[]{:S(2)}) collective-permute-start(bf16[64,48,128]{2,1,0:T(8,128)(2,1)S(1)} %collective-permute-done.5.refs_1_), channel_id=1, source_target_pairs={{0,1},{1,0},{2,3},{3,2},{4,5},{5,4},{6,7},{7,6},{8,9},{9,8},{10,11... | collective-permute-start | bytes 2359304 | tf_op jit(solution)/shard_map/ppermute | solution.py:269
  156.7 19.1 %collective-permute-start.8 = (bf16[64,48,128]{2,1,0:T(8,128)(2,1)S(1)}, bf16[64,48,128]{2,1,0:T(8,128)(2,1)}, u32[]{:S(2)}, u32[]{:S(2)}) collective-permute-start(bf16[64,48,128]{2,1,0:T(8,128)(2,1)S(1)} %collective-permute-done.7.refs_2_), channel_id=1, source_target_pairs={{0,1},{1,0},{2,3},{3,2},{4,5},{5,4},{6,7},{7,6},{8,9},{9,8},{10,11... | collective-permute-start | bytes 2359304 | tf_op jit(solution)/shard_map/ppermute | solution.py:269
  157.1 18.7 %collective-permute-start.10 = (bf16[64,48,128]{2,1,0:T(8,128)(2,1)S(1)}, bf16[64,48,128]{2,1,0:T(8,128)(2,1)}, u32[]{:S(2)}, u32[]{:S(2)}) collective-permute-start(bf16[64,48,128]{2,1,0:T(8,128)(2,1)S(1)} %collective-permute-done.9.refs_3_), channel_id=1, source_target_pairs={{0,1},{1,0},{2,3},{3,2},{4,5},{5,4},{6,7},{7,6},{8,9},{9,8},{10,11... | collective-permute-start | bytes 2359304 | tf_op jit(solution)/shard_map/ppermute | solution.py:269
  157.3 2.8 %collective-permute-start.17 = (bf16[64,16,128]{2,1,0:T(8,128)(2,1)}, bf16[64,16,128]{2,1,0:T(8,128)(2,1)S(1)}, u32[]{:S(2)}, u32[]{:S(2)}) collective-permute-start(bf16[64,16,128]{2,1,0:T(8,128)(2,1)} %copy-done.1), channel_id=1, source_target_pairs={{0,1},{1,0},{2,3},{3,2},{4,5},{5,4},{6,7},{7,6},{8,9},{9,8},{10,11... | collective-permute-start | bytes 786440 | tf_op jit(solution)/shard_map/ppermute | solution.py:269
  160.1 0.7 copy-start.7
  160.8 14.9 %collective-permute-start.15 = (bf16[64,16,128]{2,1,0:T(8,128)(2,1)}, bf16[64,16,128]{2,1,0:T(8,128)(2,1)}, u32[]{:S(2)}, u32[]{:S(2)}) collective-permute-start(bf16[64,16,128]{2,1,0:T(8,128)(2,1)} %copy-done.3), channel_id=1, source_target_pairs={{0,1},{1,0},{2,3},{3,2},{4,5},{5,4},{6,7},{7,6},{8,9},{9,8},{10,11... | collective-permute-start | bytes 786440 | tf_op jit(solution)/shard_map/ppermute | solution.py:269
  161.0 1.0 copy-start.2
  162.0 0.9 copy-start.4
  162.9 12.9 %copy-start.6 = (bf16[64,16,128]{2,1,0:T(8,128)(2,1)S(1)}, bf16[64,16,128]{2,1,0:T(8,128)(2,1)}, u32[]{:S(2)}) copy-start(bf16[64,16,128]{2,1,0:T(8,128)(2,1)} %copy-done.5) | copy-start | bytes 786436
  162.9 12.9 %copy-start.8 = (bf16[64,16,128]{2,1,0:T(8,128)(2,1)S(1)}, bf16[64,16,128]{2,1,0:T(8,128)(2,1)}, u32[]{:S(2)}) copy-start(bf16[64,16,128]{2,1,0:T(8,128)(2,1)} %copy-done.7) | copy-start | bytes 786436

commit v4 on v3

--- a/solution.py
+++ b/solution.py
@@ -204,10 +204,10 @@
         for table, places in ((long_ref, long_at_ref), (short_ref, short_at_ref)):
             spots = [places[j, at] for j in range(count)]
             for first in range(0, table.shape[1], tile):
-                total = table[spots[0], first : first + tile, :].astype(F32)
-                for spot in spots[1:]:
-                    total = total + table[spot, first : first + tile, :].astype(F32)
-                value = jnp.maximum(total * scale + bias, 0.0).astype(BF16)
+                pieces = [table[spot, first : first + tile, :] for spot in spots]
+                pieces = [(a + b).astype(F32) for a, b in zip(pieces[0::2], pieces[1::2])]
+                total = sum(pieces[1:], pieces[0])
+                value = jnp.maximum((total * scale + bias).astype(BF16), BF16(0.0))
                 out_ref[i, start : start + tile, :] = value
                 start += tile
         return carry
@@ -221,7 +221,7 @@
     zones = longs[0].shape[1] + shorts[0].shape[1]
     rows = min(32, anchors)
     smem = pl.BlockSpec(memory_space=pltpu.SMEM)
-    anywhere = pl.BlockSpec(memory_space=pl.ANY)
+    anywhere = pl.BlockSpec(memory_space=pltpu.HBM)
     tables = [pltpu.VMEM((len(pieces) * pieces[0].shape[0],) + pieces[0].shape[1:], BF16) for pieces in (longs, shorts)]
     operands = [half, long_at, short_at, root, bias] + longs + shorts
     specs = [smem, smem, smem, pl.BlockSpec((1, lanes), lambda i, h: (0, 0))] + [anywhere] * len(longs + shorts)
@@ -243,7 +243,7 @@
         input_output_aliases=aliases,
         compiler_params=pltpu.CompilerParams(vmem_limit_bytes=24 * 1024 * 1024),
         cost_estimate=pl.CostEstimate(
-            flops=8 * anchors * zones * lanes, bytes_accessed=2 * anchors * zones * lanes, transcendentals=0
+            flops=4096 * anchors * zones * lanes, bytes_accessed=4 * anchors * zones * lanes, transcendentals=0
         ),
     )(*operands)
 
@@ -274,10 +274,13 @@
     block = jnp.concatenate([keep, swapped(give)], axis=0)
     split = block.shape[1] * 3 // 4
     long, short = block[:, :split], block[:, split:]
-    line = [long] + [shifted(long, k) for k in range(1, size)]
+    line = [long] + [shifted(long, k) for k in range(1, size - 1)]
     short = jnp.concatenate([short, crossed(short, 0)], axis=0)
+    short, long = lax.optimization_barrier((short, long))
+    line.append(shifted(long, size - 1))
     short = jnp.concatenate([short, crossed(short, 1)], axis=0)
     long = jnp.concatenate(line, axis=0)
+    short, long = lax.optimization_barrier((short, long))
     first = crossed(long, 0)
     second = crossed(long, 1)
     both = crossed(first, 1)

time: 190 us -> 177 us (0.932)
  waiting for transfers between devices: 118 us -> 106 us
  local copies, waits for them, and re-layouts: 6.42 us -> 3.07 us
  starting transfers between devices: 21.9 us -> 24.5 us
    ppermute x5, waiting for transfers between devices: 28.6 us -> 20.7 us  [crossed(): return lax.ppermute(x, SQUARE, pairs)]
    ppermute x6, waiting for transfers between devices: 34.9 us -> 31.5 us  [shifted(): lax.ppermute(x, LINE, [(i, (i + amount) % size) for i in range(size)])]
    unnamed x33 -> x19, local copies, waits for them, and re-layouts: 6.22 us -> 2.87 us
    ppermute x6, starting transfers between devices: 7.73 us -> 9.8 us  [shifted(): lax.ppermute(x, LINE, [(i, (i + amount) % size) for i in range(size)])]
  transfers between devices with their start and end apart: 21 -> 21, of which waited for: 10 -> 10; matrix products, arithmetic and copies ran while one was open for 0% -> 1% of each run, Pallas kernels for 7% -> 8%
where the time goes in v4:
time: 177 us
  waiting for transfers between devices  106 us (60%)
  Pallas kernels  42.5 us (24%)
  starting transfers between devices  24.5 us (14%)
  local copies, waits for them, and re-layouts  3.07 us (2%)
    all_to_all x1, waiting for transfers between devices, shards(): lax.all_to_all(parts, everyone, split_axis=0, concat_axis=0, tiled=True)  51 us
    ppermute x6, waiting for transfers between devices, shifted(): lax.ppermute(x, LINE, [(i, (i + amount) % size) for i in range(size)])  31.5 us
    pallas_call x2, Pallas kernels, spread(): pl.pallas_call(functools.partial(spread_kernel, len(longs), len(shorts)),...  27 us
    ppermute x5, waiting for transfers between devices, crossed(): return lax.ppermute(x, SQUARE, pairs)  20.7 us
    pallas_call x1, Pallas kernels, partial_sums(): pl.pallas_call(functools.partial(gather_kernel, own, group, pitch), grid=...  14.8 us
    ppermute x6, starting transfers between devices, shifted(): lax.ppermute(x, LINE, [(i, (i + amount) % size) for i in range(size)])  9.8 us
    all_to_all x1, starting transfers between devices, shards(): lax.all_to_all(parts, everyone, split_axis=0, concat_axis=0, tiled=True)  7.29 us
    ppermute x5, starting transfers between devices, crossed(): return lax.ppermute(x, SQUARE, pairs)  5.99 us
  transfers between devices with their start and end apart: 21, of which 10 were waited for; matrix products, arithmetic and copies ran while one was open for 1% of the time, Pallas kernels for 8%

profile of v4, /device:TPU:0, one launch (start us, length us, event | category | flops | bytes accessed | tf_op | source)
XLA Modules:
  0.0 177.2 jit_solution(3614926699180398358)
XLA Ops:
  0.0 0.8 copy-done.1
  0.8 0.7 copy-done.4
  1.5 14.8 %shard_map.73 = (bf16[32,272,128]{2,1,0:T(8,128)(2,1)S(1)}, f32[1,2048]{1,0:T(1,128)S(1)}) custom-call(s32[4,2048]{1,0:T(4,128)S(1)} %bitcast.31, f32[1,256]{1,0:T(1,128)S(1)} %bitcast.32, bf16[2048,32,128]{2,1,0:T(8,128)(2,1)} %cells_ref.1), custom_call_target="tpu_custom_call" | custom-call | flops 4294967296 | bytes 16777216 | tf_op jit(solution)/shard_map/pallas_call | solution.py:106
  16.3 0.0 copy-start
  16.3 1.4 copy-done
  17.6 7.3 %all-to-all-start = ((bf16[32,272,128]{2,1,0:T(8,128)(2,1)}), bf16[32,272,128]{2,1,0:T(8,128)(2,1)S(1)}, u32[]{:S(2)}, u32[]{:S(2)}) async-start(bf16[32,272,128]{2,1,0:T(8,128)(2,1)} %copy-done), calls=%async_computation | async-start | bytes 4456448 | tf_op jit(solution)/shard_map/all_to_all | solution.py:311
  24.9 0.1 dynamic_slice.11
  25.0 0.1 convert_reduce_fusion
  25.2 0.1 multiply_reduce_fusion
  25.3 0.3 convolution_convert_fusion
  25.7 51.0 %all-to-all-done.parts_ref = bf16[32,272,128]{2,1,0:T(8,128)(2,1)S(1)} async-done(((bf16[32,272,128]{2,1,0:T(8,128)(2,1)}), bf16[32,272,128]{2,1,0:T(8,128)(2,1)S(1)}, u32[]{:S(2)}, u32[]{:S(2)}) %all-to-all-start) | async-done | bytes 2228256 | tf_op jit(solution)/shard_map/all_to_all | solution.py:311
  76.6 0.1 broadcast_in_dim.32.weight_ref
  76.7 0.7 shard_map.74
  77.4 0.1 collective-permute-start
  77.5 1.3 collective-permute-done
  78.9 1.5 collective-permute-start.1
  80.3 2.9 %collective-permute-done.1 = bf16[16,16,128]{2,1,0:T(8,128)(2,1)S(1)} collective-permute-done((bf16[16,16,128]{2,1,0:T(8,128)(2,1)S(1)}, bf16[16,16,128]{2,1,0:T(8,128)(2,1)S(1)}, u32[]{:S(2)}, u32[]{:S(2)}) %collective-permute-start.1) | collective-permute-done | bytes 65568 | tf_op jit(solution)/shard_map/ppermute | solution.py:265
  83.2 1.3 collective-permute-start.2
  84.5 0.0 collective-permute-start.4
  84.6 2.0 %collective-permute-start.3 = (bf16[16,48,128]{2,1,0:T(8,128)(2,1)S(1)}, bf16[16,48,128]{2,1,0:T(8,128)(2,1)S(1)}, u32[]{:S(2)}, u32[]{:S(2)}) collective-permute-start(bf16[16,48,128]{2,1,0:T(8,128)(2,1)S(1)} %slice.19), channel_id=1, source_target_pairs={{0,8},{8,16},{16,24},{24,0},{1,9},{9,17},{17,25},{25,1},{2,10},{10... | collective-permute-start | bytes 589832 | tf_op jit(solution)/shard_map/ppermute | solution.py:257
  86.6 1.8 %collective-permute-start.5 = (bf16[16,48,128]{2,1,0:T(8,128)(2,1)S(1)}, bf16[16,48,128]{2,1,0:T(8,128)(2,1)S(1)}, u32[]{:S(2)}, u32[]{:S(2)}) collective-permute-start(bf16[16,48,128]{2,1,0:T(8,128)(2,1)S(1)} %slice.19), channel_id=1, source_target_pairs={{0,24},{8,0},{16,8},{24,16},{1,25},{9,1},{17,9},{25,17},{2,26},{10... | collective-permute-start | bytes 589832 | tf_op jit(solution)/shard_map/ppermute | solution.py:257
  88.4 11.0 %collective-permute-done.4 = bf16[16,48,128]{2,1,0:T(8,128)(2,1)S(1)} collective-permute-done((bf16[16,48,128]{2,1,0:T(8,128)(2,1)S(1)}, bf16[16,48,128]{2,1,0:T(8,128)(2,1)S(1)}, u32[]{:S(2)}, u32[]{:S(2)}) %collective-permute-start.4) | collective-permute-done | bytes 196640 | tf_op jit(solution)/shard_map/ppermute | solution.py:257
  99.4 0.0 collective-permute-done.3
  99.4 1.0 collective-permute-done.5
  100.5 0.1 pad_maximum_fusion.refs_0_
  100.6 0.7 collective-permute-start.7
  101.3 1.2 collective-permute-start.9
  102.4 17.8 %collective-permute-done.7.refs_1_ = bf16[64,48,128]{2,1,0:T(8,128)(2,1)S(1)} collective-permute-done((bf16[64,48,128]{2,1,0:T(8,128)(2,1)S(1)}, bf16[64,48,128]{2,1,0:T(8,128)(2,1)S(1)}, u32[]{:S(2)}, u32[]{:S(2)}) %collective-permute-start.7) | collective-permute-done | bytes 786464 | tf_op jit(solution)/shard_map/ppermute | solution.py:265
  120.3 1.3 collective-permute-start.11
  121.6 0.7 collective-permute-start.18
  122.3 4.6 %collective-permute-start.16 = (bf16[64,16,128]{2,1,0:T(8,128)(2,1)S(1)}, bf16[64,16,128]{2,1,0:T(8,128)(2,1)}, u32[]{:S(2)}, u32[]{:S(2)}) collective-permute-start(bf16[64,16,128]{2,1,0:T(8,128)(2,1)S(1)} %pad_maximum_fusion.1.refs_4_), channel_id=1, source_target_pairs={{0,16},{8,24},{16,0},{24,8},{1,17},{9,25},{17,1},{25,9},{2,18},{10... | collective-permute-start | bytes 786440 | tf_op jit(solution)/shard_map/ppermute | solution.py:257
  127.0 0.6 collective-permute-start.14
  127.6 0.1 multiply_add_fusion
  127.7 2.2 %collective-permute-done.18.refs_7_ = bf16[64,16,128]{2,1,0:T(8,128)(2,1)S(1)} collective-permute-done((bf16[64,16,128]{2,1,0:T(8,128)(2,1)S(1)}, bf16[64,16,128]{2,1,0:T(8,128)(2,1)S(1)}, u32[]{:S(2)}, u32[]{:S(2)}) %collective-permute-start.18) | collective-permute-done | bytes 262176 | tf_op jit(solution)/shard_map/ppermute | solution.py:257
  129.8 17.2 %collective-permute-done.16.refs_6_ = bf16[64,16,128]{2,1,0:T(8,128)(2,1)} collective-permute-done((bf16[64,16,128]{2,1,0:T(8,128)(2,1)S(1)}, bf16[64,16,128]{2,1,0:T(8,128)(2,1)}, u32[]{:S(2)}, u32[]{:S(2)}) %collective-permute-start.16) | collective-permute-done | bytes 262176 | tf_op jit(solution)/shard_map/ppermute | solution.py:257
  147.1 0.0 collective-permute-start.19
  147.1 0.5 collective-permute-start.17
  147.7 0.1 collective-permute-start.6
  147.7 1.3 collective-permute-done.19.refs_7_
  149.0 0.1 collective-permute-start.15
  149.2 0.2 collective-permute-done.17.refs_6_
  149.4 0.1 collective-permute-start.8
  149.6 0.4 collective-permute-start.10
  149.9 0.0 collective-permute-done.11.refs_3_
  149.9 0.1 collective-permute-start.12
  150.1 13.5 %shard_map.75.refs_8_ = bf16[512,128,128]{2,1,0:T(8,128)(2,1)} custom-call(s32[1]{0:T(128)} %bitcast.5.half_ref, s32[4,512]{1,0:T(4,128)S(1)} %get-tuple-element.29.long_at_ref, s32[4,512]{1,0:T(4,128)S(1)} %get-tuple-element.23.short_at_ref, f32[1,512]{1,0:T(1,128)S(1)} %constant_dynamic-slice_fusion.root_ref, f32[1,128]{1,0:T(1,128)S(1)} %bitcast.33, ...), custom_call_target="tpu_custom_call" | custom-call | flops 17179869184 | bytes 16777216 | tf_op jit(solution)/shard_map/pallas_call | solution.py:233
  163.6 0.0 collective-permute-done.10.refs_2_
  163.6 13.5 %shard_map.76 = bf16[512,128,128]{2,1,0:T(8,128)(2,1)} custom-call(s32[1]{0:T(128)} %bitcast.half_ref, s32[4,512]{1,0:T(4,128)S(1)} %get-tuple-element.31.long_at_ref, s32[4,512]{1,0:T(4,128)S(1)} %get-tuple-element.30.short_at_ref, f32[1,512]{1,0:T(1,128)S(1)} %constant_dynamic-slice_fusion.root_ref, ...), custom_call_target="tpu_custom_call", output_to_operand_aliasing={{}: (13, {})} | custom-call | flops 17179869184 | bytes 16777216 | tf_op jit(solution)/shard_map/pallas_call | solution.py:233
  (36 shorter events, 0.3 us)
Async XLA Ops:
  0.0 24.9 %copy-start.5 = (f32[256]{0:T(256)S(1)}, f32[256]{0:T(256)}, u32[]{:S(2)}) copy-start(f32[256]{0:T(256)} %param.9) | copy-start | bytes 3076
  0.0 25.0 %copy-start.7 = (s32[128,3]{0,1:T(4,128)S(1)}, s32[128,3]{0,1:T(4,128)}, u32[]{:S(2)}) copy-start(s32[128,3]{0,1:T(4,128)} %param.11) | copy-start | bytes 4612
  0.0 150.1 %copy-start.6 = (f32[128]{0:T(128)S(1)}, f32[128]{0:T(128)}, u32[]{:S(2)}) copy-start(f32[128]{0:T(128)} %param.13) | copy-start | bytes 1540
  0.0 0.8 copy-start.1
  0.8 0.7 copy-start.4
  1.5 23.7 %copy-start.8 = (f32[128]{0:T(128)S(1)}, f32[128]{0:T(128)}, u32[]{:S(2)}) copy-start(f32[128]{0:T(128)} %param.12) | copy-start | bytes 1540
  1.5 75.2 %copy-start.3 = (bf16[128,128]{1,0:T(8,128)(2,1)S(1)}, bf16[128,128]{1,0:T(8,128)(2,1)}, u32[]{:S(2)}) copy-start(bf16[128,128]{1,0:T(8,128)(2,1)} %mixing_ref.1) | copy-start | bytes 98308
  1.5 126.1 %copy-start.2 = (s32[2048,4]{0,1:T(4,128)S(1)}, s32[2048,4]{0,1:T(4,128)}, u32[]{:S(2)}) copy-start(s32[2048,4]{0,1:T(4,128)} %param.8) | copy-start | bytes 98308
  16.3 1.4 copy-start
  17.6 59.0 %all-to-all-start = ((bf16[32,272,128]{2,1,0:T(8,128)(2,1)}), bf16[32,272,128]{2,1,0:T(8,128)(2,1)S(1)}, u32[]{:S(2)}, u32[]{:S(2)}) async-start(bf16[32,272,128]{2,1,0:T(8,128)(2,1)} %copy-done), calls=%async_computation | async-start | bytes 4456448 | tf_op jit(solution)/shard_map/all_to_all | solution.py:311
  77.4 1.4 collective-permute-start
  78.9 4.3 %collective-permute-start.1 = (bf16[16,16,128]{2,1,0:T(8,128)(2,1)S(1)}, bf16[16,16,128]{2,1,0:T(8,128)(2,1)S(1)}, u32[]{:S(2)}, u32[]{:S(2)}) collective-permute-start(bf16[16,16,128]{2,1,0:T(8,128)(2,1)S(1)} %slice.18), channel_id=1, source_target_pairs={{0,2},{1,5},{2,0},{3,7},{4,6},{5,1},{6,4},{7,3},{8,10},{9,13},{10,... | collective-permute-start | bytes 196616 | tf_op jit(solution)/shard_map/ppermute | solution.py:265
  83.2 5.2 %collective-permute-start.2 = (bf16[32,16,128]{2,1,0:T(8,128)(2,1)S(1)}, bf16[32,16,128]{2,1,0:T(8,128)(2,1)S(1)}, u32[]{:S(2)}, u32[]{:S(2)}) collective-permute-start(bf16[32,16,128]{2,1,0:T(8,128)(2,1)S(1)} %pad_maximum_fusion.2), channel_id=1, source_target_pairs={{0,4},{1,3},{2,6},{3,1},{4,0},{5,7},{6,2},{7,5},{8,12},{9,11},{10,... | collective-permute-start | bytes 393224 | tf_op jit(solution)/shard_map/ppermute | solution.py:265
  84.5 14.9 %collective-permute-start.4 = (bf16[16,48,128]{2,1,0:T(8,128)(2,1)S(1)}, bf16[16,48,128]{2,1,0:T(8,128)(2,1)S(1)}, u32[]{:S(2)}, u32[]{:S(2)}) collective-permute-start(bf16[16,48,128]{2,1,0:T(8,128)(2,1)S(1)} %slice.19), channel_id=1, source_target_pairs={{0,16},{8,24},{16,0},{24,8},{1,17},{9,25},{17,1},{25,9},{2,18},{10... | collective-permute-start | bytes 589832 | tf_op jit(solution)/shard_map/ppermute | solution.py:257
  84.6 14.9 %collective-permute-start.3 = (bf16[16,48,128]{2,1,0:T(8,128)(2,1)S(1)}, bf16[16,48,128]{2,1,0:T(8,128)(2,1)S(1)}, u32[]{:S(2)}, u32[]{:S(2)}) collective-permute-start(bf16[16,48,128]{2,1,0:T(8,128)(2,1)S(1)} %slice.19), channel_id=1, source_target_pairs={{0,8},{8,16},{16,24},{24,0},{1,9},{9,17},{17,25},{25,1},{2,10},{10... | collective-permute-start | bytes 589832 | tf_op jit(solution)/shard_map/ppermute | solution.py:257
  86.6 13.9 %collective-permute-start.5 = (bf16[16,48,128]{2,1,0:T(8,128)(2,1)S(1)}, bf16[16,48,128]{2,1,0:T(8,128)(2,1)S(1)}, u32[]{:S(2)}, u32[]{:S(2)}) collective-permute-start(bf16[16,48,128]{2,1,0:T(8,128)(2,1)S(1)} %slice.19), channel_id=1, source_target_pairs={{0,24},{8,0},{16,8},{24,16},{1,25},{9,1},{17,9},{25,17},{2,26},{10... | collective-permute-start | bytes 589832 | tf_op jit(solution)/shard_map/ppermute | solution.py:257
  100.6 19.7 %collective-permute-start.7 = (bf16[64,48,128]{2,1,0:T(8,128)(2,1)S(1)}, bf16[64,48,128]{2,1,0:T(8,128)(2,1)S(1)}, u32[]{:S(2)}, u32[]{:S(2)}) collective-permute-start(bf16[64,48,128]{2,1,0:T(8,128)(2,1)S(1)} %pad_maximum_fusion.refs_0_), channel_id=1, source_target_pairs={{0,2},{1,5},{2,0},{3,7},{4,6},{5,1},{6,4},{7,3},{8,10},{9,13},{10,... | collective-permute-start | bytes 2359304 | tf_op jit(solution)/shard_map/ppermute | solution.py:265
  101.3 48.3 %collective-permute-start.9 = (bf16[64,48,128]{2,1,0:T(8,128)(2,1)S(1)}, bf16[64,48,128]{2,1,0:T(8,128)(2,1)}, u32[]{:S(2)}, u32[]{:S(2)}) collective-permute-start(bf16[64,48,128]{2,1,0:T(8,128)(2,1)S(1)} %pad_maximum_fusion.refs_0_), channel_id=1, source_target_pairs={{0,4},{1,3},{2,6},{3,1},{4,0},{5,7},{6,2},{7,5},{8,12},{9,11},{10,... | collective-permute-start | bytes 2359304 | tf_op jit(solution)/shard_map/ppermute | solution.py:265
  120.3 29.7 %collective-permute-start.11 = (bf16[64,48,128]{2,1,0:T(8,128)(2,1)S(1)}, bf16[64,48,128]{2,1,0:T(8,128)(2,1)S(1)}, u32[]{:S(2)}, u32[]{:S(2)}) collective-permute-start(bf16[64,48,128]{2,1,0:T(8,128)(2,1)S(1)} %collective-permute-done.7.refs_1_), channel_id=1, source_target_pairs={{0,4},{1,3},{2,6},{3,1},{4,0},{5,7},{6,2},{7,5},{8,12},{9,11},{10,... | collective-permute-start | bytes 2359304 | tf_op jit(solution)/shard_map/ppermute | solution.py:265
  121.6 8.3 %collective-permute-start.18 = (bf16[64,16,128]{2,1,0:T(8,128)(2,1)S(1)}, bf16[64,16,128]{2,1,0:T(8,128)(2,1)S(1)}, u32[]{:S(2)}, u32[]{:S(2)}) collective-permute-start(bf16[64,16,128]{2,1,0:T(8,128)(2,1)S(1)} %pad_maximum_fusion.1.refs_4_), channel_id=1, source_target_pairs={{0,24},{8,0},{16,8},{24,16},{1,25},{9,1},{17,9},{25,17},{2,26},{10... | collective-permute-start | bytes 786440 | tf_op jit(solution)/shard_map/ppermute | solution.py:257
  122.3 24.7 %collective-permute-start.16 = (bf16[64,16,128]{2,1,0:T(8,128)(2,1)S(1)}, bf16[64,16,128]{2,1,0:T(8,128)(2,1)}, u32[]{:S(2)}, u32[]{:S(2)}) collective-permute-start(bf16[64,16,128]{2,1,0:T(8,128)(2,1)S(1)} %pad_maximum_fusion.1.refs_4_), channel_id=1, source_target_pairs={{0,16},{8,24},{16,0},{24,8},{1,17},{9,25},{17,1},{25,9},{2,18},{10... | collective-permute-start | bytes 786440 | tf_op jit(solution)/shard_map/ppermute | solution.py:257
  127.0 20.1 %collective-permute-start.14 = (bf16[64,16,128]{2,1,0:T(8,128)(2,1)S(1)}, bf16[64,16,128]{2,1,0:T(8,128)(2,1)S(1)}, u32[]{:S(2)}, u32[]{:S(2)}) collective-permute-start(bf16[64,16,128]{2,1,0:T(8,128)(2,1)S(1)} %pad_maximum_fusion.1.refs_4_), channel_id=1, source_target_pairs={{0,8},{8,16},{16,24},{24,0},{1,9},{9,17},{17,25},{25,1},{2,10},{10... | collective-permute-start | bytes 786440 | tf_op jit(solution)/shard_map/ppermute | solution.py:257
  129.8 17.8 %collective-permute-start.13 = (bf16[64,16,128]{2,1,0:T(8,128)(2,1)S(1)}, bf16[64,16,128]{2,1,0:T(8,128)(2,1)S(1)}, u32[]{:S(2)}, u32[]{:S(2)}) collective-permute-start(bf16[64,16,128]{2,1,0:T(8,128)(2,1)S(1)} %pad_maximum_fusion.1.refs_4_), channel_id=1, source_target_pairs={{0,1},{1,0},{2,3},{3,2},{4,5},{5,4},{6,7},{7,6},{8,9},{9,8},{10,11... | collective-permute-start | bytes 786440 | tf_op jit(solution)/shard_map/ppermute | solution.py:269
  147.1 2.0 %collective-permute-start.19 = (bf16[64,16,128]{2,1,0:T(8,128)(2,1)S(1)}, bf16[64,16,128]{2,1,0:T(8,128)(2,1)}, u32[]{:S(2)}, u32[]{:S(2)}) collective-permute-start(bf16[64,16,128]{2,1,0:T(8,128)(2,1)S(1)} %collective-permute-done.18.refs_7_), channel_id=1, source_target_pairs={{0,1},{1,0},{2,3},{3,2},{4,5},{5,4},{6,7},{7,6},{8,9},{9,8},{10,11... | collective-permute-start | bytes 786440 | tf_op jit(solution)/shard_map/ppermute | solution.py:269
  147.1 2.3 %collective-permute-start.17 = (bf16[64,16,128]{2,1,0:T(8,128)(2,1)}, bf16[64,16,128]{2,1,0:T(8,128)(2,1)}, u32[]{:S(2)}, u32[]{:S(2)}) collective-permute-start(bf16[64,16,128]{2,1,0:T(8,128)(2,1)} %collective-permute-done.16.refs_6_), channel_id=1, source_target_pairs={{0,1},{1,0},{2,3},{3,2},{4,5},{5,4},{6,7},{7,6},{8,9},{9,8},{10,11... | collective-permute-start | bytes 786440 | tf_op jit(solution)/shard_map/ppermute | solution.py:269
  147.7 15.9 %collective-permute-start.6 = (bf16[64,48,128]{2,1,0:T(8,128)(2,1)S(1)}, bf16[64,48,128]{2,1,0:T(8,128)(2,1)S(1)}, u32[]{:S(2)}, u32[]{:S(2)}) collective-permute-start(bf16[64,48,128]{2,1,0:T(8,128)(2,1)S(1)} %pad_maximum_fusion.refs_0_), channel_id=1, source_target_pairs={{0,1},{1,0},{2,3},{3,2},{4,5},{5,4},{6,7},{7,6},{8,9},{9,8},{10,11... | collective-permute-start | bytes 2359304 | tf_op jit(solution)/shard_map/ppermute | solution.py:269
  149.0 14.5 %collective-permute-start.15 = (bf16[64,16,128]{2,1,0:T(8,128)(2,1)S(1)}, bf16[64,16,128]{2,1,0:T(8,128)(2,1)S(1)}, u32[]{:S(2)}, u32[]{:S(2)}) collective-permute-start(bf16[64,16,128]{2,1,0:T(8,128)(2,1)S(1)} %collective-permute-done.14.refs_5_), channel_id=1, source_target_pairs={{0,1},{1,0},{2,3},{3,2},{4,5},{5,4},{6,7},{7,6},{8,9},{9,8},{10,11... | collective-permute-start | bytes 786440 | tf_op jit(solution)/shard_map/ppermute | solution.py:269
  149.4 14.2 %collective-permute-start.8 = (bf16[64,48,128]{2,1,0:T(8,128)(2,1)S(1)}, bf16[64,48,128]{2,1,0:T(8,128)(2,1)S(1)}, u32[]{:S(2)}, u32[]{:S(2)}) collective-permute-start(bf16[64,48,128]{2,1,0:T(8,128)(2,1)S(1)} %collective-permute-done.7.refs_1_), channel_id=1, source_target_pairs={{0,1},{1,0},{2,3},{3,2},{4,5},{5,4},{6,7},{7,6},{8,9},{9,8},{10,11... | collective-permute-start | bytes 2359304 | tf_op jit(solution)/shard_map/ppermute | solution.py:269
  149.6 14.0 %collective-permute-start.10 = (bf16[64,48,128]{2,1,0:T(8,128)(2,1)}, bf16[64,48,128]{2,1,0:T(8,128)(2,1)S(1)}, u32[]{:S(2)}, u32[]{:S(2)}) collective-permute-start(bf16[64,48,128]{2,1,0:T(8,128)(2,1)} %collective-permute-done.9.refs_2_), channel_id=1, source_target_pairs={{0,1},{1,0},{2,3},{3,2},{4,5},{5,4},{6,7},{7,6},{8,9},{9,8},{10,11... | collective-permute-start | bytes 2359304 | tf_op jit(solution)/shard_map/ppermute | solution.py:269
  149.9 13.7 %collective-permute-start.12 = (bf16[64,48,128]{2,1,0:T(8,128)(2,1)S(1)}, bf16[64,48,128]{2,1,0:T(8,128)(2,1)S(1)}, u32[]{:S(2)}, u32[]{:S(2)}) collective-permute-start(bf16[64,48,128]{2,1,0:T(8,128)(2,1)S(1)} %collective-permute-done.11.refs_3_), channel_id=1, source_target_pairs={{0,1},{1,0},{2,3},{3,2},{4,5},{5,4},{6,7},{7,6},{8,9},{9,8},{10,11... | collective-permute-start | bytes 2359304 | tf_op jit(solution)/shard_map/ppermute | solution.py:269

commit v5 on v4

--- a/solution.py
+++ b/solution.py
@@ -28,7 +28,7 @@
     return result.astype(BF16)
 
 
-def gather_kernel(own, group, pitch, edges_ref, weight_ref, cells_ref, out_ref, root_ref, wide_ref, total_ref, count_ref):
+def gather_kernel(own, group, pitch, edges_ref, weight_ref, cells_ref, out_ref, root_ref, total_ref, count_ref, *wide_refs):
     step = pl.program_id(0)
     last = pl.num_programs(0) - 1
     rows, zones, lanes = cells_ref.shape
@@ -57,25 +57,28 @@
     groups = zones // group
     pairs = group // 2
 
-    def widen(g, first):
-        piece = cells_ref[pl.ds(first, part), g * group : (g + 1) * group, :].astype(F32)
+    def load(g, first):
+        return cells_ref[pl.ds(first, part), g * group : (g + 1) * group, :].astype(F32)
+
+    def store(g, first, piece):
         for i in range(part):
-            wide_ref[g, pl.ds(pl.multiple_of((first + i) * pitch, 8), group), :] = piece[i]
+            wide_refs[g][pl.ds(pl.multiple_of((first + i) * pitch, 8), group), :] = piece[i]
 
     def widen_first(i, carry):
-        widen(0, i * part)
+        store(0, i * part, load(0, i * part))
         return carry
 
     lax.fori_loop(0, rows // part, widen_first, 0)
     share = rows // part // pairs
     for g in range(groups):
         for pair in range(pairs):
+            left = wide_refs[g][pl.ds(2 * pair, rows, stride=pitch), :].astype(BF16)
+            right = wide_refs[g][pl.ds(2 * pair + 1, rows, stride=pitch), :].astype(BF16)
+            both = jnp.concatenate([left, right], axis=1)
             if g + 1 < groups:
                 for i in range(share):
-                    widen(g + 1, (pair * share + i) * part)
-            left = wide_ref[g, pl.ds(2 * pair, rows, stride=pitch), :].astype(BF16)
-            right = wide_ref[g, pl.ds(2 * pair + 1, rows, stride=pitch), :].astype(BF16)
-            both = jnp.concatenate([left, right], axis=1)
+                    first = (pair * share + i) * part
+                    store(g + 1, first, load(g + 1, first))
             total_ref[g * pairs + pair] += jnp.dot(weighted, both, preferred_element_type=F32)
 
     @pl.when(step == last)
@@ -120,10 +123,10 @@
             jax.ShapeDtypeStruct((1, anchors), F32),
         ],
         scratch_shapes=[
-            pltpu.VMEM((zones // group, rows * pitch, lanes), F32),
             pltpu.VMEM((zones // 2, edges, 2 * lanes), F32),
             pltpu.VMEM((edges, lanes), F32),
-        ],
+        ]
+        + [pltpu.VMEM((rows * pitch, lanes), F32)] * (zones // group),
         compiler_params=pltpu.CompilerParams(vmem_limit_bytes=48 * 1024 * 1024),
         cost_estimate=pl.CostEstimate(
             flops=2 * anchors * edges * zones * lanes, bytes_accessed=2 * anchors * zones * lanes, transcendentals=0
@@ -196,23 +199,27 @@
     bias = bias_ref[...]
     count = long_at_ref.shape[0]
     tile = 16
-
-    def one(i, carry):
-        at = step * rows + i
-        scale = root_ref[0, at]
-        start = 0
-        for table, places in ((long_ref, long_at_ref), (short_ref, short_at_ref)):
-            spots = [places[j, at] for j in range(count)]
-            for first in range(0, table.shape[1], tile):
-                pieces = [table[spot, first : first + tile, :] for spot in spots]
-                pieces = [(a + b).astype(F32) for a, b in zip(pieces[0::2], pieces[1::2])]
-                total = sum(pieces[1:], pieces[0])
-                value = jnp.maximum((total * scale + bias).astype(BF16), BF16(0.0))
-                out_ref[i, start : start + tile, :] = value
-                start += tile
+    batch = 4
+
+    def several(group, carry):
+        values = []
+        for i in range(batch):
+            at = step * rows + group * batch + i
+            scale = root_ref[0, at]
+            for table, places in ((long_ref, long_at_ref), (short_ref, short_at_ref)):
+                spots = [places[j, at] for j in range(count)]
+                for first in range(0, table.shape[1], tile):
+                    pieces = [table[spot, first : first + tile, :] for spot in spots]
+                    pieces = [(a + b).astype(F32) for a, b in zip(pieces[0::2], pieces[1::2])]
+                    total = sum(pieces[1:], pieces[0])
+                    values.append(jnp.maximum((total * scale + bias).astype(BF16), BF16(0.0)))
+        tiles = zones // tile
+        for n, value in enumerate(values):
+            start = n % tiles * tile
+            out_ref[group * batch + n // tiles, start : start + tile, :] = value
         return carry
 
-    lax.fori_loop(0, rows, one, 0, unroll=4)
+    lax.fori_loop(0, rows // batch, several, 0)
 
 
 def spread(half, long_at, short_at, root, bias, longs, shorts, before=None):
@@ -283,8 +290,9 @@
     short, long = lax.optimization_barrier((short, long))
     first = crossed(long, 0)
     second = crossed(long, 1)
+    shorts = [short] + [shifted(short, k) for k in range(1, size)]
+    first, *shorts[1:-1] = lax.optimization_barrier((first, *shorts[1:-1]))
     both = crossed(first, 1)
-    shorts = [short] + [shifted(short, k) for k in range(1, size)]
     return [long, first, second, both], shorts
 
 

time: 177 us -> 163 us (0.921)
  the two profiles are of different devices: /device:TPU:0 before, /device:TPU:13 now
where the time goes in v5:
time: 163 us; the launch traced here: 161 us
  waiting for transfers between devices  85.4 us (52%)
  Pallas kernels  42.6 us (26%)
  starting transfers between devices  28.8 us (18%)
  local copies, waits for them, and re-layouts  3.06 us (2%)
    all_to_all x1, waiting for transfers between devices, shards(): lax.all_to_all(parts, everyone, split_axis=0, concat_axis=0, tiled=True)  47.6 us
    ppermute x6, waiting for transfers between devices, shifted(): lax.ppermute(x, LINE, [(i, (i + amount) % size) for i in range(size)])  33.2 us
    pallas_call x2, Pallas kernels, spread(): pl.pallas_call(functools.partial(spread_kernel, len(longs), len(shorts)),...  27.1 us
    pallas_call x1, Pallas kernels, partial_sums(): pl.pallas_call(functools.partial(gather_kernel, own, group, pitch), grid=...  14.8 us
    ppermute x9, starting transfers between devices, swapped(): return lax.ppermute(x, 'core', [(0, 1), (1, 0)])  12.9 us
    ppermute x6, starting transfers between devices, shifted(): lax.ppermute(x, LINE, [(i, (i + amount) % size) for i in range(size)])  6.63 us
    all_to_all x1, starting transfers between devices, shards(): lax.all_to_all(parts, everyone, split_axis=0, concat_axis=0, tiled=True)  6.33 us
  transfers between devices with their start and end apart: 21, of which 10 were waited for; matrix products, arithmetic and copies ran while one was open for 1% of the time, Pallas kernels for 9%

profile of v5, /device:TPU:13, one launch (start us, length us, event | category | flops | bytes accessed | tf_op | source)
XLA Modules:
  0.0 161.0 jit_solution(12189516514220869252)
XLA Ops:
  0.0 0.8 copy-done.1
  0.8 0.7 copy-done.4
  1.5 14.8 %shard_map.73 = (bf16[32,272,128]{2,1,0:T(8,128)(2,1)S(1)}, f32[1,2048]{1,0:T(1,128)S(1)}) custom-call(s32[4,2048]{1,0:T(4,128)S(1)} %bitcast.31, f32[1,256]{1,0:T(1,128)S(1)} %bitcast.32, bf16[2048,32,128]{2,1,0:T(8,128)(2,1)} %cells_ref.1), custom_call_target="tpu_custom_call" | custom-call | flops 4294967296 | bytes 16777216 | tf_op jit(solution)/shard_map/pallas_call | solution.py:109
  16.2 0.0 copy-start
  16.3 1.4 copy-done
  17.6 6.3 %all-to-all-start = ((bf16[32,272,128]{2,1,0:T(8,128)(2,1)}), bf16[32,272,128]{2,1,0:T(8,128)(2,1)S(1)}, u32[]{:S(2)}, u32[]{:S(2)}) async-start(bf16[32,272,128]{2,1,0:T(8,128)(2,1)} %copy-done), calls=%async_computation | async-start | bytes 4456448 | tf_op jit(solution)/shard_map/all_to_all | solution.py:319
  24.0 0.1 dynamic_slice.11
  24.1 0.1 convert_reduce_fusion
  24.2 0.1 multiply_reduce_fusion
  24.3 0.4 convolution_convert_fusion
  24.7 47.6 %all-to-all-done.parts_ref = bf16[32,272,128]{2,1,0:T(8,128)(2,1)S(1)} async-done(((bf16[32,272,128]{2,1,0:T(8,128)(2,1)}), bf16[32,272,128]{2,1,0:T(8,128)(2,1)S(1)}, u32[]{:S(2)}, u32[]{:S(2)}) %all-to-all-start) | async-done | bytes 2228256 | tf_op jit(solution)/shard_map/all_to_all | solution.py:319
  72.4 0.1 broadcast_in_dim.32.weight_ref
  72.4 0.7 shard_map.74
  73.1 1.3 collective-permute-start
  74.4 1.0 collective-permute-done
  75.5 0.9 collective-permute-start.1
  76.4 2.2 %collective-permute-done.1 = bf16[16,16,128]{2,1,0:T(8,128)(2,1)S(1)} collective-permute-done((bf16[16,16,128]{2,1,0:T(8,128)(2,1)S(1)}, bf16[16,16,128]{2,1,0:T(8,128)(2,1)S(1)}, u32[]{:S(2)}, u32[]{:S(2)}) %collective-permute-start.1) | collective-permute-done | bytes 65568 | tf_op jit(solution)/shard_map/ppermute | solution.py:272
  78.7 1.0 collective-permute-start.2
  79.7 3.0 %collective-permute-start.4 = (bf16[16,48,128]{2,1,0:T(8,128)(2,1)S(1)}, bf16[16,48,128]{2,1,0:T(8,128)(2,1)S(1)}, u32[]{:S(2)}, u32[]{:S(2)}) collective-permute-start(bf16[16,48,128]{2,1,0:T(8,128)(2,1)S(1)} %slice.19), channel_id=1, source_target_pairs={{0,16},{8,24},{16,0},{24,8},{1,17},{9,25},{17,1},{25,9},{2,18},{10... | collective-permute-start | bytes 589832 | tf_op jit(solution)/shard_map/ppermute | solution.py:264
  82.7 0.6 collective-permute-start.3
  83.3 0.8 collective-permute-start.5
  84.2 0.0 collective-permute-done.2
  84.2 8.1 %collective-permute-done.4 = bf16[16,48,128]{2,1,0:T(8,128)(2,1)S(1)} collective-permute-done((bf16[16,48,128]{2,1,0:T(8,128)(2,1)S(1)}, bf16[16,48,128]{2,1,0:T(8,128)(2,1)S(1)}, u32[]{:S(2)}, u32[]{:S(2)}) %collective-permute-start.4) | collective-permute-done | bytes 196640 | tf_op jit(solution)/shard_map/ppermute | solution.py:264
  92.3 6.9 %collective-permute-done.3 = bf16[16,48,128]{2,1,0:T(8,128)(2,1)S(1)} collective-permute-done((bf16[16,48,128]{2,1,0:T(8,128)(2,1)S(1)}, bf16[16,48,128]{2,1,0:T(8,128)(2,1)S(1)}, u32[]{:S(2)}, u32[]{:S(2)}) %collective-permute-start.3) | collective-permute-done | bytes 196640 | tf_op jit(solution)/shard_map/ppermute | solution.py:264
  99.2 1.6 collective-permute-done.5
  100.7 0.1 pad_maximum_fusion.refs_0_
  100.9 0.8 collective-permute-start.7
  101.7 0.0 collective-permute-start.9
  101.7 0.3 collective-permute-start.8
  102.0 0.1 collective-permute-start.11
  102.2 2.0 %collective-permute-start.6 = (bf16[64,48,128]{2,1,0:T(8,128)(2,1)S(1)}, bf16[64,48,128]{2,1,0:T(8,128)(2,1)S(1)}, u32[]{:S(2)}, u32[]{:S(2)}) collective-permute-start(bf16[64,48,128]{2,1,0:T(8,128)(2,1)S(1)} %pad_maximum_fusion.refs_0_), channel_id=1, source_target_pairs={{0,1},{1,0},{2,3},{3,2},{4,5},{5,4},{6,7},{7,6},{8,9},{9,8},{10,11... | collective-permute-start | bytes 2359304 | tf_op jit(solution)/shard_map/ppermute | solution.py:276
  104.1 9.1 %collective-permute-done.9.refs_6_ = bf16[64,16,128]{2,1,0:T(8,128)(2,1)S(1)} collective-permute-done((bf16[64,16,128]{2,1,0:T(8,128)(2,1)S(1)}, bf16[64,16,128]{2,1,0:T(8,128)(2,1)S(1)}, u32[]{:S(2)}, u32[]{:S(2)}) %collective-permute-start.9) | collective-permute-done | bytes 262176 | tf_op jit(solution)/shard_map/ppermute | solution.py:264
  113.3 5.6 %collective-permute-done.8.refs_5_ = bf16[64,16,128]{2,1,0:T(8,128)(2,1)S(1)} collective-permute-done((bf16[64,16,128]{2,1,0:T(8,128)(2,1)S(1)}, bf16[64,16,128]{2,1,0:T(8,128)(2,1)S(1)}, u32[]{:S(2)}, u32[]{:S(2)}) %collective-permute-start.8) | collective-permute-done | bytes 262176 | tf_op jit(solution)/shard_map/ppermute | solution.py:264
  118.9 1.8 %collective-permute-start.18 = (bf16[64,16,128]{2,1,0:T(8,128)(2,1)S(1)}, bf16[64,16,128]{2,1,0:T(8,128)(2,1)}, u32[]{:S(2)}, u32[]{:S(2)}) collective-permute-start(bf16[64,16,128]{2,1,0:T(8,128)(2,1)S(1)} %pad_maximum_fusion.1.refs_4_), channel_id=1, source_target_pairs={{0,24},{8,0},{16,8},{24,16},{1,25},{9,1},{17,9},{25,17},{2,26},{10... | collective-permute-start | bytes 786440 | tf_op jit(solution)/shard_map/ppermute | solution.py:264
  120.8 0.1 multiply_add_fusion
  120.8 2.6 %collective-permute-start.15 = (bf16[64,16,128]{2,1,0:T(8,128)(2,1)S(1)}, bf16[64,16,128]{2,1,0:T(8,128)(2,1)}, u32[]{:S(2)}, u32[]{:S(2)}) collective-permute-start(bf16[64,16,128]{2,1,0:T(8,128)(2,1)S(1)} %pad_maximum_fusion.1.refs_4_), channel_id=1, source_target_pairs={{0,1},{1,0},{2,3},{3,2},{4,5},{5,4},{6,7},{7,6},{8,9},{9,8},{10,11... | collective-permute-start | bytes 786440 | tf_op jit(solution)/shard_map/ppermute | solution.py:276
  123.4 1.9 %collective-permute-done.18.refs_7_ = bf16[64,16,128]{2,1,0:T(8,128)(2,1)} collective-permute-done((bf16[64,16,128]{2,1,0:T(8,128)(2,1)S(1)}, bf16[64,16,128]{2,1,0:T(8,128)(2,1)}, u32[]{:S(2)}, u32[]{:S(2)}) %collective-permute-start.18) | collective-permute-done | bytes 262176 | tf_op jit(solution)/shard_map/ppermute | solution.py:264
  125.4 3.7 %collective-permute-start.19 = (bf16[64,16,128]{2,1,0:T(8,128)(2,1)}, bf16[64,16,128]{2,1,0:T(8,128)(2,1)}, u32[]{:S(2)}, u32[]{:S(2)}) collective-permute-start(bf16[64,16,128]{2,1,0:T(8,128)(2,1)} %collective-permute-done.18.refs_7_), channel_id=1, source_target_pairs={{0,1},{1,0},{2,3},{3,2},{4,5},{5,4},{6,7},{7,6},{8,9},{9,8},{10,11... | collective-permute-start | bytes 786440 | tf_op jit(solution)/shard_map/ppermute | solution.py:276
  129.1 0.0 collective-permute-done.15.refs_4_
  129.1 0.1 collective-permute-start.10
  129.2 1.4 collective-permute-done.19.refs_7_
  130.6 0.4 collective-permute-start.16
  130.9 0.0 collective-permute-done.11.refs_2_
  130.9 0.1 collective-permute-start.17
  131.1 0.4 collective-permute-start.12
  131.5 2.3 %collective-permute-start.14 = (bf16[64,48,128]{2,1,0:T(8,128)(2,1)}, bf16[64,48,128]{2,1,0:T(8,128)(2,1)S(1)}, u32[]{:S(2)}, u32[]{:S(2)}) collective-permute-start(bf16[64,48,128]{2,1,0:T(8,128)(2,1)} %collective-permute-done.13.refs_3_), channel_id=1, source_target_pairs={{0,1},{1,0},{2,3},{3,2},{4,5},{5,4},{6,7},{7,6},{8,9},{9,8},{10,11... | collective-permute-start | bytes 2359304 | tf_op jit(solution)/shard_map/ppermute | solution.py:276
  133.8 13.7 %shard_map.75.refs_8_ = bf16[512,128,128]{2,1,0:T(8,128)(2,1)} custom-call(s32[1]{0:T(128)} %bitcast.5.half_ref, s32[4,512]{1,0:T(4,128)S(1)} %get-tuple-element.35.long_at_ref, s32[4,512]{1,0:T(4,128)S(1)} %get-tuple-element.29.short_at_ref, f32[1,512]{1,0:T(1,128)S(1)} %constant_dynamic-slice_fusion.root_ref, f32[1,128]{1,0:T(1,128)S(1)} %bitcast.33, ...), custom_call_target="tpu_custom_call" | custom-call | flops 17179869184 | bytes 16777216 | tf_op jit(solution)/shard_map/pallas_call | solution.py:240
  147.5 13.4 %shard_map.76 = bf16[512,128,128]{2,1,0:T(8,128)(2,1)} custom-call(s32[1]{0:T(128)} %bitcast.half_ref, s32[4,512]{1,0:T(4,128)S(1)} %get-tuple-element.37.long_at_ref, s32[4,512]{1,0:T(4,128)S(1)} %get-tuple-element.36.short_at_ref, f32[1,512]{1,0:T(1,128)S(1)} %constant_dynamic-slice_fusion.root_ref, ...), custom_call_target="tpu_custom_call", output_to_operand_aliasing={{}: (13, {})} | custom-call | flops 17179869184 | bytes 16777216 | tf_op jit(solution)/shard_map/pallas_call | solution.py:240
  (36 shorter events, 0.3 us)
Async XLA Ops:
  0.0 24.0 %copy-start.5 = (f32[256]{0:T(256)S(1)}, f32[256]{0:T(256)}, u32[]{:S(2)}) copy-start(f32[256]{0:T(256)} %param.9) | copy-start | bytes 3076
  0.0 24.1 %copy-start.7 = (s32[128,3]{0,1:T(4,128)S(1)}, s32[128,3]{0,1:T(4,128)}, u32[]{:S(2)}) copy-start(s32[128,3]{0,1:T(4,128)} %param.11) | copy-start | bytes 4612
  0.0 133.8 %copy-start.6 = (f32[128]{0:T(128)S(1)}, f32[128]{0:T(128)}, u32[]{:S(2)}) copy-start(f32[128]{0:T(128)} %param.13) | copy-start | bytes 1540
  0.0 0.8 copy-start.1
  0.8 0.7 copy-start.4
  1.5 22.7 %copy-start.8 = (f32[128]{0:T(128)S(1)}, f32[128]{0:T(128)}, u32[]{:S(2)}) copy-start(f32[128]{0:T(128)} %param.12) | copy-start | bytes 1540
  1.5 70.9 %copy-start.3 = (bf16[128,128]{1,0:T(8,128)(2,1)S(1)}, bf16[128,128]{1,0:T(8,128)(2,1)}, u32[]{:S(2)}) copy-start(bf16[128,128]{1,0:T(8,128)(2,1)} %mixing_ref.1) | copy-start | bytes 98308
  1.5 119.2 %copy-start.2 = (s32[2048,4]{0,1:T(4,128)S(1)}, s32[2048,4]{0,1:T(4,128)}, u32[]{:S(2)}) copy-start(s32[2048,4]{0,1:T(4,128)} %param.8) | copy-start | bytes 98308
  16.2 1.4 copy-start
  17.6 54.7 %all-to-all-start = ((bf16[32,272,128]{2,1,0:T(8,128)(2,1)}), bf16[32,272,128]{2,1,0:T(8,128)(2,1)S(1)}, u32[]{:S(2)}, u32[]{:S(2)}) async-start(bf16[32,272,128]{2,1,0:T(8,128)(2,1)} %copy-done), calls=%async_computation | async-start | bytes 4456448 | tf_op jit(solution)/shard_map/all_to_all | solution.py:319
  73.1 2.3 %collective-permute-start = (bf16[8,64,128]{2,1,0:T(8,128)(2,1)S(1)}, bf16[8,64,128]{2,1,0:T(8,128)(2,1)S(1)}, u32[]{:S(2)}, u32[]{:S(2)}) collective-permute-start(bf16[8,64,128]{2,1,0:T(8,128)(2,1)S(1)} %get-tuple-element.19), channel_id=1, source_target_pairs={{0,1},{1,0},{2,3},{3,2},{4,5},{5,4},{6,7},{7,6},{8,9},{9,8},{10,11... | collective-permute-start | bytes 393224 | tf_op jit(solution)/shard_map/ppermute | solution.py:276
  75.5 3.2 %collective-permute-start.1 = (bf16[16,16,128]{2,1,0:T(8,128)(2,1)S(1)}, bf16[16,16,128]{2,1,0:T(8,128)(2,1)S(1)}, u32[]{:S(2)}, u32[]{:S(2)}) collective-permute-start(bf16[16,16,128]{2,1,0:T(8,128)(2,1)S(1)} %slice.18), channel_id=1, source_target_pairs={{0,2},{1,5},{2,0},{3,7},{4,6},{5,1},{6,4},{7,3},{8,10},{9,13},{10,... | collective-permute-start | bytes 196616 | tf_op jit(solution)/shard_map/ppermute | solution.py:272
  78.7 5.5 %collective-permute-start.2 = (bf16[32,16,128]{2,1,0:T(8,128)(2,1)S(1)}, bf16[32,16,128]{2,1,0:T(8,128)(2,1)S(1)}, u32[]{:S(2)}, u32[]{:S(2)}) collective-permute-start(bf16[32,16,128]{2,1,0:T(8,128)(2,1)S(1)} %pad_maximum_fusion.2), channel_id=1, source_target_pairs={{0,4},{1,3},{2,6},{3,1},{4,0},{5,7},{6,2},{7,5},{8,12},{9,11},{10,... | collective-permute-start | bytes 393224 | tf_op jit(solution)/shard_map/ppermute | solution.py:272
  79.7 12.6 %collective-permute-start.4 = (bf16[16,48,128]{2,1,0:T(8,128)(2,1)S(1)}, bf16[16,48,128]{2,1,0:T(8,128)(2,1)S(1)}, u32[]{:S(2)}, u32[]{:S(2)}) collective-permute-start(bf16[16,48,128]{2,1,0:T(8,128)(2,1)S(1)} %slice.19), channel_id=1, source_target_pairs={{0,16},{8,24},{16,0},{24,8},{1,17},{9,25},{17,1},{25,9},{2,18},{10... | collective-permute-start | bytes 589832 | tf_op jit(solution)/shard_map/ppermute | solution.py:264
  82.7 16.5 %collective-permute-start.3 = (bf16[16,48,128]{2,1,0:T(8,128)(2,1)S(1)}, bf16[16,48,128]{2,1,0:T(8,128)(2,1)S(1)}, u32[]{:S(2)}, u32[]{:S(2)}) collective-permute-start(bf16[16,48,128]{2,1,0:T(8,128)(2,1)S(1)} %slice.19), channel_id=1, source_target_pairs={{0,8},{8,16},{16,24},{24,0},{1,9},{9,17},{17,25},{25,1},{2,10},{10... | collective-permute-start | bytes 589832 | tf_op jit(solution)/shard_map/ppermute | solution.py:264
  83.3 17.4 %collective-permute-start.5 = (bf16[16,48,128]{2,1,0:T(8,128)(2,1)S(1)}, bf16[16,48,128]{2,1,0:T(8,128)(2,1)S(1)}, u32[]{:S(2)}, u32[]{:S(2)}) collective-permute-start(bf16[16,48,128]{2,1,0:T(8,128)(2,1)S(1)} %slice.19), channel_id=1, source_target_pairs={{0,24},{8,0},{16,8},{24,16},{1,25},{9,1},{17,9},{25,17},{2,26},{10... | collective-permute-start | bytes 589832 | tf_op jit(solution)/shard_map/ppermute | solution.py:264
  100.9 18.0 %collective-permute-start.7 = (bf16[64,48,128]{2,1,0:T(8,128)(2,1)S(1)}, bf16[64,48,128]{2,1,0:T(8,128)(2,1)S(1)}, u32[]{:S(2)}, u32[]{:S(2)}) collective-permute-start(bf16[64,48,128]{2,1,0:T(8,128)(2,1)S(1)} %pad_maximum_fusion.refs_0_), channel_id=1, source_target_pairs={{0,2},{1,5},{2,0},{3,7},{4,6},{5,1},{6,4},{7,3},{8,10},{9,13},{10,... | collective-permute-start | bytes 2359304 | tf_op jit(solution)/shard_map/ppermute | solution.py:272
  101.7 11.6 %collective-permute-start.9 = (bf16[64,16,128]{2,1,0:T(8,128)(2,1)S(1)}, bf16[64,16,128]{2,1,0:T(8,128)(2,1)S(1)}, u32[]{:S(2)}, u32[]{:S(2)}) collective-permute-start(bf16[64,16,128]{2,1,0:T(8,128)(2,1)S(1)} %pad_maximum_fusion.1.refs_4_), channel_id=1, source_target_pairs={{0,16},{8,24},{16,0},{24,8},{1,17},{9,25},{17,1},{25,9},{2,18},{10... | collective-permute-start | bytes 786440 | tf_op jit(solution)/shard_map/ppermute | solution.py:264
  101.7 17.2 %collective-permute-start.8 = (bf16[64,16,128]{2,1,0:T(8,128)(2,1)S(1)}, bf16[64,16,128]{2,1,0:T(8,128)(2,1)S(1)}, u32[]{:S(2)}, u32[]{:S(2)}) collective-permute-start(bf16[64,16,128]{2,1,0:T(8,128)(2,1)S(1)} %pad_maximum_fusion.1.refs_4_), channel_id=1, source_target_pairs={{0,8},{8,16},{16,24},{24,0},{1,9},{9,17},{17,25},{25,1},{2,10},{10... | collective-permute-start | bytes 786440 | tf_op jit(solution)/shard_map/ppermute | solution.py:264
  102.0 28.9 %collective-permute-start.11 = (bf16[64,48,128]{2,1,0:T(8,128)(2,1)S(1)}, bf16[64,48,128]{2,1,0:T(8,128)(2,1)}, u32[]{:S(2)}, u32[]{:S(2)}) collective-permute-start(bf16[64,48,128]{2,1,0:T(8,128)(2,1)S(1)} %pad_maximum_fusion.refs_0_), channel_id=1, source_target_pairs={{0,4},{1,3},{2,6},{3,1},{4,0},{5,7},{6,2},{7,5},{8,12},{9,11},{10,... | collective-permute-start | bytes 2359304 | tf_op jit(solution)/shard_map/ppermute | solution.py:272
  102.2 28.9 %collective-permute-start.6 = (bf16[64,48,128]{2,1,0:T(8,128)(2,1)S(1)}, bf16[64,48,128]{2,1,0:T(8,128)(2,1)S(1)}, u32[]{:S(2)}, u32[]{:S(2)}) collective-permute-start(bf16[64,48,128]{2,1,0:T(8,128)(2,1)S(1)} %pad_maximum_fusion.refs_0_), channel_id=1, source_target_pairs={{0,1},{1,0},{2,3},{3,2},{4,5},{5,4},{6,7},{7,6},{8,9},{9,8},{10,11... | collective-permute-start | bytes 2359304 | tf_op jit(solution)/shard_map/ppermute | solution.py:276
  118.9 12.6 %collective-permute-start.13 = (bf16[64,48,128]{2,1,0:T(8,128)(2,1)S(1)}, bf16[64,48,128]{2,1,0:T(8,128)(2,1)}, u32[]{:S(2)}, u32[]{:S(2)}) collective-permute-start(bf16[64,48,128]{2,1,0:T(8,128)(2,1)S(1)} %collective-permute-done.7.refs_1_), channel_id=1, source_target_pairs={{0,4},{1,3},{2,6},{3,1},{4,0},{5,7},{6,2},{7,5},{8,12},{9,11},{10,... | collective-permute-start | bytes 2359304 | tf_op jit(solution)/shard_map/ppermute | solution.py:272
  118.9 6.5 %collective-permute-start.18 = (bf16[64,16,128]{2,1,0:T(8,128)(2,1)S(1)}, bf16[64,16,128]{2,1,0:T(8,128)(2,1)}, u32[]{:S(2)}, u32[]{:S(2)}) collective-permute-start(bf16[64,16,128]{2,1,0:T(8,128)(2,1)S(1)} %pad_maximum_fusion.1.refs_4_), channel_id=1, source_target_pairs={{0,24},{8,0},{16,8},{24,16},{1,25},{9,1},{17,9},{25,17},{2,26},{10... | collective-permute-start | bytes 786440 | tf_op jit(solution)/shard_map/ppermute | solution.py:264
  120.8 8.3 %collective-permute-start.15 = (bf16[64,16,128]{2,1,0:T(8,128)(2,1)S(1)}, bf16[64,16,128]{2,1,0:T(8,128)(2,1)}, u32[]{:S(2)}, u32[]{:S(2)}) collective-permute-start(bf16[64,16,128]{2,1,0:T(8,128)(2,1)S(1)} %pad_maximum_fusion.1.refs_4_), channel_id=1, source_target_pairs={{0,1},{1,0},{2,3},{3,2},{4,5},{5,4},{6,7},{7,6},{8,9},{9,8},{10,11... | collective-permute-start | bytes 786440 | tf_op jit(solution)/shard_map/ppermute | solution.py:276
  125.4 5.2 %collective-permute-start.19 = (bf16[64,16,128]{2,1,0:T(8,128)(2,1)}, bf16[64,16,128]{2,1,0:T(8,128)(2,1)}, u32[]{:S(2)}, u32[]{:S(2)}) collective-permute-start(bf16[64,16,128]{2,1,0:T(8,128)(2,1)} %collective-permute-done.18.refs_7_), channel_id=1, source_target_pairs={{0,1},{1,0},{2,3},{3,2},{4,5},{5,4},{6,7},{7,6},{8,9},{9,8},{10,11... | collective-permute-start | bytes 786440 | tf_op jit(solution)/shard_map/ppermute | solution.py:276
  129.1 18.4 %collective-permute-start.10 = (bf16[64,48,128]{2,1,0:T(8,128)(2,1)S(1)}, bf16[64,48,128]{2,1,0:T(8,128)(2,1)S(1)}, u32[]{:S(2)}, u32[]{:S(2)}) collective-permute-start(bf16[64,48,128]{2,1,0:T(8,128)(2,1)S(1)} %collective-permute-done.7.refs_1_), channel_id=1, source_target_pairs={{0,1},{1,0},{2,3},{3,2},{4,5},{5,4},{6,7},{7,6},{8,9},{9,8},{10,11... | collective-permute-start | bytes 2359304 | tf_op jit(solution)/shard_map/ppermute | solution.py:276
  130.6 16.9 %collective-permute-start.16 = (bf16[64,16,128]{2,1,0:T(8,128)(2,1)S(1)}, bf16[64,16,128]{2,1,0:T(8,128)(2,1)S(1)}, u32[]{:S(2)}, u32[]{:S(2)}) collective-permute-start(bf16[64,16,128]{2,1,0:T(8,128)(2,1)S(1)} %collective-permute-done.8.refs_5_), channel_id=1, source_target_pairs={{0,1},{1,0},{2,3},{3,2},{4,5},{5,4},{6,7},{7,6},{8,9},{9,8},{10,11... | collective-permute-start | bytes 786440 | tf_op jit(solution)/shard_map/ppermute | solution.py:276
  130.9 16.5 %collective-permute-start.17 = (bf16[64,16,128]{2,1,0:T(8,128)(2,1)S(1)}, bf16[64,16,128]{2,1,0:T(8,128)(2,1)S(1)}, u32[]{:S(2)}, u32[]{:S(2)}) collective-permute-start(bf16[64,16,128]{2,1,0:T(8,128)(2,1)S(1)} %collective-permute-done.9.refs_6_), channel_id=1, source_target_pairs={{0,1},{1,0},{2,3},{3,2},{4,5},{5,4},{6,7},{7,6},{8,9},{9,8},{10,11... | collective-permute-start | bytes 786440 | tf_op jit(solution)/shard_map/ppermute | solution.py:276
  131.1 16.4 %collective-permute-start.12 = (bf16[64,48,128]{2,1,0:T(8,128)(2,1)}, bf16[64,48,128]{2,1,0:T(8,128)(2,1)S(1)}, u32[]{:S(2)}, u32[]{:S(2)}) collective-permute-start(bf16[64,48,128]{2,1,0:T(8,128)(2,1)} %collective-permute-done.11.refs_2_), channel_id=1, source_target_pairs={{0,1},{1,0},{2,3},{3,2},{4,5},{5,4},{6,7},{7,6},{8,9},{9,8},{10,11... | collective-permute-start | bytes 2359304 | tf_op jit(solution)/shard_map/ppermute | solution.py:276
  131.5 16.1 %collective-permute-start.14 = (bf16[64,48,128]{2,1,0:T(8,128)(2,1)}, bf16[64,48,128]{2,1,0:T(8,128)(2,1)S(1)}, u32[]{:S(2)}, u32[]{:S(2)}) collective-permute-start(bf16[64,48,128]{2,1,0:T(8,128)(2,1)} %collective-permute-done.13.refs_3_), channel_id=1, source_target_pairs={{0,1},{1,0},{2,3},{3,2},{4,5},{5,4},{6,7},{7,6},{8,9},{9,8},{10,11... | collective-permute-start | bytes 2359304 | tf_op jit(solution)/shard_map/ppermute | solution.py:276

commit v6 on v5

v6 whole, which is shorter than its diff:
```python
import functools

import jax
import jax.numpy as jnp
from jax import lax
from jax.experimental import pallas as pl
from jax.experimental.pallas import tpu as pltpu
from jax.sharding import Mesh, PartitionSpec as P

BF16 = jnp.bfloat16
F32 = jnp.float32
COUNT_BASE = 256.0
HEAD = 16


def corridor_table(edge_ids, edge_count):
    columns = jnp.arange(edge_count, dtype=jnp.int32)
    return jnp.sum((edge_ids[:, :, None] == columns[None, None, :]).astype(F32), axis=1)


def dest_operator(dst_edges, dst_weight):
    dst_member = corridor_table(dst_edges, dst_weight.shape[0])
    dst_degree = jnp.sum(dst_member * dst_weight[None, :], axis=1)
    edge_sizes = jnp.sum(dst_member, axis=0)
    left_factor = dst_member * lax.rsqrt(dst_degree)[:, None]
    right_factor = left_factor * (dst_weight / edge_sizes)[None, :]
    result = jnp.dot(right_factor, left_factor.T, precision=lax.Precision.HIGHEST)
    return result.astype(BF16)


class Plan:
    def __init__(self, zones, own, rest, line, anchors):
        self.own = own
        self.rest = rest
        self.line = line
        self.cut = zones * 5 // 8
        self.first_rows = self.cut * own
        self.second_rows = HEAD + (zones - self.cut) * own
        self.streams = 4 if anchors % 512 == 0 else 1

    def spot(self, device):
        core, near = device % 2, device // 2 % 2
        rest, mid, slow = device // 4 % self.rest, device // (4 * self.rest) % 2, device // (8 * self.rest)
        return mid * 4 + near * 2 + core, slow * self.rest + rest


def halves_of(counts):
    high = jnp.floor(counts * (1.0 / COUNT_BASE))
    return high, counts - high * COUNT_BASE


def head_rows(high, low):
    parts = [high, low]
    if high.shape[0] < HEAD // 2:
        pad = jnp.zeros((HEAD // 2 - high.shape[0], high.shape[1]), F32)
        parts = [high, pad, low, pad]
    return jnp.concatenate(parts, axis=0).astype(BF16)


def gather_kernel(own, group, pitch, plan, edges_ref, weight_ref, *refs):
    n_cells = plan.streams
    cells_refs = refs[:n_cells]
    first_ref, second_ref, root_ref, total_ref, count_ref = refs[n_cells : n_cells + 5]
    wide_refs = refs[n_cells + 5 :]
    step = pl.program_id(0)
    last = pl.num_programs(0) - 1
    strip, zones, lanes = cells_refs[0].shape
    rows = strip * n_cells
    edges = total_ref.shape[1]

    @pl.when(step == 0)
    def _():
        total_ref[...] = jnp.zeros_like(total_ref)
        count_ref[...] = jnp.zeros_like(count_ref)

    columns = lax.broadcasted_iota(jnp.int32, (edges, rows), 0)
    ids = edges_ref[...]
    member = columns == ids[0:1, :]
    for j in range(1, ids.shape[0]):
        member = jnp.logical_or(member, columns == ids[j : j + 1, :])
    upright = jnp.transpose(jnp.broadcast_to(weight_ref[...], (lanes, edges)))
    upright = jnp.concatenate([upright] * (rows // lanes), axis=1)
    root = lax.rsqrt(jnp.sum(jnp.where(member, upright, 0.0), axis=0, keepdims=True))
    root_ref[...] = root
    rounded = root.astype(BF16).astype(F32)
    weighted = jnp.where(member, rounded, 0.0).astype(BF16)
    hot = jnp.where(member, 1.0, 0.0).astype(BF16)
    count_ref[...] += jnp.dot(hot, jnp.ones((rows, lanes), BF16), preferred_element_type=F32)

    part = 32
    groups = zones // group
    pairs = group // 2

    def load(g, stream, first):
        return cells_refs[stream][pl.ds(first, part), g * group : (g + 1) * group, :].astype(F32)

    def store(g, first, piece):
        for i in range(part):
            wide_refs[g][pl.ds(pl.multiple_of((first + i) * pitch, 8), group), :] = piece[i]

    for stream in range(n_cells):

        def widen_first(i, carry):
            store(0, stream * strip + i * part, load(0, stream, i * part))
            return carry

        lax.fori_loop(0, strip // part, widen_first, 0)
    share = rows // part // pairs
    for g in range(groups):
        for pair in range(pairs):
            left = wide_refs[g][pl.ds(2 * pair, rows, stride=pitch), :].astype(BF16)
            right = wide_refs[g][pl.ds(2 * pair + 1, rows, stride=pitch), :].astype(BF16)
            both = jnp.concatenate([left, right], axis=1)
            if g + 1 < groups:
                for i in range(share):
                    first = (pair * share + i) * part
                    store(g + 1, first, load(g + 1, first // strip, first % strip))
            total_ref[g * pairs + pair] += jnp.dot(weighted, both, preferred_element_type=F32)

    @pl.when(step == last)
    def _():
        high, low = halves_of(count_ref[...])
        for device in range(edges // own):
            square, line = plan.spot(device)
            at = slice(device * own, (device + 1) * own)

            def columns_of(start, stop):
                data = []
                for d in range(start, stop):
                    data.append(total_ref[d // 2, at, (d % 2) * lanes : (d % 2 + 1) * lanes])
                return jnp.concatenate(data, axis=0).astype(BF16)

            first_ref[square, line] = columns_of(0, plan.cut)
            second_ref[line, square, HEAD:, :] = columns_of(plan.cut, zones)
            second_ref[line, square, 0:HEAD, :] = head_rows(high[at], low[at])


def partial_sums(cells, edges_t, edge_weight, plan):
    anchors, zones, lanes = cells.shape
    edges = edge_weight.shape[0]
    rows = min(512, anchors)
    strip = rows // plan.streams
    group = min(zones, 16)
    pitch = group + 8
    specs = []
    for stream in range(plan.streams):
        specs.append(pl.BlockSpec((strip, zones, lanes), lambda i, stream=stream: (i * plan.streams + stream, 0, 0)))
    shapes = [(8, plan.line, plan.first_rows, lanes), (plan.line, 8, plan.second_rows, lanes)]
    return pl.pallas_call(
        functools.partial(gather_kernel, plan.own, group, pitch, plan),
        grid=(anchors // rows,),
        in_specs=[
            pl.BlockSpec((edges_t.shape[0], rows), lambda i: (0, i)),
            pl.BlockSpec((1, edges), lambda i: (0, 0)),
        ]
        + specs,
        out_specs=[pl.BlockSpec(shape, lambda i: (0, 0, 0, 0)) for shape in shapes]
        + [pl.BlockSpec((1, rows), lambda i: (0, i))],
        out_shape=[jax.ShapeDtypeStruct(shape, BF16) for shape in shapes] + [jax.ShapeDtypeStruct((1, anchors), F32)],
        scratch_shapes=[
            pltpu.VMEM((zones // 2, edges, 2 * lanes), F32),
            pltpu.VMEM((edges, lanes), F32),
        ]
        + [pltpu.VMEM((rows * pitch, lanes), F32)] * (zones // group),
        compiler_params=pltpu.CompilerParams(vmem_limit_bytes=48 * 1024 * 1024),
        cost_estimate=pl.CostEstimate(
            flops=2 * anchors * edges * zones * lanes, bytes_accessed=2 * anchors * zones * lanes, transcendentals=0
        ),
    )(edges_t, edge_weight[None, :], *([cells] * plan.streams))


def add_rows(ref, spots):
    total = ref[spots[0]].astype(F32)
    for spot in spots[1:]:
        total = total + ref[spot].astype(F32)
    return total


def fold_first_kernel(plan, parts_ref, out_ref):
    for line in range(plan.line):
        for quarter in range(4):
            out_ref[line, quarter] = add_rows(parts_ref, [(quarter, line), (4 + quarter, line)]).astype(BF16)


def fold_second_kernel(plan, parts_ref, out_ref):
    for square in range(8):
        for rest in range(plan.rest):
            spots = [(line, square) for line in range(rest, plan.line, plan.rest)]
            total = add_rows(parts_ref, spots)
            half = HEAD // 2
            high, low = halves_of(total[0:half] * COUNT_BASE + total[half:HEAD])
            out_ref[square, rest, 0:HEAD, :] = head_rows(high, low)
            out_ref[square, rest, HEAD:, :] = total[HEAD:].astype(BF16)


def fold(kernel, plan, parts, shape):
    whole = pl.BlockSpec(memory_space=pltpu.VMEM)
    return pl.pallas_call(
        functools.partial(kernel, plan),
        in_specs=[whole],
        out_specs=whole,
        out_shape=jax.ShapeDtypeStruct(shape, BF16),
        compiler_params=pltpu.CompilerParams(vmem_limit_bytes=16 * 1024 * 1024),
        cost_estimate=pl.CostEstimate(flops=parts.size, bytes_accessed=parts.size * 4, transcendentals=0),
    )(parts)


def org_sums(first, second, plan):
    lanes = first.shape[-1]
    first = lax.all_to_all(first, SQUARE, split_axis=0, concat_axis=0, tiled=True)
    second = lax.all_to_all(second, LINE, split_axis=0, concat_axis=0, tiled=True)
    second = fold(fold_second_kernel, plan, second, (8, plan.rest, plan.second_rows, lanes))
    first = fold(fold_first_kernel, plan, first, (plan.line, 4, plan.first_rows, lanes))
    second = lax.all_to_all(second, SQUARE, split_axis=0, concat_axis=0, tiled=True)
    first = lax.all_to_all(first, LINE, split_axis=0, concat_axis=0, tiled=True)
    return first, second


def table_kernel(plan, first_ref, second_ref, weight_ref, mixing_ref, matrix_ref, keep_ref, give_ref, mixed_ref):
    own = plan.own
    lanes = first_ref.shape[-1]
    head_lines = [second_ref[mid * 4, 0, 0:HEAD, :].astype(F32) for mid in range(2)]
    head = head_lines[0] + head_lines[1]
    half = HEAD // 2
    counts = head[0:half] * COUNT_BASE + head[half:HEAD]
    scale = weight_ref[...] / counts[0:own]
    rows = plan.first_rows + plan.second_rows - HEAD
    zones = rows // own
    n_dst = 4 * plan.rest
    for k in range(n_dst):
        rest, quarter = k // 4, k % 4
        first = add_rows(first_ref, [(line, quarter) for line in range(rest, plan.line, plan.rest)])
        second = add_rows(second_ref, [(quarter, rest), (4 + quarter, rest)])[HEAD:]
        start = k * rows
        for total in (first, second):
            size = total.shape[0]
            totals = (total * jnp.concatenate([scale] * (size // own), axis=0)).astype(BF16)
            mixed = jnp.dot(totals, mixing_ref[...], preferred_element_type=F32)
            mixed_ref[start : start + size, :] = mixed
            start += size
    whole = n_dst * zones
    for e in range(own):
        mixed = mixed_ref[pl.ds(e, whole, stride=own), :] if own > 1 else mixed_ref[...]
        high = mixed.astype(BF16)
        low = (mixed - high.astype(F32)).astype(BF16)
        both = jnp.dot(matrix_ref[...], jnp.concatenate([high, low], axis=1), preferred_element_type=F32)
        result = (both[:, 0:lanes] + both[:, lanes : 2 * lanes]).astype(BF16)
        keep_ref[e] = result[0 : whole // 2]
        give_ref[e] = result[whole // 2 :]


def table_rows(first, second, weight_rows, mixing, matrix, plan):
    zones = matrix.shape[0]
    lanes = first.shape[-1]
    whole = pl.BlockSpec(memory_space=pltpu.VMEM)
    half = jax.ShapeDtypeStruct((plan.own, zones // 2, lanes), BF16)
    return pl.pallas_call(
        functools.partial(table_kernel, plan),
        in_specs=[whole] * 5,
        out_specs=[whole] * 2,
        out_shape=[half, half],
        scratch_shapes=[pltpu.VMEM((zones * plan.own, lanes), F32)],
        compiler_params=pltpu.CompilerParams(vmem_limit_bytes=32 * 1024 * 1024),
        cost_estimate=pl.CostEstimate(
            flops=8 * plan.own * zones * lanes * lanes, bytes_accessed=first.size * 4, transcendentals=0
        ),
    )(first, second, weight_rows, mixing, matrix)


def spread_kernel(n_long, n_short, half_ref, long_at_ref, short_at_ref, root_ref, bias_ref, *refs):
    longs = refs[:n_long]
    shorts = refs[n_long : n_long + n_short]
    out_ref, long_ref, short_ref, ring_ref, sems, ring_sems = refs[-6:]
    slots, rows, zones, lanes = ring_ref.shape
    steps = out_ref.shape[0] // rows
    half = half_ref[0]

    copies = []
    for table, sources in ((long_ref, longs), (short_ref, shorts)):
        size = sources[0].shape[0]
        for i, source in enumerate(sources):
            copies.append(pltpu.make_async_copy(source, table.at[pl.ds(i * size, size)], sems.at[len(copies)]))
    for copy in copies:
        copy.start()
    for copy in copies:
        copy.wait()

    bias = bias_ref[...]
    count = long_at_ref.shape[0]
    tile = 16
    batch = 4
    tiles = zones // tile

    def leaving(step, slot):
        place = out_ref.at[pl.ds(step * rows, rows), pl.ds(pl.multiple_of(half * zones, zones), zones), :]
        return pltpu.make_async_copy(ring_ref.at[slot], place, ring_sems.at[slot])

    def one_step(step, carry):
        slot = lax.rem(step, slots)

        @pl.when(step >= slots)
        def _():
            leaving(step - slots, slot).wait()

        def several(group, inner):
            values = []
            for i in range(batch):
                at = step * rows + group * batch + i
                scale = root_ref[0, at]
                for table, places in ((long_ref, long_at_ref), (short_ref, short_at_ref)):
                    spots = [places[j, at] for j in range(count)]
                    for first in range(0, table.shape[1], tile):
                        pieces = [table[spot, first : first + tile, :] for spot in spots]
                        pieces = [(a + b).astype(F32) for a, b in zip(pieces[0::2], pieces[1::2])]
                        total = sum(pieces[1:], pieces[0])
                        values.append(jnp.maximum((total * scale + bias).astype(BF16), BF16(0.0)))
            for n, value in enumerate(values):
                start = n % tiles * tile
                ring_ref[slot, group * batch + n // tiles, start : start + tile, :] = value
            return inner

        lax.fori_loop(0, rows // batch, several, 0)
        leaving(step, slot).start()
        return carry

    lax.fori_loop(0, steps, one_step, 0)
    for step in range(steps - slots, steps):
        leaving(step, step % slots).wait()


def spread(half, long_at, short_at, root, bias, longs, shorts, before=None):
    anchors = long_at.shape[1]
    lanes = bias.shape[1]
    zones = longs[0].shape[1] + shorts[0].shape[1]
    rows = min(16, anchors // 8)
    slots = min(8, anchors // rows)
    smem = pl.BlockSpec(memory_space=pltpu.SMEM)
    anywhere = pl.BlockSpec(memory_space=pltpu.HBM)
    tables = [pltpu.VMEM((len(pieces) * pieces[0].shape[0],) + pieces[0].shape[1:], BF16) for pieces in (longs, shorts)]
    operands = [half, long_at, short_at, root, bias] + longs + shorts
    specs = [smem, smem, smem, smem, pl.BlockSpec(memory_space=pltpu.VMEM)] + [anywhere] * len(longs + shorts)
    aliases = {}
    if before is not None:
        aliases = {len(operands): 0}
        operands.append(before)
        specs.append(anywhere)
    return pl.pallas_call(
        functools.partial(spread_kernel, len(longs), len(shorts)),
        in_specs=specs,
        out_specs=anywhere,
        out_shape=jax.ShapeDtypeStruct((anchors, 2 * zones, lanes), BF16),
        scratch_shapes=tables
        + [
            pltpu.VMEM((slots, rows, zones, lanes), BF16),
            pltpu.SemaphoreType.DMA((len(longs) + len(shorts),)),
            pltpu.SemaphoreType.DMA((slots,)),
        ],
        input_output_aliases=aliases,
        compiler_params=pltpu.CompilerParams(vmem_limit_bytes=24 * 1024 * 1024),
        cost_estimate=pl.CostEstimate(
            flops=4096 * anchors * zones * lanes, bytes_accessed=4 * anchors * zones * lanes, transcendentals=0
        ),
    )(*operands)


LINE = ("slow", "rest")
SQUARE = ("mid", "near", "core")


def shifted(x, amount):
    size = lax.axis_size(LINE)
    return lax.ppermute(x, LINE, [(i, (i + amount) % size) for i in range(size)])


def crossed(x, turn):
    pairs = []
    for device in range(8):
        core = device % 2
        pairs.append((device, device ^ (2 if core == turn else 4)))
    return lax.ppermute(x, SQUARE, pairs)


def swapped(x):
    return lax.ppermute(x, "core", [(0, 1), (1, 0)])


def gather_table(keep, give):
    size = lax.axis_size(LINE)
    block = jnp.concatenate([keep, swapped(give)], axis=0)
    split = block.shape[1] * 3 // 4
    long, short = block[:, :split], block[:, split:]
    line = [long] + [shifted(long, k) for k in range(1, size - 1)]
    short = jnp.concatenate([short, crossed(short, 0)], axis=0)
    short, long = lax.optimization_barrier((short, long))
    line.append(shifted(long, size - 1))
    short = jnp.concatenate([short, crossed(short, 1)], axis=0)
    long = jnp.concatenate(line, axis=0)
    short, long = lax.optimization_barrier((short, long))
    first = crossed(long, 0)
    second = crossed(long, 1)
    shorts = [short] + [shifted(short, k) for k in range(1, size)]
    first, *shorts[1:-1] = lax.optimization_barrier((first, *shorts[1:-1]))
    both = crossed(first, 1)
    return [long, first, second, both], shorts


def places_of(ids, core, own):
    rest, size = lax.axis_size("rest"), lax.axis_size(LINE)
    owner = ids // own
    slot = jnp.where(owner % 2 == core, 0, own) + ids % own
    near = jnp.bitwise_xor(owner // 2 % 2, lax.axis_index("near"))
    mid = jnp.bitwise_xor(owner // (4 * rest) % 2, lax.axis_index("mid"))
    line = owner // (8 * rest) * rest + owner // 4 % rest
    line = lax.rem(lax.axis_index(LINE) - line + size, size)
    square = jnp.where(core == 0, 2 * mid + near, 2 * near + mid)
    return (square * size + line) * (2 * own) + slot, (line * 4 + square) * (2 * own) + slot


def shards(od_cells, anchor_edges, edge_weight, mixing, dst_edges, dst_weight, out_bias):
    n_org = lax.axis_size("slow") * lax.axis_size("mid")
    n_dst = lax.axis_size("rest") * lax.axis_size("near") * lax.axis_size("core")
    own = edge_weight.shape[0] // (n_org * n_dst)
    everyone = ("slow", "mid", "rest", "near", "core")
    core = lax.axis_index("core")
    edges_t = anchor_edges.T
    plan = Plan(od_cells.shape[1], own, lax.axis_size("rest"), lax.axis_size(LINE), od_cells.shape[0])
    first, second, roots = partial_sums(od_cells, edges_t, edge_weight, plan)
    first, second = org_sums(first, second, plan)
    own_weight = lax.dynamic_slice_in_dim(edge_weight, lax.axis_index(everyone) * own, own, 0)
    weight_rows = jnp.broadcast_to(own_weight[:, None], (own, mixing.shape[0]))
    matrix = dest_operator(dst_edges, dst_weight)
    half = matrix.shape[0] // 2
    matrix = jnp.where(core == 0, matrix, jnp.concatenate([matrix[half:], matrix[:half]], axis=0))
    keep, give = table_rows(first, second, weight_rows, mixing, matrix, plan)
    longs, shorts = gather_table(keep, give)
    rows = anchor_edges.shape[0] // n_dst
    start = lax.axis_index(("rest", "near", "core")) * rows
    ids = lax.dynamic_slice_in_dim(edges_t, start, rows, 1)
    own_root = lax.dynamic_slice_in_dim(roots, start, rows, 1)
    bias = out_bias[None, :]
    other = 1 - core
    result = spread(core[None], *places_of(ids, core, own), own_root, bias, longs, shorts)
    longs, shorts = [swapped(x) for x in longs], [swapped(x) for x in shorts]
    return spread(other[None], *places_of(ids, other, own), own_root, bias, longs, shorts, result)


def solution(mesh):
    n_org, n_dst = mesh.devices.shape
    fine = Mesh(mesh.devices.reshape(n_org // 2, 2, n_dst // 4, 2, 2), ("slow", "mid", "rest", "near", "core"))
    org, dst = ("slow", "mid"), ("rest", "near", "core")
    in_specs = (P(org, dst, None), P(org, None), P(), P(), P(), P(), P())
    out_specs = P(org + dst, None, None)
    return jax.shard_map(shards, mesh=fine, in_specs=in_specs, out_specs=out_specs, check_vma=False)
```

time: 163 us -> 180 us (1.10)
  blocking collectives: 0 us -> 24.7 us
  waiting for transfers between devices: 85.4 us -> 68.5 us
  starting transfers between devices: 28.8 us -> 39.3 us
    all_to_all x0 -> x1, blocking collectives: none -> 24.7 us  [org_sums(): lax.all_to_all(second, LINE, split_axis=0, concat_axis=0, tiled=True)]
    all_to_all x1 -> x3, waiting for transfers between devices: 47.6 us -> 29.5 us  [the longest x1 13.7 us: org_sums(): lax.all_to_all(first, SQUARE, split_axis=0, concat_axis=0, tiled=True)]
    all_to_all x1 -> x3, starting transfers between devices: 6.33 us -> 18.1 us  [the longest x1 7.07 us: org_sums(): lax.all_to_all(second, SQUARE, split_axis=0, concat_axis=0, tiled=True)]
    ppermute x9, starting transfers between devices: 12.9 us -> 7.71 us  [swapped(): return lax.ppermute(x, 'core', [(0, 1), (1, 0)])]
    pallas_call x2, Pallas kernels: 27.1 us -> 23.6 us  [spread(): pl.pallas_call(functools.partial(spread_kernel, len(longs), len(shorts)),...]
    pallas_call x2 -> x4, Pallas kernels: 15.4 us -> 18.3 us  [the longest x1 15.9 us: partial_sums(): pl.pallas_call(functools.partial(gather_kernel, plan.own, group, pitch, p...]
    ppermute x6, starting transfers between devices: 6.63 us -> 8.68 us  [shifted(): lax.ppermute(x, LINE, [(i, (i + amount) % size) for i in range(size)])]
    ppermute x5, starting transfers between devices: 2.95 us -> 4.83 us  [crossed(): return lax.ppermute(x, SQUARE, pairs)]
  transfers between devices with their start and end apart: 21 -> 23, of which waited for: 10 -> 12; matrix products, arithmetic and copies ran while one was open for 1% -> 0% of each run, Pallas kernels for 9% -> 8%
where the time goes in v6:
time: 180 us; the launch traced here: 177 us
  waiting for transfers between devices  68.5 us (38%)
  Pallas kernels  41.9 us (23%)
  starting transfers between devices  39.3 us (22%)
  blocking collectives  24.7 us (14%)
    ppermute x6, waiting for transfers between devices, shifted(): lax.ppermute(x, LINE, [(i, (i + amount) % size) for i in range(size)])  34.8 us
    all_to_all x1, blocking collectives, org_sums(): lax.all_to_all(second, LINE, split_axis=0, concat_axis=0, tiled=True)  24.7 us
    pallas_call x2, Pallas kernels, spread(): pl.pallas_call(functools.partial(spread_kernel, len(longs), len(shorts)),...  23.6 us
    pallas_call x1, Pallas kernels, partial_sums(): pl.pallas_call(functools.partial(gather_kernel, plan.own, group, pitch, p...  15.9 us
    all_to_all x1, waiting for transfers between devices, org_sums(): lax.all_to_all(first, SQUARE, split_axis=0, concat_axis=0, tiled=True)  13.7 us
    all_to_all x1, waiting for transfers between devices, org_sums(): first = lax.all_to_all(first, LINE, split_axis=0, concat_axis=0, tiled=True)  12.5 us
    ppermute x6, starting transfers between devices, shifted(): lax.ppermute(x, LINE, [(i, (i + amount) % size) for i in range(size)])  8.68 us
    ppermute x9, starting transfers between devices, swapped(): return lax.ppermute(x, 'core', [(0, 1), (1, 0)])  7.71 us
  transfers between devices with their start and end apart: 23, of which 12 were waited for; matrix products, arithmetic and copies ran while one was open for 0% of the time, Pallas kernels for 8%

profile of v6, /device:TPU:13, one launch (start us, length us, event | category | flops | bytes accessed | tf_op | source)
XLA Modules:
  0.0 177.2 jit_solution(16674327008851720542)
XLA Ops:
  0.0 0.8 copy-done
  0.8 0.7 copy-done.3
  1.5 15.9 %shard_map.73 = (bf16[8,4,160,128]{3,2,1,0:T(8,128)(2,1)}, bf16[4,8,112,128]{3,2,1,0:T(8,128)(2,1)S(1)}, f32[1,2048]{1,0:T(1,128)S(1)}) custom-call(s32[4,2048]{1,0:T(4,128)S(1)} %bitcast.31, f32[1,256]{1,0:T(1,128)S(1)} %bitcast.32, bf16[2048,32,128]{2,1,0:T(8,128)(2,1)} %refs_3_.1, bf16[2048,32,128]{2,1,0:T(8,128)(2,1)} %refs_3_.1, ...), custom_call_target="tpu_custom_call" | custom-call | flops 4294967296 | bytes 16777216 | tf_op jit(solution)/shard_map/pallas_call | solution.py:149
  17.4 24.7 %all_to_all.20.parts_ref = bf16[4,8,112,128]{3,2,1,0:T(8,128)(2,1)S(1)} all-to-all(bf16[4,8,112,128]{3,2,1,0:T(8,128)(2,1)S(1)} %get-tuple-element.19), channel_id=1, replica_groups=mesh['slow'=4,'mid'=2,'rest'=1,'near'=2,'core'=2] {'slow','rest'}, dimensions={0} | all-to-all | bytes 1835008 | tf_op jit(solution)/shard_map/all_to_all | solution.py:211
  42.1 6.0 %all-to-all-start = ((bf16[8,4,160,128]{3,2,1,0:T(8,128)(2,1)}), bf16[8,4,160,128]{3,2,1,0:T(8,128)(2,1)S(1)}, u32[]{:S(2)}, u32[]{:S(2)}) async-start(bf16[8,4,160,128]{3,2,1,0:T(8,128)(2,1)} %get-tuple-element.18), calls=%async_computation | async-start | bytes 2621440 | tf_op jit(solution)/shard_map/all_to_all | solution.py:210
  48.2 0.8 shard_map.75
  49.0 13.7 %all-to-all-done.parts_ref = bf16[8,4,160,128]{3,2,1,0:T(8,128)(2,1)S(1)} async-done(((bf16[8,4,160,128]{3,2,1,0:T(8,128)(2,1)}), bf16[8,4,160,128]{3,2,1,0:T(8,128)(2,1)S(1)}, u32[]{:S(2)}, u32[]{:S(2)}) %all-to-all-start) | async-done | bytes 1310752 | tf_op jit(solution)/shard_map/all_to_all | solution.py:210
  62.6 7.1 %all-to-all-start.3 = ((bf16[8,1,112,128]{3,2,1,0:T(8,128)(2,1)}), bf16[8,1,112,128]{3,2,1,0:T(8,128)(2,1)S(1)}, u32[]{:S(2)}, u32[]{:S(2)}) async-start(bf16[8,1,112,128]{3,2,1,0:T(8,128)(2,1)} %shard_map.75), calls=%async_computation.3 | async-start | bytes 458752 | tf_op jit(solution)/shard_map/all_to_all | solution.py:214
  69.7 1.0 shard_map.74
  70.7 3.3 %all-to-all-done.3.second_ref = bf16[8,1,112,128]{3,2,1,0:T(8,128)(2,1)S(1)} async-done(((bf16[8,1,112,128]{3,2,1,0:T(8,128)(2,1)}), bf16[8,1,112,128]{3,2,1,0:T(8,128)(2,1)S(1)}, u32[]{:S(2)}, u32[]{:S(2)}) %all-to-all-start.3) | async-done | bytes 229408 | tf_op jit(solution)/shard_map/all_to_all | solution.py:214
  74.0 5.0 %all-to-all-start.1 = ((bf16[4,4,160,128]{3,2,1,0:T(8,128)(2,1)}), bf16[4,4,160,128]{3,2,1,0:T(8,128)(2,1)S(1)}, u32[]{:S(2)}, u32[]{:S(2)}) async-start(bf16[4,4,160,128]{3,2,1,0:T(8,128)(2,1)} %shard_map.74), calls=%async_computation.1 | async-start | bytes 1310720 | tf_op jit(solution)/shard_map/all_to_all | solution.py:215
  79.0 0.1 dynamic_slice.11
  79.1 0.1 convert_reduce_fusion
  79.2 0.1 multiply_reduce_fusion
  79.4 0.3 convolution_convert_fusion
  79.7 12.5 %all-to-all-done.1.first_ref = bf16[4,4,160,128]{3,2,1,0:T(8,128)(2,1)S(1)} async-done(((bf16[4,4,160,128]{3,2,1,0:T(8,128)(2,1)}), bf16[4,4,160,128]{3,2,1,0:T(8,128)(2,1)S(1)}, u32[]{:S(2)}, u32[]{:S(2)}) %all-to-all-start.1) | async-done | bytes 655392 | tf_op jit(solution)/shard_map/all_to_all | solution.py:215
  92.3 0.6 shard_map.76
  92.8 2.1 %collective-permute-start = (bf16[8,64,128]{2,1,0:T(8,128)(2,1)S(1)}, bf16[8,64,128]{2,1,0:T(8,128)(2,1)S(1)}, u32[]{:S(2)}, u32[]{:S(2)}) collective-permute-start(bf16[8,64,128]{2,1,0:T(8,128)(2,1)S(1)} %get-tuple-element.21), channel_id=1, source_target_pairs={{0,1},{1,0},{2,3},{3,2},{4,5},{5,4},{6,7},{7,6},{8,9},{9,8},{10,11... | collective-permute-start | bytes 393224 | tf_op jit(solution)/shard_map/ppermute | solution.py:384
  95.0 1.0 collective-permute-done
  96.0 1.3 collective-permute-start.1
  97.3 1.9 %collective-permute-done.1 = bf16[16,16,128]{2,1,0:T(8,128)(2,1)S(1)} collective-permute-done((bf16[16,16,128]{2,1,0:T(8,128)(2,1)S(1)}, bf16[16,16,128]{2,1,0:T(8,128)(2,1)S(1)}, u32[]{:S(2)}, u32[]{:S(2)}) %collective-permute-start.1) | collective-permute-done | bytes 65568 | tf_op jit(solution)/shard_map/ppermute | solution.py:380
  99.2 0.7 collective-permute-start.2
  99.9 3.0 %collective-permute-start.4 = (bf16[16,48,128]{2,1,0:T(8,128)(2,1)S(1)}, bf16[16,48,128]{2,1,0:T(8,128)(2,1)S(1)}, u32[]{:S(2)}, u32[]{:S(2)}) collective-permute-start(bf16[16,48,128]{2,1,0:T(8,128)(2,1)S(1)} %slice.19), channel_id=1, source_target_pairs={{0,16},{8,24},{16,0},{24,8},{1,17},{9,25},{17,1},{25,9},{2,18},{10... | collective-permute-start | bytes 589832 | tf_op jit(solution)/shard_map/ppermute | solution.py:372
  102.9 1.2 collective-permute-start.3
  104.1 0.3 collective-permute-start.5
  104.4 7.6 %collective-permute-done.4 = bf16[16,48,128]{2,1,0:T(8,128)(2,1)S(1)} collective-permute-done((bf16[16,48,128]{2,1,0:T(8,128)(2,1)S(1)}, bf16[16,48,128]{2,1,0:T(8,128)(2,1)S(1)}, u32[]{:S(2)}, u32[]{:S(2)}) %collective-permute-start.4) | collective-permute-done | bytes 196640 | tf_op jit(solution)/shard_map/ppermute | solution.py:372
  112.0 7.2 %collective-permute-done.3 = bf16[16,48,128]{2,1,0:T(8,128)(2,1)S(1)} collective-permute-done((bf16[16,48,128]{2,1,0:T(8,128)(2,1)S(1)}, bf16[16,48,128]{2,1,0:T(8,128)(2,1)S(1)}, u32[]{:S(2)}, u32[]{:S(2)}) %collective-permute-start.3) | collective-permute-done | bytes 196640 | tf_op jit(solution)/shard_map/ppermute | solution.py:372
  119.2 1.7 collective-permute-done.5
  120.9 0.1 pad_maximum_fusion.refs_0_
  121.0 1.5 collective-permute-start.7
  122.5 1.2 collective-permute-start.8
  123.7 0.7 collective-permute-start.11
  124.3 1.3 collective-permute-start.6
  125.7 8.3 %collective-permute-done.9.refs_6_ = bf16[64,16,128]{2,1,0:T(8,128)(2,1)S(1)} collective-permute-done((bf16[64,16,128]{2,1,0:T(8,128)(2,1)S(1)}, bf16[64,16,128]{2,1,0:T(8,128)(2,1)S(1)}, u32[]{:S(2)}, u32[]{:S(2)}) %collective-permute-start.9) | collective-permute-done | bytes 262176 | tf_op jit(solution)/shard_map/ppermute | solution.py:372
  133.9 5.6 %collective-permute-done.8.refs_5_ = bf16[64,16,128]{2,1,0:T(8,128)(2,1)S(1)} collective-permute-done((bf16[64,16,128]{2,1,0:T(8,128)(2,1)S(1)}, bf16[64,16,128]{2,1,0:T(8,128)(2,1)S(1)}, u32[]{:S(2)}, u32[]{:S(2)}) %collective-permute-start.8) | collective-permute-done | bytes 262176 | tf_op jit(solution)/shard_map/ppermute | solution.py:372
  139.6 0.7 collective-permute-start.13
  140.3 3.0 %collective-permute-start.18 = (bf16[64,16,128]{2,1,0:T(8,128)(2,1)S(1)}, bf16[64,16,128]{2,1,0:T(8,128)(2,1)}, u32[]{:S(2)}, u32[]{:S(2)}) collective-permute-start(bf16[64,16,128]{2,1,0:T(8,128)(2,1)S(1)} %pad_maximum_fusion.1.refs_4_), channel_id=1, source_target_pairs={{0,24},{8,0},{16,8},{24,16},{1,25},{9,1},{17,9},{25,17},{2,26},{10... | collective-permute-start | bytes 786440 | tf_op jit(solution)/shard_map/ppermute | solution.py:372
  143.4 0.8 collective-permute-start.15
  144.2 4.4 %collective-permute-done.18.refs_7_ = bf16[64,16,128]{2,1,0:T(8,128)(2,1)} collective-permute-done((bf16[64,16,128]{2,1,0:T(8,128)(2,1)S(1)}, bf16[64,16,128]{2,1,0:T(8,128)(2,1)}, u32[]{:S(2)}, u32[]{:S(2)}) %collective-permute-start.18) | collective-permute-done | bytes 262176 | tf_op jit(solution)/shard_map/ppermute | solution.py:372
  148.5 1.4 collective-permute-start.19
  150.0 0.1 collective-permute-start.10
  150.1 1.4 collective-permute-done.19.refs_7_
  151.4 0.4 collective-permute-start.16
  151.8 0.1 collective-permute-start.17
  151.9 0.4 collective-permute-start.12
  152.3 1.1 collective-permute-start.14
  153.5 12.0 %shard_map.77.refs_8_ = bf16[512,128,128]{2,1,0:T(8,128)(2,1)} custom-call(s32[1]{0:T(128)} %bitcast.5.half_ref, s32[4,512]{1,0:T(4,128)S(1)} %get-tuple-element.37.long_at_ref, s32[4,512]{1,0:T(4,128)S(1)} %get-tuple-element.31.short_at_ref, f32[1,512]{1,0:T(1,128)S(1)} %constant_dynamic-slice_fusion.root_ref, f32[1,128]{1,0:T(1,128)S(1)} %bitcast.33, ...), custom_call_target="tpu_custom_call" | custom-call | flops 17179869184 | bytes 16777216 | tf_op jit(solution)/shard_map/pallas_call | solution.py:347
  165.5 11.7 %shard_map.78 = bf16[512,128,128]{2,1,0:T(8,128)(2,1)} custom-call(s32[1]{0:T(128)} %bitcast.half_ref, s32[4,512]{1,0:T(4,128)S(1)} %get-tuple-element.39.long_at_ref, s32[4,512]{1,0:T(4,128)S(1)} %get-tuple-element.38.short_at_ref, f32[1,512]{1,0:T(1,128)S(1)} %constant_dynamic-slice_fusion.root_ref, ...), custom_call_target="tpu_custom_call", output_to_operand_aliasing={{}: (13, {})} | custom-call | flops 17179869184 | bytes 16777216 | tf_op jit(solution)/shard_map/pallas_call | solution.py:347
  (41 shorter events, 0.4 us)
Async XLA Ops:
  0.0 0.8 copy-start
  0.8 0.7 copy-start.3
  1.4 77.6 %copy-start.4 = (f32[256]{0:T(256)S(1)}, f32[256]{0:T(256)}, u32[]{:S(2)}) copy-start(f32[256]{0:T(256)} %param.9) | copy-start | bytes 3076
  1.4 77.6 %copy-start.6 = (s32[128,3]{0,1:T(4,128)S(1)}, s32[128,3]{0,1:T(4,128)}, u32[]{:S(2)}) copy-start(s32[128,3]{0,1:T(4,128)} %param.11) | copy-start | bytes 4612
  1.4 77.8 %copy-start.7 = (f32[128]{0:T(128)S(1)}, f32[128]{0:T(128)}, u32[]{:S(2)}) copy-start(f32[128]{0:T(128)} %param.12) | copy-start | bytes 1540
  1.4 90.8 %copy-start.2 = (bf16[128,128]{1,0:T(8,128)(2,1)S(1)}, bf16[128,128]{1,0:T(8,128)(2,1)}, u32[]{:S(2)}) copy-start(bf16[128,128]{1,0:T(8,128)(2,1)} %mixing_ref.1) | copy-start | bytes 98308
  1.4 141.8 %copy-start.1 = (s32[2048,4]{0,1:T(4,128)S(1)}, s32[2048,4]{0,1:T(4,128)}, u32[]{:S(2)}) copy-start(s32[2048,4]{0,1:T(4,128)} %param.8) | copy-start | bytes 98308
  1.5 152.0 %copy-start.5 = (f32[128]{0:T(128)S(1)}, f32[128]{0:T(128)}, u32[]{:S(2)}) copy-start(f32[128]{0:T(128)} %param.13) | copy-start | bytes 1540
  42.1 20.5 %all-to-all-start = ((bf16[8,4,160,128]{3,2,1,0:T(8,128)(2,1)}), bf16[8,4,160,128]{3,2,1,0:T(8,128)(2,1)S(1)}, u32[]{:S(2)}, u32[]{:S(2)}) async-start(bf16[8,4,160,128]{3,2,1,0:T(8,128)(2,1)} %get-tuple-element.18), calls=%async_computation | async-start | bytes 2621440 | tf_op jit(solution)/shard_map/all_to_all | solution.py:210
  62.6 11.4 %all-to-all-start.3 = ((bf16[8,1,112,128]{3,2,1,0:T(8,128)(2,1)}), bf16[8,1,112,128]{3,2,1,0:T(8,128)(2,1)S(1)}, u32[]{:S(2)}, u32[]{:S(2)}) async-start(bf16[8,1,112,128]{3,2,1,0:T(8,128)(2,1)} %shard_map.75), calls=%async_computation.3 | async-start | bytes 458752 | tf_op jit(solution)/shard_map/all_to_all | solution.py:214
  74.0 18.2 %all-to-all-start.1 = ((bf16[4,4,160,128]{3,2,1,0:T(8,128)(2,1)}), bf16[4,4,160,128]{3,2,1,0:T(8,128)(2,1)S(1)}, u32[]{:S(2)}, u32[]{:S(2)}) async-start(bf16[4,4,160,128]{3,2,1,0:T(8,128)(2,1)} %shard_map.74), calls=%async_computation.1 | async-start | bytes 1310720 | tf_op jit(solution)/shard_map/all_to_all | solution.py:215
  92.8 3.1 %collective-permute-start = (bf16[8,64,128]{2,1,0:T(8,128)(2,1)S(1)}, bf16[8,64,128]{2,1,0:T(8,128)(2,1)S(1)}, u32[]{:S(2)}, u32[]{:S(2)}) collective-permute-start(bf16[8,64,128]{2,1,0:T(8,128)(2,1)S(1)} %get-tuple-element.21), channel_id=1, source_target_pairs={{0,1},{1,0},{2,3},{3,2},{4,5},{5,4},{6,7},{7,6},{8,9},{9,8},{10,11... | collective-permute-start | bytes 393224 | tf_op jit(solution)/shard_map/ppermute | solution.py:384
  96.0 3.2 %collective-permute-start.1 = (bf16[16,16,128]{2,1,0:T(8,128)(2,1)S(1)}, bf16[16,16,128]{2,1,0:T(8,128)(2,1)S(1)}, u32[]{:S(2)}, u32[]{:S(2)}) collective-permute-start(bf16[16,16,128]{2,1,0:T(8,128)(2,1)S(1)} %slice.18), channel_id=1, source_target_pairs={{0,2},{1,5},{2,0},{3,7},{4,6},{5,1},{6,4},{7,3},{8,10},{9,13},{10,... | collective-permute-start | bytes 196616 | tf_op jit(solution)/shard_map/ppermute | solution.py:380
  99.2 5.2 %collective-permute-start.2 = (bf16[32,16,128]{2,1,0:T(8,128)(2,1)S(1)}, bf16[32,16,128]{2,1,0:T(8,128)(2,1)S(1)}, u32[]{:S(2)}, u32[]{:S(2)}) collective-permute-start(bf16[32,16,128]{2,1,0:T(8,128)(2,1)S(1)} %pad_maximum_fusion.2), channel_id=1, source_target_pairs={{0,4},{1,3},{2,6},{3,1},{4,0},{5,7},{6,2},{7,5},{8,12},{9,11},{10,... | collective-permute-start | bytes 393224 | tf_op jit(solution)/shard_map/ppermute | solution.py:380
  99.9 12.1 %collective-permute-start.4 = (bf16[16,48,128]{2,1,0:T(8,128)(2,1)S(1)}, bf16[16,48,128]{2,1,0:T(8,128)(2,1)S(1)}, u32[]{:S(2)}, u32[]{:S(2)}) collective-permute-start(bf16[16,48,128]{2,1,0:T(8,128)(2,1)S(1)} %slice.19), channel_id=1, source_target_pairs={{0,16},{8,24},{16,0},{24,8},{1,17},{9,25},{17,1},{25,9},{2,18},{10... | collective-permute-start | bytes 589832 | tf_op jit(solution)/shard_map/ppermute | solution.py:372
  102.9 16.3 %collective-permute-start.3 = (bf16[16,48,128]{2,1,0:T(8,128)(2,1)S(1)}, bf16[16,48,128]{2,1,0:T(8,128)(2,1)S(1)}, u32[]{:S(2)}, u32[]{:S(2)}) collective-permute-start(bf16[16,48,128]{2,1,0:T(8,128)(2,1)S(1)} %slice.19), channel_id=1, source_target_pairs={{0,8},{8,16},{16,24},{24,0},{1,9},{9,17},{17,25},{25,1},{2,10},{10... | collective-permute-start | bytes 589832 | tf_op jit(solution)/shard_map/ppermute | solution.py:372
  104.1 16.8 %collective-permute-start.5 = (bf16[16,48,128]{2,1,0:T(8,128)(2,1)S(1)}, bf16[16,48,128]{2,1,0:T(8,128)(2,1)S(1)}, u32[]{:S(2)}, u32[]{:S(2)}) collective-permute-start(bf16[16,48,128]{2,1,0:T(8,128)(2,1)S(1)} %slice.19), channel_id=1, source_target_pairs={{0,24},{8,0},{16,8},{24,16},{1,25},{9,1},{17,9},{25,17},{2,26},{10... | collective-permute-start | bytes 589832 | tf_op jit(solution)/shard_map/ppermute | solution.py:372
  121.0 18.6 %collective-permute-start.7 = (bf16[64,48,128]{2,1,0:T(8,128)(2,1)S(1)}, bf16[64,48,128]{2,1,0:T(8,128)(2,1)S(1)}, u32[]{:S(2)}, u32[]{:S(2)}) collective-permute-start(bf16[64,48,128]{2,1,0:T(8,128)(2,1)S(1)} %pad_maximum_fusion.refs_0_), channel_id=1, source_target_pairs={{0,2},{1,5},{2,0},{3,7},{4,6},{5,1},{6,4},{7,3},{8,10},{9,13},{10,... | collective-permute-start | bytes 2359304 | tf_op jit(solution)/shard_map/ppermute | solution.py:380
  122.5 11.5 %collective-permute-start.9 = (bf16[64,16,128]{2,1,0:T(8,128)(2,1)S(1)}, bf16[64,16,128]{2,1,0:T(8,128)(2,1)S(1)}, u32[]{:S(2)}, u32[]{:S(2)}) collective-permute-start(bf16[64,16,128]{2,1,0:T(8,128)(2,1)S(1)} %pad_maximum_fusion.1.refs_4_), channel_id=1, source_target_pairs={{0,16},{8,24},{16,0},{24,8},{1,17},{9,25},{17,1},{25,9},{2,18},{10... | collective-permute-start | bytes 786440 | tf_op jit(solution)/shard_map/ppermute | solution.py:372
  122.5 17.1 %collective-permute-start.8 = (bf16[64,16,128]{2,1,0:T(8,128)(2,1)S(1)}, bf16[64,16,128]{2,1,0:T(8,128)(2,1)S(1)}, u32[]{:S(2)}, u32[]{:S(2)}) collective-permute-start(bf16[64,16,128]{2,1,0:T(8,128)(2,1)S(1)} %pad_maximum_fusion.1.refs_4_), channel_id=1, source_target_pairs={{0,8},{8,16},{16,24},{24,0},{1,9},{9,17},{17,25},{25,1},{2,10},{10... | collective-permute-start | bytes 786440 | tf_op jit(solution)/shard_map/ppermute | solution.py:372
  123.7 28.1 %collective-permute-start.11 = (bf16[64,48,128]{2,1,0:T(8,128)(2,1)S(1)}, bf16[64,48,128]{2,1,0:T(8,128)(2,1)}, u32[]{:S(2)}, u32[]{:S(2)}) collective-permute-start(bf16[64,48,128]{2,1,0:T(8,128)(2,1)S(1)} %pad_maximum_fusion.refs_0_), channel_id=1, source_target_pairs={{0,4},{1,3},{2,6},{3,1},{4,0},{5,7},{6,2},{7,5},{8,12},{9,11},{10,... | collective-permute-start | bytes 2359304 | tf_op jit(solution)/shard_map/ppermute | solution.py:380
  124.3 27.6 %collective-permute-start.6 = (bf16[64,48,128]{2,1,0:T(8,128)(2,1)S(1)}, bf16[64,48,128]{2,1,0:T(8,128)(2,1)S(1)}, u32[]{:S(2)}, u32[]{:S(2)}) collective-permute-start(bf16[64,48,128]{2,1,0:T(8,128)(2,1)S(1)} %pad_maximum_fusion.refs_0_), channel_id=1, source_target_pairs={{0,1},{1,0},{2,3},{3,2},{4,5},{5,4},{6,7},{7,6},{8,9},{9,8},{10,11... | collective-permute-start | bytes 2359304 | tf_op jit(solution)/shard_map/ppermute | solution.py:384
  139.6 12.8 %collective-permute-start.13 = (bf16[64,48,128]{2,1,0:T(8,128)(2,1)S(1)}, bf16[64,48,128]{2,1,0:T(8,128)(2,1)}, u32[]{:S(2)}, u32[]{:S(2)}) collective-permute-start(bf16[64,48,128]{2,1,0:T(8,128)(2,1)S(1)} %collective-permute-done.7.refs_1_), channel_id=1, source_target_pairs={{0,4},{1,3},{2,6},{3,1},{4,0},{5,7},{6,2},{7,5},{8,12},{9,11},{10,... | collective-permute-start | bytes 2359304 | tf_op jit(solution)/shard_map/ppermute | solution.py:380
  140.3 8.3 %collective-permute-start.18 = (bf16[64,16,128]{2,1,0:T(8,128)(2,1)S(1)}, bf16[64,16,128]{2,1,0:T(8,128)(2,1)}, u32[]{:S(2)}, u32[]{:S(2)}) collective-permute-start(bf16[64,16,128]{2,1,0:T(8,128)(2,1)S(1)} %pad_maximum_fusion.1.refs_4_), channel_id=1, source_target_pairs={{0,24},{8,0},{16,8},{24,16},{1,25},{9,1},{17,9},{25,17},{2,26},{10... | collective-permute-start | bytes 786440 | tf_op jit(solution)/shard_map/ppermute | solution.py:372
  143.4 6.6 %collective-permute-start.15 = (bf16[64,16,128]{2,1,0:T(8,128)(2,1)S(1)}, bf16[64,16,128]{2,1,0:T(8,128)(2,1)}, u32[]{:S(2)}, u32[]{:S(2)}) collective-permute-start(bf16[64,16,128]{2,1,0:T(8,128)(2,1)S(1)} %pad_maximum_fusion.1.refs_4_), channel_id=1, source_target_pairs={{0,1},{1,0},{2,3},{3,2},{4,5},{5,4},{6,7},{7,6},{8,9},{9,8},{10,11... | collective-permute-start | bytes 786440 | tf_op jit(solution)/shard_map/ppermute | solution.py:384
  148.5 2.9 %collective-permute-start.19 = (bf16[64,16,128]{2,1,0:T(8,128)(2,1)}, bf16[64,16,128]{2,1,0:T(8,128)(2,1)}, u32[]{:S(2)}, u32[]{:S(2)}) collective-permute-start(bf16[64,16,128]{2,1,0:T(8,128)(2,1)} %collective-permute-done.18.refs_7_), channel_id=1, source_target_pairs={{0,1},{1,0},{2,3},{3,2},{4,5},{5,4},{6,7},{7,6},{8,9},{9,8},{10,11... | collective-permute-start | bytes 786440 | tf_op jit(solution)/shard_map/ppermute | solution.py:384
  150.0 15.5 %collective-permute-start.10 = (bf16[64,48,128]{2,1,0:T(8,128)(2,1)S(1)}, bf16[64,48,128]{2,1,0:T(8,128)(2,1)S(1)}, u32[]{:S(2)}, u32[]{:S(2)}) collective-permute-start(bf16[64,48,128]{2,1,0:T(8,128)(2,1)S(1)} %collective-permute-done.7.refs_1_), channel_id=1, source_target_pairs={{0,1},{1,0},{2,3},{3,2},{4,5},{5,4},{6,7},{7,6},{8,9},{9,8},{10,11... | collective-permute-start | bytes 2359304 | tf_op jit(solution)/shard_map/ppermute | solution.py:384
  151.4 14.0 %collective-permute-start.16 = (bf16[64,16,128]{2,1,0:T(8,128)(2,1)S(1)}, bf16[64,16,128]{2,1,0:T(8,128)(2,1)S(1)}, u32[]{:S(2)}, u32[]{:S(2)}) collective-permute-start(bf16[64,16,128]{2,1,0:T(8,128)(2,1)S(1)} %collective-permute-done.8.refs_5_), channel_id=1, source_target_pairs={{0,1},{1,0},{2,3},{3,2},{4,5},{5,4},{6,7},{7,6},{8,9},{9,8},{10,11... | collective-permute-start | bytes 786440 | tf_op jit(solution)/shard_map/ppermute | solution.py:384
  151.8 13.6 %collective-permute-start.17 = (bf16[64,16,128]{2,1,0:T(8,128)(2,1)S(1)}, bf16[64,16,128]{2,1,0:T(8,128)(2,1)S(1)}, u32[]{:S(2)}, u32[]{:S(2)}) collective-permute-start(bf16[64,16,128]{2,1,0:T(8,128)(2,1)S(1)} %collective-permute-done.9.refs_6_), channel_id=1, source_target_pairs={{0,1},{1,0},{2,3},{3,2},{4,5},{5,4},{6,7},{7,6},{8,9},{9,8},{10,11... | collective-permute-start | bytes 786440 | tf_op jit(solution)/shard_map/ppermute | solution.py:384
  151.9 13.5 %collective-permute-start.12 = (bf16[64,48,128]{2,1,0:T(8,128)(2,1)}, bf16[64,48,128]{2,1,0:T(8,128)(2,1)S(1)}, u32[]{:S(2)}, u32[]{:S(2)}) collective-permute-start(bf16[64,48,128]{2,1,0:T(8,128)(2,1)} %collective-permute-done.11.refs_2_), channel_id=1, source_target_pairs={{0,1},{1,0},{2,3},{3,2},{4,5},{5,4},{6,7},{7,6},{8,9},{9,8},{10,11... | collective-permute-start | bytes 2359304 | tf_op jit(solution)/shard_map/ppermute | solution.py:384
  152.3 13.2 %collective-permute-start.14 = (bf16[64,48,128]{2,1,0:T(8,128)(2,1)}, bf16[64,48,128]{2,1,0:T(8,128)(2,1)S(1)}, u32[]{:S(2)}, u32[]{:S(2)}) collective-permute-start(bf16[64,48,128]{2,1,0:T(8,128)(2,1)} %collective-permute-done.13.refs_3_), channel_id=1, source_target_pairs={{0,1},{1,0},{2,3},{3,2},{4,5},{5,4},{6,7},{7,6},{8,9},{9,8},{10,11... | collective-permute-start | bytes 2359304 | tf_op jit(solution)/shard_map/ppermute | solution.py:384

commit v7 on v6

v7 whole, which is shorter than its diff:
```python
import functools

import jax
import jax.numpy as jnp
from jax import lax
from jax.experimental import pallas as pl
from jax.experimental.pallas import tpu as pltpu
from jax.sharding import Mesh, PartitionSpec as P

BF16 = jnp.bfloat16
F32 = jnp.float32
COUNT_BASE = 256.0
HEAD = 16


def corridor_table(edge_ids, edge_count):
    columns = jnp.arange(edge_count, dtype=jnp.int32)
    return jnp.sum((edge_ids[:, :, None] == columns[None, None, :]).astype(F32), axis=1)


def dest_operator(dst_edges, dst_weight):
    dst_member = corridor_table(dst_edges, dst_weight.shape[0])
    dst_degree = jnp.sum(dst_member * dst_weight[None, :], axis=1)
    edge_sizes = jnp.sum(dst_member, axis=0)
    left_factor = dst_member * lax.rsqrt(dst_degree)[:, None]
    right_factor = left_factor * (dst_weight / edge_sizes)[None, :]
    result = jnp.dot(right_factor, left_factor.T, precision=lax.Precision.HIGHEST)
    return result.astype(BF16)


class Plan:
    def __init__(self, zones, own, rest, line):
        self.own = own
        self.rest = rest
        self.line = line
        self.cut = zones * 5 // 8
        self.first_rows = self.cut * own
        self.second_rows = HEAD + (zones - self.cut) * own

        self.relative = own % 8 == 0

    def device(self, square, line):
        core, near, mid = square % 2, square // 2 % 2, square // 4
        if isinstance(line, int):
            slow, rest = line // self.rest, line % self.rest
        else:
            slow, rest = lax.div(line, self.rest), lax.rem(line, self.rest)
        return (((slow * 2 + mid) * self.rest + rest) * 2 + near) * 2 + core


def halves_of(counts):
    high = jnp.floor(counts * (1.0 / COUNT_BASE))
    return high, counts - high * COUNT_BASE


def head_rows(high, low):
    parts = [high, low]
    if high.shape[0] < HEAD // 2:
        pad = jnp.zeros((HEAD // 2 - high.shape[0], high.shape[1]), F32)
        parts = [high, pad, low, pad]
    return jnp.concatenate(parts, axis=0).astype(BF16)


def gather_kernel(plan, group, pitch, line_ref, edges_ref, weight_ref, cells_ref, *refs):
    own = plan.own
    first_ref = refs[0]
    second_refs = refs[1 : 1 + plan.line]
    root_ref, total_ref, count_ref = refs[1 + plan.line : 4 + plan.line]
    wide_refs = refs[4 + plan.line :]
    step = pl.program_id(0)
    last = pl.num_programs(0) - 1
    rows, zones, lanes = cells_ref.shape
    edges = total_ref.shape[1]

    @pl.when(step == 0)
    def _():
        total_ref[...] = jnp.zeros_like(total_ref)
        count_ref[...] = jnp.zeros_like(count_ref)

    columns = lax.broadcasted_iota(jnp.int32, (edges, rows), 0)
    ids = edges_ref[...]
    member = columns == ids[0:1, :]
    for j in range(1, ids.shape[0]):
        member = jnp.logical_or(member, columns == ids[j : j + 1, :])
    upright = jnp.transpose(jnp.broadcast_to(weight_ref[...], (lanes, edges)))
    upright = jnp.concatenate([upright] * (rows // lanes), axis=1)
    root = lax.rsqrt(jnp.sum(jnp.where(member, upright, 0.0), axis=0, keepdims=True))
    root_ref[...] = root
    rounded = root.astype(BF16).astype(F32)
    weighted = jnp.where(member, rounded, 0.0).astype(BF16)
    hot = jnp.where(member, 1.0, 0.0).astype(BF16)
    count_ref[...] += jnp.dot(hot, jnp.ones((rows, lanes), BF16), preferred_element_type=F32)

    part = 32
    groups = zones // group
    pairs = group // 2

    def load(g, first):
        return cells_ref[pl.ds(first, part), g * group : (g + 1) * group, :].astype(F32)

    def store(g, first, piece):
        for i in range(part):
            wide_refs[g][pl.ds(pl.multiple_of((first + i) * pitch, 8), group), :] = piece[i]

    def widen_first(i, carry):
        store(0, i * part, load(0, i * part))
        return carry

    lax.fori_loop(0, rows // part, widen_first, 0)
    share = rows // part // pairs
    for g in range(groups):
        for pair in range(pairs):
            left = wide_refs[g][pl.ds(2 * pair, rows, stride=pitch), :].astype(BF16)
            right = wide_refs[g][pl.ds(2 * pair + 1, rows, stride=pitch), :].astype(BF16)
            both = jnp.concatenate([left, right], axis=1)
            if g + 1 < groups:
                for i in range(share):
                    first = (pair * share + i) * part
                    store(g + 1, first, load(g + 1, first))
            total_ref[g * pairs + pair] += jnp.dot(weighted, both, preferred_element_type=F32)

    @pl.when(step == last)
    def _():
        for square in range(8):
            for shift in range(plan.line):
                if plan.relative:
                    device = plan.device(square, lax.rem(line_ref[0] + shift, plan.line))
                    at = pl.ds(pl.multiple_of(device * own, own), own)
                else:
                    device = plan.device(square, shift)
                    at = slice(device * own, (device + 1) * own)

                def columns_of(start, stop):
                    data = []
                    for d in range(start, stop):
                        data.append(total_ref[d // 2, at, (d % 2) * lanes : (d % 2 + 1) * lanes])
                    return jnp.concatenate(data, axis=0).astype(BF16)

                first_ref[square, shift] = columns_of(0, plan.cut)
                second_refs[shift][square, HEAD:, :] = columns_of(plan.cut, zones)
                second_refs[shift][square, 0:HEAD, :] = head_rows(*halves_of(count_ref[at, :]))


def partial_sums(line, cells, edges_t, edge_weight, plan):
    anchors, zones, lanes = cells.shape
    edges = edge_weight.shape[0]
    rows = min(512, anchors)
    group = min(zones, 16)
    pitch = group + 8
    shapes = [(8, plan.line, plan.first_rows, lanes)] + [(8, plan.second_rows, lanes)] * plan.line
    outs = pl.pallas_call(
        functools.partial(gather_kernel, plan, group, pitch),
        grid=(anchors // rows,),
        in_specs=[
            pl.BlockSpec(memory_space=pltpu.SMEM),
            pl.BlockSpec((edges_t.shape[0], rows), lambda i: (0, i)),
            pl.BlockSpec((1, edges), lambda i: (0, 0)),
            pl.BlockSpec((rows, zones, lanes), lambda i: (i, 0, 0)),
        ],
        out_specs=[pl.BlockSpec(shape, lambda i, zeros=(0,) * len(shape): zeros) for shape in shapes]
        + [pl.BlockSpec((1, rows), lambda i: (0, i))],
        out_shape=[jax.ShapeDtypeStruct(shape, BF16) for shape in shapes] + [jax.ShapeDtypeStruct((1, anchors), F32)],
        scratch_shapes=[
            pltpu.VMEM((zones // 2, edges, 2 * lanes), F32),
            pltpu.VMEM((edges, lanes), F32),
        ]
        + [pltpu.VMEM((rows * pitch, lanes), F32)] * (zones // group),
        compiler_params=pltpu.CompilerParams(vmem_limit_bytes=48 * 1024 * 1024),
        cost_estimate=pl.CostEstimate(
            flops=2 * anchors * edges * zones * lanes, bytes_accessed=2 * anchors * zones * lanes, transcendentals=0
        ),
    )(line[None], edges_t, edge_weight[None, :], cells)
    first, seconds = outs[0], outs[1:-1]
    if not plan.relative:
        first = lax.dynamic_slice_in_dim(jnp.concatenate([first, first], axis=1), line, plan.line, 1)
        seconds = jnp.stack(seconds * 2)
        seconds = [lax.dynamic_index_in_dim(seconds, line + k, 0, keepdims=False) for k in range(plan.line)]
    return first, seconds, outs[-1]


def add_up(pieces):
    total = pieces[0].astype(F32)
    for piece in pieces[1:]:
        total = total + piece.astype(F32)
    return total


def fold_first_kernel(plan, part_ref, *outs):
    for shift in range(plan.line):
        for quarter in range(4):
            outs[shift][quarter] = add_up([part_ref[quarter, shift], part_ref[4 + quarter, shift]]).astype(BF16)


def fold_second_kernel(plan, *refs):
    parts, out_ref = refs[: plan.line], refs[plan.line]
    for square in range(8):
        for rest in range(plan.rest):
            total = add_up([parts[shift][square] for shift in range(rest, plan.line, plan.rest)])
            half = HEAD // 2
            out_ref[square, rest, 0:HEAD, :] = head_rows(*halves_of(total[0:half] * COUNT_BASE + total[half:HEAD]))
            out_ref[square, rest, HEAD:, :] = total[HEAD:].astype(BF16)


def fold(kernel, plan, parts, shapes):
    whole = pl.BlockSpec(memory_space=pltpu.VMEM)
    size = sum(part.size for part in parts)
    return pl.pallas_call(
        functools.partial(kernel, plan),
        in_specs=[whole] * len(parts),
        out_specs=[whole] * len(shapes),
        out_shape=[jax.ShapeDtypeStruct(shape, BF16) for shape in shapes],
        compiler_params=pltpu.CompilerParams(vmem_limit_bytes=16 * 1024 * 1024),
        cost_estimate=pl.CostEstimate(flops=size, bytes_accessed=size * 4, transcendentals=0),
    )(*parts)


def org_sums(first, seconds, plan):
    lanes = first.shape[-1]
    seconds = [shifted(part, shift) if shift else part for shift, part in enumerate(seconds)]
    first = lax.all_to_all(first, SQUARE, split_axis=0, concat_axis=0, tiled=True)
    second = fold(fold_second_kernel, plan, seconds, [(8, plan.rest, plan.second_rows, lanes)])[0]
    firsts = fold(fold_first_kernel, plan, [first], [(4, plan.first_rows, lanes)] * plan.line)
    firsts = [shifted(part, shift) if shift else part for shift, part in enumerate(firsts)]
    second = lax.all_to_all(second, SQUARE, split_axis=0, concat_axis=0, tiled=True)
    return firsts, second


def table_kernel(plan, weight_ref, mixing_ref, matrix_ref, *refs):
    firsts = refs[: plan.line]
    second_ref, keep_ref, give_ref, mixed_ref = refs[plan.line :]
    own = plan.own
    lanes = mixing_ref.shape[0]
    half = HEAD // 2
    head = add_up([second_ref[0, 0, 0:HEAD, :], second_ref[4, 0, 0:HEAD, :]])
    counts = head[0:half] * COUNT_BASE + head[half:HEAD]
    scale = weight_ref[...] / counts[0:own]
    rows = plan.first_rows + plan.second_rows - HEAD
    zones = rows // own
    n_dst = 4 * plan.rest
    for k in range(n_dst):
        rest, quarter = k // 4, k % 4
        first = add_up([firsts[shift][quarter] for shift in range(rest, plan.line, plan.rest)])
        second = add_up([second_ref[quarter, rest, HEAD:, :], second_ref[4 + quarter, rest, HEAD:, :]])
        start = k * rows
        for total in (first, second):
            size = total.shape[0]
            totals = (total * jnp.concatenate([scale] * (size // own), axis=0)).astype(BF16)
            mixed = jnp.dot(totals, mixing_ref[...], preferred_element_type=F32)
            mixed_ref[start : start + size, :] = mixed
            start += size
    whole = n_dst * zones
    for e in range(own):
        mixed = mixed_ref[pl.ds(e, whole, stride=own), :] if own > 1 else mixed_ref[...]
        high = mixed.astype(BF16)
        low = (mixed - high.astype(F32)).astype(BF16)
        both = jnp.dot(matrix_ref[...], jnp.concatenate([high, low], axis=1), preferred_element_type=F32)
        result = (both[:, 0:lanes] + both[:, lanes : 2 * lanes]).astype(BF16)
        keep_ref[e] = result[0 : whole // 2]
        give_ref[e] = result[whole // 2 :]


def table_rows(firsts, second, weight_rows, mixing, matrix, plan):
    zones = matrix.shape[0]
    lanes = mixing.shape[0]
    whole = pl.BlockSpec(memory_space=pltpu.VMEM)
    half = jax.ShapeDtypeStruct((plan.own, zones // 2, lanes), BF16)
    return pl.pallas_call(
        functools.partial(table_kernel, plan),
        in_specs=[whole] * (4 + len(firsts)),
        out_specs=[whole] * 2,
        out_shape=[half, half],
        scratch_shapes=[pltpu.VMEM((zones * plan.own, lanes), F32)],
        compiler_params=pltpu.CompilerParams(vmem_limit_bytes=32 * 1024 * 1024),
        cost_estimate=pl.CostEstimate(
            flops=8 * plan.own * zones * lanes * lanes, bytes_accessed=4 * zones * plan.own * lanes, transcendentals=0
        ),
    )(weight_rows, mixing, matrix, *firsts, second)


def spread_kernel(n_long, n_short, half_ref, places_ref, root_ref, bias_ref, *refs):
    longs = refs[:n_long]
    shorts = refs[n_long : n_long + n_short]
    out_ref, table_ref, ring_ref, sems, ring_sems = refs[-5:]
    slots, rows, zones, lanes = ring_ref.shape
    steps = out_ref.shape[0] // rows
    half = half_ref[0]

    copies = []

    def bring(source, first, start):
        place = table_ref.at[pl.ds(first, source.shape[0]), pl.ds(start, source.shape[1]), :]
        copies.append(pltpu.make_async_copy(source, place, sems.at[len(copies)]))

    split = longs[0].shape[1]
    size = shorts[0].shape[0] // n_long
    for square, source in enumerate(longs):
        bring(source, square * n_short * size, 0)
    for shift, source in enumerate(shorts):
        for square in range(n_long):
            bring(source.at[pl.ds(square * size, size)], (square * n_short + shift) * size, split)
    for copy in copies:
        copy.start()
    for copy in copies:
        copy.wait()

    bias = bias_ref[...]
    count = places_ref.shape[0]
    tile = 16
    batch = min(8, rows)
    tiles = zones // tile

    def leaving(step, slot):
        place = out_ref.at[pl.ds(step * rows, rows), pl.ds(pl.multiple_of(half * zones, zones), zones), :]
        return pltpu.make_async_copy(ring_ref.at[slot], place, ring_sems.at[slot])

    def one_step(step, carry):
        slot = lax.rem(step, slots)

        @pl.when(step >= slots)
        def _():
            leaving(step - slots, slot).wait()

        def several(group, inner):
            values = []
            for i in range(batch):
                at = step * rows + group * batch + i
                scale = root_ref[0, at]
                spots = [places_ref[j, at] for j in range(count)]
                for first in range(0, zones, tile):
                    pieces = [table_ref[spot, first : first + tile, :] for spot in spots]
                    pieces = [(a + b).astype(F32) for a, b in zip(pieces[0::2], pieces[1::2])]
                    total = sum(pieces[1:], pieces[0])
                    values.append(jnp.maximum((total * scale + bias).astype(BF16), BF16(0.0)))
            for n, value in enumerate(values):
                start = n % tiles * tile
                ring_ref[slot, group * batch + n // tiles, start : start + tile, :] = value
            return inner

        lax.fori_loop(0, rows // batch, several, 0)
        leaving(step, slot).start()
        return carry

    lax.fori_loop(0, steps, one_step, 0)
    for step in range(steps - slots, steps):
        leaving(step, step % slots).wait()


def spread(half, places, root, bias, longs, shorts, before=None):
    anchors = places.shape[1]
    lanes = bias.shape[1]
    zones = longs[0].shape[1] + shorts[0].shape[1]
    rows = min(16, anchors // 8)
    slots = min(8, anchors // rows)
    smem = pl.BlockSpec(memory_space=pltpu.SMEM)
    anywhere = pl.BlockSpec(memory_space=pltpu.HBM)
    pieces = longs + shorts
    operands = [half, places, root, bias] + pieces
    specs = [smem, smem, smem, pl.BlockSpec(memory_space=pltpu.VMEM)] + [anywhere] * len(pieces)
    aliases = {}
    if before is not None:
        aliases = {len(operands): 0}
        operands.append(before)
        specs.append(anywhere)
    return pl.pallas_call(
        functools.partial(spread_kernel, len(longs), len(shorts)),
        in_specs=specs,
        out_specs=anywhere,
        out_shape=jax.ShapeDtypeStruct((anchors, 2 * zones, lanes), BF16),
        scratch_shapes=[
            pltpu.VMEM((len(longs) * longs[0].shape[0], zones, lanes), BF16),
            pltpu.VMEM((slots, rows, zones, lanes), BF16),
            pltpu.SemaphoreType.DMA((len(longs) * (1 + len(shorts)),)),
            pltpu.SemaphoreType.DMA((slots,)),
        ],
        input_output_aliases=aliases,
        compiler_params=pltpu.CompilerParams(vmem_limit_bytes=24 * 1024 * 1024),
        cost_estimate=pl.CostEstimate(
            flops=4096 * anchors * zones * lanes, bytes_accessed=4 * anchors * zones * lanes, transcendentals=0
        ),
    )(*operands)


LINE = ("slow", "rest")
SQUARE = ("mid", "near", "core")


def shifted(x, amount):
    size = lax.axis_size(LINE)
    return lax.ppermute(x, LINE, [(i, (i + amount) % size) for i in range(size)])


def crossed(x, turn):
    pairs = []
    for device in range(8):
        core = device % 2
        pairs.append((device, device ^ (2 if core == turn else 4)))
    return lax.ppermute(x, SQUARE, pairs)


def masked(x, mask):
    return lax.ppermute(x, SQUARE, [(device, device ^ mask) for device in range(8)])


def swapped(x):
    return lax.ppermute(x, "core", [(0, 1), (1, 0)])


def gather_table(keep, give):
    size = lax.axis_size(LINE)
    block = jnp.concatenate([keep, swapped(give)], axis=0)
    split = block.shape[1] * 3 // 4
    long, short = block[:, :split], block[:, split:]
    line = [long] + [shifted(long, k) for k in range(1, size)]
    short = jnp.concatenate([short, crossed(short, 0), crossed(short, 1), masked(short, 6)], axis=0)
    long = jnp.concatenate(line, axis=0)
    short, long = lax.optimization_barrier((short, long))
    first = crossed(long, 0)
    second = crossed(long, 1)
    shorts = [short] + [shifted(short, k) for k in range(1, size)]
    first, *shorts[1:-1] = lax.optimization_barrier((first, *shorts[1:-1]))
    both = crossed(first, 1)
    return [long, first, second, both], shorts


def places_of(ids, core, own):
    rest, size = lax.axis_size("rest"), lax.axis_size(LINE)
    owner = ids // own
    slot = jnp.where(owner % 2 == core, 0, own) + ids % own
    near = jnp.bitwise_xor(owner // 2 % 2, lax.axis_index("near"))
    mid = jnp.bitwise_xor(owner // (4 * rest) % 2, lax.axis_index("mid"))
    line = owner // (8 * rest) * rest + owner // 4 % rest
    line = lax.rem(lax.axis_index(LINE) - line + size, size)
    square = jnp.where(core == 0, 2 * mid + near, 2 * near + mid)
    return (square * size + line) * (2 * own) + slot


def relative_columns(matrix):
    zones, rest = matrix.shape[0], lax.axis_size("rest")
    if rest == 1:
        return matrix
    back = jnp.flip(matrix.reshape(zones, rest, -1), 1)
    back = jnp.concatenate([back, back], axis=1)
    return lax.dynamic_slice_in_dim(back, rest - 1 - lax.axis_index("rest"), rest, 1).reshape(zones, zones)


def shards(od_cells, anchor_edges, edge_weight, mixing, dst_edges, dst_weight, out_bias):
    n_org = lax.axis_size("slow") * lax.axis_size("mid")
    n_dst = lax.axis_size("rest") * lax.axis_size("near") * lax.axis_size("core")
    own = edge_weight.shape[0] // (n_org * n_dst)
    everyone = ("slow", "mid", "rest", "near", "core")
    core = lax.axis_index("core")
    edges_t = anchor_edges.T
    plan = Plan(od_cells.shape[1], own, lax.axis_size("rest"), lax.axis_size(LINE))
    first, seconds, roots = partial_sums(lax.axis_index(LINE), od_cells, edges_t, edge_weight, plan)
    firsts, second = org_sums(first, seconds, plan)
    own_weight = lax.dynamic_slice_in_dim(edge_weight, lax.axis_index(everyone) * own, own, 0)
    weight_rows = jnp.broadcast_to(own_weight[:, None], (own, mixing.shape[0]))
    matrix = relative_columns(dest_operator(dst_edges, dst_weight))
    half = matrix.shape[0] // 2
    matrix = jnp.where(core == 0, matrix, jnp.concatenate([matrix[half:], matrix[:half]], axis=0))
    keep, give = table_rows(firsts, second, weight_rows, mixing, matrix, plan)
    longs, shorts = gather_table(keep, give)
    rows = anchor_edges.shape[0] // n_dst
    start = lax.axis_index(("rest", "near", "core")) * rows
    ids = lax.dynamic_slice_in_dim(edges_t, start, rows, 1)
    own_root = lax.dynamic_slice_in_dim(roots, start, rows, 1)
    bias = out_bias[None, :]
    other = 1 - core
    result = spread(core[None], places_of(ids, core, own), own_root, bias, longs, shorts)
    longs, shorts = [swapped(x) for x in longs], [swapped(x) for x in shorts]
    return spread(other[None], places_of(ids, other, own), own_root, bias, longs, shorts, result)


def solution(mesh):
    n_org, n_dst = mesh.devices.shape
    fine = Mesh(mesh.devices.reshape(n_org // 2, 2, n_dst // 4, 2, 2), ("slow", "mid", "rest", "near", "core"))
    org, dst = ("slow", "mid"), ("rest", "near", "core")
    in_specs = (P(org, dst, None), P(org, None), P(), P(), P(), P(), P())
    out_specs = P(org + dst, None, None)
    return jax.shard_map(shards, mesh=fine, in_specs=in_specs, out_specs=out_specs, check_vma=False)
```

time: 180 us -> 146 us (0.81)
  the two profiles are of different devices: /device:TPU:13 before, /device:TPU:1 now
where the time goes in v7:
time: 146 us; the launch traced here: 145 us
  waiting for transfers between devices  62.8 us (43%)
  starting transfers between devices  42.7 us (29%)
  Pallas kernels  36.9 us (25%)
  local copies, waits for them, and re-layouts  1.68 us (1%)
    ppermute x12, waiting for transfers between devices, shifted(): lax.ppermute(x, LINE, [(i, (i + amount) % size) for i in range(size)])  57.1 us
    pallas_call x2, Pallas kernels, spread(): pl.pallas_call(functools.partial(spread_kernel, len(longs), len(shorts)),...  19.4 us
    ppermute x12, starting transfers between devices, shifted(): lax.ppermute(x, LINE, [(i, (i + amount) % size) for i in range(size)])  18.3 us
    pallas_call x1, Pallas kernels, partial_sums(): pl.pallas_call(functools.partial(gather_kernel, plan, group, pitch), grid...  15.9 us
    ppermute x9, starting transfers between devices, swapped(): return lax.ppermute(x, 'core', [(0, 1), (1, 0)])  11.5 us
    all_to_all x1, starting transfers between devices, org_sums(): lax.all_to_all(first, SQUARE, split_axis=0, concat_axis=0, tiled=True)  5.24 us
    all_to_all x1, starting transfers between devices, org_sums(): lax.all_to_all(second, SQUARE, split_axis=0, concat_axis=0, tiled=True)  4.4 us
    ppermute x5, waiting for transfers between devices, crossed(): return lax.ppermute(x, SQUARE, pairs)  3.32 us
  transfers between devices with their start and end apart: 29, of which 11 were waited for; matrix products, arithmetic and copies ran while one was open for 1% of the time, Pallas kernels for 7%

profile of v7, /device:TPU:1, one launch (start us, length us, event | category | flops | bytes accessed | tf_op | source)
XLA Modules:
  0.0 145.1 jit_solution(18159920568273939098)
XLA Ops:
  0.0 0.8 copy-done
  0.8 0.7 copy-done.3
  1.5 15.9 %shard_map.73 = (bf16[8,4,160,128]{3,2,1,0:T(8,128)(2,1)}, bf16[8,112,128]{2,1,0:T(8,128)(2,1)S(1)}, bf16[8,112,128]{2,1,0:T(8,128)(2,1)S(1)}, bf16[8,112,128]{2...) custom-call(s32[1]{0:T(128)} %bitcast.2.line_ref, s32[4,2048]{1,0:T(4,128)S(1)} %bitcast.31, ...), custom_call_target="tpu_custom_call" | custom-call | flops 4294967296 | bytes 16777216 | tf_op jit(solution)/shard_map/pallas_call | solution.py:151
  17.4 5.2 %all-to-all-start = ((bf16[8,4,160,128]{3,2,1,0:T(8,128)(2,1)}), bf16[8,4,160,128]{3,2,1,0:T(8,128)(2,1)S(1)}, u32[]{:S(2)}, u32[]{:S(2)}) async-start(bf16[8,4,160,128]{3,2,1,0:T(8,128)(2,1)} %get-tuple-element.23), calls=%async_computation | async-start | bytes 2621440 | tf_op jit(solution)/shard_map/all_to_all | solution.py:220
  22.6 1.3 collective-permute-start.3
  23.9 2.3 %collective-permute-start.4 = (bf16[8,112,128]{2,1,0:T(8,128)(2,1)S(1)}, bf16[8,112,128]{2,1,0:T(8,128)(2,1)S(1)}, u32[]{:S(2)}, u32[]{:S(2)}) collective-permute-start(bf16[8,112,128]{2,1,0:T(8,128)(2,1)S(1)} %get-tuple-element.30), channel_id=1, source_target_pairs={{0,16},{8,24},{16,0},{24,8},{1,17},{9,25},{17,1},{25,9},{2,18},{10... | collective-permute-start | bytes 688136 | tf_op jit(solution)/shard_map/ppermute | solution.py:389
  26.2 1.1 collective-permute-start.5
  27.3 0.1 convert_reduce_fusion
  27.5 0.1 multiply_reduce_fusion
  27.6 0.3 convolution_convert_fusion
  28.0 3.8 %collective-permute-done.3.refs_1_ = bf16[8,112,128]{2,1,0:T(8,128)(2,1)S(1)} collective-permute-done((bf16[8,112,128]{2,1,0:T(8,128)(2,1)S(1)}, bf16[8,112,128]{2,1,0:T(8,128)(2,1)S(1)}, u32[]{:S(2)}, u32[]{:S(2)}) %collective-permute-start.3) | collective-permute-done | bytes 229408 | tf_op jit(solution)/shard_map/ppermute | solution.py:389
  31.8 10.1 %collective-permute-done.4.refs_2_ = bf16[8,112,128]{2,1,0:T(8,128)(2,1)S(1)} collective-permute-done((bf16[8,112,128]{2,1,0:T(8,128)(2,1)S(1)}, bf16[8,112,128]{2,1,0:T(8,128)(2,1)S(1)}, u32[]{:S(2)}, u32[]{:S(2)}) %collective-permute-start.4) | collective-permute-done | bytes 229408 | tf_op jit(solution)/shard_map/ppermute | solution.py:389
  41.9 0.8 shard_map.75
  42.7 4.4 %all-to-all-start.1 = ((bf16[8,1,112,128]{3,2,1,0:T(8,128)(2,1)}), bf16[8,1,112,128]{3,2,1,0:T(8,128)(2,1)S(1)}, u32[]{:S(2)}, u32[]{:S(2)}) async-start(bf16[8,1,112,128]{3,2,1,0:T(8,128)(2,1)} %shard_map.75), calls=%async_computation.1 | async-start | bytes 458752 | tf_op jit(solution)/shard_map/all_to_all | solution.py:224
  47.1 0.2 shard_map.74
  47.3 5.2 %collective-permute-start = (bf16[4,160,128]{2,1,0:T(8,128)(2,1)S(1)}, bf16[4,160,128]{2,1,0:T(8,128)(2,1)S(1)}, u32[]{:S(2)}, u32[]{:S(2)}) collective-permute-start(bf16[4,160,128]{2,1,0:T(8,128)(2,1)S(1)} %get-tuple-element.25), channel_id=1, source_target_pairs={{0,8},{8,16},{16,24},{24,0},{1,9},{9,17},{17,25},{25,1},{2,10},{10... | collective-permute-start | bytes 491528 | tf_op jit(solution)/shard_map/ppermute | solution.py:389
  52.4 1.3 collective-permute-start.1
  53.7 0.8 collective-permute-start.2
  54.6 3.5 %collective-permute-done.refs_1_ = bf16[4,160,128]{2,1,0:T(8,128)(2,1)S(1)} collective-permute-done((bf16[4,160,128]{2,1,0:T(8,128)(2,1)S(1)}, bf16[4,160,128]{2,1,0:T(8,128)(2,1)S(1)}, u32[]{:S(2)}, u32[]{:S(2)}) %collective-permute-start) | collective-permute-done | bytes 163872 | tf_op jit(solution)/shard_map/ppermute | solution.py:389
  58.1 7.1 %collective-permute-done.1.refs_2_ = bf16[4,160,128]{2,1,0:T(8,128)(2,1)S(1)} collective-permute-done((bf16[4,160,128]{2,1,0:T(8,128)(2,1)S(1)}, bf16[4,160,128]{2,1,0:T(8,128)(2,1)S(1)}, u32[]{:S(2)}, u32[]{:S(2)}) %collective-permute-start.1) | collective-permute-done | bytes 163872 | tf_op jit(solution)/shard_map/ppermute | solution.py:389
  65.3 0.6 shard_map.76
  65.8 0.6 collective-permute-start.6
  66.4 1.0 collective-permute-done.6
  67.5 2.4 %collective-permute-start.9 = (bf16[16,16,128]{2,1,0:T(8,128)(2,1)S(1)}, bf16[16,16,128]{2,1,0:T(8,128)(2,1)S(1)}, u32[]{:S(2)}, u32[]{:S(2)}) collective-permute-start(bf16[16,16,128]{2,1,0:T(8,128)(2,1)S(1)} %slice.18), channel_id=1, source_target_pairs={{0,6},{1,7},{2,4},{3,5},{4,2},{5,3},{6,0},{7,1},{8,14},{9,15},{10,... | collective-permute-start | bytes 196616 | tf_op jit(solution)/shard_map/ppermute | solution.py:401
  69.8 4.5 %collective-permute-start.12 = (bf16[16,48,128]{2,1,0:T(8,128)(2,1)S(1)}, bf16[16,48,128]{2,1,0:T(8,128)(2,1)S(1)}, u32[]{:S(2)}, u32[]{:S(2)}) collective-permute-start(bf16[16,48,128]{2,1,0:T(8,128)(2,1)S(1)} %slice.19), channel_id=1, source_target_pairs={{0,24},{8,0},{16,8},{24,16},{1,25},{9,1},{17,9},{25,17},{2,26},{10... | collective-permute-start | bytes 589832 | tf_op jit(solution)/shard_map/ppermute | solution.py:389
  74.3 0.4 collective-permute-start.11
  74.8 0.3 collective-permute-start.8
  75.1 0.1 collective-permute-start.7
  75.2 3.0 %collective-permute-done.8 = bf16[16,16,128]{2,1,0:T(8,128)(2,1)S(1)} collective-permute-done((bf16[16,16,128]{2,1,0:T(8,128)(2,1)S(1)}, bf16[16,16,128]{2,1,0:T(8,128)(2,1)S(1)}, u32[]{:S(2)}, u32[]{:S(2)}) %collective-permute-start.8) | collective-permute-done | bytes 65568 | tf_op jit(solution)/shard_map/ppermute | solution.py:397
  78.2 0.3 collective-permute-done.7
  78.5 13.2 %collective-permute-done.11 = bf16[16,48,128]{2,1,0:T(8,128)(2,1)S(1)} collective-permute-done((bf16[16,48,128]{2,1,0:T(8,128)(2,1)S(1)}, bf16[16,48,128]{2,1,0:T(8,128)(2,1)S(1)}, u32[]{:S(2)}, u32[]{:S(2)}) %collective-permute-start.11) | collective-permute-done | bytes 196640 | tf_op jit(solution)/shard_map/ppermute | solution.py:389
  91.8 0.1 pad_maximum_fusion.refs_0_
  91.9 0.3 collective-permute-start.14
  92.2 1.3 collective-permute-start.16
  93.6 0.1 collective-permute-start.18
  93.7 2.2 %collective-permute-start.13 = (bf16[64,48,128]{2,1,0:T(8,128)(2,1)S(1)}, bf16[64,48,128]{2,1,0:T(8,128)(2,1)S(1)}, u32[]{:S(2)}, u32[]{:S(2)}) collective-permute-start(bf16[64,48,128]{2,1,0:T(8,128)(2,1)S(1)} %pad_maximum_fusion.refs_0_), channel_id=1, source_target_pairs={{0,1},{1,0},{2,3},{3,2},{4,5},{5,4},{6,7},{7,6},{8,9},{9,8},{10,11... | collective-permute-start | bytes 2359304 | tf_op jit(solution)/shard_map/ppermute | solution.py:405
  95.8 15.9 %collective-permute-done.16.refs_6_ = bf16[64,16,128]{2,1,0:T(8,128)(2,1)S(1)} collective-permute-done((bf16[64,16,128]{2,1,0:T(8,128)(2,1)S(1)}, bf16[64,16,128]{2,1,0:T(8,128)(2,1)S(1)}, u32[]{:S(2)}, u32[]{:S(2)}) %collective-permute-start.16) | collective-permute-done | bytes 262176 | tf_op jit(solution)/shard_map/ppermute | solution.py:389
  111.8 0.1 add_add_fusion
  111.9 2.2 %collective-permute-start.22 = (bf16[64,16,128]{2,1,0:T(8,128)(2,1)S(1)}, bf16[64,16,128]{2,1,0:T(8,128)(2,1)}, u32[]{:S(2)}, u32[]{:S(2)}) collective-permute-start(bf16[64,16,128]{2,1,0:T(8,128)(2,1)S(1)} %pad_maximum_fusion.1.refs_4_), channel_id=1, source_target_pairs={{0,1},{1,0},{2,3},{3,2},{4,5},{5,4},{6,7},{7,6},{8,9},{9,8},{10,11... | collective-permute-start | bytes 786440 | tf_op jit(solution)/shard_map/ppermute | solution.py:405
  114.1 3.5 %collective-permute-done.25.refs_7_ = bf16[64,16,128]{2,1,0:T(8,128)(2,1)} collective-permute-done((bf16[64,16,128]{2,1,0:T(8,128)(2,1)S(1)}, bf16[64,16,128]{2,1,0:T(8,128)(2,1)}, u32[]{:S(2)}, u32[]{:S(2)}) %collective-permute-start.25) | collective-permute-done | bytes 262176 | tf_op jit(solution)/shard_map/ppermute | solution.py:389
  117.6 3.0 %collective-permute-start.26 = (bf16[64,16,128]{2,1,0:T(8,128)(2,1)}, bf16[64,16,128]{2,1,0:T(8,128)(2,1)}, u32[]{:S(2)}, u32[]{:S(2)}) collective-permute-start(bf16[64,16,128]{2,1,0:T(8,128)(2,1)} %collective-permute-done.25.refs_7_), channel_id=1, source_target_pairs={{0,1},{1,0},{2,3},{3,2},{4,5},{5,4},{6,7},{7,6},{8,9},{9,8},{10,11... | collective-permute-start | bytes 786440 | tf_op jit(solution)/shard_map/ppermute | solution.py:405
  120.8 1.3 collective-permute-done.26.refs_7_
  122.1 0.4 collective-permute-start.23
  122.5 0.1 collective-permute-start.24
  122.6 0.4 collective-permute-start.19
  123.0 2.6 %collective-permute-start.21 = (bf16[64,48,128]{2,1,0:T(8,128)(2,1)}, bf16[64,48,128]{2,1,0:T(8,128)(2,1)S(1)}, u32[]{:S(2)}, u32[]{:S(2)}) collective-permute-start(bf16[64,48,128]{2,1,0:T(8,128)(2,1)} %collective-permute-done.20.refs_3_), channel_id=1, source_target_pairs={{0,1},{1,0},{2,3},{3,2},{4,5},{5,4},{6,7},{7,6},{8,9},{9,8},{10,11... | collective-permute-start | bytes 2359304 | tf_op jit(solution)/shard_map/ppermute | solution.py:405
  125.6 9.8 %shard_map.77.refs_8_ = bf16[512,128,128]{2,1,0:T(8,128)(2,1)} custom-call(s32[1]{0:T(128)} %bitcast.6.half_ref, s32[4,512]{1,0:T(4,128)S(1)} %get-tuple-element.41.places_ref, f32[1,512]{1,0:T(1,128)S(1)} %constant_dynamic-slice_fusion.root_ref, f32[1,128]{1,0:T(1,128)S(1)} %bitcast.33, bf16[64,48,128]{2,1,0:T(8,128)(2,1)S(1)} %pad_maximum_fusion.refs_0_, ...), custom_call_target="tpu_custom_call" | custom-call | flops 17179869184 | bytes 16777216 | tf_op jit(solution)/shard_map/pallas_call | solution.py:364
  135.4 9.7 %shard_map.78 = bf16[512,128,128]{2,1,0:T(8,128)(2,1)} custom-call(s32[1]{0:T(128)} %bitcast.half_ref, s32[4,512]{1,0:T(4,128)S(1)} %add_add_fusion.1.places_ref, f32[1,512]{1,0:T(1,128)S(1)} %constant_dynamic-slice_fusion.root_ref, f32[1,128]{1,0:T(1,128)S(1)} %bitcast.34, ...), custom_call_target="tpu_custom_call", output_to_operand_aliasing={{}: (12, {})} | custom-call | flops 17179869184 | bytes 16777216 | tf_op jit(solution)/shard_map/pallas_call | solution.py:364
  (50 shorter events, 0.6 us)
Async XLA Ops:
  0.0 27.9 %copy-start.4 = (f32[256]{0:T(256)S(1)}, f32[256]{0:T(256)}, u32[]{:S(2)}) copy-start(f32[256]{0:T(256)} %param.9) | copy-start | bytes 3076
  0.0 27.3 %copy-start.6 = (s32[128,3]{0,1:T(4,128)S(1)}, s32[128,3]{0,1:T(4,128)}, u32[]{:S(2)}) copy-start(s32[128,3]{0,1:T(4,128)} %param.11) | copy-start | bytes 4612
  0.0 27.4 %copy-start.7 = (f32[128]{0:T(128)S(1)}, f32[128]{0:T(128)}, u32[]{:S(2)}) copy-start(f32[128]{0:T(128)} %param.12) | copy-start | bytes 1540
  0.0 125.6 %copy-start.5 = (f32[128]{0:T(128)S(1)}, f32[128]{0:T(128)}, u32[]{:S(2)}) copy-start(f32[128]{0:T(128)} %param.13) | copy-start | bytes 1540
  0.0 0.8 copy-start
  0.8 0.7 copy-start.3
  1.5 63.8 %copy-start.2 = (bf16[128,128]{1,0:T(8,128)(2,1)S(1)}, bf16[128,128]{1,0:T(8,128)(2,1)}, u32[]{:S(2)}) copy-start(bf16[128,128]{1,0:T(8,128)(2,1)} %mixing_ref.1) | copy-start | bytes 98308
  1.5 110.3 %copy-start.1 = (s32[2048,4]{0,1:T(4,128)S(1)}, s32[2048,4]{0,1:T(4,128)}, u32[]{:S(2)}) copy-start(s32[2048,4]{0,1:T(4,128)} %param.8) | copy-start | bytes 98308
  17.4 25.3 %all-to-all-start = ((bf16[8,4,160,128]{3,2,1,0:T(8,128)(2,1)}), bf16[8,4,160,128]{3,2,1,0:T(8,128)(2,1)S(1)}, u32[]{:S(2)}, u32[]{:S(2)}) async-start(bf16[8,4,160,128]{3,2,1,0:T(8,128)(2,1)} %get-tuple-element.23), calls=%async_computation | async-start | bytes 2621440 | tf_op jit(solution)/shard_map/all_to_all | solution.py:220
  22.6 9.2 %collective-permute-start.3 = (bf16[8,112,128]{2,1,0:T(8,128)(2,1)S(1)}, bf16[8,112,128]{2,1,0:T(8,128)(2,1)S(1)}, u32[]{:S(2)}, u32[]{:S(2)}) collective-permute-start(bf16[8,112,128]{2,1,0:T(8,128)(2,1)S(1)} %get-tuple-element.29), channel_id=1, source_target_pairs={{0,8},{8,16},{16,24},{24,0},{1,9},{9,17},{17,25},{25,1},{2,10},{10... | collective-permute-start | bytes 688136 | tf_op jit(solution)/shard_map/ppermute | solution.py:389
  23.9 18.0 %collective-permute-start.4 = (bf16[8,112,128]{2,1,0:T(8,128)(2,1)S(1)}, bf16[8,112,128]{2,1,0:T(8,128)(2,1)S(1)}, u32[]{:S(2)}, u32[]{:S(2)}) collective-permute-start(bf16[8,112,128]{2,1,0:T(8,128)(2,1)S(1)} %get-tuple-element.30), channel_id=1, source_target_pairs={{0,16},{8,24},{16,0},{24,8},{1,17},{9,25},{17,1},{25,9},{2,18},{10... | collective-permute-start | bytes 688136 | tf_op jit(solution)/shard_map/ppermute | solution.py:389
  26.2 15.7 %collective-permute-start.5 = (bf16[8,112,128]{2,1,0:T(8,128)(2,1)S(1)}, bf16[8,112,128]{2,1,0:T(8,128)(2,1)S(1)}, u32[]{:S(2)}, u32[]{:S(2)}) collective-permute-start(bf16[8,112,128]{2,1,0:T(8,128)(2,1)S(1)} %get-tuple-element.31), channel_id=1, source_target_pairs={{0,24},{8,0},{16,8},{24,16},{1,25},{9,1},{17,9},{25,17},{2,26},{10... | collective-permute-start | bytes 688136 | tf_op jit(solution)/shard_map/ppermute | solution.py:389
  42.7 11.9 %all-to-all-start.1 = ((bf16[8,1,112,128]{3,2,1,0:T(8,128)(2,1)}), bf16[8,1,112,128]{3,2,1,0:T(8,128)(2,1)S(1)}, u32[]{:S(2)}, u32[]{:S(2)}) async-start(bf16[8,1,112,128]{3,2,1,0:T(8,128)(2,1)} %shard_map.75), calls=%async_computation.1 | async-start | bytes 458752 | tf_op jit(solution)/shard_map/all_to_all | solution.py:224
  47.3 10.8 %collective-permute-start = (bf16[4,160,128]{2,1,0:T(8,128)(2,1)S(1)}, bf16[4,160,128]{2,1,0:T(8,128)(2,1)S(1)}, u32[]{:S(2)}, u32[]{:S(2)}) collective-permute-start(bf16[4,160,128]{2,1,0:T(8,128)(2,1)S(1)} %get-tuple-element.25), channel_id=1, source_target_pairs={{0,8},{8,16},{16,24},{24,0},{1,9},{9,17},{17,25},{25,1},{2,10},{10... | collective-permute-start | bytes 491528 | tf_op jit(solution)/shard_map/ppermute | solution.py:389
  52.4 12.8 %collective-permute-start.1 = (bf16[4,160,128]{2,1,0:T(8,128)(2,1)S(1)}, bf16[4,160,128]{2,1,0:T(8,128)(2,1)S(1)}, u32[]{:S(2)}, u32[]{:S(2)}) collective-permute-start(bf16[4,160,128]{2,1,0:T(8,128)(2,1)S(1)} %get-tuple-element.26), channel_id=1, source_target_pairs={{0,16},{8,24},{16,0},{24,8},{1,17},{9,25},{17,1},{25,9},{2,18},{10... | collective-permute-start | bytes 491528 | tf_op jit(solution)/shard_map/ppermute | solution.py:389
  53.7 11.4 %collective-permute-start.2 = (bf16[4,160,128]{2,1,0:T(8,128)(2,1)S(1)}, bf16[4,160,128]{2,1,0:T(8,128)(2,1)S(1)}, u32[]{:S(2)}, u32[]{:S(2)}) collective-permute-start(bf16[4,160,128]{2,1,0:T(8,128)(2,1)S(1)} %get-tuple-element.27), channel_id=1, source_target_pairs={{0,24},{8,0},{16,8},{24,16},{1,25},{9,1},{17,9},{25,17},{2,26},{10... | collective-permute-start | bytes 491528 | tf_op jit(solution)/shard_map/ppermute | solution.py:389
  65.8 1.6 %collective-permute-start.6 = (bf16[8,64,128]{2,1,0:T(8,128)(2,1)S(1)}, bf16[8,64,128]{2,1,0:T(8,128)(2,1)S(1)}, u32[]{:S(2)}, u32[]{:S(2)}) collective-permute-start(bf16[8,64,128]{2,1,0:T(8,128)(2,1)S(1)} %get-tuple-element.33), channel_id=1, source_target_pairs={{0,1},{1,0},{2,3},{3,2},{4,5},{5,4},{6,7},{7,6},{8,9},{9,8},{10,11... | collective-permute-start | bytes 393224 | tf_op jit(solution)/shard_map/ppermute | solution.py:405
  67.5 7.6 %collective-permute-start.9 = (bf16[16,16,128]{2,1,0:T(8,128)(2,1)S(1)}, bf16[16,16,128]{2,1,0:T(8,128)(2,1)S(1)}, u32[]{:S(2)}, u32[]{:S(2)}) collective-permute-start(bf16[16,16,128]{2,1,0:T(8,128)(2,1)S(1)} %slice.18), channel_id=1, source_target_pairs={{0,6},{1,7},{2,4},{3,5},{4,2},{5,3},{6,0},{7,1},{8,14},{9,15},{10,... | collective-permute-start | bytes 196616 | tf_op jit(solution)/shard_map/ppermute | solution.py:401
  69.8 8.7 %collective-permute-start.12 = (bf16[16,48,128]{2,1,0:T(8,128)(2,1)S(1)}, bf16[16,48,128]{2,1,0:T(8,128)(2,1)S(1)}, u32[]{:S(2)}, u32[]{:S(2)}) collective-permute-start(bf16[16,48,128]{2,1,0:T(8,128)(2,1)S(1)} %slice.19), channel_id=1, source_target_pairs={{0,24},{8,0},{16,8},{24,16},{1,25},{9,1},{17,9},{25,17},{2,26},{10... | collective-permute-start | bytes 589832 | tf_op jit(solution)/shard_map/ppermute | solution.py:389
  74.3 17.4 %collective-permute-start.11 = (bf16[16,48,128]{2,1,0:T(8,128)(2,1)S(1)}, bf16[16,48,128]{2,1,0:T(8,128)(2,1)S(1)}, u32[]{:S(2)}, u32[]{:S(2)}) collective-permute-start(bf16[16,48,128]{2,1,0:T(8,128)(2,1)S(1)} %slice.19), channel_id=1, source_target_pairs={{0,16},{8,24},{16,0},{24,8},{1,17},{9,25},{17,1},{25,9},{2,18},{10... | collective-permute-start | bytes 589832 | tf_op jit(solution)/shard_map/ppermute | solution.py:389
  74.8 17.0 %collective-permute-start.10 = (bf16[16,48,128]{2,1,0:T(8,128)(2,1)S(1)}, bf16[16,48,128]{2,1,0:T(8,128)(2,1)S(1)}, u32[]{:S(2)}, u32[]{:S(2)}) collective-permute-start(bf16[16,48,128]{2,1,0:T(8,128)(2,1)S(1)} %slice.19), channel_id=1, source_target_pairs={{0,8},{8,16},{16,24},{24,0},{1,9},{9,17},{17,25},{25,1},{2,10},{10... | collective-permute-start | bytes 589832 | tf_op jit(solution)/shard_map/ppermute | solution.py:389
  74.8 3.4 %collective-permute-start.8 = (bf16[16,16,128]{2,1,0:T(8,128)(2,1)S(1)}, bf16[16,16,128]{2,1,0:T(8,128)(2,1)S(1)}, u32[]{:S(2)}, u32[]{:S(2)}) collective-permute-start(bf16[16,16,128]{2,1,0:T(8,128)(2,1)S(1)} %slice.18), channel_id=1, source_target_pairs={{0,4},{1,3},{2,6},{3,1},{4,0},{5,7},{6,2},{7,5},{8,12},{9,11},{10,... | collective-permute-start | bytes 196616 | tf_op jit(solution)/shard_map/ppermute | solution.py:397
  75.1 3.4 %collective-permute-start.7 = (bf16[16,16,128]{2,1,0:T(8,128)(2,1)S(1)}, bf16[16,16,128]{2,1,0:T(8,128)(2,1)S(1)}, u32[]{:S(2)}, u32[]{:S(2)}) collective-permute-start(bf16[16,16,128]{2,1,0:T(8,128)(2,1)S(1)} %slice.18), channel_id=1, source_target_pairs={{0,2},{1,5},{2,0},{3,7},{4,6},{5,1},{6,4},{7,3},{8,10},{9,13},{10,... | collective-permute-start | bytes 196616 | tf_op jit(solution)/shard_map/ppermute | solution.py:397
  91.9 19.9 %collective-permute-start.14 = (bf16[64,48,128]{2,1,0:T(8,128)(2,1)S(1)}, bf16[64,48,128]{2,1,0:T(8,128)(2,1)S(1)}, u32[]{:S(2)}, u32[]{:S(2)}) collective-permute-start(bf16[64,48,128]{2,1,0:T(8,128)(2,1)S(1)} %pad_maximum_fusion.refs_0_), channel_id=1, source_target_pairs={{0,2},{1,5},{2,0},{3,7},{4,6},{5,1},{6,4},{7,3},{8,10},{9,13},{10,... | collective-permute-start | bytes 2359304 | tf_op jit(solution)/shard_map/ppermute | solution.py:397
  92.2 19.5 %collective-permute-start.16 = (bf16[64,16,128]{2,1,0:T(8,128)(2,1)S(1)}, bf16[64,16,128]{2,1,0:T(8,128)(2,1)S(1)}, u32[]{:S(2)}, u32[]{:S(2)}) collective-permute-start(bf16[64,16,128]{2,1,0:T(8,128)(2,1)S(1)} %pad_maximum_fusion.1.refs_4_), channel_id=1, source_target_pairs={{0,16},{8,24},{16,0},{24,8},{1,17},{9,25},{17,1},{25,9},{2,18},{10... | collective-permute-start | bytes 786440 | tf_op jit(solution)/shard_map/ppermute | solution.py:389
  93.6 18.2 %collective-permute-start.15 = (bf16[64,16,128]{2,1,0:T(8,128)(2,1)S(1)}, bf16[64,16,128]{2,1,0:T(8,128)(2,1)S(1)}, u32[]{:S(2)}, u32[]{:S(2)}) collective-permute-start(bf16[64,16,128]{2,1,0:T(8,128)(2,1)S(1)} %pad_maximum_fusion.1.refs_4_), channel_id=1, source_target_pairs={{0,8},{8,16},{16,24},{24,0},{1,9},{9,17},{17,25},{25,1},{2,10},{10... | collective-permute-start | bytes 786440 | tf_op jit(solution)/shard_map/ppermute | solution.py:389
  93.6 28.9 %collective-permute-start.18 = (bf16[64,48,128]{2,1,0:T(8,128)(2,1)S(1)}, bf16[64,48,128]{2,1,0:T(8,128)(2,1)}, u32[]{:S(2)}, u32[]{:S(2)}) collective-permute-start(bf16[64,48,128]{2,1,0:T(8,128)(2,1)S(1)} %pad_maximum_fusion.refs_0_), channel_id=1, source_target_pairs={{0,4},{1,3},{2,6},{3,1},{4,0},{5,7},{6,2},{7,5},{8,12},{9,11},{10,... | collective-permute-start | bytes 2359304 | tf_op jit(solution)/shard_map/ppermute | solution.py:397
  93.7 29.0 %collective-permute-start.13 = (bf16[64,48,128]{2,1,0:T(8,128)(2,1)S(1)}, bf16[64,48,128]{2,1,0:T(8,128)(2,1)S(1)}, u32[]{:S(2)}, u32[]{:S(2)}) collective-permute-start(bf16[64,48,128]{2,1,0:T(8,128)(2,1)S(1)} %pad_maximum_fusion.refs_0_), channel_id=1, source_target_pairs={{0,1},{1,0},{2,3},{3,2},{4,5},{5,4},{6,7},{7,6},{8,9},{9,8},{10,11... | collective-permute-start | bytes 2359304 | tf_op jit(solution)/shard_map/ppermute | solution.py:405
  111.7 11.3 %collective-permute-start.20 = (bf16[64,48,128]{2,1,0:T(8,128)(2,1)S(1)}, bf16[64,48,128]{2,1,0:T(8,128)(2,1)}, u32[]{:S(2)}, u32[]{:S(2)}) collective-permute-start(bf16[64,48,128]{2,1,0:T(8,128)(2,1)S(1)} %collective-permute-done.14.refs_1_), channel_id=1, source_target_pairs={{0,4},{1,3},{2,6},{3,1},{4,0},{5,7},{6,2},{7,5},{8,12},{9,11},{10,... | collective-permute-start | bytes 2359304 | tf_op jit(solution)/shard_map/ppermute | solution.py:397
  111.7 5.8 %collective-permute-start.25 = (bf16[64,16,128]{2,1,0:T(8,128)(2,1)S(1)}, bf16[64,16,128]{2,1,0:T(8,128)(2,1)}, u32[]{:S(2)}, u32[]{:S(2)}) collective-permute-start(bf16[64,16,128]{2,1,0:T(8,128)(2,1)S(1)} %pad_maximum_fusion.1.refs_4_), channel_id=1, source_target_pairs={{0,24},{8,0},{16,8},{24,16},{1,25},{9,1},{17,9},{25,17},{2,26},{10... | collective-permute-start | bytes 786440 | tf_op jit(solution)/shard_map/ppermute | solution.py:389
  111.9 8.8 %collective-permute-start.22 = (bf16[64,16,128]{2,1,0:T(8,128)(2,1)S(1)}, bf16[64,16,128]{2,1,0:T(8,128)(2,1)}, u32[]{:S(2)}, u32[]{:S(2)}) collective-permute-start(bf16[64,16,128]{2,1,0:T(8,128)(2,1)S(1)} %pad_maximum_fusion.1.refs_4_), channel_id=1, source_target_pairs={{0,1},{1,0},{2,3},{3,2},{4,5},{5,4},{6,7},{7,6},{8,9},{9,8},{10,11... | collective-permute-start | bytes 786440 | tf_op jit(solution)/shard_map/ppermute | solution.py:405
  117.6 4.6 %collective-permute-start.26 = (bf16[64,16,128]{2,1,0:T(8,128)(2,1)}, bf16[64,16,128]{2,1,0:T(8,128)(2,1)}, u32[]{:S(2)}, u32[]{:S(2)}) collective-permute-start(bf16[64,16,128]{2,1,0:T(8,128)(2,1)} %collective-permute-done.25.refs_7_), channel_id=1, source_target_pairs={{0,1},{1,0},{2,3},{3,2},{4,5},{5,4},{6,7},{7,6},{8,9},{9,8},{10,11... | collective-permute-start | bytes 786440 | tf_op jit(solution)/shard_map/ppermute | solution.py:405
  120.7 14.7 %collective-permute-start.17 = (bf16[64,48,128]{2,1,0:T(8,128)(2,1)S(1)}, bf16[64,48,128]{2,1,0:T(8,128)(2,1)S(1)}, u32[]{:S(2)}, u32[]{:S(2)}) collective-permute-start(bf16[64,48,128]{2,1,0:T(8,128)(2,1)S(1)} %collective-permute-done.14.refs_1_), channel_id=1, source_target_pairs={{0,1},{1,0},{2,3},{3,2},{4,5},{5,4},{6,7},{7,6},{8,9},{9,8},{10,11... | collective-permute-start | bytes 2359304 | tf_op jit(solution)/shard_map/ppermute | solution.py:405
  122.1 13.3 %collective-permute-start.23 = (bf16[64,16,128]{2,1,0:T(8,128)(2,1)S(1)}, bf16[64,16,128]{2,1,0:T(8,128)(2,1)S(1)}, u32[]{:S(2)}, u32[]{:S(2)}) collective-permute-start(bf16[64,16,128]{2,1,0:T(8,128)(2,1)S(1)} %collective-permute-done.15.refs_5_), channel_id=1, source_target_pairs={{0,1},{1,0},{2,3},{3,2},{4,5},{5,4},{6,7},{7,6},{8,9},{9,8},{10,11... | collective-permute-start | bytes 786440 | tf_op jit(solution)/shard_map/ppermute | solution.py:405
  122.5 12.9 %collective-permute-start.24 = (bf16[64,16,128]{2,1,0:T(8,128)(2,1)S(1)}, bf16[64,16,128]{2,1,0:T(8,128)(2,1)S(1)}, u32[]{:S(2)}, u32[]{:S(2)}) collective-permute-start(bf16[64,16,128]{2,1,0:T(8,128)(2,1)S(1)} %collective-permute-done.16.refs_6_), channel_id=1, source_target_pairs={{0,1},{1,0},{2,3},{3,2},{4,5},{5,4},{6,7},{7,6},{8,9},{9,8},{10,11... | collective-permute-start | bytes 786440 | tf_op jit(solution)/shard_map/ppermute | solution.py:405
  122.6 12.8 %collective-permute-start.19 = (bf16[64,48,128]{2,1,0:T(8,128)(2,1)}, bf16[64,48,128]{2,1,0:T(8,128)(2,1)S(1)}, u32[]{:S(2)}, u32[]{:S(2)}) collective-permute-start(bf16[64,48,128]{2,1,0:T(8,128)(2,1)} %collective-permute-done.18.refs_2_), channel_id=1, source_target_pairs={{0,1},{1,0},{2,3},{3,2},{4,5},{5,4},{6,7},{7,6},{8,9},{9,8},{10,11... | collective-permute-start | bytes 2359304 | tf_op jit(solution)/shard_map/ppermute | solution.py:405
  123.0 12.4 %collective-permute-start.21 = (bf16[64,48,128]{2,1,0:T(8,128)(2,1)}, bf16[64,48,128]{2,1,0:T(8,128)(2,1)S(1)}, u32[]{:S(2)}, u32[]{:S(2)}) collective-permute-start(bf16[64,48,128]{2,1,0:T(8,128)(2,1)} %collective-permute-done.20.refs_3_), channel_id=1, source_target_pairs={{0,1},{1,0},{2,3},{3,2},{4,5},{5,4},{6,7},{7,6},{8,9},{9,8},{10,11... | collective-permute-start | bytes 2359304 | tf_op jit(solution)/shard_map/ppermute | solution.py:405

commit v8 on v7

--- a/solution.py
+++ b/solution.py
@@ -29,11 +29,12 @@
 
 
 class Plan:
-    def __init__(self, zones, own, rest, line):
+    def __init__(self, zones, edges, own, rest, line):
+        self.edges = edges
         self.own = own
         self.rest = rest
         self.line = line
-        self.cut = zones * 5 // 8
+        self.cut = zones // 2
         self.first_rows = self.cut * own
         self.second_rows = HEAD + (zones - self.cut) * own
 
@@ -61,121 +62,153 @@
     return jnp.concatenate(parts, axis=0).astype(BF16)
 
 
-def gather_kernel(plan, group, pitch, line_ref, edges_ref, weight_ref, cells_ref, *refs):
-    own = plan.own
-    first_ref = refs[0]
-    second_refs = refs[1 : 1 + plan.line]
-    root_ref, total_ref, count_ref = refs[1 + plan.line : 4 + plan.line]
-    wide_refs = refs[4 + plan.line :]
-    step = pl.program_id(0)
-    last = pl.num_programs(0) - 1
-    rows, zones, lanes = cells_ref.shape
-    edges = total_ref.shape[1]
-
-    @pl.when(step == 0)
-    def _():
-        total_ref[...] = jnp.zeros_like(total_ref)
-        count_ref[...] = jnp.zeros_like(count_ref)
-
+def one_hot(edges_ref, weight_ref, edges, lanes):
+    ids = edges_ref[...]
+    rows = ids.shape[1]
     columns = lax.broadcasted_iota(jnp.int32, (edges, rows), 0)
-    ids = edges_ref[...]
     member = columns == ids[0:1, :]
     for j in range(1, ids.shape[0]):
         member = jnp.logical_or(member, columns == ids[j : j + 1, :])
     upright = jnp.transpose(jnp.broadcast_to(weight_ref[...], (lanes, edges)))
     upright = jnp.concatenate([upright] * (rows // lanes), axis=1)
     root = lax.rsqrt(jnp.sum(jnp.where(member, upright, 0.0), axis=0, keepdims=True))
-    root_ref[...] = root
     rounded = root.astype(BF16).astype(F32)
     weighted = jnp.where(member, rounded, 0.0).astype(BF16)
     hot = jnp.where(member, 1.0, 0.0).astype(BF16)
-    count_ref[...] += jnp.dot(hot, jnp.ones((rows, lanes), BF16), preferred_element_type=F32)
-
+    return root, weighted, jnp.dot(hot, jnp.ones((rows, lanes), BF16), preferred_element_type=F32)
+
+
+def accumulate(weighted, cells_ref, begin, zones, pitch, total_ref, wide_ref):
+    rows, _, lanes = cells_ref.shape
     part = 32
-    groups = zones // group
-    pairs = group // 2
-
-    def load(g, first):
-        return cells_ref[pl.ds(first, part), g * group : (g + 1) * group, :].astype(F32)
-
-    def store(g, first, piece):
-        for i in range(part):
-            wide_refs[g][pl.ds(pl.multiple_of((first + i) * pitch, 8), group), :] = piece[i]
-
-    def widen_first(i, carry):
-        store(0, i * part, load(0, i * part))
+
+    def widen(i, carry):
+        first = i * part
+        piece = cells_ref[pl.ds(first, part), begin : begin + zones, :].astype(F32)
+        for j in range(part):
+            wide_ref[pl.ds(pl.multiple_of((first + j) * pitch, 8), zones), :] = piece[j]
         return carry
 
-    lax.fori_loop(0, rows // part, widen_first, 0)
-    share = rows // part // pairs
-    for g in range(groups):
-        for pair in range(pairs):
-            left = wide_refs[g][pl.ds(2 * pair, rows, stride=pitch), :].astype(BF16)
-            right = wide_refs[g][pl.ds(2 * pair + 1, rows, stride=pitch), :].astype(BF16)
-            both = jnp.concatenate([left, right], axis=1)
-            if g + 1 < groups:
-                for i in range(share):
-                    first = (pair * share + i) * part
-                    store(g + 1, first, load(g + 1, first))
-            total_ref[g * pairs + pair] += jnp.dot(weighted, both, preferred_element_type=F32)
-
-    @pl.when(step == last)
+    lax.fori_loop(0, rows // part, widen, 0)
+    for pair in range(zones // 2):
+        left = wide_ref[pl.ds(2 * pair, rows, stride=pitch), :].astype(BF16)
+        right = wide_ref[pl.ds(2 * pair + 1, rows, stride=pitch), :].astype(BF16)
+        both = jnp.concatenate([left, right], axis=1)
+        total_ref[pair] += jnp.dot(weighted, both, preferred_element_type=F32)
+
+
+def columns_of(total_ref, at, zones, lanes):
+    data = []
+    for d in range(zones):
+        data.append(total_ref[d // 2, at, (d % 2) * lanes : (d % 2 + 1) * lanes])
+    return jnp.concatenate(data, axis=0).astype(BF16)
+
+
+def rows_for(plan, square, shift, line_ref):
+    own = plan.own
+    if plan.relative:
+        device = plan.device(square, lax.rem(line_ref[0] + shift, plan.line))
+        return pl.ds(pl.multiple_of(device * own, own), own)
+    device = plan.device(square, shift)
+    return slice(device * own, (device + 1) * own)
+
+
+def second_kernel(plan, begin, zones, pitch, line_ref, edges_ref, weight_ref, cells_ref, *refs):
+    out_refs = refs[: plan.line]
+    root_ref, weighted_ref, total_ref, count_ref, wide_ref = refs[plan.line :]
+    lanes = cells_ref.shape[2]
+
+    @pl.when(pl.program_id(0) == 0)
+    def _():
+        total_ref[...] = jnp.zeros_like(total_ref)
+        count_ref[...] = jnp.zeros_like(count_ref)
+
+    root, weighted, counts = one_hot(edges_ref, weight_ref, total_ref.shape[1], lanes)
+    root_ref[...] = root
+    weighted_ref[...] = weighted
+    count_ref[...] += counts
+    accumulate(weighted, cells_ref, begin, zones, pitch, total_ref, wide_ref)
+
+    @pl.when(pl.program_id(0) == pl.num_programs(0) - 1)
     def _():
         for square in range(8):
             for shift in range(plan.line):
-                if plan.relative:
-                    device = plan.device(square, lax.rem(line_ref[0] + shift, plan.line))
-                    at = pl.ds(pl.multiple_of(device * own, own), own)
-                else:
-                    device = plan.device(square, shift)
-                    at = slice(device * own, (device + 1) * own)
-
-                def columns_of(start, stop):
-                    data = []
-                    for d in range(start, stop):
-                        data.append(total_ref[d // 2, at, (d % 2) * lanes : (d % 2 + 1) * lanes])
-                    return jnp.concatenate(data, axis=0).astype(BF16)
-
-                first_ref[square, shift] = columns_of(0, plan.cut)
-                second_refs[shift][square, HEAD:, :] = columns_of(plan.cut, zones)
-                second_refs[shift][square, 0:HEAD, :] = head_rows(*halves_of(count_ref[at, :]))
-
-
-def partial_sums(line, cells, edges_t, edge_weight, plan):
+                at = rows_for(plan, square, shift, line_ref)
+                out_refs[shift][square, HEAD:, :] = columns_of(total_ref, at, zones, lanes)
+                out_refs[shift][square, 0:HEAD, :] = head_rows(*halves_of(count_ref[at, :]))
+
+
+def first_kernel(plan, begin, zones, pitch, line_ref, weighted_ref, cells_ref, out_ref, total_ref, wide_ref):
+    @pl.when(pl.program_id(0) == 0)
+    def _():
+        total_ref[...] = jnp.zeros_like(total_ref)
+
+    accumulate(weighted_ref[...], cells_ref, begin, zones, pitch, total_ref, wide_ref)
+
+    @pl.when(pl.program_id(0) == pl.num_programs(0) - 1)
+    def _():
+        for square in range(8):
+            for shift in range(plan.line):
+                at = rows_for(plan, square, shift, line_ref)
+                out_ref[square, shift] = columns_of(total_ref, at, zones, cells_ref.shape[2])
+
+
+def fixed(shape):
+    return pl.BlockSpec(shape, lambda i: (0,) * len(shape))
+
+
+def half_sums(kernel, plan, part, line, cells, operands, specs, outs, out_specs, counted):
     anchors, zones, lanes = cells.shape
-    edges = edge_weight.shape[0]
+    edges = plan.edges
+    half = zones // 2
     rows = min(512, anchors)
-    group = min(zones, 16)
-    pitch = group + 8
-    shapes = [(8, plan.line, plan.first_rows, lanes)] + [(8, plan.second_rows, lanes)] * plan.line
-    outs = pl.pallas_call(
-        functools.partial(gather_kernel, plan, group, pitch),
+    pitch = -(-half // 8) * 8 + 8
+    if half % 16 == 0:
+        block, begin = pl.BlockSpec((rows, half, lanes), lambda i: (i, part, 0)), 0
+    else:
+        block, begin = pl.BlockSpec((rows, zones, lanes), lambda i: (i, 0, 0)), part * half
+    counts = [pltpu.VMEM((edges, lanes), F32)] if counted else []
+    return pl.pallas_call(
+        functools.partial(kernel, plan, begin, half, pitch),
         grid=(anchors // rows,),
-        in_specs=[
-            pl.BlockSpec(memory_space=pltpu.SMEM),
-            pl.BlockSpec((edges_t.shape[0], rows), lambda i: (0, i)),
-            pl.BlockSpec((1, edges), lambda i: (0, 0)),
-            pl.BlockSpec((rows, zones, lanes), lambda i: (i, 0, 0)),
-        ],
-        out_specs=[pl.BlockSpec(shape, lambda i, zeros=(0,) * len(shape): zeros) for shape in shapes]
-        + [pl.BlockSpec((1, rows), lambda i: (0, i))],
-        out_shape=[jax.ShapeDtypeStruct(shape, BF16) for shape in shapes] + [jax.ShapeDtypeStruct((1, anchors), F32)],
-        scratch_shapes=[
-            pltpu.VMEM((zones // 2, edges, 2 * lanes), F32),
-            pltpu.VMEM((edges, lanes), F32),
-        ]
-        + [pltpu.VMEM((rows * pitch, lanes), F32)] * (zones // group),
-        compiler_params=pltpu.CompilerParams(vmem_limit_bytes=48 * 1024 * 1024),
+        in_specs=[pl.BlockSpec(memory_space=pltpu.SMEM)] + specs + [block],
+        out_specs=out_specs,
+        out_shape=outs,
+        scratch_shapes=[pltpu.VMEM((half // 2, edges, 2 * lanes), F32)] + counts + [pltpu.VMEM((rows * pitch, lanes), F32)],
+        compiler_params=pltpu.CompilerParams(vmem_limit_bytes=40 * 1024 * 1024),
         cost_estimate=pl.CostEstimate(
-            flops=2 * anchors * edges * zones * lanes, bytes_accessed=2 * anchors * zones * lanes, transcendentals=0
+            flops=4 * anchors * edges * zones * lanes, bytes_accessed=2 * anchors * zones * lanes, transcendentals=0
         ),
-    )(line[None], edges_t, edge_weight[None, :], cells)
-    first, seconds = outs[0], outs[1:-1]
+    )(line[None], *operands, cells)
+
+
+def second_sums(line, cells, edges_t, edge_weight, plan):
+    anchors, _, lanes = cells.shape
+    rows = min(512, anchors)
+    edges = plan.edges
+    shape = (8, plan.second_rows, lanes)
+    outs = [jax.ShapeDtypeStruct(shape, BF16)] * plan.line
+    outs += [jax.ShapeDtypeStruct((1, anchors), F32), jax.ShapeDtypeStruct((edges, anchors), BF16)]
+    out_specs = [fixed(shape)] * plan.line
+    out_specs += [pl.BlockSpec((1, rows), lambda i: (0, i)), pl.BlockSpec((edges, rows), lambda i: (0, i))]
+    specs = [pl.BlockSpec((edges_t.shape[0], rows), lambda i: (0, i)), fixed((1, edges))]
+    operands = (edges_t, edge_weight[None, :])
+    *seconds, roots, weighted = half_sums(second_kernel, plan, 1, line, cells, operands, specs, outs, out_specs, True)
+    if not plan.relative:
+        seconds = jnp.stack(seconds * 2)
+        seconds = [lax.dynamic_index_in_dim(seconds, line + k, 0, keepdims=False) for k in range(plan.line)]
+    return seconds, roots, weighted
+
+
+def first_sums(line, cells, weighted, plan):
+    rows = min(512, cells.shape[0])
+    shape = (8, plan.line, plan.first_rows, cells.shape[2])
+    specs = [pl.BlockSpec((plan.edges, rows), lambda i: (0, i))]
+    out = jax.ShapeDtypeStruct(shape, BF16)
+    first = half_sums(first_kernel, plan, 0, line, cells, (weighted,), specs, out, fixed(shape), False)
     if not plan.relative:
         first = lax.dynamic_slice_in_dim(jnp.concatenate([first, first], axis=1), line, plan.line, 1)
-        seconds = jnp.stack(seconds * 2)
-        seconds = [lax.dynamic_index_in_dim(seconds, line + k, 0, keepdims=False) for k in range(plan.line)]
-    return first, seconds, outs[-1]
+    return first
 
 
 def add_up(pieces):
@@ -214,15 +247,17 @@
     )(*parts)
 
 
-def org_sums(first, seconds, plan):
-    lanes = first.shape[-1]
+def org_sums(line, cells, edges_t, edge_weight, plan):
+    lanes = cells.shape[-1]
+    seconds, roots, weighted = second_sums(line, cells, edges_t, edge_weight, plan)
     seconds = [shifted(part, shift) if shift else part for shift, part in enumerate(seconds)]
+    first = first_sums(line, cells, weighted, plan)
     first = lax.all_to_all(first, SQUARE, split_axis=0, concat_axis=0, tiled=True)
     second = fold(fold_second_kernel, plan, seconds, [(8, plan.rest, plan.second_rows, lanes)])[0]
     firsts = fold(fold_first_kernel, plan, [first], [(4, plan.first_rows, lanes)] * plan.line)
     firsts = [shifted(part, shift) if shift else part for shift, part in enumerate(firsts)]
     second = lax.all_to_all(second, SQUARE, split_axis=0, concat_axis=0, tiled=True)
-    return firsts, second
+    return firsts, second, roots
 
 
 def table_kernel(plan, weight_ref, mixing_ref, matrix_ref, *refs):
@@ -450,9 +485,8 @@
     everyone = ("slow", "mid", "rest", "near", "core")
     core = lax.axis_index("core")
     edges_t = anchor_edges.T
-    plan = Plan(od_cells.shape[1], own, lax.axis_size("rest"), lax.axis_size(LINE))
-    first, seconds, roots = partial_sums(lax.axis_index(LINE), od_cells, edges_t, edge_weight, plan)
-    firsts, second = org_sums(first, seconds, plan)
+    plan = Plan(od_cells.shape[1], edge_weight.shape[0], own, lax.axis_size("rest"), lax.axis_size(LINE))
+    firsts, second, roots = org_sums(lax.axis_index(LINE), od_cells, edges_t, edge_weight, plan)
     own_weight = lax.dynamic_slice_in_dim(edge_weight, lax.axis_index(everyone) * own, own, 0)
     weight_rows = jnp.broadcast_to(own_weight[:, None], (own, mixing.shape[0]))
     matrix = relative_columns(dest_operator(dst_edges, dst_weight))

time: 146 us -> 150 us (1.027)
  waiting for transfers between devices: 62.8 us -> 65 us
    ppermute x12, waiting for transfers between devices: 57.1 us -> 59.3 us  [shifted(): lax.ppermute(x, LINE, [(i, (i + amount) % size) for i in range(size)])]
    pallas_call x1 -> x2, Pallas kernels: 15.9 us -> 17.3 us  [half_sums(): pl.pallas_call(functools.partial(kernel, plan, begin, half, pitch), grid=...]
where the time goes in v8:
time: 150 us; the launch traced here: 149 us
  waiting for transfers between devices  65 us (43%)
  starting transfers between devices  43.3 us (29%)
  Pallas kernels  38.3 us (26%)
  local copies, waits for them, and re-layouts  1.67 us (1%)
    ppermute x12, waiting for transfers between devices, shifted(): lax.ppermute(x, LINE, [(i, (i + amount) % size) for i in range(size)])  59.3 us
    pallas_call x2, Pallas kernels, spread(): pl.pallas_call(functools.partial(spread_kernel, len(longs), len(shorts)),...  19.4 us
    ppermute x12, starting transfers between devices, shifted(): lax.ppermute(x, LINE, [(i, (i + amount) % size) for i in range(size)])  19.1 us
    pallas_call x2, Pallas kernels, half_sums(): pl.pallas_call(functools.partial(kernel, plan, begin, half, pitch), grid=...  17.3 us
    ppermute x9, starting transfers between devices, swapped(): return lax.ppermute(x, 'core', [(0, 1), (1, 0)])  11.5 us
    all_to_all x1, starting transfers between devices, org_sums(): lax.all_to_all(first, SQUARE, split_axis=0, concat_axis=0, tiled=True)  5.22 us
    all_to_all x1, starting transfers between devices, org_sums(): lax.all_to_all(second, SQUARE, split_axis=0, concat_axis=0, tiled=True)  4.4 us
    ppermute x5, waiting for transfers between devices, crossed(): return lax.ppermute(x, SQUARE, pairs)  3.33 us
  transfers between devices with their start and end apart: 29, of which 11 were waited for; matrix products, arithmetic and copies ran while one was open for 1% of the time, Pallas kernels for 7%

profile of v8, /device:TPU:1, one launch (start us, length us, event | category | flops | bytes accessed | tf_op | source)
XLA Modules:
  0.0 149.4 jit_solution(10983665736900354860)
XLA Ops:
  0.0 0.8 copy-done.1
  0.8 0.7 copy-done.3
  1.4 8.8 %shard_map.73 = (bf16[8,144,128]{2,1,0:T(8,128)(2,1)S(1)}, bf16[8,144,128]{2,1,0:T(8,128)(2,1)S(1)}, bf16[8,144,128]{2,1,0:T(8,128)(2,1)S(1)}, bf16[8,144,128]{2...) custom-call(s32[1]{0:T(128)} %bitcast.2.line_ref, s32[4,2048]{1,0:T(4,128)S(1)} %bitcast.31, ...), custom_call_target="tpu_custom_call" | custom-call | flops 8589934592 | bytes 16777216 | tf_op jit(solution)/shard_map/pallas_call | solution.py:171
  10.3 8.5 %shard_map.74 = bf16[8,4,128,128]{3,2,1,0:T(8,128)(2,1)} custom-call(s32[1]{0:T(128)} %bitcast.2.line_ref, bf16[256,2048]{1,0:T(8,128)(2,1)S(1)} %get-tuple-element.23.weighted_ref, bf16[2048,32,128]{2,1,0:T(8,128)(2,1)} %cells_ref.3), custom_call_target="tpu_custom_call" | custom-call | flops 8589934592 | bytes 16777216 | tf_op jit(solution)/shard_map/pallas_call | solution.py:171
  18.8 5.2 %all-to-all-start = ((bf16[8,4,128,128]{3,2,1,0:T(8,128)(2,1)}), bf16[8,4,128,128]{3,2,1,0:T(8,128)(2,1)S(1)}, u32[]{:S(2)}, u32[]{:S(2)}) async-start(bf16[8,4,128,128]{3,2,1,0:T(8,128)(2,1)} %shard_map.74), calls=%async_computation | async-start | bytes 2097152 | tf_op jit(solution)/shard_map/all_to_all | solution.py:255
  24.0 1.3 collective-permute-start.3
  25.3 2.3 %collective-permute-start.4 = (bf16[8,144,128]{2,1,0:T(8,128)(2,1)S(1)}, bf16[8,144,128]{2,1,0:T(8,128)(2,1)S(1)}, u32[]{:S(2)}, u32[]{:S(2)}) collective-permute-start(bf16[8,144,128]{2,1,0:T(8,128)(2,1)S(1)} %get-tuple-element.30), channel_id=1, source_target_pairs={{0,16},{8,24},{16,0},{24,8},{1,17},{9,25},{17,1},{25,9},{2,18},{10... | collective-permute-start | bytes 884744 | tf_op jit(solution)/shard_map/ppermute | solution.py:424
  27.6 1.1 collective-permute-start.5
  28.7 0.1 convert_reduce_fusion
  28.9 0.1 multiply_reduce_fusion
  29.0 0.3 convolution_convert_fusion
  29.3 5.4 %collective-permute-done.3.refs_1_ = bf16[8,144,128]{2,1,0:T(8,128)(2,1)S(1)} collective-permute-done((bf16[8,144,128]{2,1,0:T(8,128)(2,1)S(1)}, bf16[8,144,128]{2,1,0:T(8,128)(2,1)S(1)}, u32[]{:S(2)}, u32[]{:S(2)}) %collective-permute-start.3) | collective-permute-done | bytes 294944 | tf_op jit(solution)/shard_map/ppermute | solution.py:424
  34.7 12.8 %collective-permute-done.4.refs_2_ = bf16[8,144,128]{2,1,0:T(8,128)(2,1)S(1)} collective-permute-done((bf16[8,144,128]{2,1,0:T(8,128)(2,1)S(1)}, bf16[8,144,128]{2,1,0:T(8,128)(2,1)S(1)}, u32[]{:S(2)}, u32[]{:S(2)}) %collective-permute-start.4) | collective-permute-done | bytes 294944 | tf_op jit(solution)/shard_map/ppermute | solution.py:424
  47.5 0.9 shard_map.76
  48.4 4.4 %all-to-all-start.1 = ((bf16[8,1,144,128]{3,2,1,0:T(8,128)(2,1)}), bf16[8,1,144,128]{3,2,1,0:T(8,128)(2,1)S(1)}, u32[]{:S(2)}, u32[]{:S(2)}) async-start(bf16[8,1,144,128]{3,2,1,0:T(8,128)(2,1)} %shard_map.76), calls=%async_computation.1 | async-start | bytes 589824 | tf_op jit(solution)/shard_map/all_to_all | solution.py:259
  52.9 0.1 shard_map.75
  53.0 6.6 %collective-permute-start = (bf16[4,128,128]{2,1,0:T(8,128)(2,1)S(1)}, bf16[4,128,128]{2,1,0:T(8,128)(2,1)S(1)}, u32[]{:S(2)}, u32[]{:S(2)}) collective-permute-start(bf16[4,128,128]{2,1,0:T(8,128)(2,1)S(1)} %get-tuple-element.25), channel_id=1, source_target_pairs={{0,8},{8,16},{16,24},{24,0},{1,9},{9,17},{17,25},{25,1},{2,10},{10... | collective-permute-start | bytes 393224 | tf_op jit(solution)/shard_map/ppermute | solution.py:424
  59.6 1.3 collective-permute-start.1
  60.9 0.8 collective-permute-start.2
  61.8 2.7 %collective-permute-done.refs_1_ = bf16[4,128,128]{2,1,0:T(8,128)(2,1)S(1)} collective-permute-done((bf16[4,128,128]{2,1,0:T(8,128)(2,1)S(1)}, bf16[4,128,128]{2,1,0:T(8,128)(2,1)S(1)}, u32[]{:S(2)}, u32[]{:S(2)}) %collective-permute-start) | collective-permute-done | bytes 131104 | tf_op jit(solution)/shard_map/ppermute | solution.py:424
  64.4 5.8 %collective-permute-done.1.refs_2_ = bf16[4,128,128]{2,1,0:T(8,128)(2,1)S(1)} collective-permute-done((bf16[4,128,128]{2,1,0:T(8,128)(2,1)S(1)}, bf16[4,128,128]{2,1,0:T(8,128)(2,1)S(1)}, u32[]{:S(2)}, u32[]{:S(2)}) %collective-permute-start.1) | collective-permute-done | bytes 131104 | tf_op jit(solution)/shard_map/ppermute | solution.py:424
  70.3 0.5 shard_map.77
  70.8 0.6 collective-permute-start.6
  71.4 1.0 collective-permute-done.6
  72.5 2.4 %collective-permute-start.9 = (bf16[16,16,128]{2,1,0:T(8,128)(2,1)S(1)}, bf16[16,16,128]{2,1,0:T(8,128)(2,1)S(1)}, u32[]{:S(2)}, u32[]{:S(2)}) collective-permute-start(bf16[16,16,128]{2,1,0:T(8,128)(2,1)S(1)} %slice.18), channel_id=1, source_target_pairs={{0,6},{1,7},{2,4},{3,5},{4,2},{5,3},{6,0},{7,1},{8,14},{9,15},{10,... | collective-permute-start | bytes 196616 | tf_op jit(solution)/shard_map/ppermute | solution.py:436
  74.8 3.8 %collective-permute-start.12 = (bf16[16,48,128]{2,1,0:T(8,128)(2,1)S(1)}, bf16[16,48,128]{2,1,0:T(8,128)(2,1)S(1)}, u32[]{:S(2)}, u32[]{:S(2)}) collective-permute-start(bf16[16,48,128]{2,1,0:T(8,128)(2,1)S(1)} %slice.19), channel_id=1, source_target_pairs={{0,24},{8,0},{16,8},{24,16},{1,25},{9,1},{17,9},{25,17},{2,26},{10... | collective-permute-start | bytes 589832 | tf_op jit(solution)/shard_map/ppermute | solution.py:424
  78.7 0.4 collective-permute-start.11
  79.1 0.3 collective-permute-start.8
  79.4 0.1 collective-permute-start.7
  79.5 3.0 %collective-permute-done.8 = bf16[16,16,128]{2,1,0:T(8,128)(2,1)S(1)} collective-permute-done((bf16[16,16,128]{2,1,0:T(8,128)(2,1)S(1)}, bf16[16,16,128]{2,1,0:T(8,128)(2,1)S(1)}, u32[]{:S(2)}, u32[]{:S(2)}) %collective-permute-start.8) | collective-permute-done | bytes 65568 | tf_op jit(solution)/shard_map/ppermute | solution.py:432
  82.5 0.3 collective-permute-done.7
  82.8 13.2 %collective-permute-done.11 = bf16[16,48,128]{2,1,0:T(8,128)(2,1)S(1)} collective-permute-done((bf16[16,48,128]{2,1,0:T(8,128)(2,1)S(1)}, bf16[16,48,128]{2,1,0:T(8,128)(2,1)S(1)}, u32[]{:S(2)}, u32[]{:S(2)}) %collective-permute-start.11) | collective-permute-done | bytes 196640 | tf_op jit(solution)/shard_map/ppermute | solution.py:424
  96.1 0.1 pad_maximum_fusion.refs_0_
  96.2 0.4 collective-permute-start.14
  96.5 1.4 collective-permute-start.16
  97.9 0.1 collective-permute-start.18
  98.0 2.2 %collective-permute-start.13 = (bf16[64,48,128]{2,1,0:T(8,128)(2,1)S(1)}, bf16[64,48,128]{2,1,0:T(8,128)(2,1)S(1)}, u32[]{:S(2)}, u32[]{:S(2)}) collective-permute-start(bf16[64,48,128]{2,1,0:T(8,128)(2,1)S(1)} %pad_maximum_fusion.refs_0_), channel_id=1, source_target_pairs={{0,1},{1,0},{2,3},{3,2},{4,5},{5,4},{6,7},{7,6},{8,9},{9,8},{10,11... | collective-permute-start | bytes 2359304 | tf_op jit(solution)/shard_map/ppermute | solution.py:440
  100.1 15.9 %collective-permute-done.16.refs_6_ = bf16[64,16,128]{2,1,0:T(8,128)(2,1)S(1)} collective-permute-done((bf16[64,16,128]{2,1,0:T(8,128)(2,1)S(1)}, bf16[64,16,128]{2,1,0:T(8,128)(2,1)S(1)}, u32[]{:S(2)}, u32[]{:S(2)}) %collective-permute-start.16) | collective-permute-done | bytes 262176 | tf_op jit(solution)/shard_map/ppermute | solution.py:424
  116.2 2.1 %collective-permute-start.22 = (bf16[64,16,128]{2,1,0:T(8,128)(2,1)S(1)}, bf16[64,16,128]{2,1,0:T(8,128)(2,1)}, u32[]{:S(2)}, u32[]{:S(2)}) collective-permute-start(bf16[64,16,128]{2,1,0:T(8,128)(2,1)S(1)} %pad_maximum_fusion.1.refs_4_), channel_id=1, source_target_pairs={{0,1},{1,0},{2,3},{3,2},{4,5},{5,4},{6,7},{7,6},{8,9},{9,8},{10,11... | collective-permute-start | bytes 786440 | tf_op jit(solution)/shard_map/ppermute | solution.py:440
  118.4 3.6 %collective-permute-done.25.refs_7_ = bf16[64,16,128]{2,1,0:T(8,128)(2,1)} collective-permute-done((bf16[64,16,128]{2,1,0:T(8,128)(2,1)S(1)}, bf16[64,16,128]{2,1,0:T(8,128)(2,1)}, u32[]{:S(2)}, u32[]{:S(2)}) %collective-permute-start.25) | collective-permute-done | bytes 262176 | tf_op jit(solution)/shard_map/ppermute | solution.py:424
  121.9 3.0 %collective-permute-start.26 = (bf16[64,16,128]{2,1,0:T(8,128)(2,1)}, bf16[64,16,128]{2,1,0:T(8,128)(2,1)}, u32[]{:S(2)}, u32[]{:S(2)}) collective-permute-start(bf16[64,16,128]{2,1,0:T(8,128)(2,1)} %collective-permute-done.25.refs_7_), channel_id=1, source_target_pairs={{0,1},{1,0},{2,3},{3,2},{4,5},{5,4},{6,7},{7,6},{8,9},{9,8},{10,11... | collective-permute-start | bytes 786440 | tf_op jit(solution)/shard_map/ppermute | solution.py:440
  125.1 1.3 collective-permute-done.26.refs_7_
  126.4 0.4 collective-permute-start.23
  126.8 0.1 collective-permute-start.24
  127.0 0.4 collective-permute-start.19
  127.3 2.6 %collective-permute-start.21 = (bf16[64,48,128]{2,1,0:T(8,128)(2,1)}, bf16[64,48,128]{2,1,0:T(8,128)(2,1)S(1)}, u32[]{:S(2)}, u32[]{:S(2)}) collective-permute-start(bf16[64,48,128]{2,1,0:T(8,128)(2,1)} %collective-permute-done.20.refs_3_), channel_id=1, source_target_pairs={{0,1},{1,0},{2,3},{3,2},{4,5},{5,4},{6,7},{7,6},{8,9},{9,8},{10,11... | collective-permute-start | bytes 2359304 | tf_op jit(solution)/shard_map/ppermute | solution.py:440
  129.9 9.8 %shard_map.78.refs_8_ = bf16[512,128,128]{2,1,0:T(8,128)(2,1)} custom-call(s32[1]{0:T(128)} %bitcast.6.half_ref, s32[4,512]{1,0:T(4,128)S(1)} %get-tuple-element.41.places_ref, f32[1,512]{1,0:T(1,128)S(1)} %constant_dynamic-slice_fusion.root_ref, f32[1,128]{1,0:T(1,128)S(1)} %bitcast.33, bf16[64,48,128]{2,1,0:T(8,128)(2,1)S(1)} %pad_maximum_fusion.refs_0_, ...), custom_call_target="tpu_custom_call" | custom-call | flops 17179869184 | bytes 16777216 | tf_op jit(solution)/shard_map/pallas_call | solution.py:399
  139.8 9.7 %shard_map.79 = bf16[512,128,128]{2,1,0:T(8,128)(2,1)} custom-call(s32[1]{0:T(128)} %bitcast.half_ref, s32[4,512]{1,0:T(4,128)S(1)} %add_add_fusion.1.places_ref, f32[1,512]{1,0:T(1,128)S(1)} %constant_dynamic-slice_fusion.root_ref, f32[1,128]{1,0:T(1,128)S(1)} %bitcast.34, ...), custom_call_target="tpu_custom_call", output_to_operand_aliasing={{}: (12, {})} | custom-call | flops 17179869184 | bytes 16777216 | tf_op jit(solution)/shard_map/pallas_call | solution.py:399
  (49 shorter events, 0.6 us)
Async XLA Ops:
  0.0 0.8 copy-start.1
  0.8 0.7 copy-start.3
  10.2 18.5 %copy-start.5 = (s32[128,3]{0,1:T(4,128)S(1)}, s32[128,3]{0,1:T(4,128)}, u32[]{:S(2)}) copy-start(s32[128,3]{0,1:T(4,128)} %param.11) | copy-start | bytes 4612
  10.2 18.6 %copy-start.6 = (f32[128]{0:T(128)S(1)}, f32[128]{0:T(128)}, u32[]{:S(2)}) copy-start(f32[128]{0:T(128)} %param.12) | copy-start | bytes 1540
  10.3 60.0 %copy-start = (bf16[128,128]{1,0:T(8,128)(2,1)S(1)}, bf16[128,128]{1,0:T(8,128)(2,1)}, u32[]{:S(2)}) copy-start(bf16[128,128]{1,0:T(8,128)(2,1)} %mixing_ref.1) | copy-start | bytes 98308
  10.3 105.8 %copy-start.2 = (s32[2048,4]{0,1:T(4,128)S(1)}, s32[2048,4]{0,1:T(4,128)}, u32[]{:S(2)}) copy-start(s32[2048,4]{0,1:T(4,128)} %param.8) | copy-start | bytes 98308
  10.3 119.6 %copy-start.4 = (f32[128]{0:T(128)S(1)}, f32[128]{0:T(128)}, u32[]{:S(2)}) copy-start(f32[128]{0:T(128)} %param.13) | copy-start | bytes 1540
  18.8 29.6 %all-to-all-start = ((bf16[8,4,128,128]{3,2,1,0:T(8,128)(2,1)}), bf16[8,4,128,128]{3,2,1,0:T(8,128)(2,1)S(1)}, u32[]{:S(2)}, u32[]{:S(2)}) async-start(bf16[8,4,128,128]{3,2,1,0:T(8,128)(2,1)} %shard_map.74), calls=%async_computation | async-start | bytes 2097152 | tf_op jit(solution)/shard_map/all_to_all | solution.py:255
  24.0 10.7 %collective-permute-start.3 = (bf16[8,144,128]{2,1,0:T(8,128)(2,1)S(1)}, bf16[8,144,128]{2,1,0:T(8,128)(2,1)S(1)}, u32[]{:S(2)}, u32[]{:S(2)}) collective-permute-start(bf16[8,144,128]{2,1,0:T(8,128)(2,1)S(1)} %get-tuple-element.29), channel_id=1, source_target_pairs={{0,8},{8,16},{16,24},{24,0},{1,9},{9,17},{17,25},{25,1},{2,10},{10... | collective-permute-start | bytes 884744 | tf_op jit(solution)/shard_map/ppermute | solution.py:424
  25.3 22.2 %collective-permute-start.4 = (bf16[8,144,128]{2,1,0:T(8,128)(2,1)S(1)}, bf16[8,144,128]{2,1,0:T(8,128)(2,1)S(1)}, u32[]{:S(2)}, u32[]{:S(2)}) collective-permute-start(bf16[8,144,128]{2,1,0:T(8,128)(2,1)S(1)} %get-tuple-element.30), channel_id=1, source_target_pairs={{0,16},{8,24},{16,0},{24,8},{1,17},{9,25},{17,1},{25,9},{2,18},{10... | collective-permute-start | bytes 884744 | tf_op jit(solution)/shard_map/ppermute | solution.py:424
  27.6 19.9 %collective-permute-start.5 = (bf16[8,144,128]{2,1,0:T(8,128)(2,1)S(1)}, bf16[8,144,128]{2,1,0:T(8,128)(2,1)S(1)}, u32[]{:S(2)}, u32[]{:S(2)}) collective-permute-start(bf16[8,144,128]{2,1,0:T(8,128)(2,1)S(1)} %get-tuple-element.31), channel_id=1, source_target_pairs={{0,24},{8,0},{16,8},{24,16},{1,25},{9,1},{17,9},{25,17},{2,26},{10... | collective-permute-start | bytes 884744 | tf_op jit(solution)/shard_map/ppermute | solution.py:424
  48.4 13.3 %all-to-all-start.1 = ((bf16[8,1,144,128]{3,2,1,0:T(8,128)(2,1)}), bf16[8,1,144,128]{3,2,1,0:T(8,128)(2,1)S(1)}, u32[]{:S(2)}, u32[]{:S(2)}) async-start(bf16[8,1,144,128]{3,2,1,0:T(8,128)(2,1)} %shard_map.76), calls=%async_computation.1 | async-start | bytes 589824 | tf_op jit(solution)/shard_map/all_to_all | solution.py:259
  53.0 11.4 %collective-permute-start = (bf16[4,128,128]{2,1,0:T(8,128)(2,1)S(1)}, bf16[4,128,128]{2,1,0:T(8,128)(2,1)S(1)}, u32[]{:S(2)}, u32[]{:S(2)}) collective-permute-start(bf16[4,128,128]{2,1,0:T(8,128)(2,1)S(1)} %get-tuple-element.25), channel_id=1, source_target_pairs={{0,8},{8,16},{16,24},{24,0},{1,9},{9,17},{17,25},{25,1},{2,10},{10... | collective-permute-start | bytes 393224 | tf_op jit(solution)/shard_map/ppermute | solution.py:424
  59.6 10.6 %collective-permute-start.1 = (bf16[4,128,128]{2,1,0:T(8,128)(2,1)S(1)}, bf16[4,128,128]{2,1,0:T(8,128)(2,1)S(1)}, u32[]{:S(2)}, u32[]{:S(2)}) collective-permute-start(bf16[4,128,128]{2,1,0:T(8,128)(2,1)S(1)} %get-tuple-element.26), channel_id=1, source_target_pairs={{0,16},{8,24},{16,0},{24,8},{1,17},{9,25},{17,1},{25,9},{2,18},{10... | collective-permute-start | bytes 393224 | tf_op jit(solution)/shard_map/ppermute | solution.py:424
  60.9 9.3 %collective-permute-start.2 = (bf16[4,128,128]{2,1,0:T(8,128)(2,1)S(1)}, bf16[4,128,128]{2,1,0:T(8,128)(2,1)S(1)}, u32[]{:S(2)}, u32[]{:S(2)}) collective-permute-start(bf16[4,128,128]{2,1,0:T(8,128)(2,1)S(1)} %get-tuple-element.27), channel_id=1, source_target_pairs={{0,24},{8,0},{16,8},{24,16},{1,25},{9,1},{17,9},{25,17},{2,26},{10... | collective-permute-start | bytes 393224 | tf_op jit(solution)/shard_map/ppermute | solution.py:424
  70.8 1.6 %collective-permute-start.6 = (bf16[8,64,128]{2,1,0:T(8,128)(2,1)S(1)}, bf16[8,64,128]{2,1,0:T(8,128)(2,1)S(1)}, u32[]{:S(2)}, u32[]{:S(2)}) collective-permute-start(bf16[8,64,128]{2,1,0:T(8,128)(2,1)S(1)} %get-tuple-element.33), channel_id=1, source_target_pairs={{0,1},{1,0},{2,3},{3,2},{4,5},{5,4},{6,7},{7,6},{8,9},{9,8},{10,11... | collective-permute-start | bytes 393224 | tf_op jit(solution)/shard_map/ppermute | solution.py:440
  72.5 6.9 %collective-permute-start.9 = (bf16[16,16,128]{2,1,0:T(8,128)(2,1)S(1)}, bf16[16,16,128]{2,1,0:T(8,128)(2,1)S(1)}, u32[]{:S(2)}, u32[]{:S(2)}) collective-permute-start(bf16[16,16,128]{2,1,0:T(8,128)(2,1)S(1)} %slice.18), channel_id=1, source_target_pairs={{0,6},{1,7},{2,4},{3,5},{4,2},{5,3},{6,0},{7,1},{8,14},{9,15},{10,... | collective-permute-start | bytes 196616 | tf_op jit(solution)/shard_map/ppermute | solution.py:436
  74.8 8.0 %collective-permute-start.12 = (bf16[16,48,128]{2,1,0:T(8,128)(2,1)S(1)}, bf16[16,48,128]{2,1,0:T(8,128)(2,1)S(1)}, u32[]{:S(2)}, u32[]{:S(2)}) collective-permute-start(bf16[16,48,128]{2,1,0:T(8,128)(2,1)S(1)} %slice.19), channel_id=1, source_target_pairs={{0,24},{8,0},{16,8},{24,16},{1,25},{9,1},{17,9},{25,17},{2,26},{10... | collective-permute-start | bytes 589832 | tf_op jit(solution)/shard_map/ppermute | solution.py:424
  78.7 17.4 %collective-permute-start.11 = (bf16[16,48,128]{2,1,0:T(8,128)(2,1)S(1)}, bf16[16,48,128]{2,1,0:T(8,128)(2,1)S(1)}, u32[]{:S(2)}, u32[]{:S(2)}) collective-permute-start(bf16[16,48,128]{2,1,0:T(8,128)(2,1)S(1)} %slice.19), channel_id=1, source_target_pairs={{0,16},{8,24},{16,0},{24,8},{1,17},{9,25},{17,1},{25,9},{2,18},{10... | collective-permute-start | bytes 589832 | tf_op jit(solution)/shard_map/ppermute | solution.py:424
  79.1 17.0 %collective-permute-start.10 = (bf16[16,48,128]{2,1,0:T(8,128)(2,1)S(1)}, bf16[16,48,128]{2,1,0:T(8,128)(2,1)S(1)}, u32[]{:S(2)}, u32[]{:S(2)}) collective-permute-start(bf16[16,48,128]{2,1,0:T(8,128)(2,1)S(1)} %slice.19), channel_id=1, source_target_pairs={{0,8},{8,16},{16,24},{24,0},{1,9},{9,17},{17,25},{25,1},{2,10},{10... | collective-permute-start | bytes 589832 | tf_op jit(solution)/shard_map/ppermute | solution.py:424
  79.1 3.4 %collective-permute-start.8 = (bf16[16,16,128]{2,1,0:T(8,128)(2,1)S(1)}, bf16[16,16,128]{2,1,0:T(8,128)(2,1)S(1)}, u32[]{:S(2)}, u32[]{:S(2)}) collective-permute-start(bf16[16,16,128]{2,1,0:T(8,128)(2,1)S(1)} %slice.18), channel_id=1, source_target_pairs={{0,4},{1,3},{2,6},{3,1},{4,0},{5,7},{6,2},{7,5},{8,12},{9,11},{10,... | collective-permute-start | bytes 196616 | tf_op jit(solution)/shard_map/ppermute | solution.py:432
  79.4 3.4 %collective-permute-start.7 = (bf16[16,16,128]{2,1,0:T(8,128)(2,1)S(1)}, bf16[16,16,128]{2,1,0:T(8,128)(2,1)S(1)}, u32[]{:S(2)}, u32[]{:S(2)}) collective-permute-start(bf16[16,16,128]{2,1,0:T(8,128)(2,1)S(1)} %slice.18), channel_id=1, source_target_pairs={{0,2},{1,5},{2,0},{3,7},{4,6},{5,1},{6,4},{7,3},{8,10},{9,13},{10,... | collective-permute-start | bytes 196616 | tf_op jit(solution)/shard_map/ppermute | solution.py:432
  96.2 19.9 %collective-permute-start.14 = (bf16[64,48,128]{2,1,0:T(8,128)(2,1)S(1)}, bf16[64,48,128]{2,1,0:T(8,128)(2,1)S(1)}, u32[]{:S(2)}, u32[]{:S(2)}) collective-permute-start(bf16[64,48,128]{2,1,0:T(8,128)(2,1)S(1)} %pad_maximum_fusion.refs_0_), channel_id=1, source_target_pairs={{0,2},{1,5},{2,0},{3,7},{4,6},{5,1},{6,4},{7,3},{8,10},{9,13},{10,... | collective-permute-start | bytes 2359304 | tf_op jit(solution)/shard_map/ppermute | solution.py:432
  96.5 19.5 %collective-permute-start.16 = (bf16[64,16,128]{2,1,0:T(8,128)(2,1)S(1)}, bf16[64,16,128]{2,1,0:T(8,128)(2,1)S(1)}, u32[]{:S(2)}, u32[]{:S(2)}) collective-permute-start(bf16[64,16,128]{2,1,0:T(8,128)(2,1)S(1)} %pad_maximum_fusion.1.refs_4_), channel_id=1, source_target_pairs={{0,16},{8,24},{16,0},{24,8},{1,17},{9,25},{17,1},{25,9},{2,18},{10... | collective-permute-start | bytes 786440 | tf_op jit(solution)/shard_map/ppermute | solution.py:424
  97.9 18.2 %collective-permute-start.15 = (bf16[64,16,128]{2,1,0:T(8,128)(2,1)S(1)}, bf16[64,16,128]{2,1,0:T(8,128)(2,1)S(1)}, u32[]{:S(2)}, u32[]{:S(2)}) collective-permute-start(bf16[64,16,128]{2,1,0:T(8,128)(2,1)S(1)} %pad_maximum_fusion.1.refs_4_), channel_id=1, source_target_pairs={{0,8},{8,16},{16,24},{24,0},{1,9},{9,17},{17,25},{25,1},{2,10},{10... | collective-permute-start | bytes 786440 | tf_op jit(solution)/shard_map/ppermute | solution.py:424
  97.9 28.9 %collective-permute-start.18 = (bf16[64,48,128]{2,1,0:T(8,128)(2,1)S(1)}, bf16[64,48,128]{2,1,0:T(8,128)(2,1)}, u32[]{:S(2)}, u32[]{:S(2)}) collective-permute-start(bf16[64,48,128]{2,1,0:T(8,128)(2,1)S(1)} %pad_maximum_fusion.refs_0_), channel_id=1, source_target_pairs={{0,4},{1,3},{2,6},{3,1},{4,0},{5,7},{6,2},{7,5},{8,12},{9,11},{10,... | collective-permute-start | bytes 2359304 | tf_op jit(solution)/shard_map/ppermute | solution.py:432
  98.0 29.0 %collective-permute-start.13 = (bf16[64,48,128]{2,1,0:T(8,128)(2,1)S(1)}, bf16[64,48,128]{2,1,0:T(8,128)(2,1)S(1)}, u32[]{:S(2)}, u32[]{:S(2)}) collective-permute-start(bf16[64,48,128]{2,1,0:T(8,128)(2,1)S(1)} %pad_maximum_fusion.refs_0_), channel_id=1, source_target_pairs={{0,1},{1,0},{2,3},{3,2},{4,5},{5,4},{6,7},{7,6},{8,9},{9,8},{10,11... | collective-permute-start | bytes 2359304 | tf_op jit(solution)/shard_map/ppermute | solution.py:440
  116.0 11.3 %collective-permute-start.20 = (bf16[64,48,128]{2,1,0:T(8,128)(2,1)S(1)}, bf16[64,48,128]{2,1,0:T(8,128)(2,1)}, u32[]{:S(2)}, u32[]{:S(2)}) collective-permute-start(bf16[64,48,128]{2,1,0:T(8,128)(2,1)S(1)} %collective-permute-done.14.refs_1_), channel_id=1, source_target_pairs={{0,4},{1,3},{2,6},{3,1},{4,0},{5,7},{6,2},{7,5},{8,12},{9,11},{10,... | collective-permute-start | bytes 2359304 | tf_op jit(solution)/shard_map/ppermute | solution.py:432
  116.0 5.9 %collective-permute-start.25 = (bf16[64,16,128]{2,1,0:T(8,128)(2,1)S(1)}, bf16[64,16,128]{2,1,0:T(8,128)(2,1)}, u32[]{:S(2)}, u32[]{:S(2)}) collective-permute-start(bf16[64,16,128]{2,1,0:T(8,128)(2,1)S(1)} %pad_maximum_fusion.1.refs_4_), channel_id=1, source_target_pairs={{0,24},{8,0},{16,8},{24,16},{1,25},{9,1},{17,9},{25,17},{2,26},{10... | collective-permute-start | bytes 786440 | tf_op jit(solution)/shard_map/ppermute | solution.py:424
  116.2 8.8 %collective-permute-start.22 = (bf16[64,16,128]{2,1,0:T(8,128)(2,1)S(1)}, bf16[64,16,128]{2,1,0:T(8,128)(2,1)}, u32[]{:S(2)}, u32[]{:S(2)}) collective-permute-start(bf16[64,16,128]{2,1,0:T(8,128)(2,1)S(1)} %pad_maximum_fusion.1.refs_4_), channel_id=1, source_target_pairs={{0,1},{1,0},{2,3},{3,2},{4,5},{5,4},{6,7},{7,6},{8,9},{9,8},{10,11... | collective-permute-start | bytes 786440 | tf_op jit(solution)/shard_map/ppermute | solution.py:440
  121.9 4.5 %collective-permute-start.26 = (bf16[64,16,128]{2,1,0:T(8,128)(2,1)}, bf16[64,16,128]{2,1,0:T(8,128)(2,1)}, u32[]{:S(2)}, u32[]{:S(2)}) collective-permute-start(bf16[64,16,128]{2,1,0:T(8,128)(2,1)} %collective-permute-done.25.refs_7_), channel_id=1, source_target_pairs={{0,1},{1,0},{2,3},{3,2},{4,5},{5,4},{6,7},{7,6},{8,9},{9,8},{10,11... | collective-permute-start | bytes 786440 | tf_op jit(solution)/shard_map/ppermute | solution.py:440
  125.0 14.7 %collective-permute-start.17 = (bf16[64,48,128]{2,1,0:T(8,128)(2,1)S(1)}, bf16[64,48,128]{2,1,0:T(8,128)(2,1)S(1)}, u32[]{:S(2)}, u32[]{:S(2)}) collective-permute-start(bf16[64,48,128]{2,1,0:T(8,128)(2,1)S(1)} %collective-permute-done.14.refs_1_), channel_id=1, source_target_pairs={{0,1},{1,0},{2,3},{3,2},{4,5},{5,4},{6,7},{7,6},{8,9},{9,8},{10,11... | collective-permute-start | bytes 2359304 | tf_op jit(solution)/shard_map/ppermute | solution.py:440
  126.4 13.3 %collective-permute-start.23 = (bf16[64,16,128]{2,1,0:T(8,128)(2,1)S(1)}, bf16[64,16,128]{2,1,0:T(8,128)(2,1)S(1)}, u32[]{:S(2)}, u32[]{:S(2)}) collective-permute-start(bf16[64,16,128]{2,1,0:T(8,128)(2,1)S(1)} %collective-permute-done.15.refs_5_), channel_id=1, source_target_pairs={{0,1},{1,0},{2,3},{3,2},{4,5},{5,4},{6,7},{7,6},{8,9},{9,8},{10,11... | collective-permute-start | bytes 786440 | tf_op jit(solution)/shard_map/ppermute | solution.py:440
  126.8 12.9 %collective-permute-start.24 = (bf16[64,16,128]{2,1,0:T(8,128)(2,1)S(1)}, bf16[64,16,128]{2,1,0:T(8,128)(2,1)S(1)}, u32[]{:S(2)}, u32[]{:S(2)}) collective-permute-start(bf16[64,16,128]{2,1,0:T(8,128)(2,1)S(1)} %collective-permute-done.16.refs_6_), channel_id=1, source_target_pairs={{0,1},{1,0},{2,3},{3,2},{4,5},{5,4},{6,7},{7,6},{8,9},{9,8},{10,11... | collective-permute-start | bytes 786440 | tf_op jit(solution)/shard_map/ppermute | solution.py:440
  127.0 12.8 %collective-permute-start.19 = (bf16[64,48,128]{2,1,0:T(8,128)(2,1)}, bf16[64,48,128]{2,1,0:T(8,128)(2,1)S(1)}, u32[]{:S(2)}, u32[]{:S(2)}) collective-permute-start(bf16[64,48,128]{2,1,0:T(8,128)(2,1)} %collective-permute-done.18.refs_2_), channel_id=1, source_target_pairs={{0,1},{1,0},{2,3},{3,2},{4,5},{5,4},{6,7},{7,6},{8,9},{9,8},{10,11... | collective-permute-start | bytes 2359304 | tf_op jit(solution)/shard_map/ppermute | solution.py:440
  127.3 12.4 %collective-permute-start.21 = (bf16[64,48,128]{2,1,0:T(8,128)(2,1)}, bf16[64,48,128]{2,1,0:T(8,128)(2,1)S(1)}, u32[]{:S(2)}, u32[]{:S(2)}) collective-permute-start(bf16[64,48,128]{2,1,0:T(8,128)(2,1)} %collective-permute-done.20.refs_3_), channel_id=1, source_target_pairs={{0,1},{1,0},{2,3},{3,2},{4,5},{5,4},{6,7},{7,6},{8,9},{9,8},{10,11... | collective-permute-start | bytes 2359304 | tf_op jit(solution)/shard_map/ppermute | solution.py:440

commit v9 on v8

--- a/solution.py
+++ b/solution.py
@@ -252,6 +252,7 @@
     seconds, roots, weighted = second_sums(line, cells, edges_t, edge_weight, plan)
     seconds = [shifted(part, shift) if shift else part for shift, part in enumerate(seconds)]
     first = first_sums(line, cells, weighted, plan)
+    first, *seconds[1::2] = lax.optimization_barrier((first, *seconds[1::2]))
     first = lax.all_to_all(first, SQUARE, split_axis=0, concat_axis=0, tiled=True)
     second = fold(fold_second_kernel, plan, seconds, [(8, plan.rest, plan.second_rows, lanes)])[0]
     firsts = fold(fold_first_kernel, plan, [first], [(4, plan.first_rows, lanes)] * plan.line)
@@ -312,27 +313,16 @@
     )(weight_rows, mixing, matrix, *firsts, second)
 
 
-def spread_kernel(n_long, n_short, half_ref, places_ref, root_ref, bias_ref, *refs):
-    longs = refs[:n_long]
-    shorts = refs[n_long : n_long + n_short]
+def spread_kernel(n_pieces, stride, offset, half_ref, places_ref, root_ref, bias_ref, *refs):
     out_ref, table_ref, ring_ref, sems, ring_sems = refs[-5:]
     slots, rows, zones, lanes = ring_ref.shape
     steps = out_ref.shape[0] // rows
-    half = half_ref[0]
+    first_zone = pl.multiple_of(half_ref[0] * stride + offset, 16)
 
     copies = []
-
-    def bring(source, first, start):
-        place = table_ref.at[pl.ds(first, source.shape[0]), pl.ds(start, source.shape[1]), :]
-        copies.append(pltpu.make_async_copy(source, place, sems.at[len(copies)]))
-
-    split = longs[0].shape[1]
-    size = shorts[0].shape[0] // n_long
-    for square, source in enumerate(longs):
-        bring(source, square * n_short * size, 0)
-    for shift, source in enumerate(shorts):
-        for square in range(n_long):
-            bring(source.at[pl.ds(square * size, size)], (square * n_short + shift) * size, split)
+    for i, source in enumerate(refs[:n_pieces]):
+        size = source.shape[0]
+        copies.append(pltpu.make_async_copy(source, table_ref.at[pl.ds(i * size, size)], sems.at[i]))
     for copy in copies:
         copy.start()
     for copy in copies:
@@ -341,11 +331,11 @@
     bias = bias_ref[...]
     count = places_ref.shape[0]
     tile = 16
-    batch = min(8, rows)
+    batch = min(8 if zones > tile else 16, rows)
     tiles = zones // tile
 
     def leaving(step, slot):
-        place = out_ref.at[pl.ds(step * rows, rows), pl.ds(pl.multiple_of(half * zones, zones), zones), :]
+        place = out_ref.at[pl.ds(step * rows, rows), pl.ds(first_zone, zones), :]
         return pltpu.make_async_copy(ring_ref.at[slot], place, ring_sems.at[slot])
 
     def one_step(step, carry):
@@ -380,15 +370,14 @@
         leaving(step, step % slots).wait()
 
 
-def spread(half, places, root, bias, longs, shorts, before=None):
+def spread(half, places, root, bias, pieces, offset, stride, before=None):
     anchors = places.shape[1]
     lanes = bias.shape[1]
-    zones = longs[0].shape[1] + shorts[0].shape[1]
+    zones = pieces[0].shape[1]
     rows = min(16, anchors // 8)
     slots = min(8, anchors // rows)
     smem = pl.BlockSpec(memory_space=pltpu.SMEM)
     anywhere = pl.BlockSpec(memory_space=pltpu.HBM)
-    pieces = longs + shorts
     operands = [half, places, root, bias] + pieces
     specs = [smem, smem, smem, pl.BlockSpec(memory_space=pltpu.VMEM)] + [anywhere] * len(pieces)
     aliases = {}
@@ -397,14 +386,14 @@
         operands.append(before)
         specs.append(anywhere)
     return pl.pallas_call(
-        functools.partial(spread_kernel, len(longs), len(shorts)),
+        functools.partial(spread_kernel, len(pieces), stride, offset),
         in_specs=specs,
         out_specs=anywhere,
-        out_shape=jax.ShapeDtypeStruct((anchors, 2 * zones, lanes), BF16),
+        out_shape=jax.ShapeDtypeStruct((anchors, 2 * stride, lanes), BF16),
         scratch_shapes=[
-            pltpu.VMEM((len(longs) * longs[0].shape[0], zones, lanes), BF16),
+            pltpu.VMEM((len(pieces) * pieces[0].shape[0], zones, lanes), BF16),
             pltpu.VMEM((slots, rows, zones, lanes), BF16),
-            pltpu.SemaphoreType.DMA((len(longs) * (1 + len(shorts)),)),
+            pltpu.SemaphoreType.DMA((len(pieces),)),
             pltpu.SemaphoreType.DMA((slots,)),
         ],
         input_output_aliases=aliases,
@@ -466,7 +455,7 @@
     line = owner // (8 * rest) * rest + owner // 4 % rest
     line = lax.rem(lax.axis_index(LINE) - line + size, size)
     square = jnp.where(core == 0, 2 * mid + near, 2 * near + mid)
-    return (square * size + line) * (2 * own) + slot
+    return (square * size + line) * (2 * own) + slot, (line * 4 + square) * (2 * own) + slot
 
 
 def relative_columns(matrix):
@@ -500,9 +489,16 @@
     own_root = lax.dynamic_slice_in_dim(roots, start, rows, 1)
     bias = out_bias[None, :]
     other = 1 - core
-    result = spread(core[None], places_of(ids, core, own), own_root, bias, longs, shorts)
-    longs, shorts = [swapped(x) for x in longs], [swapped(x) for x in shorts]
-    return spread(other[None], places_of(ids, other, own), own_root, bias, longs, shorts, result)
+    long_places, short_places = places_of(ids, core, own)
+    far_long_places, far_short_places = places_of(ids, other, own)
+    split = longs[0].shape[1]
+    here, there = core[None], other[None]
+    result = spread(here, short_places, own_root, bias, shorts, split, half)
+    far = [swapped(x) for x in shorts]
+    result = spread(there, far_short_places, own_root, bias, far, split, half, result)
+    result = spread(here, long_places, own_root, bias, longs, 0, half, result)
+    far = [swapped(x) for x in longs]
+    return spread(there, far_long_places, own_root, bias, far, 0, half, result)
 
 
 def solution(mesh):

time: 150 us -> 144 us (0.960)
  the two profiles are of different devices: /device:TPU:1 before, /device:TPU:13 now
where the time goes in v9:
time: 144 us; the launch traced here: 143 us
  waiting for transfers between devices  62.5 us (43%)
  Pallas kernels  44.5 us (31%)
  starting transfers between devices  33.5 us (23%)
  local copies, waits for them, and re-layouts  1.67 us (1%)
    ppermute x12, waiting for transfers between devices, shifted(): lax.ppermute(x, LINE, [(i, (i + amount) % size) for i in range(size)])  58.7 us
    pallas_call x4, Pallas kernels, spread(): pl.pallas_call(functools.partial(spread_kernel, len(pieces), stride, offs...  25.6 us
    pallas_call x2, Pallas kernels, half_sums(): pl.pallas_call(functools.partial(kernel, plan, begin, half, pitch), grid=...  17.3 us
    ppermute x12, starting transfers between devices, shifted(): lax.ppermute(x, LINE, [(i, (i + amount) % size) for i in range(size)])  11.9 us
    ppermute x9, starting transfers between devices, swapped(): return lax.ppermute(x, 'core', [(0, 1), (1, 0)])  6.22 us
    ppermute x5, starting transfers between devices, crossed(): return lax.ppermute(x, SQUARE, pairs)  5.57 us
    all_to_all x1, starting transfers between devices, org_sums(): lax.all_to_all(first, SQUARE, split_axis=0, concat_axis=0, tiled=True)  4.36 us
    all_to_all x1, starting transfers between devices, org_sums(): lax.all_to_all(second, SQUARE, split_axis=0, concat_axis=0, tiled=True)  4.32 us
  transfers between devices with their start and end apart: 29, of which 12 were waited for; matrix products, arithmetic and copies ran while one was open for 1% of the time, Pallas kernels for 20%

profile of v9, /device:TPU:13, one launch (start us, length us, event | category | flops | bytes accessed | tf_op | source)
XLA Modules:
  0.0 143.3 jit_solution(5073020120552700920)
XLA Ops:
  0.0 0.8 copy-done.1
  0.8 0.7 copy-done.4
  1.4 8.8 %shard_map.73 = (bf16[8,144,128]{2,1,0:T(8,128)(2,1)S(1)}, bf16[8,144,128]{2,1,0:T(8,128)(2,1)S(1)}, bf16[8,144,128]{2,1,0:T(8,128)(2,1)S(1)}, bf16[8,144,128]{2...) custom-call(s32[1]{0:T(128)} %bitcast.2.line_ref, s32[4,2048]{1,0:T(4,128)S(1)} %bitcast.32, ...), custom_call_target="tpu_custom_call" | custom-call | flops 8589934592 | bytes 16777216 | tf_op jit(solution)/shard_map/pallas_call | solution.py:171
  10.3 1.4 collective-permute-start
  11.6 0.2 collective-permute-start.1
  11.8 8.5 %shard_map.74 = bf16[8,4,128,128]{3,2,1,0:T(8,128)(2,1)} custom-call(s32[1]{0:T(128)} %bitcast.2.line_ref, bf16[256,2048]{1,0:T(8,128)(2,1)S(1)} %get-tuple-element.26.weighted_ref, bf16[2048,32,128]{2,1,0:T(8,128)(2,1)} %cells_ref.3), custom_call_target="tpu_custom_call" | custom-call | flops 8589934592 | bytes 16777216 | tf_op jit(solution)/shard_map/pallas_call | solution.py:171
  20.3 6.1 %collective-permute-done.1.refs_3_ = bf16[8,144,128]{2,1,0:T(8,128)(2,1)S(1)} collective-permute-done((bf16[8,144,128]{2,1,0:T(8,128)(2,1)S(1)}, bf16[8,144,128]{2,1,0:T(8,128)(2,1)S(1)}, u32[]{:S(2)}, u32[]{:S(2)}) %collective-permute-start.1) | collective-permute-done | bytes 294944 | tf_op jit(solution)/shard_map/ppermute | solution.py:413
  26.4 4.4 %all-to-all-start = ((bf16[8,4,128,128]{3,2,1,0:T(8,128)(2,1)}), bf16[8,4,128,128]{3,2,1,0:T(8,128)(2,1)S(1)}, u32[]{:S(2)}, u32[]{:S(2)}) async-start(bf16[8,4,128,128]{3,2,1,0:T(8,128)(2,1)} %shard_map.74), calls=%async_computation | async-start | bytes 2097152 | tf_op jit(solution)/shard_map/all_to_all | solution.py:256
  30.8 1.5 %collective-permute-start.5 = (bf16[8,144,128]{2,1,0:T(8,128)(2,1)S(1)}, bf16[8,144,128]{2,1,0:T(8,128)(2,1)S(1)}, u32[]{:S(2)}, u32[]{:S(2)}) collective-permute-start(bf16[8,144,128]{2,1,0:T(8,128)(2,1)S(1)} %get-tuple-element.36), channel_id=1, source_target_pairs={{0,16},{8,24},{16,0},{24,8},{1,17},{9,25},{17,1},{25,9},{2,18},{10... | collective-permute-start | bytes 884744 | tf_op jit(solution)/shard_map/ppermute | solution.py:413
  32.2 0.1 convert_reduce_fusion
  32.5 0.3 convolution_convert_fusion
  32.9 12.3 %collective-permute-done.5.refs_2_ = bf16[8,144,128]{2,1,0:T(8,128)(2,1)S(1)} collective-permute-done((bf16[8,144,128]{2,1,0:T(8,128)(2,1)S(1)}, bf16[8,144,128]{2,1,0:T(8,128)(2,1)S(1)}, u32[]{:S(2)}, u32[]{:S(2)}) %collective-permute-start.5) | collective-permute-done | bytes 294944 | tf_op jit(solution)/shard_map/ppermute | solution.py:413
  45.2 0.9 shard_map.76
  46.1 4.3 %all-to-all-start.1 = ((bf16[8,1,144,128]{3,2,1,0:T(8,128)(2,1)}), bf16[8,1,144,128]{3,2,1,0:T(8,128)(2,1)S(1)}, u32[]{:S(2)}, u32[]{:S(2)}) async-start(bf16[8,1,144,128]{3,2,1,0:T(8,128)(2,1)} %shard_map.76), calls=%async_computation.1 | async-start | bytes 589824 | tf_op jit(solution)/shard_map/all_to_all | solution.py:260
  50.5 0.1 shard_map.75
  50.6 0.5 collective-permute-start.2
  51.1 4.0 %collective-permute-start.3 = (bf16[4,128,128]{2,1,0:T(8,128)(2,1)S(1)}, bf16[4,128,128]{2,1,0:T(8,128)(2,1)S(1)}, u32[]{:S(2)}, u32[]{:S(2)}) collective-permute-start(bf16[4,128,128]{2,1,0:T(8,128)(2,1)S(1)} %get-tuple-element.32), channel_id=1, source_target_pairs={{0,16},{8,24},{16,0},{24,8},{1,17},{9,25},{17,1},{25,9},{2,18},{10... | collective-permute-start | bytes 393224 | tf_op jit(solution)/shard_map/ppermute | solution.py:413
  55.2 1.4 collective-permute-done.2.refs_1_
  56.6 6.9 %collective-permute-done.3.refs_2_ = bf16[4,128,128]{2,1,0:T(8,128)(2,1)S(1)} collective-permute-done((bf16[4,128,128]{2,1,0:T(8,128)(2,1)S(1)}, bf16[4,128,128]{2,1,0:T(8,128)(2,1)S(1)}, u32[]{:S(2)}, u32[]{:S(2)}) %collective-permute-start.3) | collective-permute-done | bytes 131104 | tf_op jit(solution)/shard_map/ppermute | solution.py:413
  63.4 2.5 %collective-permute-done.4.refs_3_ = bf16[4,128,128]{2,1,0:T(8,128)(2,1)S(1)} collective-permute-done((bf16[4,128,128]{2,1,0:T(8,128)(2,1)S(1)}, bf16[4,128,128]{2,1,0:T(8,128)(2,1)S(1)}, u32[]{:S(2)}, u32[]{:S(2)}) %collective-permute-start.4) | collective-permute-done | bytes 131104 | tf_op jit(solution)/shard_map/ppermute | solution.py:413
  66.0 0.5 shard_map.77
  66.6 1.2 collective-permute-start.6
  67.9 1.0 collective-permute-done.6
  68.9 0.2 collective-permute-start.7
  69.1 1.2 collective-permute-start.11
  70.3 0.6 collective-permute-start.12
  70.9 1.4 collective-permute-start.8
  72.3 1.2 collective-permute-start.9
  73.5 0.9 collective-permute-done.8
  74.3 2.0 %collective-permute-done.9 = bf16[16,16,128]{2,1,0:T(8,128)(2,1)S(1)} collective-permute-done((bf16[16,16,128]{2,1,0:T(8,128)(2,1)S(1)}, bf16[16,16,128]{2,1,0:T(8,128)(2,1)S(1)}, u32[]{:S(2)}, u32[]{:S(2)}) %collective-permute-start.9) | collective-permute-done | bytes 65568 | tf_op jit(solution)/shard_map/ppermute | solution.py:425
  76.4 8.1 %collective-permute-done.11 = bf16[16,48,128]{2,1,0:T(8,128)(2,1)S(1)} collective-permute-done((bf16[16,48,128]{2,1,0:T(8,128)(2,1)S(1)}, bf16[16,48,128]{2,1,0:T(8,128)(2,1)S(1)}, u32[]{:S(2)}, u32[]{:S(2)}) %collective-permute-start.11) | collective-permute-done | bytes 196640 | tf_op jit(solution)/shard_map/ppermute | solution.py:413
  84.5 3.8 %collective-permute-done.12 = bf16[16,48,128]{2,1,0:T(8,128)(2,1)S(1)} collective-permute-done((bf16[16,48,128]{2,1,0:T(8,128)(2,1)S(1)}, bf16[16,48,128]{2,1,0:T(8,128)(2,1)S(1)}, u32[]{:S(2)}, u32[]{:S(2)}) %collective-permute-start.12) | collective-permute-done | bytes 196640 | tf_op jit(solution)/shard_map/ppermute | solution.py:413
  88.4 1.6 %collective-permute-start.14 = (bf16[64,48,128]{2,1,0:T(8,128)(2,1)S(1)}, bf16[64,48,128]{2,1,0:T(8,128)(2,1)S(1)}, u32[]{:S(2)}, u32[]{:S(2)}) collective-permute-start(bf16[64,48,128]{2,1,0:T(8,128)(2,1)S(1)} %pad_maximum_fusion.refs_0_), channel_id=1, source_target_pairs={{0,2},{1,5},{2,0},{3,7},{4,6},{5,1},{6,4},{7,3},{8,10},{9,13},{10,... | collective-permute-start | bytes 2359304 | tf_op jit(solution)/shard_map/ppermute | solution.py:421
  90.0 1.0 collective-permute-start.18
  91.0 1.0 collective-permute-start.16
  92.0 1.5 %collective-permute-start.25 = (bf16[64,16,128]{2,1,0:T(8,128)(2,1)S(1)}, bf16[64,16,128]{2,1,0:T(8,128)(2,1)S(1)}, u32[]{:S(2)}, u32[]{:S(2)}) collective-permute-start(bf16[64,16,128]{2,1,0:T(8,128)(2,1)S(1)} %pad_maximum_fusion.1.refs_0_), channel_id=1, source_target_pairs={{0,24},{8,0},{16,8},{24,16},{1,25},{9,1},{17,9},{25,17},{2,26},{10... | collective-permute-start | bytes 786440 | tf_op jit(solution)/shard_map/ppermute | solution.py:413
  93.5 3.6 %collective-permute-done.15.refs_1_ = bf16[64,16,128]{2,1,0:T(8,128)(2,1)S(1)} collective-permute-done((bf16[64,16,128]{2,1,0:T(8,128)(2,1)S(1)}, bf16[64,16,128]{2,1,0:T(8,128)(2,1)S(1)}, u32[]{:S(2)}, u32[]{:S(2)}) %collective-permute-start.15) | collective-permute-done | bytes 262176 | tf_op jit(solution)/shard_map/ppermute | solution.py:413
  97.1 2.8 %collective-permute-start.22 = (bf16[64,16,128]{2,1,0:T(8,128)(2,1)S(1)}, bf16[64,16,128]{2,1,0:T(8,128)(2,1)S(1)}, u32[]{:S(2)}, u32[]{:S(2)}) collective-permute-start(bf16[64,16,128]{2,1,0:T(8,128)(2,1)S(1)} %pad_maximum_fusion.1.refs_0_), channel_id=1, source_target_pairs={{0,1},{1,0},{2,3},{3,2},{4,5},{5,4},{6,7},{7,6},{8,9},{9,8},{10,11... | collective-permute-start | bytes 786440 | tf_op jit(solution)/shard_map/ppermute | solution.py:429
  100.0 14.0 %collective-permute-done.25.refs_3_ = bf16[64,16,128]{2,1,0:T(8,128)(2,1)S(1)} collective-permute-done((bf16[64,16,128]{2,1,0:T(8,128)(2,1)S(1)}, bf16[64,16,128]{2,1,0:T(8,128)(2,1)S(1)}, u32[]{:S(2)}, u32[]{:S(2)}) %collective-permute-start.25) | collective-permute-done | bytes 262176 | tf_op jit(solution)/shard_map/ppermute | solution.py:413
  113.9 0.5 collective-permute-start.26
  114.5 0.4 collective-permute-start.24
  115.0 1.5 %collective-permute-start.20 = (bf16[64,48,128]{2,1,0:T(8,128)(2,1)S(1)}, bf16[64,48,128]{2,1,0:T(8,128)(2,1)S(1)}, u32[]{:S(2)}, u32[]{:S(2)}) collective-permute-start(bf16[64,48,128]{2,1,0:T(8,128)(2,1)S(1)} %collective-permute-done.14.refs_1_), channel_id=1, source_target_pairs={{0,4},{1,3},{2,6},{3,1},{4,0},{5,7},{6,2},{7,5},{8,12},{9,11},{10,... | collective-permute-start | bytes 2359304 | tf_op jit(solution)/shard_map/ppermute | solution.py:421
  116.5 5.2 %shard_map.78.refs_4_ = bf16[512,128,128]{2,1,0:T(8,128)(2,1)} custom-call(s32[1]{0:T(128)} %bitcast.6.half_ref, s32[4,512]{1,0:T(4,128)S(1)} %get-tuple-element.47.places_ref, f32[1,512]{1,0:T(1,128)S(1)} %constant_dynamic-slice_fusion.root_ref, f32[1,128]{1,0:T(1,128)S(1)} %bitcast.33, bf16[64,16,128]{2,1,0:T(8,128)(2,1)S(1)} %pad_maximum_fusion.1.refs_0_, ...), custom_call_target="tpu_custom_call" | custom-call | flops 4294967296 | bytes 4194304 | tf_op jit(solution)/shard_map/pallas_call | solution.py:388
  121.8 0.5 collective-permute-start.17
  122.3 5.2 %shard_map.79.refs_4_ = bf16[512,128,128]{2,1,0:T(8,128)(2,1)} custom-call(s32[1]{0:T(128)} %bitcast.half_ref, s32[4,512]{1,0:T(4,128)S(1)} %get-tuple-element.53.places_ref, f32[1,512]{1,0:T(1,128)S(1)} %constant_dynamic-slice_fusion.root_ref, f32[1,128]{1,0:T(1,128)S(1)} %bitcast.34, ...), custom_call_target="tpu_custom_call", output_to_operand_aliasing={{}: (8, {})} | custom-call | flops 4294967296 | bytes 4194304 | tf_op jit(solution)/shard_map/pallas_call | solution.py:388
  127.6 0.5 collective-permute-start.21
  128.1 8.1 %shard_map.80.refs_4_ = bf16[512,128,128]{2,1,0:T(8,128)(2,1)} custom-call(s32[1]{0:T(128)} %bitcast.6.half_ref, s32[4,512]{1,0:T(4,128)S(1)} %get-tuple-element.54.places_ref, f32[1,512]{1,0:T(1,128)S(1)} %constant_dynamic-slice_fusion.root_ref, f32[1,128]{1,0:T(1,128)S(1)} %bitcast.35, ...), custom_call_target="tpu_custom_call", output_to_operand_aliasing={{}: (8, {})} | custom-call | flops 12884901888 | bytes 12582912 | tf_op jit(solution)/shard_map/pallas_call | solution.py:388
  136.2 7.1 %shard_map.81 = bf16[512,128,128]{2,1,0:T(8,128)(2,1)} custom-call(s32[1]{0:T(128)} %bitcast.half_ref, s32[4,512]{1,0:T(4,128)S(1)} %get-tuple-element.55.places_ref, f32[1,512]{1,0:T(1,128)S(1)} %constant_dynamic-slice_fusion.root_ref, f32[1,128]{1,0:T(1,128)S(1)} %bitcast.36, ...), custom_call_target="tpu_custom_call", output_to_operand_aliasing={{}: (8, {})} | custom-call | flops 12884901888 | bytes 12582912 | tf_op jit(solution)/shard_map/pallas_call | solution.py:388
  (54 shorter events, 1.1 us)
Async XLA Ops:
  0.0 0.8 copy-start.1
  0.8 0.7 copy-start.4
  10.3 10.1 %collective-permute-start = (bf16[8,144,128]{2,1,0:T(8,128)(2,1)S(1)}, bf16[8,144,128]{2,1,0:T(8,128)(2,1)S(1)}, u32[]{:S(2)}, u32[]{:S(2)}) collective-permute-start(bf16[8,144,128]{2,1,0:T(8,128)(2,1)S(1)} %get-tuple-element.27), channel_id=1, source_target_pairs={{0,8},{8,16},{16,24},{24,0},{1,9},{9,17},{17,25},{25,1},{2,10},{10... | collective-permute-start | bytes 884744 | tf_op jit(solution)/shard_map/ppermute | solution.py:413
  11.6 14.8 %collective-permute-start.1 = (bf16[8,144,128]{2,1,0:T(8,128)(2,1)S(1)}, bf16[8,144,128]{2,1,0:T(8,128)(2,1)S(1)}, u32[]{:S(2)}, u32[]{:S(2)}) collective-permute-start(bf16[8,144,128]{2,1,0:T(8,128)(2,1)S(1)} %get-tuple-element.28), channel_id=1, source_target_pairs={{0,24},{8,0},{16,8},{24,16},{1,25},{9,1},{17,9},{25,17},{2,26},{10... | collective-permute-start | bytes 884744 | tf_op jit(solution)/shard_map/ppermute | solution.py:413
  11.8 20.5 %copy-start.6 = (s32[128,3]{0,1:T(4,128)S(1)}, s32[128,3]{0,1:T(4,128)}, u32[]{:S(2)}) copy-start(s32[128,3]{0,1:T(4,128)} %param.11) | copy-start | bytes 4612
  11.8 20.6 %copy-start.7 = (f32[128]{0:T(128)S(1)}, f32[128]{0:T(128)}, u32[]{:S(2)}) copy-start(f32[128]{0:T(128)} %param.12) | copy-start | bytes 1540
  11.8 38.6 %copy-start.5 = (f32[256]{0:T(256)S(1)}, f32[256]{0:T(256)}, u32[]{:S(2)}) copy-start(f32[256]{0:T(256)} %param.9) | copy-start | bytes 3076
  11.8 54.3 %copy-start = (bf16[128,128]{1,0:T(8,128)(2,1)S(1)}, bf16[128,128]{1,0:T(8,128)(2,1)}, u32[]{:S(2)}) copy-start(bf16[128,128]{1,0:T(8,128)(2,1)} %mixing_ref.1) | copy-start | bytes 98308
  11.8 78.2 %copy-start.2 = (s32[2048,4]{0,1:T(4,128)S(1)}, s32[2048,4]{0,1:T(4,128)}, u32[]{:S(2)}) copy-start(s32[2048,4]{0,1:T(4,128)} %param.8) | copy-start | bytes 98308
  11.8 104.7 %copy-start.3 = (f32[128]{0:T(128)S(1)}, f32[128]{0:T(128)}, u32[]{:S(2)}) copy-start(f32[128]{0:T(128)} %param.13) | copy-start | bytes 1540
  26.4 19.6 %all-to-all-start = ((bf16[8,4,128,128]{3,2,1,0:T(8,128)(2,1)}), bf16[8,4,128,128]{3,2,1,0:T(8,128)(2,1)S(1)}, u32[]{:S(2)}, u32[]{:S(2)}) async-start(bf16[8,4,128,128]{3,2,1,0:T(8,128)(2,1)} %shard_map.74), calls=%async_computation | async-start | bytes 2097152 | tf_op jit(solution)/shard_map/all_to_all | solution.py:256
  30.8 14.4 %collective-permute-start.5 = (bf16[8,144,128]{2,1,0:T(8,128)(2,1)S(1)}, bf16[8,144,128]{2,1,0:T(8,128)(2,1)S(1)}, u32[]{:S(2)}, u32[]{:S(2)}) collective-permute-start(bf16[8,144,128]{2,1,0:T(8,128)(2,1)S(1)} %get-tuple-element.36), channel_id=1, source_target_pairs={{0,16},{8,24},{16,0},{24,8},{1,17},{9,25},{17,1},{25,9},{2,18},{10... | collective-permute-start | bytes 884744 | tf_op jit(solution)/shard_map/ppermute | solution.py:413
  46.1 9.2 %all-to-all-start.1 = ((bf16[8,1,144,128]{3,2,1,0:T(8,128)(2,1)}), bf16[8,1,144,128]{3,2,1,0:T(8,128)(2,1)S(1)}, u32[]{:S(2)}, u32[]{:S(2)}) async-start(bf16[8,1,144,128]{3,2,1,0:T(8,128)(2,1)} %shard_map.76), calls=%async_computation.1 | async-start | bytes 589824 | tf_op jit(solution)/shard_map/all_to_all | solution.py:260
  50.6 6.0 %collective-permute-start.2 = (bf16[4,128,128]{2,1,0:T(8,128)(2,1)S(1)}, bf16[4,128,128]{2,1,0:T(8,128)(2,1)S(1)}, u32[]{:S(2)}, u32[]{:S(2)}) collective-permute-start(bf16[4,128,128]{2,1,0:T(8,128)(2,1)S(1)} %get-tuple-element.31), channel_id=1, source_target_pairs={{0,8},{8,16},{16,24},{24,0},{1,9},{9,17},{17,25},{25,1},{2,10},{10... | collective-permute-start | bytes 393224 | tf_op jit(solution)/shard_map/ppermute | solution.py:413
  51.1 12.4 %collective-permute-start.3 = (bf16[4,128,128]{2,1,0:T(8,128)(2,1)S(1)}, bf16[4,128,128]{2,1,0:T(8,128)(2,1)S(1)}, u32[]{:S(2)}, u32[]{:S(2)}) collective-permute-start(bf16[4,128,128]{2,1,0:T(8,128)(2,1)S(1)} %get-tuple-element.32), channel_id=1, source_target_pairs={{0,16},{8,24},{16,0},{24,8},{1,17},{9,25},{17,1},{25,9},{2,18},{10... | collective-permute-start | bytes 393224 | tf_op jit(solution)/shard_map/ppermute | solution.py:413
  55.1 10.9 %collective-permute-start.4 = (bf16[4,128,128]{2,1,0:T(8,128)(2,1)S(1)}, bf16[4,128,128]{2,1,0:T(8,128)(2,1)S(1)}, u32[]{:S(2)}, u32[]{:S(2)}) collective-permute-start(bf16[4,128,128]{2,1,0:T(8,128)(2,1)S(1)} %get-tuple-element.33), channel_id=1, source_target_pairs={{0,24},{8,0},{16,8},{24,16},{1,25},{9,1},{17,9},{25,17},{2,26},{10... | collective-permute-start | bytes 393224 | tf_op jit(solution)/shard_map/ppermute | solution.py:413
  66.6 2.2 %collective-permute-start.6 = (bf16[8,64,128]{2,1,0:T(8,128)(2,1)S(1)}, bf16[8,64,128]{2,1,0:T(8,128)(2,1)S(1)}, u32[]{:S(2)}, u32[]{:S(2)}) collective-permute-start(bf16[8,64,128]{2,1,0:T(8,128)(2,1)S(1)} %get-tuple-element.39), channel_id=1, source_target_pairs={{0,1},{1,0},{2,3},{3,2},{4,5},{5,4},{6,7},{7,6},{8,9},{9,8},{10,11... | collective-permute-start | bytes 393224 | tf_op jit(solution)/shard_map/ppermute | solution.py:429
  68.9 3.4 %collective-permute-start.7 = (bf16[16,16,128]{2,1,0:T(8,128)(2,1)S(1)}, bf16[16,16,128]{2,1,0:T(8,128)(2,1)S(1)}, u32[]{:S(2)}, u32[]{:S(2)}) collective-permute-start(bf16[16,16,128]{2,1,0:T(8,128)(2,1)S(1)} %slice.18), channel_id=1, source_target_pairs={{0,2},{1,5},{2,0},{3,7},{4,6},{5,1},{6,4},{7,3},{8,10},{9,13},{10,... | collective-permute-start | bytes 196616 | tf_op jit(solution)/shard_map/ppermute | solution.py:421
  69.1 7.3 %collective-permute-start.10 = (bf16[16,48,128]{2,1,0:T(8,128)(2,1)S(1)}, bf16[16,48,128]{2,1,0:T(8,128)(2,1)S(1)}, u32[]{:S(2)}, u32[]{:S(2)}) collective-permute-start(bf16[16,48,128]{2,1,0:T(8,128)(2,1)S(1)} %slice.19), channel_id=1, source_target_pairs={{0,8},{8,16},{16,24},{24,0},{1,9},{9,17},{17,25},{25,1},{2,10},{10... | collective-permute-start | bytes 589832 | tf_op jit(solution)/shard_map/ppermute | solution.py:413
  69.1 15.4 %collective-permute-start.11 = (bf16[16,48,128]{2,1,0:T(8,128)(2,1)S(1)}, bf16[16,48,128]{2,1,0:T(8,128)(2,1)S(1)}, u32[]{:S(2)}, u32[]{:S(2)}) collective-permute-start(bf16[16,48,128]{2,1,0:T(8,128)(2,1)S(1)} %slice.19), channel_id=1, source_target_pairs={{0,16},{8,24},{16,0},{24,8},{1,17},{9,25},{17,1},{25,9},{2,18},{10... | collective-permute-start | bytes 589832 | tf_op jit(solution)/shard_map/ppermute | solution.py:413
  70.3 18.0 %collective-permute-start.12 = (bf16[16,48,128]{2,1,0:T(8,128)(2,1)S(1)}, bf16[16,48,128]{2,1,0:T(8,128)(2,1)S(1)}, u32[]{:S(2)}, u32[]{:S(2)}) collective-permute-start(bf16[16,48,128]{2,1,0:T(8,128)(2,1)S(1)} %slice.19), channel_id=1, source_target_pairs={{0,24},{8,0},{16,8},{24,16},{1,25},{9,1},{17,9},{25,17},{2,26},{10... | collective-permute-start | bytes 589832 | tf_op jit(solution)/shard_map/ppermute | solution.py:413
  70.9 3.4 %collective-permute-start.8 = (bf16[16,16,128]{2,1,0:T(8,128)(2,1)S(1)}, bf16[16,16,128]{2,1,0:T(8,128)(2,1)S(1)}, u32[]{:S(2)}, u32[]{:S(2)}) collective-permute-start(bf16[16,16,128]{2,1,0:T(8,128)(2,1)S(1)} %slice.18), channel_id=1, source_target_pairs={{0,4},{1,3},{2,6},{3,1},{4,0},{5,7},{6,2},{7,5},{8,12},{9,11},{10,... | collective-permute-start | bytes 196616 | tf_op jit(solution)/shard_map/ppermute | solution.py:421
  72.3 4.0 %collective-permute-start.9 = (bf16[16,16,128]{2,1,0:T(8,128)(2,1)S(1)}, bf16[16,16,128]{2,1,0:T(8,128)(2,1)S(1)}, u32[]{:S(2)}, u32[]{:S(2)}) collective-permute-start(bf16[16,16,128]{2,1,0:T(8,128)(2,1)S(1)} %slice.18), channel_id=1, source_target_pairs={{0,6},{1,7},{2,4},{3,5},{4,2},{5,3},{6,0},{7,1},{8,14},{9,15},{10,... | collective-permute-start | bytes 196616 | tf_op jit(solution)/shard_map/ppermute | solution.py:425
  88.4 26.1 %collective-permute-start.14 = (bf16[64,48,128]{2,1,0:T(8,128)(2,1)S(1)}, bf16[64,48,128]{2,1,0:T(8,128)(2,1)S(1)}, u32[]{:S(2)}, u32[]{:S(2)}) collective-permute-start(bf16[64,48,128]{2,1,0:T(8,128)(2,1)S(1)} %pad_maximum_fusion.refs_0_), channel_id=1, source_target_pairs={{0,2},{1,5},{2,0},{3,7},{4,6},{5,1},{6,4},{7,3},{8,10},{9,13},{10,... | collective-permute-start | bytes 2359304 | tf_op jit(solution)/shard_map/ppermute | solution.py:421
  89.9 7.2 %collective-permute-start.15 = (bf16[64,16,128]{2,1,0:T(8,128)(2,1)S(1)}, bf16[64,16,128]{2,1,0:T(8,128)(2,1)S(1)}, u32[]{:S(2)}, u32[]{:S(2)}) collective-permute-start(bf16[64,16,128]{2,1,0:T(8,128)(2,1)S(1)} %pad_maximum_fusion.1.refs_0_), channel_id=1, source_target_pairs={{0,8},{8,16},{16,24},{24,0},{1,9},{9,17},{17,25},{25,1},{2,10},{10... | collective-permute-start | bytes 786440 | tf_op jit(solution)/shard_map/ppermute | solution.py:413
  90.0 31.8 %collective-permute-start.18 = (bf16[64,48,128]{2,1,0:T(8,128)(2,1)S(1)}, bf16[64,48,128]{2,1,0:T(8,128)(2,1)}, u32[]{:S(2)}, u32[]{:S(2)}) collective-permute-start(bf16[64,48,128]{2,1,0:T(8,128)(2,1)S(1)} %pad_maximum_fusion.refs_0_), channel_id=1, source_target_pairs={{0,4},{1,3},{2,6},{3,1},{4,0},{5,7},{6,2},{7,5},{8,12},{9,11},{10,... | collective-permute-start | bytes 2359304 | tf_op jit(solution)/shard_map/ppermute | solution.py:421
  91.0 23.4 %collective-permute-start.16 = (bf16[64,16,128]{2,1,0:T(8,128)(2,1)S(1)}, bf16[64,16,128]{2,1,0:T(8,128)(2,1)S(1)}, u32[]{:S(2)}, u32[]{:S(2)}) collective-permute-start(bf16[64,16,128]{2,1,0:T(8,128)(2,1)S(1)} %pad_maximum_fusion.1.refs_0_), channel_id=1, source_target_pairs={{0,16},{8,24},{16,0},{24,8},{1,17},{9,25},{17,1},{25,9},{2,18},{10... | collective-permute-start | bytes 786440 | tf_op jit(solution)/shard_map/ppermute | solution.py:413
  92.0 21.9 %collective-permute-start.25 = (bf16[64,16,128]{2,1,0:T(8,128)(2,1)S(1)}, bf16[64,16,128]{2,1,0:T(8,128)(2,1)S(1)}, u32[]{:S(2)}, u32[]{:S(2)}) collective-permute-start(bf16[64,16,128]{2,1,0:T(8,128)(2,1)S(1)} %pad_maximum_fusion.1.refs_0_), channel_id=1, source_target_pairs={{0,24},{8,0},{16,8},{24,16},{1,25},{9,1},{17,9},{25,17},{2,26},{10... | collective-permute-start | bytes 786440 | tf_op jit(solution)/shard_map/ppermute | solution.py:413
  97.1 17.9 %collective-permute-start.22 = (bf16[64,16,128]{2,1,0:T(8,128)(2,1)S(1)}, bf16[64,16,128]{2,1,0:T(8,128)(2,1)S(1)}, u32[]{:S(2)}, u32[]{:S(2)}) collective-permute-start(bf16[64,16,128]{2,1,0:T(8,128)(2,1)S(1)} %pad_maximum_fusion.1.refs_0_), channel_id=1, source_target_pairs={{0,1},{1,0},{2,3},{3,2},{4,5},{5,4},{6,7},{7,6},{8,9},{9,8},{10,11... | collective-permute-start | bytes 786440 | tf_op jit(solution)/shard_map/ppermute | solution.py:429
  113.9 7.7 %collective-permute-start.26 = (bf16[64,16,128]{2,1,0:T(8,128)(2,1)S(1)}, bf16[64,16,128]{2,1,0:T(8,128)(2,1)S(1)}, u32[]{:S(2)}, u32[]{:S(2)}) collective-permute-start(bf16[64,16,128]{2,1,0:T(8,128)(2,1)S(1)} %collective-permute-done.25.refs_3_), channel_id=1, source_target_pairs={{0,1},{1,0},{2,3},{3,2},{4,5},{5,4},{6,7},{7,6},{8,9},{9,8},{10,11... | collective-permute-start | bytes 786440 | tf_op jit(solution)/shard_map/ppermute | solution.py:429
  114.4 7.8 %collective-permute-start.23 = (bf16[64,16,128]{2,1,0:T(8,128)(2,1)S(1)}, bf16[64,16,128]{2,1,0:T(8,128)(2,1)S(1)}, u32[]{:S(2)}, u32[]{:S(2)}) collective-permute-start(bf16[64,16,128]{2,1,0:T(8,128)(2,1)S(1)} %collective-permute-done.15.refs_1_), channel_id=1, source_target_pairs={{0,1},{1,0},{2,3},{3,2},{4,5},{5,4},{6,7},{7,6},{8,9},{9,8},{10,11... | collective-permute-start | bytes 786440 | tf_op jit(solution)/shard_map/ppermute | solution.py:429
  114.5 7.8 %collective-permute-start.24 = (bf16[64,16,128]{2,1,0:T(8,128)(2,1)S(1)}, bf16[64,16,128]{2,1,0:T(8,128)(2,1)S(1)}, u32[]{:S(2)}, u32[]{:S(2)}) collective-permute-start(bf16[64,16,128]{2,1,0:T(8,128)(2,1)S(1)} %collective-permute-done.16.refs_2_), channel_id=1, source_target_pairs={{0,1},{1,0},{2,3},{3,2},{4,5},{5,4},{6,7},{7,6},{8,9},{9,8},{10,11... | collective-permute-start | bytes 786440 | tf_op jit(solution)/shard_map/ppermute | solution.py:429
  115.0 12.6 %collective-permute-start.20 = (bf16[64,48,128]{2,1,0:T(8,128)(2,1)S(1)}, bf16[64,48,128]{2,1,0:T(8,128)(2,1)S(1)}, u32[]{:S(2)}, u32[]{:S(2)}) collective-permute-start(bf16[64,48,128]{2,1,0:T(8,128)(2,1)S(1)} %collective-permute-done.14.refs_1_), channel_id=1, source_target_pairs={{0,4},{1,3},{2,6},{3,1},{4,0},{5,7},{6,2},{7,5},{8,12},{9,11},{10,... | collective-permute-start | bytes 2359304 | tf_op jit(solution)/shard_map/ppermute | solution.py:421
  121.7 14.5 %collective-permute-start.13 = (bf16[64,48,128]{2,1,0:T(8,128)(2,1)S(1)}, bf16[64,48,128]{2,1,0:T(8,128)(2,1)S(1)}, u32[]{:S(2)}, u32[]{:S(2)}) collective-permute-start(bf16[64,48,128]{2,1,0:T(8,128)(2,1)S(1)} %pad_maximum_fusion.refs_0_), channel_id=1, source_target_pairs={{0,1},{1,0},{2,3},{3,2},{4,5},{5,4},{6,7},{7,6},{8,9},{9,8},{10,11... | collective-permute-start | bytes 2359304 | tf_op jit(solution)/shard_map/ppermute | solution.py:429
  121.8 14.4 %collective-permute-start.17 = (bf16[64,48,128]{2,1,0:T(8,128)(2,1)S(1)}, bf16[64,48,128]{2,1,0:T(8,128)(2,1)S(1)}, u32[]{:S(2)}, u32[]{:S(2)}) collective-permute-start(bf16[64,48,128]{2,1,0:T(8,128)(2,1)S(1)} %collective-permute-done.14.refs_1_), channel_id=1, source_target_pairs={{0,1},{1,0},{2,3},{3,2},{4,5},{5,4},{6,7},{7,6},{8,9},{9,8},{10,11... | collective-permute-start | bytes 2359304 | tf_op jit(solution)/shard_map/ppermute | solution.py:429
  122.3 14.0 %collective-permute-start.19 = (bf16[64,48,128]{2,1,0:T(8,128)(2,1)}, bf16[64,48,128]{2,1,0:T(8,128)(2,1)S(1)}, u32[]{:S(2)}, u32[]{:S(2)}) collective-permute-start(bf16[64,48,128]{2,1,0:T(8,128)(2,1)} %collective-permute-done.18.refs_2_), channel_id=1, source_target_pairs={{0,1},{1,0},{2,3},{3,2},{4,5},{5,4},{6,7},{7,6},{8,9},{9,8},{10,11... | collective-permute-start | bytes 2359304 | tf_op jit(solution)/shard_map/ppermute | solution.py:429
  127.6 8.7 %collective-permute-start.21 = (bf16[64,48,128]{2,1,0:T(8,128)(2,1)S(1)}, bf16[64,48,128]{2,1,0:T(8,128)(2,1)S(1)}, u32[]{:S(2)}, u32[]{:S(2)}) collective-permute-start(bf16[64,48,128]{2,1,0:T(8,128)(2,1)S(1)} %collective-permute-done.20.refs_3_), channel_id=1, source_target_pairs={{0,1},{1,0},{2,3},{3,2},{4,5},{5,4},{6,7},{7,6},{8,9},{9,8},{10,11... | collective-permute-start | bytes 2359304 | tf_op jit(solution)/shard_map/ppermute | solution.py:429

commit v10 on v9

--- a/solution.py
+++ b/solution.py
@@ -252,11 +252,12 @@
     seconds, roots, weighted = second_sums(line, cells, edges_t, edge_weight, plan)
     seconds = [shifted(part, shift) if shift else part for shift, part in enumerate(seconds)]
     first = first_sums(line, cells, weighted, plan)
-    first, *seconds[1::2] = lax.optimization_barrier((first, *seconds[1::2]))
+    first, seconds[1] = lax.optimization_barrier((first, seconds[1]))
     first = lax.all_to_all(first, SQUARE, split_axis=0, concat_axis=0, tiled=True)
-    second = fold(fold_second_kernel, plan, seconds, [(8, plan.rest, plan.second_rows, lanes)])[0]
     firsts = fold(fold_first_kernel, plan, [first], [(4, plan.first_rows, lanes)] * plan.line)
     firsts = [shifted(part, shift) if shift else part for shift, part in enumerate(firsts)]
+    firsts[1], seconds[2] = lax.optimization_barrier((firsts[1], seconds[2]))
+    second = fold(fold_second_kernel, plan, seconds, [(8, plan.rest, plan.second_rows, lanes)])[0]
     second = lax.all_to_all(second, SQUARE, split_axis=0, concat_axis=0, tiled=True)
     return firsts, second, roots
 
@@ -322,14 +323,15 @@
     copies = []
     for i, source in enumerate(refs[:n_pieces]):
         size = source.shape[0]
-        copies.append(pltpu.make_async_copy(source, table_ref.at[pl.ds(i * size, size)], sems.at[i]))
+        copies.append(pltpu.make_async_copy(source, table_ref.at[pl.ds(i * size, size), :], sems.at[i]))
     for copy in copies:
         copy.start()
     for copy in copies:
         copy.wait()
 
     bias = bias_ref[...]
-    count = places_ref.shape[0]
+    anchors = root_ref.shape[0]
+    count = places_ref.shape[0] // anchors
     tile = 16
     batch = min(8 if zones > tile else 16, rows)
     tiles = zones // tile
@@ -349,10 +351,10 @@
             values = []
             for i in range(batch):
                 at = step * rows + group * batch + i
-                scale = root_ref[0, at]
-                spots = [places_ref[j, at] for j in range(count)]
+                scale = root_ref[at]
+                spots = [pl.multiple_of(places_ref[j * anchors + at], tile) for j in range(count)]
                 for first in range(0, zones, tile):
-                    pieces = [table_ref[spot, first : first + tile, :] for spot in spots]
+                    pieces = [table_ref[pl.ds(spot + first, tile), :] for spot in spots]
                     pieces = [(a + b).astype(F32) for a, b in zip(pieces[0::2], pieces[1::2])]
                     total = sum(pieces[1:], pieces[0])
                     values.append(jnp.maximum((total * scale + bias).astype(BF16), BF16(0.0)))
@@ -374,11 +376,13 @@
     anchors = places.shape[1]
     lanes = bias.shape[1]
     zones = pieces[0].shape[1]
+    edges = len(pieces) * pieces[0].shape[0]
+    pieces = [piece.reshape(-1, lanes) for piece in pieces]
     rows = min(16, anchors // 8)
     slots = min(8, anchors // rows)
     smem = pl.BlockSpec(memory_space=pltpu.SMEM)
     anywhere = pl.BlockSpec(memory_space=pltpu.HBM)
-    operands = [half, places, root, bias] + pieces
+    operands = [half, (places * zones).reshape(-1), root.reshape(-1), bias] + pieces
     specs = [smem, smem, smem, pl.BlockSpec(memory_space=pltpu.VMEM)] + [anywhere] * len(pieces)
     aliases = {}
     if before is not None:
@@ -391,7 +395,7 @@
         out_specs=anywhere,
         out_shape=jax.ShapeDtypeStruct((anchors, 2 * stride, lanes), BF16),
         scratch_shapes=[
-            pltpu.VMEM((len(pieces) * pieces[0].shape[0], zones, lanes), BF16),
+            pltpu.VMEM((edges * zones, lanes), BF16),
             pltpu.VMEM((slots, rows, zones, lanes), BF16),
             pltpu.SemaphoreType.DMA((len(pieces),)),
             pltpu.SemaphoreType.DMA((slots,)),

time: 144 us -> 148 us (1.028)
  Pallas kernels: 44.5 us -> 48.8 us
  waiting for transfers between devices: 62.5 us -> 60 us
  starting transfers between devices: 33.5 us -> 35.1 us
    ppermute x12, waiting for transfers between devices: 58.7 us -> 47.2 us  [shifted(): lax.ppermute(x, LINE, [(i, (i + amount) % size) for i in range(size)])]
    all_to_all x1, waiting for transfers between devices: 0.01 us -> 8.91 us  [org_sums(): lax.all_to_all(first, SQUARE, split_axis=0, concat_axis=0, tiled=True)]
    pallas_call x4, Pallas kernels: 25.6 us -> 29.9 us  [spread(): pl.pallas_call(functools.partial(spread_kernel, len(pieces), stride, offs...]
  transfers between devices with their start and end apart: 29 -> 29, of which waited for: 12 -> 12; matrix products, arithmetic and copies ran while one was open for 1% -> 1% of each run, Pallas kernels for 20% -> 19%
where the time goes in v10:
time: 148 us; the launch traced here: 147 us
  waiting for transfers between devices  60 us (41%)
  Pallas kernels  48.8 us (33%)
  starting transfers between devices  35.1 us (24%)
  local copies, waits for them, and re-layouts  1.7 us (1%)
    ppermute x12, waiting for transfers between devices, shifted(): lax.ppermute(x, LINE, [(i, (i + amount) % size) for i in range(size)])  47.2 us
    pallas_call x4, Pallas kernels, spread(): pl.pallas_call(functools.partial(spread_kernel, len(pieces), stride, offs...  29.9 us
    pallas_call x2, Pallas kernels, half_sums(): pl.pallas_call(functools.partial(kernel, plan, begin, half, pitch), grid=...  17.3 us
    ppermute x12, starting transfers between devices, shifted(): lax.ppermute(x, LINE, [(i, (i + amount) % size) for i in range(size)])  13.1 us
    all_to_all x1, waiting for transfers between devices, org_sums(): lax.all_to_all(first, SQUARE, split_axis=0, concat_axis=0, tiled=True)  8.91 us
    ppermute x9, starting transfers between devices, swapped(): return lax.ppermute(x, 'core', [(0, 1), (1, 0)])  5.98 us
    ppermute x5, starting transfers between devices, crossed(): return lax.ppermute(x, SQUARE, pairs)  5.14 us
    all_to_all x1, starting transfers between devices, org_sums(): lax.all_to_all(second, SQUARE, split_axis=0, concat_axis=0, tiled=True)  4.84 us
  transfers between devices with their start and end apart: 29, of which 12 were waited for; matrix products, arithmetic and copies ran while one was open for 1% of the time, Pallas kernels for 19%

profile of v10, /device:TPU:13, one launch (start us, length us, event | category | flops | bytes accessed | tf_op | source)
XLA Modules:
  0.0 146.7 jit_solution(15917709416822473508)
XLA Ops:
  0.0 0.8 copy-done.1
  0.8 0.7 copy-done.4
  1.4 8.8 %shard_map.73 = (bf16[8,144,128]{2,1,0:T(8,128)(2,1)S(1)}, bf16[8,144,128]{2,1,0:T(8,128)(2,1)S(1)}, bf16[8,144,128]{2,1,0:T(8,128)(2,1)S(1)}, bf16[8,144,128]{2...) custom-call(s32[1]{0:T(128)} %bitcast.2.line_ref, s32[4,2048]{1,0:T(4,128)S(1)} %bitcast.76, ...), custom_call_target="tpu_custom_call" | custom-call | flops 8589934592 | bytes 16777216 | tf_op jit(solution)/shard_map/pallas_call | solution.py:171
  10.3 1.4 collective-permute-start
  11.6 8.5 %shard_map.74 = bf16[8,4,128,128]{3,2,1,0:T(8,128)(2,1)} custom-call(s32[1]{0:T(128)} %bitcast.2.line_ref, bf16[256,2048]{1,0:T(8,128)(2,1)S(1)} %get-tuple-element.27.weighted_ref, bf16[2048,32,128]{2,1,0:T(8,128)(2,1)} %cells_ref.3), custom_call_target="tpu_custom_call" | custom-call | flops 8589934592 | bytes 16777216 | tf_op jit(solution)/shard_map/pallas_call | solution.py:171
  20.2 4.8 %all-to-all-start = ((bf16[8,4,128,128]{3,2,1,0:T(8,128)(2,1)}), bf16[8,4,128,128]{3,2,1,0:T(8,128)(2,1)S(1)}, u32[]{:S(2)}, u32[]{:S(2)}) async-start(bf16[8,4,128,128]{3,2,1,0:T(8,128)(2,1)} %shard_map.74), calls=%async_computation | async-start | bytes 2097152 | tf_op jit(solution)/shard_map/all_to_all | solution.py:256
  25.0 0.9 collective-permute-start.2
  25.9 1.5 %collective-permute-start.5 = (bf16[8,144,128]{2,1,0:T(8,128)(2,1)S(1)}, bf16[8,144,128]{2,1,0:T(8,128)(2,1)S(1)}, u32[]{:S(2)}, u32[]{:S(2)}) collective-permute-start(bf16[8,144,128]{2,1,0:T(8,128)(2,1)S(1)} %get-tuple-element.39), channel_id=1, source_target_pairs={{0,24},{8,0},{16,8},{24,16},{1,25},{9,1},{17,9},{25,17},{2,26},{10... | collective-permute-start | bytes 884744 | tf_op jit(solution)/shard_map/ppermute | solution.py:417
  27.5 0.1 convert_reduce_fusion
  27.7 8.9 %all-to-all-done.part_ref = bf16[8,4,128,128]{3,2,1,0:T(8,128)(2,1)S(1)} async-done(((bf16[8,4,128,128]{3,2,1,0:T(8,128)(2,1)}), bf16[8,4,128,128]{3,2,1,0:T(8,128)(2,1)S(1)}, u32[]{:S(2)}, u32[]{:S(2)}) %all-to-all-start) | async-done | bytes 1048608 | tf_op jit(solution)/shard_map/all_to_all | solution.py:256
  36.8 1.4 collective-permute-start.1
  38.1 0.3 convolution_convert_fusion
  38.5 6.2 %collective-permute-done.2.refs_2_ = bf16[8,144,128]{2,1,0:T(8,128)(2,1)S(1)} collective-permute-done((bf16[8,144,128]{2,1,0:T(8,128)(2,1)S(1)}, bf16[8,144,128]{2,1,0:T(8,128)(2,1)S(1)}, u32[]{:S(2)}, u32[]{:S(2)}) %collective-permute-start.2) | collective-permute-done | bytes 294944 | tf_op jit(solution)/shard_map/ppermute | solution.py:417
  44.6 2.8 %collective-permute-done.1.refs_1_ = bf16[4,128,128]{2,1,0:T(8,128)(2,1)S(1)} collective-permute-done((bf16[4,128,128]{2,1,0:T(8,128)(2,1)S(1)}, bf16[4,128,128]{2,1,0:T(8,128)(2,1)S(1)}, u32[]{:S(2)}, u32[]{:S(2)}) %collective-permute-start.1) | collective-permute-done | bytes 131104 | tf_op jit(solution)/shard_map/ppermute | solution.py:417
  47.4 1.8 %collective-permute-done.5.refs_3_ = bf16[8,144,128]{2,1,0:T(8,128)(2,1)S(1)} collective-permute-done((bf16[8,144,128]{2,1,0:T(8,128)(2,1)S(1)}, bf16[8,144,128]{2,1,0:T(8,128)(2,1)S(1)}, u32[]{:S(2)}, u32[]{:S(2)}) %collective-permute-start.5) | collective-permute-done | bytes 294944 | tf_op jit(solution)/shard_map/ppermute | solution.py:417
  49.3 0.9 shard_map.76
  50.1 4.8 %all-to-all-start.1 = ((bf16[8,1,144,128]{3,2,1,0:T(8,128)(2,1)}), bf16[8,1,144,128]{3,2,1,0:T(8,128)(2,1)S(1)}, u32[]{:S(2)}, u32[]{:S(2)}) async-start(bf16[8,1,144,128]{3,2,1,0:T(8,128)(2,1)} %shard_map.76), calls=%async_computation.1 | async-start | bytes 589824 | tf_op jit(solution)/shard_map/all_to_all | solution.py:261
  55.1 1.4 collective-permute-start.3
  56.5 0.3 collective-permute-start.4
  56.8 8.4 %collective-permute-done.3.refs_2_ = bf16[4,128,128]{2,1,0:T(8,128)(2,1)S(1)} collective-permute-done((bf16[4,128,128]{2,1,0:T(8,128)(2,1)S(1)}, bf16[4,128,128]{2,1,0:T(8,128)(2,1)S(1)}, u32[]{:S(2)}, u32[]{:S(2)}) %collective-permute-start.3) | collective-permute-done | bytes 131104 | tf_op jit(solution)/shard_map/ppermute | solution.py:417
  65.4 0.5 shard_map.77
  65.9 0.6 collective-permute-start.6
  66.5 1.0 collective-permute-done.6
  67.5 0.2 collective-permute-start.7
  67.8 3.2 %collective-permute-start.11 = (bf16[16,48,128]{2,1,0:T(8,128)(2,1)S(1)}, bf16[16,48,128]{2,1,0:T(8,128)(2,1)S(1)}, u32[]{:S(2)}, u32[]{:S(2)}) collective-permute-start(bf16[16,48,128]{2,1,0:T(8,128)(2,1)S(1)} %slice.19), channel_id=1, source_target_pairs={{0,16},{8,24},{16,0},{24,8},{1,17},{9,25},{17,1},{25,9},{2,18},{10... | collective-permute-start | bytes 589832 | tf_op jit(solution)/shard_map/ppermute | solution.py:417
  70.9 1.4 collective-permute-start.12
  72.3 1.4 collective-permute-start.8
  73.7 1.2 collective-permute-start.9
  74.9 0.8 collective-permute-done.8
  75.7 2.0 %collective-permute-done.9 = bf16[16,16,128]{2,1,0:T(8,128)(2,1)S(1)} collective-permute-done((bf16[16,16,128]{2,1,0:T(8,128)(2,1)S(1)}, bf16[16,16,128]{2,1,0:T(8,128)(2,1)S(1)}, u32[]{:S(2)}, u32[]{:S(2)}) %collective-permute-start.9) | collective-permute-done | bytes 65568 | tf_op jit(solution)/shard_map/ppermute | solution.py:429
  77.8 6.3 %collective-permute-done.11 = bf16[16,48,128]{2,1,0:T(8,128)(2,1)S(1)} collective-permute-done((bf16[16,48,128]{2,1,0:T(8,128)(2,1)S(1)}, bf16[16,48,128]{2,1,0:T(8,128)(2,1)S(1)}, u32[]{:S(2)}, u32[]{:S(2)}) %collective-permute-start.11) | collective-permute-done | bytes 196640 | tf_op jit(solution)/shard_map/ppermute | solution.py:417
  84.1 4.7 %collective-permute-done.12 = bf16[16,48,128]{2,1,0:T(8,128)(2,1)S(1)} collective-permute-done((bf16[16,48,128]{2,1,0:T(8,128)(2,1)S(1)}, bf16[16,48,128]{2,1,0:T(8,128)(2,1)S(1)}, u32[]{:S(2)}, u32[]{:S(2)}) %collective-permute-start.12) | collective-permute-done | bytes 196640 | tf_op jit(solution)/shard_map/ppermute | solution.py:417
  89.0 1.5 %collective-permute-start.14 = (bf16[64,48,128]{2,1,0:T(8,128)(2,1)S(1)}, bf16[64,48,128]{2,1,0:T(8,128)(2,1)S(1)}, u32[]{:S(2)}, u32[]{:S(2)}) collective-permute-start(bf16[64,48,128]{2,1,0:T(8,128)(2,1)S(1)} %pad_maximum_fusion), channel_id=1, source_target_pairs={{0,2},{1,5},{2,0},{3,7},{4,6},{5,1},{6,4},{7,3},{8,10},{9,13},{10,... | collective-permute-start | bytes 2359304 | tf_op jit(solution)/shard_map/ppermute | solution.py:425
  90.5 1.1 collective-permute-start.18
  91.7 1.5 %collective-permute-start.25 = (bf16[64,16,128]{2,1,0:T(8,128)(2,1)S(1)}, bf16[64,16,128]{2,1,0:T(8,128)(2,1)S(1)}, u32[]{:S(2)}, u32[]{:S(2)}) collective-permute-start(bf16[64,16,128]{2,1,0:T(8,128)(2,1)S(1)} %pad_maximum_fusion.1), channel_id=1, source_target_pairs={{0,24},{8,0},{16,8},{24,16},{1,25},{9,1},{17,9},{25,17},{2,26},{10... | collective-permute-start | bytes 786440 | tf_op jit(solution)/shard_map/ppermute | solution.py:417
  93.2 4.3 %collective-permute-done.15 = bf16[64,16,128]{2,1,0:T(8,128)(2,1)S(1)} collective-permute-done((bf16[64,16,128]{2,1,0:T(8,128)(2,1)S(1)}, bf16[64,16,128]{2,1,0:T(8,128)(2,1)S(1)}, u32[]{:S(2)}, u32[]{:S(2)}) %collective-permute-start.15) | collective-permute-done | bytes 262176 | tf_op jit(solution)/shard_map/ppermute | solution.py:417
  97.5 2.9 %collective-permute-start.22 = (bf16[64,16,128]{2,1,0:T(8,128)(2,1)S(1)}, bf16[64,16,128]{2,1,0:T(8,128)(2,1)S(1)}, u32[]{:S(2)}, u32[]{:S(2)}) collective-permute-start(bf16[64,16,128]{2,1,0:T(8,128)(2,1)S(1)} %pad_maximum_fusion.1), channel_id=1, source_target_pairs={{0,1},{1,0},{2,3},{3,2},{4,5},{5,4},{6,7},{7,6},{8,9},{9,8},{10,11... | collective-permute-start | bytes 786440 | tf_op jit(solution)/shard_map/ppermute | solution.py:433
  100.5 12.6 %collective-permute-done.25 = bf16[64,16,128]{2,1,0:T(8,128)(2,1)S(1)} collective-permute-done((bf16[64,16,128]{2,1,0:T(8,128)(2,1)S(1)}, bf16[64,16,128]{2,1,0:T(8,128)(2,1)S(1)}, u32[]{:S(2)}, u32[]{:S(2)}) %collective-permute-start.25) | collective-permute-done | bytes 262176 | tf_op jit(solution)/shard_map/ppermute | solution.py:417
  113.1 0.5 collective-permute-start.26
  113.6 0.2 collective-permute-start.23
  113.8 0.3 collective-permute-start.24
  114.1 1.0 collective-permute-start.20
  115.2 4.8 %shard_map.78.refs_4_ = bf16[512,128,128]{2,1,0:T(8,128)(2,1)} custom-call(s32[1]{0:T(128)} %bitcast.11.half_ref, s32[2048]{0:T(1024)S(1)} %bitcast.70, f32[512]{0:T(512)S(1)} %bitcast.72, f32[1,128]{1,0:T(1,128)S(1)} %bitcast.79, bf16[1024,128]{1,0:T(8,128)(2,1)S(1)} %bitcast.61, bf16[1024,128]{1,0:T(8,128)(2,1)S(1)} %bitcast.63, ...), custom_call_target="tpu_custom_call" | custom-call | flops 4294967296 | bytes 4194304 | tf_op jit(solution)/shard_map/pallas_call | solution.py:392
  120.1 0.5 collective-permute-start.17
  120.7 4.8 %shard_map.79.refs_4_ = bf16[512,128,128]{2,1,0:T(8,128)(2,1)} custom-call(s32[1]{0:T(128)} %bitcast.half_ref, s32[2048]{0:T(1024)S(1)} %bitcast.71, f32[512]{0:T(512)S(1)} %bitcast.73, f32[1,128]{1,0:T(1,128)S(1)} %bitcast.80, bf16[1024,128]{1,0:T(8,128)(2,1)S(1)} %bitcast.65, bf16[1024,128]{1,0:T(8,128)(2,1)S(1)} %bitcast.68, ...), custom_call_target="tpu_custom_call", output_to_operand_aliasing={{}: (8, {})} | custom-call | flops 4294967296 | bytes 4194304 | tf_op jit(solution)/shard_map/pallas_call | solution.py:392
  125.5 0.8 collective-permute-start.21
  126.3 10.1 %shard_map.80.refs_4_ = bf16[512,128,128]{2,1,0:T(8,128)(2,1)} custom-call(s32[1]{0:T(128)} %bitcast.11.half_ref, s32[2048]{0:T(1024)S(1)} %bitcast.78, f32[512]{0:T(512)S(1)} %bitcast.74, f32[1,128]{1,0:T(1,128)S(1)} %bitcast.81, bf16[3072,128]{1,0:T(8,128)(2,1)S(1)} %bitcast.62, bf16[3072,128]{1,0:T(8,128)(2,1)S(1)} %bitcast.83, ...), custom_call_target="tpu_custom_call", output_to_operand_aliasing={{}: (8, {})} | custom-call | flops 12884901888 | bytes 12582912 | tf_op jit(solution)/shard_map/pallas_call | solution.py:392
  136.5 10.2 %shard_map.81 = bf16[512,128,128]{2,1,0:T(8,128)(2,1)} custom-call(s32[1]{0:T(128)} %bitcast.half_ref, s32[2048]{0:T(1024)S(1)} %bitcast.77, f32[512]{0:T(512)S(1)} %bitcast.75, f32[1,128]{1,0:T(1,128)S(1)} %bitcast.82, bf16[3072,128]{1,0:T(8,128)(2,1)S(1)} %bitcast.86, bf16[3072,128]{1,0:T(8,128)(2,1)S(1)} %bitcast.87, ...), custom_call_target="tpu_custom_call", output_to_operand_aliasing={{}: (8, {})} | custom-call | flops 12884901888 | bytes 12582912 | tf_op jit(solution)/shard_map/pallas_call | solution.py:392
  (58 shorter events, 1.1 us)
Async XLA Ops:
  0.0 0.8 copy-start.1
  0.8 0.7 copy-start.4
  10.3 9.9 %collective-permute-start = (bf16[8,144,128]{2,1,0:T(8,128)(2,1)S(1)}, bf16[8,144,128]{2,1,0:T(8,128)(2,1)S(1)}, u32[]{:S(2)}, u32[]{:S(2)}) collective-permute-start(bf16[8,144,128]{2,1,0:T(8,128)(2,1)S(1)} %get-tuple-element.28), channel_id=1, source_target_pairs={{0,8},{8,16},{16,24},{24,0},{1,9},{9,17},{17,25},{25,1},{2,10},{10... | collective-permute-start | bytes 884744 | tf_op jit(solution)/shard_map/ppermute | solution.py:417
  11.6 15.9 %copy-start.6 = (s32[128,3]{0,1:T(4,128)S(1)}, s32[128,3]{0,1:T(4,128)}, u32[]{:S(2)}) copy-start(s32[128,3]{0,1:T(4,128)} %param.11) | copy-start | bytes 4612
  11.6 16.0 %copy-start.7 = (f32[128]{0:T(128)S(1)}, f32[128]{0:T(128)}, u32[]{:S(2)}) copy-start(f32[128]{0:T(128)} %param.12) | copy-start | bytes 1540
  11.6 43.4 %copy-start.5 = (f32[256]{0:T(256)S(1)}, f32[256]{0:T(256)}, u32[]{:S(2)}) copy-start(f32[256]{0:T(256)} %param.9) | copy-start | bytes 3076
  11.6 53.7 %copy-start = (bf16[128,128]{1,0:T(8,128)(2,1)S(1)}, bf16[128,128]{1,0:T(8,128)(2,1)}, u32[]{:S(2)}) copy-start(bf16[128,128]{1,0:T(8,128)(2,1)} %mixing_ref.1) | copy-start | bytes 98308
  11.6 78.8 %copy-start.2 = (s32[2048,4]{0,1:T(4,128)S(1)}, s32[2048,4]{0,1:T(4,128)}, u32[]{:S(2)}) copy-start(s32[2048,4]{0,1:T(4,128)} %param.8) | copy-start | bytes 98308
  11.6 103.6 %copy-start.3 = (f32[128]{0:T(128)S(1)}, f32[128]{0:T(128)}, u32[]{:S(2)}) copy-start(f32[128]{0:T(128)} %param.13) | copy-start | bytes 1540
  20.2 16.5 %all-to-all-start = ((bf16[8,4,128,128]{3,2,1,0:T(8,128)(2,1)}), bf16[8,4,128,128]{3,2,1,0:T(8,128)(2,1)S(1)}, u32[]{:S(2)}, u32[]{:S(2)}) async-start(bf16[8,4,128,128]{3,2,1,0:T(8,128)(2,1)} %shard_map.74), calls=%async_computation | async-start | bytes 2097152 | tf_op jit(solution)/shard_map/all_to_all | solution.py:256
  25.0 19.6 %collective-permute-start.2 = (bf16[8,144,128]{2,1,0:T(8,128)(2,1)S(1)}, bf16[8,144,128]{2,1,0:T(8,128)(2,1)S(1)}, u32[]{:S(2)}, u32[]{:S(2)}) collective-permute-start(bf16[8,144,128]{2,1,0:T(8,128)(2,1)S(1)} %get-tuple-element.32), channel_id=1, source_target_pairs={{0,16},{8,24},{16,0},{24,8},{1,17},{9,25},{17,1},{25,9},{2,18},{10... | collective-permute-start | bytes 884744 | tf_op jit(solution)/shard_map/ppermute | solution.py:417
  25.9 23.3 %collective-permute-start.5 = (bf16[8,144,128]{2,1,0:T(8,128)(2,1)S(1)}, bf16[8,144,128]{2,1,0:T(8,128)(2,1)S(1)}, u32[]{:S(2)}, u32[]{:S(2)}) collective-permute-start(bf16[8,144,128]{2,1,0:T(8,128)(2,1)S(1)} %get-tuple-element.39), channel_id=1, source_target_pairs={{0,24},{8,0},{16,8},{24,16},{1,25},{9,1},{17,9},{25,17},{2,26},{10... | collective-permute-start | bytes 884744 | tf_op jit(solution)/shard_map/ppermute | solution.py:417
  36.8 10.7 %collective-permute-start.1 = (bf16[4,128,128]{2,1,0:T(8,128)(2,1)S(1)}, bf16[4,128,128]{2,1,0:T(8,128)(2,1)S(1)}, u32[]{:S(2)}, u32[]{:S(2)}) collective-permute-start(bf16[4,128,128]{2,1,0:T(8,128)(2,1)S(1)} %get-tuple-element.31), channel_id=1, source_target_pairs={{0,8},{8,16},{16,24},{24,0},{1,9},{9,17},{17,25},{25,1},{2,10},{10... | collective-permute-start | bytes 393224 | tf_op jit(solution)/shard_map/ppermute | solution.py:417
  50.1 15.2 %all-to-all-start.1 = ((bf16[8,1,144,128]{3,2,1,0:T(8,128)(2,1)}), bf16[8,1,144,128]{3,2,1,0:T(8,128)(2,1)S(1)}, u32[]{:S(2)}, u32[]{:S(2)}) async-start(bf16[8,1,144,128]{3,2,1,0:T(8,128)(2,1)} %shard_map.76), calls=%async_computation.1 | async-start | bytes 589824 | tf_op jit(solution)/shard_map/all_to_all | solution.py:261
  55.1 10.2 %collective-permute-start.3 = (bf16[4,128,128]{2,1,0:T(8,128)(2,1)S(1)}, bf16[4,128,128]{2,1,0:T(8,128)(2,1)S(1)}, u32[]{:S(2)}, u32[]{:S(2)}) collective-permute-start(bf16[4,128,128]{2,1,0:T(8,128)(2,1)S(1)} %get-tuple-element.34), channel_id=1, source_target_pairs={{0,16},{8,24},{16,0},{24,8},{1,17},{9,25},{17,1},{25,9},{2,18},{10... | collective-permute-start | bytes 393224 | tf_op jit(solution)/shard_map/ppermute | solution.py:417
  56.5 8.8 %collective-permute-start.4 = (bf16[4,128,128]{2,1,0:T(8,128)(2,1)S(1)}, bf16[4,128,128]{2,1,0:T(8,128)(2,1)S(1)}, u32[]{:S(2)}, u32[]{:S(2)}) collective-permute-start(bf16[4,128,128]{2,1,0:T(8,128)(2,1)S(1)} %get-tuple-element.35), channel_id=1, source_target_pairs={{0,24},{8,0},{16,8},{24,16},{1,25},{9,1},{17,9},{25,17},{2,26},{10... | collective-permute-start | bytes 393224 | tf_op jit(solution)/shard_map/ppermute | solution.py:417
  65.9 1.6 %collective-permute-start.6 = (bf16[8,64,128]{2,1,0:T(8,128)(2,1)S(1)}, bf16[8,64,128]{2,1,0:T(8,128)(2,1)S(1)}, u32[]{:S(2)}, u32[]{:S(2)}) collective-permute-start(bf16[8,64,128]{2,1,0:T(8,128)(2,1)S(1)} %get-tuple-element.41), channel_id=1, source_target_pairs={{0,1},{1,0},{2,3},{3,2},{4,5},{5,4},{6,7},{7,6},{8,9},{9,8},{10,11... | collective-permute-start | bytes 393224 | tf_op jit(solution)/shard_map/ppermute | solution.py:433
  67.5 6.2 %collective-permute-start.7 = (bf16[16,16,128]{2,1,0:T(8,128)(2,1)S(1)}, bf16[16,16,128]{2,1,0:T(8,128)(2,1)S(1)}, u32[]{:S(2)}, u32[]{:S(2)}) collective-permute-start(bf16[16,16,128]{2,1,0:T(8,128)(2,1)S(1)} %slice.18), channel_id=1, source_target_pairs={{0,2},{1,5},{2,0},{3,7},{4,6},{5,1},{6,4},{7,3},{8,10},{9,13},{10,... | collective-permute-start | bytes 196616 | tf_op jit(solution)/shard_map/ppermute | solution.py:425
  67.7 10.1 %collective-permute-start.10 = (bf16[16,48,128]{2,1,0:T(8,128)(2,1)S(1)}, bf16[16,48,128]{2,1,0:T(8,128)(2,1)S(1)}, u32[]{:S(2)}, u32[]{:S(2)}) collective-permute-start(bf16[16,48,128]{2,1,0:T(8,128)(2,1)S(1)} %slice.19), channel_id=1, source_target_pairs={{0,8},{8,16},{16,24},{24,0},{1,9},{9,17},{17,25},{25,1},{2,10},{10... | collective-permute-start | bytes 589832 | tf_op jit(solution)/shard_map/ppermute | solution.py:417
  67.8 16.3 %collective-permute-start.11 = (bf16[16,48,128]{2,1,0:T(8,128)(2,1)S(1)}, bf16[16,48,128]{2,1,0:T(8,128)(2,1)S(1)}, u32[]{:S(2)}, u32[]{:S(2)}) collective-permute-start(bf16[16,48,128]{2,1,0:T(8,128)(2,1)S(1)} %slice.19), channel_id=1, source_target_pairs={{0,16},{8,24},{16,0},{24,8},{1,17},{9,25},{17,1},{25,9},{2,18},{10... | collective-permute-start | bytes 589832 | tf_op jit(solution)/shard_map/ppermute | solution.py:417
  70.9 17.9 %collective-permute-start.12 = (bf16[16,48,128]{2,1,0:T(8,128)(2,1)S(1)}, bf16[16,48,128]{2,1,0:T(8,128)(2,1)S(1)}, u32[]{:S(2)}, u32[]{:S(2)}) collective-permute-start(bf16[16,48,128]{2,1,0:T(8,128)(2,1)S(1)} %slice.19), channel_id=1, source_target_pairs={{0,24},{8,0},{16,8},{24,16},{1,25},{9,1},{17,9},{25,17},{2,26},{10... | collective-permute-start | bytes 589832 | tf_op jit(solution)/shard_map/ppermute | solution.py:417
  72.3 3.4 %collective-permute-start.8 = (bf16[16,16,128]{2,1,0:T(8,128)(2,1)S(1)}, bf16[16,16,128]{2,1,0:T(8,128)(2,1)S(1)}, u32[]{:S(2)}, u32[]{:S(2)}) collective-permute-start(bf16[16,16,128]{2,1,0:T(8,128)(2,1)S(1)} %slice.18), channel_id=1, source_target_pairs={{0,4},{1,3},{2,6},{3,1},{4,0},{5,7},{6,2},{7,5},{8,12},{9,11},{10,... | collective-permute-start | bytes 196616 | tf_op jit(solution)/shard_map/ppermute | solution.py:425
  73.7 4.0 %collective-permute-start.9 = (bf16[16,16,128]{2,1,0:T(8,128)(2,1)S(1)}, bf16[16,16,128]{2,1,0:T(8,128)(2,1)S(1)}, u32[]{:S(2)}, u32[]{:S(2)}) collective-permute-start(bf16[16,16,128]{2,1,0:T(8,128)(2,1)S(1)} %slice.18), channel_id=1, source_target_pairs={{0,6},{1,7},{2,4},{3,5},{4,2},{5,3},{6,0},{7,1},{8,14},{9,15},{10,... | collective-permute-start | bytes 196616 | tf_op jit(solution)/shard_map/ppermute | solution.py:429
  89.0 24.7 %collective-permute-start.14 = (bf16[64,48,128]{2,1,0:T(8,128)(2,1)S(1)}, bf16[64,48,128]{2,1,0:T(8,128)(2,1)S(1)}, u32[]{:S(2)}, u32[]{:S(2)}) collective-permute-start(bf16[64,48,128]{2,1,0:T(8,128)(2,1)S(1)} %pad_maximum_fusion), channel_id=1, source_target_pairs={{0,2},{1,5},{2,0},{3,7},{4,6},{5,1},{6,4},{7,3},{8,10},{9,13},{10,... | collective-permute-start | bytes 2359304 | tf_op jit(solution)/shard_map/ppermute | solution.py:425
  90.5 7.1 %collective-permute-start.15 = (bf16[64,16,128]{2,1,0:T(8,128)(2,1)S(1)}, bf16[64,16,128]{2,1,0:T(8,128)(2,1)S(1)}, u32[]{:S(2)}, u32[]{:S(2)}) collective-permute-start(bf16[64,16,128]{2,1,0:T(8,128)(2,1)S(1)} %pad_maximum_fusion.1), channel_id=1, source_target_pairs={{0,8},{8,16},{16,24},{24,0},{1,9},{9,17},{17,25},{25,1},{2,10},{10... | collective-permute-start | bytes 786440 | tf_op jit(solution)/shard_map/ppermute | solution.py:417
  90.5 29.6 %collective-permute-start.18 = (bf16[64,48,128]{2,1,0:T(8,128)(2,1)S(1)}, bf16[64,48,128]{2,1,0:T(8,128)(2,1)S(1)}, u32[]{:S(2)}, u32[]{:S(2)}) collective-permute-start(bf16[64,48,128]{2,1,0:T(8,128)(2,1)S(1)} %pad_maximum_fusion), channel_id=1, source_target_pairs={{0,4},{1,3},{2,6},{3,1},{4,0},{5,7},{6,2},{7,5},{8,12},{9,11},{10,... | collective-permute-start | bytes 2359304 | tf_op jit(solution)/shard_map/ppermute | solution.py:425
  91.6 22.0 %collective-permute-start.16 = (bf16[64,16,128]{2,1,0:T(8,128)(2,1)S(1)}, bf16[64,16,128]{2,1,0:T(8,128)(2,1)S(1)}, u32[]{:S(2)}, u32[]{:S(2)}) collective-permute-start(bf16[64,16,128]{2,1,0:T(8,128)(2,1)S(1)} %pad_maximum_fusion.1), channel_id=1, source_target_pairs={{0,16},{8,24},{16,0},{24,8},{1,17},{9,25},{17,1},{25,9},{2,18},{10... | collective-permute-start | bytes 786440 | tf_op jit(solution)/shard_map/ppermute | solution.py:417
  91.7 21.4 %collective-permute-start.25 = (bf16[64,16,128]{2,1,0:T(8,128)(2,1)S(1)}, bf16[64,16,128]{2,1,0:T(8,128)(2,1)S(1)}, u32[]{:S(2)}, u32[]{:S(2)}) collective-permute-start(bf16[64,16,128]{2,1,0:T(8,128)(2,1)S(1)} %pad_maximum_fusion.1), channel_id=1, source_target_pairs={{0,24},{8,0},{16,8},{24,16},{1,25},{9,1},{17,9},{25,17},{2,26},{10... | collective-permute-start | bytes 786440 | tf_op jit(solution)/shard_map/ppermute | solution.py:417
  97.5 16.6 %collective-permute-start.22 = (bf16[64,16,128]{2,1,0:T(8,128)(2,1)S(1)}, bf16[64,16,128]{2,1,0:T(8,128)(2,1)S(1)}, u32[]{:S(2)}, u32[]{:S(2)}) collective-permute-start(bf16[64,16,128]{2,1,0:T(8,128)(2,1)S(1)} %pad_maximum_fusion.1), channel_id=1, source_target_pairs={{0,1},{1,0},{2,3},{3,2},{4,5},{5,4},{6,7},{7,6},{8,9},{9,8},{10,11... | collective-permute-start | bytes 786440 | tf_op jit(solution)/shard_map/ppermute | solution.py:433
  113.1 6.9 %collective-permute-start.26 = (bf16[64,16,128]{2,1,0:T(8,128)(2,1)S(1)}, bf16[64,16,128]{2,1,0:T(8,128)(2,1)S(1)}, u32[]{:S(2)}, u32[]{:S(2)}) collective-permute-start(bf16[64,16,128]{2,1,0:T(8,128)(2,1)S(1)} %collective-permute-done.25), channel_id=1, source_target_pairs={{0,1},{1,0},{2,3},{3,2},{4,5},{5,4},{6,7},{7,6},{8,9},{9,8},{10,11... | collective-permute-start | bytes 786440 | tf_op jit(solution)/shard_map/ppermute | solution.py:433
  113.6 7.0 %collective-permute-start.23 = (bf16[64,16,128]{2,1,0:T(8,128)(2,1)S(1)}, bf16[64,16,128]{2,1,0:T(8,128)(2,1)S(1)}, u32[]{:S(2)}, u32[]{:S(2)}) collective-permute-start(bf16[64,16,128]{2,1,0:T(8,128)(2,1)S(1)} %collective-permute-done.15), channel_id=1, source_target_pairs={{0,1},{1,0},{2,3},{3,2},{4,5},{5,4},{6,7},{7,6},{8,9},{9,8},{10,11... | collective-permute-start | bytes 786440 | tf_op jit(solution)/shard_map/ppermute | solution.py:433
  113.8 6.9 %collective-permute-start.24 = (bf16[64,16,128]{2,1,0:T(8,128)(2,1)S(1)}, bf16[64,16,128]{2,1,0:T(8,128)(2,1)S(1)}, u32[]{:S(2)}, u32[]{:S(2)}) collective-permute-start(bf16[64,16,128]{2,1,0:T(8,128)(2,1)S(1)} %collective-permute-done.16), channel_id=1, source_target_pairs={{0,1},{1,0},{2,3},{3,2},{4,5},{5,4},{6,7},{7,6},{8,9},{9,8},{10,11... | collective-permute-start | bytes 786440 | tf_op jit(solution)/shard_map/ppermute | solution.py:433
  114.1 11.4 %collective-permute-start.20 = (bf16[64,48,128]{2,1,0:T(8,128)(2,1)S(1)}, bf16[64,48,128]{2,1,0:T(8,128)(2,1)S(1)}, u32[]{:S(2)}, u32[]{:S(2)}) collective-permute-start(bf16[64,48,128]{2,1,0:T(8,128)(2,1)S(1)} %collective-permute-done.14), channel_id=1, source_target_pairs={{0,4},{1,3},{2,6},{3,1},{4,0},{5,7},{6,2},{7,5},{8,12},{9,11},{10,... | collective-permute-start | bytes 2359304 | tf_op jit(solution)/shard_map/ppermute | solution.py:425
  120.0 16.5 %collective-permute-start.13 = (bf16[64,48,128]{2,1,0:T(8,128)(2,1)S(1)}, bf16[64,48,128]{2,1,0:T(8,128)(2,1)S(1)}, u32[]{:S(2)}, u32[]{:S(2)}) collective-permute-start(bf16[64,48,128]{2,1,0:T(8,128)(2,1)S(1)} %pad_maximum_fusion), channel_id=1, source_target_pairs={{0,1},{1,0},{2,3},{3,2},{4,5},{5,4},{6,7},{7,6},{8,9},{9,8},{10,11... | collective-permute-start | bytes 2359304 | tf_op jit(solution)/shard_map/ppermute | solution.py:433
  120.1 16.4 %collective-permute-start.17 = (bf16[64,48,128]{2,1,0:T(8,128)(2,1)S(1)}, bf16[64,48,128]{2,1,0:T(8,128)(2,1)S(1)}, u32[]{:S(2)}, u32[]{:S(2)}) collective-permute-start(bf16[64,48,128]{2,1,0:T(8,128)(2,1)S(1)} %collective-permute-done.14), channel_id=1, source_target_pairs={{0,1},{1,0},{2,3},{3,2},{4,5},{5,4},{6,7},{7,6},{8,9},{9,8},{10,11... | collective-permute-start | bytes 2359304 | tf_op jit(solution)/shard_map/ppermute | solution.py:433
  120.6 15.9 %collective-permute-start.19 = (bf16[64,48,128]{2,1,0:T(8,128)(2,1)S(1)}, bf16[64,48,128]{2,1,0:T(8,128)(2,1)S(1)}, u32[]{:S(2)}, u32[]{:S(2)}) collective-permute-start(bf16[64,48,128]{2,1,0:T(8,128)(2,1)S(1)} %collective-permute-done.18), channel_id=1, source_target_pairs={{0,1},{1,0},{2,3},{3,2},{4,5},{5,4},{6,7},{7,6},{8,9},{9,8},{10,11... | collective-permute-start | bytes 2359304 | tf_op jit(solution)/shard_map/ppermute | solution.py:433
  125.5 11.0 %collective-permute-start.21 = (bf16[64,48,128]{2,1,0:T(8,128)(2,1)S(1)}, bf16[64,48,128]{2,1,0:T(8,128)(2,1)S(1)}, u32[]{:S(2)}, u32[]{:S(2)}) collective-permute-start(bf16[64,48,128]{2,1,0:T(8,128)(2,1)S(1)} %collective-permute-done.20), channel_id=1, source_target_pairs={{0,1},{1,0},{2,3},{3,2},{4,5},{5,4},{6,7},{7,6},{8,9},{9,8},{10,11... | collective-permute-start | bytes 2359304 | tf_op jit(solution)/shard_map/ppermute | solution.py:433

commit v11 on v8

--- a/solution.py
+++ b/solution.py
@@ -252,6 +252,7 @@
     seconds, roots, weighted = second_sums(line, cells, edges_t, edge_weight, plan)
     seconds = [shifted(part, shift) if shift else part for shift, part in enumerate(seconds)]
     first = first_sums(line, cells, weighted, plan)
+    first, *seconds[1::2] = lax.optimization_barrier((first, *seconds[1::2]))
     first = lax.all_to_all(first, SQUARE, split_axis=0, concat_axis=0, tiled=True)
     second = fold(fold_second_kernel, plan, seconds, [(8, plan.rest, plan.second_rows, lanes)])[0]
     firsts = fold(fold_first_kernel, plan, [first], [(4, plan.first_rows, lanes)] * plan.line)
@@ -312,27 +313,31 @@
     )(weight_rows, mixing, matrix, *firsts, second)
 
 
-def spread_kernel(n_long, n_short, half_ref, places_ref, root_ref, bias_ref, *refs):
-    longs = refs[:n_long]
-    shorts = refs[n_long : n_long + n_short]
+def spread_kernel(n_long, n_short, core_ref, places_ref, root_ref, bias_ref, *refs):
+    pieces = refs[: 2 * (n_long + n_short)]
     out_ref, table_ref, ring_ref, sems, ring_sems = refs[-5:]
     slots, rows, zones, lanes = ring_ref.shape
     steps = out_ref.shape[0] // rows
-    half = half_ref[0]
-
+    half = zones // 2
     copies = []
 
     def bring(source, first, start):
-        place = table_ref.at[pl.ds(first, source.shape[0]), pl.ds(start, source.shape[1]), :]
+        size, height = source.shape[0], source.shape[1]
+        place = table_ref.at[pl.ds(first, size), pl.ds(pl.multiple_of(start, 16), height), :]
         copies.append(pltpu.make_async_copy(source, place, sems.at[len(copies)]))
 
-    split = longs[0].shape[1]
-    size = shorts[0].shape[0] // n_long
-    for square, source in enumerate(longs):
-        bring(source, square * n_short * size, 0)
-    for shift, source in enumerate(shorts):
-        for square in range(n_long):
-            bring(source.at[pl.ds(square * size, size)], (square * n_short + shift) * size, split)
+    for side in range(2):
+        core = core_ref[0] if side == 0 else 1 - core_ref[0]
+        longs = pieces[side * (n_long + n_short) :][:n_long]
+        shorts = pieces[side * (n_long + n_short) + n_long :][:n_short]
+        split = longs[0].shape[1]
+        size = shorts[0].shape[0] // n_long
+        for turn, source in enumerate(longs):
+            square = turn if turn in (0, 3) else turn + core * (3 - 2 * turn)
+            bring(source, square * (n_short * size), core * half)
+        for shift, source in enumerate(shorts):
+            for square in range(n_long):
+                bring(source.at[pl.ds(square * size, size)], (square * n_short + shift) * size, core * half + split)
     for copy in copies:
         copy.start()
     for copy in copies:
@@ -341,12 +346,11 @@
     bias = bias_ref[...]
     count = places_ref.shape[0]
     tile = 16
-    batch = min(8, rows)
+    batch = min(4, rows)
     tiles = zones // tile
 
     def leaving(step, slot):
-        place = out_ref.at[pl.ds(step * rows, rows), pl.ds(pl.multiple_of(half * zones, zones), zones), :]
-        return pltpu.make_async_copy(ring_ref.at[slot], place, ring_sems.at[slot])
+        return pltpu.make_async_copy(ring_ref.at[slot], out_ref.at[pl.ds(step * rows, rows)], ring_sems.at[slot])
 
     def one_step(step, carry):
         slot = lax.rem(step, slots)
@@ -362,9 +366,9 @@
                 scale = root_ref[0, at]
                 spots = [places_ref[j, at] for j in range(count)]
                 for first in range(0, zones, tile):
-                    pieces = [table_ref[spot, first : first + tile, :] for spot in spots]
-                    pieces = [(a + b).astype(F32) for a, b in zip(pieces[0::2], pieces[1::2])]
-                    total = sum(pieces[1:], pieces[0])
+                    parts = [table_ref[spot, first : first + tile, :] for spot in spots]
+                    parts = [(a + b).astype(F32) for a, b in zip(parts[0::2], parts[1::2])]
+                    total = sum(parts[1:], parts[0])
                     values.append(jnp.maximum((total * scale + bias).astype(BF16), BF16(0.0)))
             for n, value in enumerate(values):
                 start = n % tiles * tile
@@ -380,39 +384,33 @@
         leaving(step, step % slots).wait()
 
 
-def spread(half, places, root, bias, longs, shorts, before=None):
+def spread(core, places, root, bias, near, far):
     anchors = places.shape[1]
     lanes = bias.shape[1]
-    zones = longs[0].shape[1] + shorts[0].shape[1]
+    longs, shorts = near
+    zones = 2 * (longs[0].shape[1] + shorts[0].shape[1])
+    edges = len(longs) * longs[0].shape[0]
     rows = min(16, anchors // 8)
     slots = min(8, anchors // rows)
     smem = pl.BlockSpec(memory_space=pltpu.SMEM)
     anywhere = pl.BlockSpec(memory_space=pltpu.HBM)
-    pieces = longs + shorts
-    operands = [half, places, root, bias] + pieces
-    specs = [smem, smem, smem, pl.BlockSpec(memory_space=pltpu.VMEM)] + [anywhere] * len(pieces)
-    aliases = {}
-    if before is not None:
-        aliases = {len(operands): 0}
-        operands.append(before)
-        specs.append(anywhere)
+    pieces = longs + shorts + far[0] + far[1]
     return pl.pallas_call(
         functools.partial(spread_kernel, len(longs), len(shorts)),
-        in_specs=specs,
+        in_specs=[smem, smem, smem, pl.BlockSpec(memory_space=pltpu.VMEM)] + [anywhere] * len(pieces),
         out_specs=anywhere,
-        out_shape=jax.ShapeDtypeStruct((anchors, 2 * zones, lanes), BF16),
+        out_shape=jax.ShapeDtypeStruct((anchors, zones, lanes), BF16),
         scratch_shapes=[
-            pltpu.VMEM((len(longs) * longs[0].shape[0], zones, lanes), BF16),
+            pltpu.VMEM((edges, zones, lanes), BF16),
             pltpu.VMEM((slots, rows, zones, lanes), BF16),
-            pltpu.SemaphoreType.DMA((len(longs) * (1 + len(shorts)),)),
+            pltpu.SemaphoreType.DMA((2 * len(longs) * (1 + len(shorts)),)),
             pltpu.SemaphoreType.DMA((slots,)),
         ],
-        input_output_aliases=aliases,
-        compiler_params=pltpu.CompilerParams(vmem_limit_bytes=24 * 1024 * 1024),
+        compiler_params=pltpu.CompilerParams(vmem_limit_bytes=32 * 1024 * 1024),
         cost_estimate=pl.CostEstimate(
             flops=4096 * anchors * zones * lanes, bytes_accessed=4 * anchors * zones * lanes, transcendentals=0
         ),
-    )(*operands)
+    )(core, places, root, bias, *pieces)
 
 
 LINE = ("slow", "rest")
@@ -440,33 +438,36 @@
     return lax.ppermute(x, "core", [(0, 1), (1, 0)])
 
 
-def gather_table(keep, give):
+def gather_table(keep, give, core):
     size = lax.axis_size(LINE)
-    block = jnp.concatenate([keep, swapped(give)], axis=0)
+    got = swapped(give)
+    block = jnp.concatenate([jnp.where(core == 0, keep, got), jnp.where(core == 0, got, keep)], axis=0)
     split = block.shape[1] * 3 // 4
     long, short = block[:, :split], block[:, split:]
     line = [long] + [shifted(long, k) for k in range(1, size)]
-    short = jnp.concatenate([short, crossed(short, 0), crossed(short, 1), masked(short, 6)], axis=0)
+    short = jnp.concatenate([short, masked(short, 2), masked(short, 4), masked(short, 6)], axis=0)
     long = jnp.concatenate(line, axis=0)
     short, long = lax.optimization_barrier((short, long))
     first = crossed(long, 0)
     second = crossed(long, 1)
     shorts = [short] + [shifted(short, k) for k in range(1, size)]
-    first, *shorts[1:-1] = lax.optimization_barrier((first, *shorts[1:-1]))
+    far_long, far_short = swapped(long), swapped(short)
+    first, far_long, far_short, *shorts[1:-1] = lax.optimization_barrier((first, far_long, far_short, *shorts[1:-1]))
     both = crossed(first, 1)
-    return [long, first, second, both], shorts
-
-
-def places_of(ids, core, own):
+    far_first, far_second = swapped(first), swapped(second)
+    far_shorts = [far_short] + [swapped(x) for x in shorts[1:]]
+    both, far_first, far_second, *far_shorts = lax.optimization_barrier((both, far_first, far_second, *far_shorts))
+    return ([long, first, second, both], shorts), ([far_long, far_first, far_second, swapped(both)], far_shorts)
+
+
+def places_of(ids, own):
     rest, size = lax.axis_size("rest"), lax.axis_size(LINE)
     owner = ids // own
-    slot = jnp.where(owner % 2 == core, 0, own) + ids % own
     near = jnp.bitwise_xor(owner // 2 % 2, lax.axis_index("near"))
     mid = jnp.bitwise_xor(owner // (4 * rest) % 2, lax.axis_index("mid"))
     line = owner // (8 * rest) * rest + owner // 4 % rest
     line = lax.rem(lax.axis_index(LINE) - line + size, size)
-    square = jnp.where(core == 0, 2 * mid + near, 2 * near + mid)
-    return (square * size + line) * (2 * own) + slot
+    return ((2 * mid + near) * size + line) * (2 * own) + owner % 2 * own + ids % own
 
 
 def relative_columns(matrix):
@@ -493,16 +494,12 @@
     half = matrix.shape[0] // 2
     matrix = jnp.where(core == 0, matrix, jnp.concatenate([matrix[half:], matrix[:half]], axis=0))
     keep, give = table_rows(firsts, second, weight_rows, mixing, matrix, plan)
-    longs, shorts = gather_table(keep, give)
+    near, far = gather_table(keep, give, core)
     rows = anchor_edges.shape[0] // n_dst
     start = lax.axis_index(("rest", "near", "core")) * rows
     ids = lax.dynamic_slice_in_dim(edges_t, start, rows, 1)
     own_root = lax.dynamic_slice_in_dim(roots, start, rows, 1)
-    bias = out_bias[None, :]
-    other = 1 - core
-    result = spread(core[None], places_of(ids, core, own), own_root, bias, longs, shorts)
-    longs, shorts = [swapped(x) for x in longs], [swapped(x) for x in shorts]
-    return spread(other[None], places_of(ids, other, own), own_root, bias, longs, shorts, result)
+    return spread(core[None], places_of(ids, own), own_root, out_bias[None, :], near, far)
 
 
 def solution(mesh):

time: 150 us -> 156 us (1.040)
  the two profiles are of different devices: /device:TPU:1 before, /device:TPU:0 now
where the time goes in v11:
time: 156 us
  waiting for transfers between devices  70.7 us (45%)
  Pallas kernels  34.9 us (22%)
  starting transfers between devices  31 us (20%)
  local copies, waits for them, and re-layouts  17.2 us (11%)
    ppermute x12, waiting for transfers between devices, shifted(): lax.ppermute(x, LINE, [(i, (i + amount) % size) for i in range(size)])  59.2 us
    pallas_call x2, Pallas kernels, half_sums(): pl.pallas_call(functools.partial(kernel, plan, begin, half, pitch), grid=...  17.3 us
    unnamed x50, local copies, waits for them, and re-layouts  17 us
    pallas_call x1, Pallas kernels, spread(): pl.pallas_call(functools.partial(spread_kernel, len(longs), len(shorts)),...  16 us
    ppermute x12, starting transfers between devices, shifted(): lax.ppermute(x, LINE, [(i, (i + amount) % size) for i in range(size)])  15.2 us
    ppermute x9, waiting for transfers between devices, swapped(): return lax.ppermute(x, 'core', [(0, 1), (1, 0)])  4.46 us
    ppermute x3, starting transfers between devices, masked(): lax.ppermute(x, SQUARE, [(device, device ^ mask) for device in range(8)])  3.92 us
    ppermute x3, waiting for transfers between devices, masked(): lax.ppermute(x, SQUARE, [(device, device ^ mask) for device in range(8)])  3.89 us
  transfers between devices with their start and end apart: 29, of which 14 were waited for; matrix products, arithmetic and copies ran while one was open for 1% of the time, Pallas kernels for 6%

profile of v11, /device:TPU:0, one launch (start us, length us, event | category | flops | bytes accessed | tf_op | source)
XLA Modules:
  0.0 155.6 jit_solution(6145725931535226335)
XLA Ops:
  0.0 0.8 copy-done.1
  1.4 8.8 %shard_map.73 = (bf16[8,144,128]{2,1,0:T(8,128)(2,1)S(1)}, bf16[8,144,128]{2,1,0:T(8,128)(2,1)S(1)}, bf16[8,144,128]{2,1,0:T(8,128)(2,1)S(1)}, bf16[8,144,128]{2...) custom-call(s32[1]{0:T(128)} %bitcast.2.line_ref, s32[4,2048]{1,0:T(4,128)S(1)} %bitcast.23, ...), custom_call_target="tpu_custom_call" | custom-call | flops 8589934592 | bytes 16777216 | tf_op jit(solution)/shard_map/pallas_call | solution.py:171
  10.3 3.1 %collective-permute-start = (bf16[8,144,128]{2,1,0:T(8,128)(2,1)S(1)}, bf16[8,144,128]{2,1,0:T(8,128)(2,1)S(1)}, u32[]{:S(2)}, u32[]{:S(2)}) collective-permute-start(bf16[8,144,128]{2,1,0:T(8,128)(2,1)S(1)} %get-tuple-element.36), channel_id=1, source_target_pairs={{0,8},{8,16},{16,24},{24,0},{1,9},{9,17},{17,25},{25,1},{2,10},{10... | collective-permute-start | bytes 884744 | tf_op jit(solution)/shard_map/ppermute | solution.py:422
  13.3 2.1 %collective-permute-start.1 = (bf16[8,144,128]{2,1,0:T(8,128)(2,1)S(1)}, bf16[8,144,128]{2,1,0:T(8,128)(2,1)S(1)}, u32[]{:S(2)}, u32[]{:S(2)}) collective-permute-start(bf16[8,144,128]{2,1,0:T(8,128)(2,1)S(1)} %get-tuple-element.37), channel_id=1, source_target_pairs={{0,24},{8,0},{16,8},{24,16},{1,25},{9,1},{17,9},{25,17},{2,26},{10... | collective-permute-start | bytes 884744 | tf_op jit(solution)/shard_map/ppermute | solution.py:422
  15.4 8.5 %shard_map.74 = bf16[8,4,128,128]{3,2,1,0:T(8,128)(2,1)} custom-call(s32[1]{0:T(128)} %bitcast.2.line_ref, bf16[256,2048]{1,0:T(8,128)(2,1)S(1)} %get-tuple-element.35.weighted_ref, bf16[2048,32,128]{2,1,0:T(8,128)(2,1)} %cells_ref.3), custom_call_target="tpu_custom_call" | custom-call | flops 8589934592 | bytes 16777216 | tf_op jit(solution)/shard_map/pallas_call | solution.py:171
  24.0 4.2 %collective-permute-done.1.refs_3_ = bf16[8,144,128]{2,1,0:T(8,128)(2,1)S(1)} collective-permute-done((bf16[8,144,128]{2,1,0:T(8,128)(2,1)S(1)}, bf16[8,144,128]{2,1,0:T(8,128)(2,1)S(1)}, u32[]{:S(2)}, u32[]{:S(2)}) %collective-permute-start.1) | collective-permute-done | bytes 294944 | tf_op jit(solution)/shard_map/ppermute | solution.py:422
  28.1 3.7 %all-to-all-start = ((bf16[8,4,128,128]{3,2,1,0:T(8,128)(2,1)}), bf16[8,4,128,128]{3,2,1,0:T(8,128)(2,1)S(1)}, u32[]{:S(2)}, u32[]{:S(2)}) async-start(bf16[8,4,128,128]{3,2,1,0:T(8,128)(2,1)} %shard_map.74), calls=%async_computation | async-start | bytes 2097152 | tf_op jit(solution)/shard_map/all_to_all | solution.py:256
  31.8 1.3 collective-permute-start.5
  33.8 14.7 %collective-permute-done.5.refs_2_ = bf16[8,144,128]{2,1,0:T(8,128)(2,1)S(1)} collective-permute-done((bf16[8,144,128]{2,1,0:T(8,128)(2,1)S(1)}, bf16[8,144,128]{2,1,0:T(8,128)(2,1)S(1)}, u32[]{:S(2)}, u32[]{:S(2)}) %collective-permute-start.5) | collective-permute-done | bytes 294944 | tf_op jit(solution)/shard_map/ppermute | solution.py:422
  48.5 0.9 shard_map.76
  49.3 3.8 %all-to-all-start.1 = ((bf16[8,1,144,128]{3,2,1,0:T(8,128)(2,1)}), bf16[8,1,144,128]{3,2,1,0:T(8,128)(2,1)S(1)}, u32[]{:S(2)}, u32[]{:S(2)}) async-start(bf16[8,1,144,128]{3,2,1,0:T(8,128)(2,1)} %shard_map.76), calls=%async_computation.1 | async-start | bytes 589824 | tf_op jit(solution)/shard_map/all_to_all | solution.py:260
  53.5 2.7 %collective-permute-start.3 = (bf16[4,128,128]{2,1,0:T(8,128)(2,1)S(1)}, bf16[4,128,128]{2,1,0:T(8,128)(2,1)S(1)}, u32[]{:S(2)}, u32[]{:S(2)}) collective-permute-start(bf16[4,128,128]{2,1,0:T(8,128)(2,1)S(1)} %get-tuple-element.41), channel_id=1, source_target_pairs={{0,16},{8,24},{16,0},{24,8},{1,17},{9,25},{17,1},{25,9},{2,18},{10... | collective-permute-start | bytes 393224 | tf_op jit(solution)/shard_map/ppermute | solution.py:422
  56.2 1.1 collective-permute-start.4
  57.3 3.2 %all-to-all-done.1.refs_4_ = bf16[8,1,144,128]{3,2,1,0:T(8,128)(2,1)S(1)} async-done(((bf16[8,1,144,128]{3,2,1,0:T(8,128)(2,1)}), bf16[8,1,144,128]{3,2,1,0:T(8,128)(2,1)S(1)}, u32[]{:S(2)}, u32[]{:S(2)}) %all-to-all-start.1) | async-done | bytes 294944 | tf_op jit(solution)/shard_map/all_to_all | solution.py:260
  60.5 1.2 collective-permute-done.2.refs_1_
  61.7 4.7 %collective-permute-done.3.refs_2_ = bf16[4,128,128]{2,1,0:T(8,128)(2,1)S(1)} collective-permute-done((bf16[4,128,128]{2,1,0:T(8,128)(2,1)S(1)}, bf16[4,128,128]{2,1,0:T(8,128)(2,1)S(1)}, u32[]{:S(2)}, u32[]{:S(2)}) %collective-permute-start.3) | collective-permute-done | bytes 131104 | tf_op jit(solution)/shard_map/ppermute | solution.py:422
  67.1 1.3 collective-permute-done.6
  68.5 3.0 %collective-permute-start.9 = (bf16[16,16,128]{2,1,0:T(8,128)(2,1)S(1)}, bf16[16,16,128]{2,1,0:T(8,128)(2,1)S(1)}, u32[]{:S(2)}, u32[]{:S(2)}) collective-permute-start(bf16[16,16,128]{2,1,0:T(8,128)(2,1)S(1)} %pad_maximum_fusion.3), channel_id=1, source_target_pairs={{0,6},{1,7},{2,4},{3,5},{4,2},{5,3},{6,0},{7,1},{8,14},{9,15},{10,... | collective-permute-start | bytes 196616 | tf_op jit(solution)/shard_map/ppermute | solution.py:434
  71.5 2.7 %collective-permute-start.12 = (bf16[16,48,128]{2,1,0:T(8,128)(2,1)S(1)}, bf16[16,48,128]{2,1,0:T(8,128)(2,1)S(1)}, u32[]{:S(2)}, u32[]{:S(2)}) collective-permute-start(bf16[16,48,128]{2,1,0:T(8,128)(2,1)S(1)} %pad_maximum_fusion.2), channel_id=1, source_target_pairs={{0,24},{8,0},{16,8},{24,16},{1,25},{9,1},{17,9},{25,17},{2,26},{10... | collective-permute-start | bytes 589832 | tf_op jit(solution)/shard_map/ppermute | solution.py:422
  74.2 1.4 collective-permute-start.11
  76.5 3.3 %collective-permute-done.8 = bf16[16,16,128]{2,1,0:T(8,128)(2,1)S(1)} collective-permute-done((bf16[16,16,128]{2,1,0:T(8,128)(2,1)S(1)}, bf16[16,16,128]{2,1,0:T(8,128)(2,1)S(1)}, u32[]{:S(2)}, u32[]{:S(2)}) %collective-permute-start.8) | collective-permute-done | bytes 65568 | tf_op jit(solution)/shard_map/ppermute | solution.py:434
  80.5 12.4 %collective-permute-done.11 = bf16[16,48,128]{2,1,0:T(8,128)(2,1)S(1)} collective-permute-done((bf16[16,48,128]{2,1,0:T(8,128)(2,1)S(1)}, bf16[16,48,128]{2,1,0:T(8,128)(2,1)S(1)}, u32[]{:S(2)}, u32[]{:S(2)}) %collective-permute-start.11) | collective-permute-done | bytes 196640 | tf_op jit(solution)/shard_map/ppermute | solution.py:422
  94.1 0.8 collective-permute-start.17
  94.9 17.7 %collective-permute-done.17.refs_6_ = bf16[64,16,128]{2,1,0:T(8,128)(2,1)S(1)} collective-permute-done((bf16[64,16,128]{2,1,0:T(8,128)(2,1)S(1)}, bf16[64,16,128]{2,1,0:T(8,128)(2,1)S(1)}, u32[]{:S(2)}, u32[]{:S(2)}) %collective-permute-start.17) | collective-permute-done | bytes 262176 | tf_op jit(solution)/shard_map/ppermute | solution.py:422
  112.6 1.5 collective-permute-done.15.refs_12_
  114.1 0.7 copy-done.10
  115.4 1.6 %collective-permute-start.19 = (bf16[64,48,128]{2,1,0:T(8,128)(2,1)S(1)}, bf16[64,48,128]{2,1,0:T(8,128)(2,1)}, u32[]{:S(2)}, u32[]{:S(2)}) collective-permute-start(bf16[64,48,128]{2,1,0:T(8,128)(2,1)S(1)} %collective-permute-done.13.refs_1_), channel_id=1, source_target_pairs={{0,4},{1,3},{2,6},{3,1},{4,0},{5,7},{6,2},{7,5},{8,12},{9,11},{10,... | collective-permute-start | bytes 2359304 | tf_op jit(solution)/shard_map/ppermute | solution.py:430
  117.1 4.3 %collective-permute-done.24.refs_7_ = bf16[64,16,128]{2,1,0:T(8,128)(2,1)S(1)} collective-permute-done((bf16[64,16,128]{2,1,0:T(8,128)(2,1)S(1)}, bf16[64,16,128]{2,1,0:T(8,128)(2,1)S(1)}, u32[]{:S(2)}, u32[]{:S(2)}) %collective-permute-start.24) | collective-permute-done | bytes 262176 | tf_op jit(solution)/shard_map/ppermute | solution.py:422
  121.3 0.7 copy-done.12
  122.5 0.7 copy-done.8
  123.2 0.7 copy-done.14
  123.9 0.7 copy-done.6
  124.7 0.7 copy-done.16
  125.5 0.7 copy-done.18
  126.2 0.9 copy-done.2
  127.1 0.9 copy-done.4
  128.3 0.8 fusion.13.places_ref
  129.1 1.5 collective-permute-done.26.refs_11_
  130.6 1.1 copy-done.3
  131.7 1.1 copy-done.5
  132.9 0.9 copy-done.7
  133.8 0.9 copy-done.9
  134.8 0.9 copy-done.11
  135.7 0.9 copy-done.13
  136.7 0.9 copy-done.15
  137.6 0.9 copy-done.17
  138.6 0.9 copy-done.19
  139.5 16.0 %shard_map.78 = bf16[512,128,128]{2,1,0:T(8,128)(2,1)} custom-call(s32[1]{0:T(128)} %bitcast.core_ref, s32[4,512]{1,0:T(4,128)S(1)} %fusion.13.places_ref, f32[1,512]{1,0:T(1,128)S(1)} %constant_dynamic-slice_fusion.root_ref, f32[1,128]{1,0:T(1,128)S(1)} %bitcast.25, bf16[64,48,128]{2,1,0:T(8,128)(2,1)S(1)} %pad_maximum_fusion.refs_0_, ...), custom_call_target="tpu_custom_call" | custom-call | flops 34359738368 | bytes 33554432 | tf_op jit(solution)/shard_map/pallas_call | solution.py:398
  (82 shorter events, 6.7 us)
Async XLA Ops:
  0.0 0.8 copy-start.1
  10.3 13.7 %collective-permute-start = (bf16[8,144,128]{2,1,0:T(8,128)(2,1)S(1)}, bf16[8,144,128]{2,1,0:T(8,128)(2,1)S(1)}, u32[]{:S(2)}, u32[]{:S(2)}) collective-permute-start(bf16[8,144,128]{2,1,0:T(8,128)(2,1)S(1)} %get-tuple-element.36), channel_id=1, source_target_pairs={{0,8},{8,16},{16,24},{24,0},{1,9},{9,17},{17,25},{25,1},{2,10},{10... | collective-permute-start | bytes 884744 | tf_op jit(solution)/shard_map/ppermute | solution.py:422
  13.3 14.8 %collective-permute-start.1 = (bf16[8,144,128]{2,1,0:T(8,128)(2,1)S(1)}, bf16[8,144,128]{2,1,0:T(8,128)(2,1)S(1)}, u32[]{:S(2)}, u32[]{:S(2)}) collective-permute-start(bf16[8,144,128]{2,1,0:T(8,128)(2,1)S(1)} %get-tuple-element.37), channel_id=1, source_target_pairs={{0,24},{8,0},{16,8},{24,16},{1,25},{9,1},{17,9},{25,17},{2,26},{10... | collective-permute-start | bytes 884744 | tf_op jit(solution)/shard_map/ppermute | solution.py:422
  15.4 17.7 %copy-start.23 = (s32[128,3]{0,1:T(4,128)S(1)}, s32[128,3]{0,1:T(4,128)}, u32[]{:S(2)}) copy-start(s32[128,3]{0,1:T(4,128)} %param.11) | copy-start | bytes 4612
  15.4 17.8 %copy-start.24 = (f32[128]{0:T(128)S(1)}, f32[128]{0:T(128)}, u32[]{:S(2)}) copy-start(f32[128]{0:T(128)} %param.12) | copy-start | bytes 1540
  15.4 37.8 %copy-start.21 = (f32[256]{0:T(256)S(1)}, f32[256]{0:T(256)}, u32[]{:S(2)}) copy-start(f32[256]{0:T(256)} %param.9) | copy-start | bytes 3076
  15.4 51.1 %copy-start = (bf16[128,128]{1,0:T(8,128)(2,1)S(1)}, bf16[128,128]{1,0:T(8,128)(2,1)}, u32[]{:S(2)}) copy-start(bf16[128,128]{1,0:T(8,128)(2,1)} %mixing_ref.1) | copy-start | bytes 98308
  15.4 115.2 %copy-start.22 = (f32[128]{0:T(128)S(1)}, f32[128]{0:T(128)}, u32[]{:S(2)}) copy-start(f32[128]{0:T(128)} %param.13) | copy-start | bytes 1540
  28.1 21.2 %all-to-all-start = ((bf16[8,4,128,128]{3,2,1,0:T(8,128)(2,1)}), bf16[8,4,128,128]{3,2,1,0:T(8,128)(2,1)S(1)}, u32[]{:S(2)}, u32[]{:S(2)}) async-start(bf16[8,4,128,128]{3,2,1,0:T(8,128)(2,1)} %shard_map.74), calls=%async_computation | async-start | bytes 2097152 | tf_op jit(solution)/shard_map/all_to_all | solution.py:256
  31.8 16.6 %collective-permute-start.5 = (bf16[8,144,128]{2,1,0:T(8,128)(2,1)S(1)}, bf16[8,144,128]{2,1,0:T(8,128)(2,1)S(1)}, u32[]{:S(2)}, u32[]{:S(2)}) collective-permute-start(bf16[8,144,128]{2,1,0:T(8,128)(2,1)S(1)} %get-tuple-element.45), channel_id=1, source_target_pairs={{0,16},{8,24},{16,0},{24,8},{1,17},{9,25},{17,1},{25,9},{2,18},{10... | collective-permute-start | bytes 884744 | tf_op jit(solution)/shard_map/ppermute | solution.py:422
  49.3 11.1 %all-to-all-start.1 = ((bf16[8,1,144,128]{3,2,1,0:T(8,128)(2,1)}), bf16[8,1,144,128]{3,2,1,0:T(8,128)(2,1)S(1)}, u32[]{:S(2)}, u32[]{:S(2)}) async-start(bf16[8,1,144,128]{3,2,1,0:T(8,128)(2,1)} %shard_map.76), calls=%async_computation.1 | async-start | bytes 589824 | tf_op jit(solution)/shard_map/all_to_all | solution.py:260
  53.4 8.3 %collective-permute-start.2 = (bf16[4,128,128]{2,1,0:T(8,128)(2,1)S(1)}, bf16[4,128,128]{2,1,0:T(8,128)(2,1)S(1)}, u32[]{:S(2)}, u32[]{:S(2)}) collective-permute-start(bf16[4,128,128]{2,1,0:T(8,128)(2,1)S(1)} %get-tuple-element.40), channel_id=1, source_target_pairs={{0,8},{8,16},{16,24},{24,0},{1,9},{9,17},{17,25},{25,1},{2,10},{10... | collective-permute-start | bytes 393224 | tf_op jit(solution)/shard_map/ppermute | solution.py:422
  53.5 12.9 %collective-permute-start.3 = (bf16[4,128,128]{2,1,0:T(8,128)(2,1)S(1)}, bf16[4,128,128]{2,1,0:T(8,128)(2,1)S(1)}, u32[]{:S(2)}, u32[]{:S(2)}) collective-permute-start(bf16[4,128,128]{2,1,0:T(8,128)(2,1)S(1)} %get-tuple-element.41), channel_id=1, source_target_pairs={{0,16},{8,24},{16,0},{24,8},{1,17},{9,25},{17,1},{25,9},{2,18},{10... | collective-permute-start | bytes 393224 | tf_op jit(solution)/shard_map/ppermute | solution.py:422
  56.2 10.2 %collective-permute-start.4 = (bf16[4,128,128]{2,1,0:T(8,128)(2,1)S(1)}, bf16[4,128,128]{2,1,0:T(8,128)(2,1)S(1)}, u32[]{:S(2)}, u32[]{:S(2)}) collective-permute-start(bf16[4,128,128]{2,1,0:T(8,128)(2,1)S(1)} %get-tuple-element.42), channel_id=1, source_target_pairs={{0,24},{8,0},{16,8},{24,16},{1,25},{9,1},{17,9},{25,17},{2,26},{10... | collective-permute-start | bytes 393224 | tf_op jit(solution)/shard_map/ppermute | solution.py:422
  67.0 1.4 collective-permute-start.6
  68.5 7.7 %collective-permute-start.9 = (bf16[16,16,128]{2,1,0:T(8,128)(2,1)S(1)}, bf16[16,16,128]{2,1,0:T(8,128)(2,1)S(1)}, u32[]{:S(2)}, u32[]{:S(2)}) collective-permute-start(bf16[16,16,128]{2,1,0:T(8,128)(2,1)S(1)} %pad_maximum_fusion.3), channel_id=1, source_target_pairs={{0,6},{1,7},{2,4},{3,5},{4,2},{5,3},{6,0},{7,1},{8,14},{9,15},{10,... | collective-permute-start | bytes 196616 | tf_op jit(solution)/shard_map/ppermute | solution.py:434
  71.5 9.0 %collective-permute-start.12 = (bf16[16,48,128]{2,1,0:T(8,128)(2,1)S(1)}, bf16[16,48,128]{2,1,0:T(8,128)(2,1)S(1)}, u32[]{:S(2)}, u32[]{:S(2)}) collective-permute-start(bf16[16,48,128]{2,1,0:T(8,128)(2,1)S(1)} %pad_maximum_fusion.2), channel_id=1, source_target_pairs={{0,24},{8,0},{16,8},{24,16},{1,25},{9,1},{17,9},{25,17},{2,26},{10... | collective-permute-start | bytes 589832 | tf_op jit(solution)/shard_map/ppermute | solution.py:422
  74.2 18.7 %collective-permute-start.11 = (bf16[16,48,128]{2,1,0:T(8,128)(2,1)S(1)}, bf16[16,48,128]{2,1,0:T(8,128)(2,1)S(1)}, u32[]{:S(2)}, u32[]{:S(2)}) collective-permute-start(bf16[16,48,128]{2,1,0:T(8,128)(2,1)S(1)} %pad_maximum_fusion.2), channel_id=1, source_target_pairs={{0,16},{8,24},{16,0},{24,8},{1,17},{9,25},{17,1},{25,9},{2,18},{10... | collective-permute-start | bytes 589832 | tf_op jit(solution)/shard_map/ppermute | solution.py:422
  75.6 17.3 %collective-permute-start.10 = (bf16[16,48,128]{2,1,0:T(8,128)(2,1)S(1)}, bf16[16,48,128]{2,1,0:T(8,128)(2,1)S(1)}, u32[]{:S(2)}, u32[]{:S(2)}) collective-permute-start(bf16[16,48,128]{2,1,0:T(8,128)(2,1)S(1)} %pad_maximum_fusion.2), channel_id=1, source_target_pairs={{0,8},{8,16},{16,24},{24,0},{1,9},{9,17},{17,25},{25,1},{2,10},{10... | collective-permute-start | bytes 589832 | tf_op jit(solution)/shard_map/ppermute | solution.py:422
  75.6 4.3 %collective-permute-start.8 = (bf16[16,16,128]{2,1,0:T(8,128)(2,1)S(1)}, bf16[16,16,128]{2,1,0:T(8,128)(2,1)S(1)}, u32[]{:S(2)}, u32[]{:S(2)}) collective-permute-start(bf16[16,16,128]{2,1,0:T(8,128)(2,1)S(1)} %pad_maximum_fusion.3), channel_id=1, source_target_pairs={{0,4},{1,5},{2,6},{3,7},{4,0},{5,1},{6,2},{7,3},{8,12},{9,13},{10,... | collective-permute-start | bytes 196616 | tf_op jit(solution)/shard_map/ppermute | solution.py:434
  76.2 4.3 %collective-permute-start.7 = (bf16[16,16,128]{2,1,0:T(8,128)(2,1)S(1)}, bf16[16,16,128]{2,1,0:T(8,128)(2,1)S(1)}, u32[]{:S(2)}, u32[]{:S(2)}) collective-permute-start(bf16[16,16,128]{2,1,0:T(8,128)(2,1)S(1)} %pad_maximum_fusion.3), channel_id=1, source_target_pairs={{0,2},{1,3},{2,0},{3,1},{4,6},{5,7},{6,4},{7,5},{8,10},{9,11},{10,... | collective-permute-start | bytes 196616 | tf_op jit(solution)/shard_map/ppermute | solution.py:434
  93.0 21.8 %collective-permute-start.14 = (bf16[64,48,128]{2,1,0:T(8,128)(2,1)S(1)}, bf16[64,48,128]{2,1,0:T(8,128)(2,1)S(1)}, u32[]{:S(2)}, u32[]{:S(2)}) collective-permute-start(bf16[64,48,128]{2,1,0:T(8,128)(2,1)S(1)} %pad_maximum_fusion.refs_0_), channel_id=1, source_target_pairs={{0,1},{1,0},{2,3},{3,2},{4,5},{5,4},{6,7},{7,6},{8,9},{9,8},{10,11... | collective-permute-start | bytes 2359304 | tf_op jit(solution)/shard_map/ppermute | solution.py:438
  93.1 21.7 %collective-permute-start.13 = (bf16[64,48,128]{2,1,0:T(8,128)(2,1)S(1)}, bf16[64,48,128]{2,1,0:T(8,128)(2,1)S(1)}, u32[]{:S(2)}, u32[]{:S(2)}) collective-permute-start(bf16[64,48,128]{2,1,0:T(8,128)(2,1)S(1)} %pad_maximum_fusion.refs_0_), channel_id=1, source_target_pairs={{0,2},{1,5},{2,0},{3,7},{4,6},{5,1},{6,4},{7,3},{8,10},{9,13},{10,... | collective-permute-start | bytes 2359304 | tf_op jit(solution)/shard_map/ppermute | solution.py:430
  93.7 21.1 %collective-permute-start.18 = (bf16[64,48,128]{2,1,0:T(8,128)(2,1)S(1)}, bf16[64,48,128]{2,1,0:T(8,128)(2,1)S(1)}, u32[]{:S(2)}, u32[]{:S(2)}) collective-permute-start(bf16[64,48,128]{2,1,0:T(8,128)(2,1)S(1)} %pad_maximum_fusion.refs_0_), channel_id=1, source_target_pairs={{0,4},{1,3},{2,6},{3,1},{4,0},{5,7},{6,2},{7,5},{8,12},{9,11},{10,... | collective-permute-start | bytes 2359304 | tf_op jit(solution)/shard_map/ppermute | solution.py:430
  94.1 18.5 %collective-permute-start.17 = (bf16[64,16,128]{2,1,0:T(8,128)(2,1)S(1)}, bf16[64,16,128]{2,1,0:T(8,128)(2,1)S(1)}, u32[]{:S(2)}, u32[]{:S(2)}) collective-permute-start(bf16[64,16,128]{2,1,0:T(8,128)(2,1)S(1)} %pad_maximum_fusion.1.refs_4_), channel_id=1, source_target_pairs={{0,16},{8,24},{16,0},{24,8},{1,17},{9,25},{17,1},{25,9},{2,18},{10... | collective-permute-start | bytes 786440 | tf_op jit(solution)/shard_map/ppermute | solution.py:422
  94.9 17.8 %collective-permute-start.16 = (bf16[64,16,128]{2,1,0:T(8,128)(2,1)S(1)}, bf16[64,16,128]{2,1,0:T(8,128)(2,1)S(1)}, u32[]{:S(2)}, u32[]{:S(2)}) collective-permute-start(bf16[64,16,128]{2,1,0:T(8,128)(2,1)S(1)} %pad_maximum_fusion.1.refs_4_), channel_id=1, source_target_pairs={{0,8},{8,16},{16,24},{24,0},{1,9},{9,17},{17,25},{25,1},{2,10},{10... | collective-permute-start | bytes 786440 | tf_op jit(solution)/shard_map/ppermute | solution.py:422
  112.6 1.5 collective-permute-start.15
  112.6 8.7 %collective-permute-start.24 = (bf16[64,16,128]{2,1,0:T(8,128)(2,1)S(1)}, bf16[64,16,128]{2,1,0:T(8,128)(2,1)S(1)}, u32[]{:S(2)}, u32[]{:S(2)}) collective-permute-start(bf16[64,16,128]{2,1,0:T(8,128)(2,1)S(1)} %pad_maximum_fusion.1.refs_4_), channel_id=1, source_target_pairs={{0,24},{8,0},{16,8},{24,16},{1,25},{9,1},{17,9},{25,17},{2,26},{10... | collective-permute-start | bytes 786440 | tf_op jit(solution)/shard_map/ppermute | solution.py:422
  114.8 11.3 %collective-permute-start.21 = (bf16[64,48,128]{2,1,0:T(8,128)(2,1)S(1)}, bf16[64,48,128]{2,1,0:T(8,128)(2,1)S(1)}, u32[]{:S(2)}, u32[]{:S(2)}) collective-permute-start(bf16[64,48,128]{2,1,0:T(8,128)(2,1)S(1)} %collective-permute-done.18.refs_2_), channel_id=1, source_target_pairs={{0,1},{1,0},{2,3},{3,2},{4,5},{5,4},{6,7},{7,6},{8,9},{9,8},{10,11... | collective-permute-start | bytes 2359304 | tf_op jit(solution)/shard_map/ppermute | solution.py:438
  115.0 12.0 %collective-permute-start.20 = (bf16[64,48,128]{2,1,0:T(8,128)(2,1)S(1)}, bf16[64,48,128]{2,1,0:T(8,128)(2,1)S(1)}, u32[]{:S(2)}, u32[]{:S(2)}) collective-permute-start(bf16[64,48,128]{2,1,0:T(8,128)(2,1)S(1)} %collective-permute-done.13.refs_1_), channel_id=1, source_target_pairs={{0,1},{1,0},{2,3},{3,2},{4,5},{5,4},{6,7},{7,6},{8,9},{9,8},{10,11... | collective-permute-start | bytes 2359304 | tf_op jit(solution)/shard_map/ppermute | solution.py:438
  115.4 12.5 %collective-permute-start.19 = (bf16[64,48,128]{2,1,0:T(8,128)(2,1)S(1)}, bf16[64,48,128]{2,1,0:T(8,128)(2,1)}, u32[]{:S(2)}, u32[]{:S(2)}) collective-permute-start(bf16[64,48,128]{2,1,0:T(8,128)(2,1)S(1)} %collective-permute-done.13.refs_1_), channel_id=1, source_target_pairs={{0,4},{1,3},{2,6},{3,1},{4,0},{5,7},{6,2},{7,5},{8,12},{9,11},{10,... | collective-permute-start | bytes 2359304 | tf_op jit(solution)/shard_map/ppermute | solution.py:430
  121.3 1.9 %collective-permute-start.25 = (bf16[64,16,128]{2,1,0:T(8,128)(2,1)S(1)}, bf16[64,16,128]{2,1,0:T(8,128)(2,1)S(1)}, u32[]{:S(2)}, u32[]{:S(2)}) collective-permute-start(bf16[64,16,128]{2,1,0:T(8,128)(2,1)S(1)} %collective-permute-done.24.refs_7_), channel_id=1, source_target_pairs={{0,1},{1,0},{2,3},{3,2},{4,5},{5,4},{6,7},{7,6},{8,9},{9,8},{10,11... | collective-permute-start | bytes 786440 | tf_op jit(solution)/shard_map/ppermute | solution.py:438
  122.0 2.6 %collective-permute-start.22 = (bf16[64,16,128]{2,1,0:T(8,128)(2,1)S(1)}, bf16[64,16,128]{2,1,0:T(8,128)(2,1)S(1)}, u32[]{:S(2)}, u32[]{:S(2)}) collective-permute-start(bf16[64,16,128]{2,1,0:T(8,128)(2,1)S(1)} %collective-permute-done.16.refs_5_), channel_id=1, source_target_pairs={{0,1},{1,0},{2,3},{3,2},{4,5},{5,4},{6,7},{7,6},{8,9},{9,8},{10,11... | collective-permute-start | bytes 786440 | tf_op jit(solution)/shard_map/ppermute | solution.py:438
  122.5 0.7 copy-start.8
  123.9 1.5 collective-permute-start.23
  123.9 0.7 copy-start.6
  126.2 0.9 copy-start.2
  127.1 0.9 copy-start.4
  127.9 2.6 %collective-permute-start.26 = (bf16[64,48,128]{2,1,0:T(8,128)(2,1)}, bf16[64,48,128]{2,1,0:T(8,128)(2,1)}, u32[]{:S(2)}, u32[]{:S(2)}) collective-permute-start(bf16[64,48,128]{2,1,0:T(8,128)(2,1)} %collective-permute-done.19.refs_3_), channel_id=1, source_target_pairs={{0,1},{1,0},{2,3},{3,2},{4,5},{5,4},{6,7},{7,6},{8,9},{9,8},{10,11... | collective-permute-start | bytes 2359304 | tf_op jit(solution)/shard_map/ppermute | solution.py:438
  130.6 1.1 copy-start.3
  131.7 1.1 copy-start.5
  132.9 0.9 copy-start.7
  133.8 0.9 copy-start.9
  134.8 0.9 copy-start.11
  135.7 0.9 copy-start.13
  136.7 0.9 copy-start.15
  137.6 0.9 copy-start.17
  138.6 0.9 copy-start.19
  (6 other events, 4.1 us)

commit v12 on v8

--- a/solution.py
+++ b/solution.py
@@ -11,6 +11,7 @@
 F32 = jnp.float32
 COUNT_BASE = 256.0
 HEAD = 16
+TILE = 16
 
 
 def corridor_table(edge_ids, edge_count):
@@ -78,8 +79,36 @@
     return root, weighted, jnp.dot(hot, jnp.ones((rows, lanes), BF16), preferred_element_type=F32)
 
 
+def turn_rows(cells_ref, turned_ref):
+    rows, zones, lanes = cells_ref.shape
+    size = TILE * zones
+    target = lax.broadcasted_iota(jnp.int32, (size, size), 0)
+    source = lax.broadcasted_iota(jnp.int32, (size, size), 1)
+    wanted = jnp.bitwise_and(target, TILE - 1) * zones + lax.shift_right_logical(target, 4)
+    turn = jnp.where(source == wanted, 1.0, 0.0).astype(BF16)
+
+    def block(i, carry):
+        first = i * 2 * TILE
+        left = cells_ref[pl.ds(first, TILE)].reshape(size, lanes)
+        right = cells_ref[pl.ds(first + TILE, TILE)].reshape(size, lanes)
+        both = jnp.dot(turn, jnp.concatenate([left, right], axis=1), preferred_element_type=F32).astype(BF16)
+        for d in range(zones):
+            at = slice(d % 2 * lanes, (d % 2 + 1) * lanes)
+            piece = both[d * TILE : (d + 1) * TILE]
+            turned_ref[d // 2, pl.ds(pl.multiple_of(first, TILE), TILE), at] = piece[:, :lanes]
+            turned_ref[d // 2, pl.ds(pl.multiple_of(first + TILE, TILE), TILE), at] = piece[:, lanes:]
+        return carry
+
+    lax.fori_loop(0, rows // (2 * TILE), block, 0, unroll=4)
+
+
 def accumulate(weighted, cells_ref, begin, zones, pitch, total_ref, wide_ref):
     rows, _, lanes = cells_ref.shape
+    if zones == TILE:
+        turn_rows(cells_ref, wide_ref)
+        for pair in range(zones // 2):
+            total_ref[pair] += jnp.dot(weighted, wide_ref[pair], preferred_element_type=F32)
+        return
     part = 32
 
     def widen(i, carry):
@@ -114,8 +143,7 @@
 
 
 def second_kernel(plan, begin, zones, pitch, line_ref, edges_ref, weight_ref, cells_ref, *refs):
-    out_refs = refs[: plan.line]
-    root_ref, weighted_ref, total_ref, count_ref, wide_ref = refs[plan.line :]
+    out_ref, root_ref, weighted_ref, total_ref, count_ref, wide_ref = refs
     lanes = cells_ref.shape[2]
 
     @pl.when(pl.program_id(0) == 0)
@@ -134,8 +162,8 @@
         for square in range(8):
             for shift in range(plan.line):
                 at = rows_for(plan, square, shift, line_ref)
-                out_refs[shift][square, HEAD:, :] = columns_of(total_ref, at, zones, lanes)
-                out_refs[shift][square, 0:HEAD, :] = head_rows(*halves_of(count_ref[at, :]))
+                out_ref[square, shift, HEAD:, :] = columns_of(total_ref, at, zones, lanes)
+                out_ref[square, shift, 0:HEAD, :] = head_rows(*halves_of(count_ref[at, :]))
 
 
 def first_kernel(plan, begin, zones, pitch, line_ref, weighted_ref, cells_ref, out_ref, total_ref, wide_ref):
@@ -168,13 +196,16 @@
     else:
         block, begin = pl.BlockSpec((rows, zones, lanes), lambda i: (i, 0, 0)), part * half
     counts = [pltpu.VMEM((edges, lanes), F32)] if counted else []
+    wide = pltpu.VMEM((rows * pitch, lanes), F32)
+    if half == TILE:
+        wide = pltpu.VMEM((half // 2, rows, 2 * lanes), BF16)
     return pl.pallas_call(
         functools.partial(kernel, plan, begin, half, pitch),
         grid=(anchors // rows,),
         in_specs=[pl.BlockSpec(memory_space=pltpu.SMEM)] + specs + [block],
         out_specs=out_specs,
         out_shape=outs,
-        scratch_shapes=[pltpu.VMEM((half // 2, edges, 2 * lanes), F32)] + counts + [pltpu.VMEM((rows * pitch, lanes), F32)],
+        scratch_shapes=[pltpu.VMEM((half // 2, edges, 2 * lanes), F32)] + counts + [wide],
         compiler_params=pltpu.CompilerParams(vmem_limit_bytes=40 * 1024 * 1024),
         cost_estimate=pl.CostEstimate(
             flops=4 * anchors * edges * zones * lanes, bytes_accessed=2 * anchors * zones * lanes, transcendentals=0
@@ -186,18 +217,21 @@
     anchors, _, lanes = cells.shape
     rows = min(512, anchors)
     edges = plan.edges
-    shape = (8, plan.second_rows, lanes)
-    outs = [jax.ShapeDtypeStruct(shape, BF16)] * plan.line
+    shape = (8, plan.line, plan.second_rows, lanes)
+    outs = [jax.ShapeDtypeStruct(shape, BF16)]
     outs += [jax.ShapeDtypeStruct((1, anchors), F32), jax.ShapeDtypeStruct((edges, anchors), BF16)]
-    out_specs = [fixed(shape)] * plan.line
+    out_specs = [fixed(shape)]
     out_specs += [pl.BlockSpec((1, rows), lambda i: (0, i)), pl.BlockSpec((edges, rows), lambda i: (0, i))]
     specs = [pl.BlockSpec((edges_t.shape[0], rows), lambda i: (0, i)), fixed((1, edges))]
     operands = (edges_t, edge_weight[None, :])
-    *seconds, roots, weighted = half_sums(second_kernel, plan, 1, line, cells, operands, specs, outs, out_specs, True)
-    if not plan.relative:
-        seconds = jnp.stack(seconds * 2)
-        seconds = [lax.dynamic_index_in_dim(seconds, line + k, 0, keepdims=False) for k in range(plan.line)]
-    return seconds, roots, weighted
+    second, roots, weighted = half_sums(second_kernel, plan, 1, line, cells, operands, specs, outs, out_specs, True)
+    return rolled(second, line, plan), roots, weighted
+
+
+def rolled(parts, line, plan):
+    if plan.relative:
+        return parts
+    return lax.dynamic_slice_in_dim(jnp.concatenate([parts, parts], axis=1), line, plan.line, 1)
 
 
 def first_sums(line, cells, weighted, plan):
@@ -205,10 +239,7 @@
     shape = (8, plan.line, plan.first_rows, cells.shape[2])
     specs = [pl.BlockSpec((plan.edges, rows), lambda i: (0, i))]
     out = jax.ShapeDtypeStruct(shape, BF16)
-    first = half_sums(first_kernel, plan, 0, line, cells, (weighted,), specs, out, fixed(shape), False)
-    if not plan.relative:
-        first = lax.dynamic_slice_in_dim(jnp.concatenate([first, first], axis=1), line, plan.line, 1)
-    return first
+    return rolled(half_sums(first_kernel, plan, 0, line, cells, (weighted,), specs, out, fixed(shape), False), line, plan)
 
 
 def add_up(pieces):
@@ -218,55 +249,53 @@
     return total
 
 
-def fold_first_kernel(plan, part_ref, *outs):
+def fold_kernel(plan, counted, part_ref, *outs):
+    half = HEAD // 2
     for shift in range(plan.line):
         for quarter in range(4):
-            outs[shift][quarter] = add_up([part_ref[quarter, shift], part_ref[4 + quarter, shift]]).astype(BF16)
-
-
-def fold_second_kernel(plan, *refs):
-    parts, out_ref = refs[: plan.line], refs[plan.line]
-    for square in range(8):
-        for rest in range(plan.rest):
-            total = add_up([parts[shift][square] for shift in range(rest, plan.line, plan.rest)])
-            half = HEAD // 2
-            out_ref[square, rest, 0:HEAD, :] = head_rows(*halves_of(total[0:half] * COUNT_BASE + total[half:HEAD]))
-            out_ref[square, rest, HEAD:, :] = total[HEAD:].astype(BF16)
-
-
-def fold(kernel, plan, parts, shapes):
+            total = add_up([part_ref[quarter, shift], part_ref[4 + quarter, shift]])
+            if counted:
+                outs[shift][quarter, 0:HEAD, :] = head_rows(*halves_of(total[0:half] * COUNT_BASE + total[half:HEAD]))
+                outs[shift][quarter, HEAD:, :] = total[HEAD:].astype(BF16)
+            else:
+                outs[shift][quarter] = total.astype(BF16)
+
+
+def fold(plan, counted, part):
     whole = pl.BlockSpec(memory_space=pltpu.VMEM)
-    size = sum(part.size for part in parts)
     return pl.pallas_call(
-        functools.partial(kernel, plan),
-        in_specs=[whole] * len(parts),
-        out_specs=[whole] * len(shapes),
-        out_shape=[jax.ShapeDtypeStruct(shape, BF16) for shape in shapes],
+        functools.partial(fold_kernel, plan, counted),
+        in_specs=[whole],
+        out_specs=[whole] * plan.line,
+        out_shape=[jax.ShapeDtypeStruct((4,) + part.shape[2:], BF16)] * plan.line,
         compiler_params=pltpu.CompilerParams(vmem_limit_bytes=16 * 1024 * 1024),
-        cost_estimate=pl.CostEstimate(flops=size, bytes_accessed=size * 4, transcendentals=0),
-    )(*parts)
+        cost_estimate=pl.CostEstimate(flops=part.size, bytes_accessed=part.size * 4, transcendentals=0),
+    )(part)
+
+
+def along_line(parts):
+    return [shifted(part, shift) if shift else part for shift, part in enumerate(parts)]
 
 
 def org_sums(line, cells, edges_t, edge_weight, plan):
-    lanes = cells.shape[-1]
-    seconds, roots, weighted = second_sums(line, cells, edges_t, edge_weight, plan)
-    seconds = [shifted(part, shift) if shift else part for shift, part in enumerate(seconds)]
+    second, roots, weighted = second_sums(line, cells, edges_t, edge_weight, plan)
+    second = lax.all_to_all(second, SQUARE, split_axis=0, concat_axis=0, tiled=True)
     first = first_sums(line, cells, weighted, plan)
+    first, second = lax.optimization_barrier((first, second))
     first = lax.all_to_all(first, SQUARE, split_axis=0, concat_axis=0, tiled=True)
-    second = fold(fold_second_kernel, plan, seconds, [(8, plan.rest, plan.second_rows, lanes)])[0]
-    firsts = fold(fold_first_kernel, plan, [first], [(4, plan.first_rows, lanes)] * plan.line)
-    firsts = [shifted(part, shift) if shift else part for shift, part in enumerate(firsts)]
-    second = lax.all_to_all(second, SQUARE, split_axis=0, concat_axis=0, tiled=True)
-    return firsts, second, roots
+    seconds = along_line(fold(plan, True, second))
+    first, *seconds = lax.optimization_barrier((first, *seconds))
+    firsts = along_line(fold(plan, False, first))
+    return firsts, seconds, roots
 
 
 def table_kernel(plan, weight_ref, mixing_ref, matrix_ref, *refs):
-    firsts = refs[: plan.line]
-    second_ref, keep_ref, give_ref, mixed_ref = refs[plan.line :]
+    firsts, seconds = refs[: plan.line], refs[plan.line : 2 * plan.line]
+    keep_ref, give_ref, mixed_ref = refs[2 * plan.line :]
     own = plan.own
     lanes = mixing_ref.shape[0]
     half = HEAD // 2
-    head = add_up([second_ref[0, 0, 0:HEAD, :], second_ref[4, 0, 0:HEAD, :]])
+    head = add_up([seconds[shift][0, 0:HEAD, :] for shift in range(0, plan.line, plan.rest)])
     counts = head[0:half] * COUNT_BASE + head[half:HEAD]
     scale = weight_ref[...] / counts[0:own]
     rows = plan.first_rows + plan.second_rows - HEAD
@@ -275,7 +304,7 @@
     for k in range(n_dst):
         rest, quarter = k // 4, k % 4
         first = add_up([firsts[shift][quarter] for shift in range(rest, plan.line, plan.rest)])
-        second = add_up([second_ref[quarter, rest, HEAD:, :], second_ref[4 + quarter, rest, HEAD:, :]])
+        second = add_up([seconds[shift][quarter, HEAD:, :] for shift in range(rest, plan.line, plan.rest)])
         start = k * rows
         for total in (first, second):
             size = total.shape[0]
@@ -294,14 +323,14 @@
         give_ref[e] = result[whole // 2 :]
 
 
-def table_rows(firsts, second, weight_rows, mixing, matrix, plan):
+def table_rows(firsts, seconds, weight_rows, mixing, matrix, plan):
     zones = matrix.shape[0]
     lanes = mixing.shape[0]
     whole = pl.BlockSpec(memory_space=pltpu.VMEM)
     half = jax.ShapeDtypeStruct((plan.own, zones // 2, lanes), BF16)
     return pl.pallas_call(
         functools.partial(table_kernel, plan),
-        in_specs=[whole] * (4 + len(firsts)),
+        in_specs=[whole] * (3 + len(firsts) + len(seconds)),
         out_specs=[whole] * 2,
         out_shape=[half, half],
         scratch_shapes=[pltpu.VMEM((zones * plan.own, lanes), F32)],
@@ -309,7 +338,7 @@
         cost_estimate=pl.CostEstimate(
             flops=8 * plan.own * zones * lanes * lanes, bytes_accessed=4 * zones * plan.own * lanes, transcendentals=0
         ),
-    )(weight_rows, mixing, matrix, *firsts, second)
+    )(weight_rows, mixing, matrix, *firsts, *seconds)
 
 
 def spread_kernel(n_long, n_short, half_ref, places_ref, root_ref, bias_ref, *refs):
@@ -486,13 +515,13 @@
     core = lax.axis_index("core")
     edges_t = anchor_edges.T
     plan = Plan(od_cells.shape[1], edge_weight.shape[0], own, lax.axis_size("rest"), lax.axis_size(LINE))
-    firsts, second, roots = org_sums(lax.axis_index(LINE), od_cells, edges_t, edge_weight, plan)
+    firsts, seconds, roots = org_sums(lax.axis_index(LINE), od_cells, edges_t, edge_weight, plan)
     own_weight = lax.dynamic_slice_in_dim(edge_weight, lax.axis_index(everyone) * own, own, 0)
     weight_rows = jnp.broadcast_to(own_weight[:, None], (own, mixing.shape[0]))
     matrix = relative_columns(dest_operator(dst_edges, dst_weight))
     half = matrix.shape[0] // 2
     matrix = jnp.where(core == 0, matrix, jnp.concatenate([matrix[half:], matrix[:half]], axis=0))
-    keep, give = table_rows(firsts, second, weight_rows, mixing, matrix, plan)
+    keep, give = table_rows(firsts, seconds, weight_rows, mixing, matrix, plan)
     longs, shorts = gather_table(keep, give)
     rows = anchor_edges.shape[0] // n_dst
     start = lax.axis_index(("rest", "near", "core")) * rows

time: 150 us -> 148 us (0.987)
  waiting for transfers between devices: 65 us -> 57.6 us
  Pallas kernels: 38.3 us -> 44.1 us
    ppermute x12, waiting for transfers between devices: 59.3 us -> 49.8 us  [shifted(): lax.ppermute(x, LINE, [(i, (i + amount) % size) for i in range(size)])]
    pallas_call x2, Pallas kernels: 17.3 us -> 23.8 us  [half_sums(): pl.pallas_call(functools.partial(kernel, plan, begin, half, pitch), grid=...]
    all_to_all x1, waiting for transfers between devices: 0.01 us -> 2.13 us  [org_sums(): lax.all_to_all(second, SQUARE, split_axis=0, concat_axis=0, tiled=True)]
    ppermute x12, starting transfers between devices: 19.1 us -> 17.3 us  [shifted(): lax.ppermute(x, LINE, [(i, (i + amount) % size) for i in range(size)])]
    all_to_all x1, starting transfers between devices: 5.22 us -> 6.92 us  [org_sums(): lax.all_to_all(first, SQUARE, split_axis=0, concat_axis=0, tiled=True)]
  transfers between devices with their start and end apart: 29 -> 29, of which waited for: 11 -> 12; matrix products, arithmetic and copies ran while one was open for 1% -> 1% of each run, Pallas kernels for 7% -> 14%
where the time goes in v12:
time: 148 us; the launch traced here: 147 us
  waiting for transfers between devices  57.6 us (39%)
  Pallas kernels  44.1 us (30%)
  starting transfers between devices  42.9 us (29%)
  local copies, waits for them, and re-layouts  1.67 us (1%)
    ppermute x12, waiting for transfers between devices, shifted(): lax.ppermute(x, LINE, [(i, (i + amount) % size) for i in range(size)])  49.8 us
    pallas_call x2, Pallas kernels, half_sums(): pl.pallas_call(functools.partial(kernel, plan, begin, half, pitch), grid=...  23.8 us
    pallas_call x2, Pallas kernels, spread(): pl.pallas_call(functools.partial(spread_kernel, len(longs), len(shorts)),...  19.4 us
    ppermute x12, starting transfers between devices, shifted(): lax.ppermute(x, LINE, [(i, (i + amount) % size) for i in range(size)])  17.3 us
    ppermute x9, starting transfers between devices, swapped(): return lax.ppermute(x, 'core', [(0, 1), (1, 0)])  10.6 us
    all_to_all x1, starting transfers between devices, org_sums(): lax.all_to_all(first, SQUARE, split_axis=0, concat_axis=0, tiled=True)  6.92 us
    all_to_all x1, starting transfers between devices, org_sums(): lax.all_to_all(second, SQUARE, split_axis=0, concat_axis=0, tiled=True)  5.22 us
    ppermute x5, waiting for transfers between devices, crossed(): return lax.ppermute(x, SQUARE, pairs)  3.34 us
  transfers between devices with their start and end apart: 29, of which 12 were waited for; matrix products, arithmetic and copies ran while one was open for 1% of the time, Pallas kernels for 14%

profile of v12, /device:TPU:1, one launch (start us, length us, event | category | flops | bytes accessed | tf_op | source)
XLA Modules:
  0.0 147.3 jit_solution(8354539743724028937)
XLA Ops:
  0.0 0.8 copy-done.1
  0.8 0.7 copy-done.3
  1.4 12.6 %shard_map.73 = (bf16[8,4,144,128]{3,2,1,0:T(8,128)(2,1)}, f32[1,2048]{1,0:T(1,128)S(1)}, bf16[256,2048]{1,0:T(8,128)(2,1)S(1)}) custom-call(s32[1]{0:T(128)} %bitcast.2.line_ref, s32[4,2048]{1,0:T(4,128)S(1)} %bitcast.31, f32[1,256]{1,0:T(1,128)S(1)} %bitcast.32, bf16[2048,32,128]{2,1,0:T(8,128)(2,1)} %cells_ref.3), custom_call_target="tpu_custom_call" | custom-call | flops 8589934592 | bytes 16777216 | tf_op jit(solution)/shard_map/pallas_call | solution.py:202
  14.1 5.2 %all-to-all-start = ((bf16[8,4,144,128]{3,2,1,0:T(8,128)(2,1)}), bf16[8,4,144,128]{3,2,1,0:T(8,128)(2,1)S(1)}, u32[]{:S(2)}, u32[]{:S(2)}) async-start(bf16[8,4,144,128]{3,2,1,0:T(8,128)(2,1)} %get-tuple-element.32), calls=%async_computation | async-start | bytes 2359296 | tf_op jit(solution)/shard_map/all_to_all | solution.py:282
  19.3 11.2 %shard_map.74 = bf16[8,4,128,128]{3,2,1,0:T(8,128)(2,1)} custom-call(s32[1]{0:T(128)} %bitcast.2.line_ref, bf16[256,2048]{1,0:T(8,128)(2,1)S(1)} %get-tuple-element.31.weighted_ref, bf16[2048,32,128]{2,1,0:T(8,128)(2,1)} %cells_ref.3), custom_call_target="tpu_custom_call" | custom-call | flops 8589934592 | bytes 16777216 | tf_op jit(solution)/shard_map/pallas_call | solution.py:202
  30.5 2.1 %all-to-all-done.part_ref = bf16[8,4,144,128]{3,2,1,0:T(8,128)(2,1)S(1)} async-done(((bf16[8,4,144,128]{3,2,1,0:T(8,128)(2,1)}), bf16[8,4,144,128]{3,2,1,0:T(8,128)(2,1)S(1)}, u32[]{:S(2)}, u32[]{:S(2)}) %all-to-all-start) | async-done | bytes 1179680 | tf_op jit(solution)/shard_map/all_to_all | solution.py:282
  32.7 6.9 %all-to-all-start.1 = ((bf16[8,4,128,128]{3,2,1,0:T(8,128)(2,1)}), bf16[8,4,128,128]{3,2,1,0:T(8,128)(2,1)S(1)}, u32[]{:S(2)}, u32[]{:S(2)}) async-start(bf16[8,4,128,128]{3,2,1,0:T(8,128)(2,1)} %shard_map.74), calls=%async_computation.1 | async-start | bytes 2097152 | tf_op jit(solution)/shard_map/all_to_all | solution.py:285
  39.7 0.1 convert_reduce_fusion
  39.8 0.1 multiply_reduce_fusion
  39.9 0.3 convolution_convert_fusion
  40.3 0.1 shard_map.75
  40.4 1.3 collective-permute-start
  41.8 2.3 %collective-permute-start.1 = (bf16[4,144,128]{2,1,0:T(8,128)(2,1)S(1)}, bf16[4,144,128]{2,1,0:T(8,128)(2,1)S(1)}, u32[]{:S(2)}, u32[]{:S(2)}) collective-permute-start(bf16[4,144,128]{2,1,0:T(8,128)(2,1)S(1)} %get-tuple-element.37), channel_id=1, source_target_pairs={{0,16},{8,24},{16,0},{24,8},{1,17},{9,25},{17,1},{25,9},{2,18},{10... | collective-permute-start | bytes 442376 | tf_op jit(solution)/shard_map/ppermute | solution.py:453
  44.1 1.1 collective-permute-start.2
  45.2 2.6 %collective-permute-done.refs_5_ = bf16[4,144,128]{2,1,0:T(8,128)(2,1)S(1)} collective-permute-done((bf16[4,144,128]{2,1,0:T(8,128)(2,1)S(1)}, bf16[4,144,128]{2,1,0:T(8,128)(2,1)S(1)}, u32[]{:S(2)}, u32[]{:S(2)}) %collective-permute-start) | collective-permute-done | bytes 147488 | tf_op jit(solution)/shard_map/ppermute | solution.py:453
  47.8 6.7 %collective-permute-done.1.refs_6_ = bf16[4,144,128]{2,1,0:T(8,128)(2,1)S(1)} collective-permute-done((bf16[4,144,128]{2,1,0:T(8,128)(2,1)S(1)}, bf16[4,144,128]{2,1,0:T(8,128)(2,1)S(1)}, u32[]{:S(2)}, u32[]{:S(2)}) %collective-permute-start.1) | collective-permute-done | bytes 147488 | tf_op jit(solution)/shard_map/ppermute | solution.py:453
  54.4 0.1 shard_map.76
  54.6 3.5 %collective-permute-start.3 = (bf16[4,128,128]{2,1,0:T(8,128)(2,1)S(1)}, bf16[4,128,128]{2,1,0:T(8,128)(2,1)S(1)}, u32[]{:S(2)}, u32[]{:S(2)}) collective-permute-start(bf16[4,128,128]{2,1,0:T(8,128)(2,1)S(1)} %get-tuple-element.41), channel_id=1, source_target_pairs={{0,8},{8,16},{16,24},{24,0},{1,9},{9,17},{17,25},{25,1},{2,10},{10... | collective-permute-start | bytes 393224 | tf_op jit(solution)/shard_map/ppermute | solution.py:453
  58.1 0.9 collective-permute-start.4
  59.0 1.3 collective-permute-start.5
  60.2 1.3 collective-permute-done.3.refs_1_
  61.6 6.7 %collective-permute-done.4.refs_2_ = bf16[4,128,128]{2,1,0:T(8,128)(2,1)S(1)} collective-permute-done((bf16[4,128,128]{2,1,0:T(8,128)(2,1)S(1)}, bf16[4,128,128]{2,1,0:T(8,128)(2,1)S(1)}, u32[]{:S(2)}, u32[]{:S(2)}) %collective-permute-start.4) | collective-permute-done | bytes 131104 | tf_op jit(solution)/shard_map/ppermute | solution.py:453
  68.3 0.6 shard_map.77
  68.9 0.7 collective-permute-start.6
  69.6 1.0 collective-permute-done.6
  70.6 2.1 %collective-permute-start.9 = (bf16[16,16,128]{2,1,0:T(8,128)(2,1)S(1)}, bf16[16,16,128]{2,1,0:T(8,128)(2,1)S(1)}, u32[]{:S(2)}, u32[]{:S(2)}) collective-permute-start(bf16[16,16,128]{2,1,0:T(8,128)(2,1)S(1)} %slice.18), channel_id=1, source_target_pairs={{0,6},{1,7},{2,4},{3,5},{4,2},{5,3},{6,0},{7,1},{8,14},{9,15},{10,... | collective-permute-start | bytes 196616 | tf_op jit(solution)/shard_map/ppermute | solution.py:465
  72.8 4.5 %collective-permute-start.12 = (bf16[16,48,128]{2,1,0:T(8,128)(2,1)S(1)}, bf16[16,48,128]{2,1,0:T(8,128)(2,1)S(1)}, u32[]{:S(2)}, u32[]{:S(2)}) collective-permute-start(bf16[16,48,128]{2,1,0:T(8,128)(2,1)S(1)} %slice.19), channel_id=1, source_target_pairs={{0,24},{8,0},{16,8},{24,16},{1,25},{9,1},{17,9},{25,17},{2,26},{10... | collective-permute-start | bytes 589832 | tf_op jit(solution)/shard_map/ppermute | solution.py:453
  77.2 0.4 collective-permute-start.10
  77.6 0.3 collective-permute-start.8
  77.9 3.1 %collective-permute-done.8 = bf16[16,16,128]{2,1,0:T(8,128)(2,1)S(1)} collective-permute-done((bf16[16,16,128]{2,1,0:T(8,128)(2,1)S(1)}, bf16[16,16,128]{2,1,0:T(8,128)(2,1)S(1)}, u32[]{:S(2)}, u32[]{:S(2)}) %collective-permute-start.8) | collective-permute-done | bytes 65568 | tf_op jit(solution)/shard_map/ppermute | solution.py:461
  81.0 0.3 collective-permute-done.7
  81.3 12.7 %collective-permute-done.11 = bf16[16,48,128]{2,1,0:T(8,128)(2,1)S(1)} collective-permute-done((bf16[16,48,128]{2,1,0:T(8,128)(2,1)S(1)}, bf16[16,48,128]{2,1,0:T(8,128)(2,1)S(1)}, u32[]{:S(2)}, u32[]{:S(2)}) %collective-permute-start.11) | collective-permute-done | bytes 196640 | tf_op jit(solution)/shard_map/ppermute | solution.py:453
  94.0 0.1 pad_maximum_fusion.refs_0_
  94.1 0.3 collective-permute-start.14
  94.4 2.0 %collective-permute-start.16 = (bf16[64,16,128]{2,1,0:T(8,128)(2,1)S(1)}, bf16[64,16,128]{2,1,0:T(8,128)(2,1)S(1)}, u32[]{:S(2)}, u32[]{:S(2)}) collective-permute-start(bf16[64,16,128]{2,1,0:T(8,128)(2,1)S(1)} %pad_maximum_fusion.1.refs_4_), channel_id=1, source_target_pairs={{0,16},{8,24},{16,0},{24,8},{1,17},{9,25},{17,1},{25,9},{2,18},{10... | collective-permute-start | bytes 786440 | tf_op jit(solution)/shard_map/ppermute | solution.py:453
  96.4 0.1 collective-permute-start.18
  96.5 2.2 %collective-permute-start.13 = (bf16[64,48,128]{2,1,0:T(8,128)(2,1)S(1)}, bf16[64,48,128]{2,1,0:T(8,128)(2,1)S(1)}, u32[]{:S(2)}, u32[]{:S(2)}) collective-permute-start(bf16[64,48,128]{2,1,0:T(8,128)(2,1)S(1)} %pad_maximum_fusion.refs_0_), channel_id=1, source_target_pairs={{0,1},{1,0},{2,3},{3,2},{4,5},{5,4},{6,7},{7,6},{8,9},{9,8},{10,11... | collective-permute-start | bytes 2359304 | tf_op jit(solution)/shard_map/ppermute | solution.py:469
  98.7 15.9 %collective-permute-done.16.refs_6_ = bf16[64,16,128]{2,1,0:T(8,128)(2,1)S(1)} collective-permute-done((bf16[64,16,128]{2,1,0:T(8,128)(2,1)S(1)}, bf16[64,16,128]{2,1,0:T(8,128)(2,1)S(1)}, u32[]{:S(2)}, u32[]{:S(2)}) %collective-permute-start.16) | collective-permute-done | bytes 262176 | tf_op jit(solution)/shard_map/ppermute | solution.py:453
  114.8 2.0 %collective-permute-start.22 = (bf16[64,16,128]{2,1,0:T(8,128)(2,1)S(1)}, bf16[64,16,128]{2,1,0:T(8,128)(2,1)S(1)}, u32[]{:S(2)}, u32[]{:S(2)}) collective-permute-start(bf16[64,16,128]{2,1,0:T(8,128)(2,1)S(1)} %pad_maximum_fusion.1.refs_4_), channel_id=1, source_target_pairs={{0,1},{1,0},{2,3},{3,2},{4,5},{5,4},{6,7},{7,6},{8,9},{9,8},{10,11... | collective-permute-start | bytes 786440 | tf_op jit(solution)/shard_map/ppermute | solution.py:469
  116.7 3.9 %collective-permute-done.25.refs_7_ = bf16[64,16,128]{2,1,0:T(8,128)(2,1)} collective-permute-done((bf16[64,16,128]{2,1,0:T(8,128)(2,1)S(1)}, bf16[64,16,128]{2,1,0:T(8,128)(2,1)}, u32[]{:S(2)}, u32[]{:S(2)}) %collective-permute-start.25) | collective-permute-done | bytes 262176 | tf_op jit(solution)/shard_map/ppermute | solution.py:453
  120.6 2.8 %collective-permute-start.26 = (bf16[64,16,128]{2,1,0:T(8,128)(2,1)}, bf16[64,16,128]{2,1,0:T(8,128)(2,1)}, u32[]{:S(2)}, u32[]{:S(2)}) collective-permute-start(bf16[64,16,128]{2,1,0:T(8,128)(2,1)} %collective-permute-done.25.refs_7_), channel_id=1, source_target_pairs={{0,1},{1,0},{2,3},{3,2},{4,5},{5,4},{6,7},{7,6},{8,9},{9,8},{10,11... | collective-permute-start | bytes 786440 | tf_op jit(solution)/shard_map/ppermute | solution.py:469
  123.6 1.3 collective-permute-done.26.refs_7_
  125.0 0.4 collective-permute-start.23
  125.3 0.1 collective-permute-start.24
  125.5 0.4 collective-permute-start.19
  125.9 2.0 %collective-permute-start.21 = (bf16[64,48,128]{2,1,0:T(8,128)(2,1)}, bf16[64,48,128]{2,1,0:T(8,128)(2,1)S(1)}, u32[]{:S(2)}, u32[]{:S(2)}) collective-permute-start(bf16[64,48,128]{2,1,0:T(8,128)(2,1)} %collective-permute-done.20.refs_3_), channel_id=1, source_target_pairs={{0,1},{1,0},{2,3},{3,2},{4,5},{5,4},{6,7},{7,6},{8,9},{9,8},{10,11... | collective-permute-start | bytes 2359304 | tf_op jit(solution)/shard_map/ppermute | solution.py:469
  127.9 9.8 %shard_map.78.refs_8_ = bf16[512,128,128]{2,1,0:T(8,128)(2,1)} custom-call(s32[1]{0:T(128)} %bitcast.6.half_ref, s32[4,512]{1,0:T(4,128)S(1)} %get-tuple-element.57.places_ref, f32[1,512]{1,0:T(1,128)S(1)} %constant_dynamic-slice_fusion.root_ref, f32[1,128]{1,0:T(1,128)S(1)} %bitcast.33, bf16[64,48,128]{2,1,0:T(8,128)(2,1)S(1)} %pad_maximum_fusion.refs_0_, ...), custom_call_target="tpu_custom_call" | custom-call | flops 17179869184 | bytes 16777216 | tf_op jit(solution)/shard_map/pallas_call | solution.py:428
  137.7 9.6 %shard_map.79 = bf16[512,128,128]{2,1,0:T(8,128)(2,1)} custom-call(s32[1]{0:T(128)} %bitcast.half_ref, s32[4,512]{1,0:T(4,128)S(1)} %add_add_fusion.1.places_ref, f32[1,512]{1,0:T(1,128)S(1)} %constant_dynamic-slice_fusion.root_ref, f32[1,128]{1,0:T(1,128)S(1)} %bitcast.34, ...), custom_call_target="tpu_custom_call", output_to_operand_aliasing={{}: (12, {})} | custom-call | flops 17179869184 | bytes 16777216 | tf_op jit(solution)/shard_map/pallas_call | solution.py:428
  (51 shorter events, 0.7 us)
Async XLA Ops:
  0.0 0.8 copy-start.1
  0.8 0.7 copy-start.3
  14.1 18.6 %all-to-all-start = ((bf16[8,4,144,128]{3,2,1,0:T(8,128)(2,1)}), bf16[8,4,144,128]{3,2,1,0:T(8,128)(2,1)S(1)}, u32[]{:S(2)}, u32[]{:S(2)}) async-start(bf16[8,4,144,128]{3,2,1,0:T(8,128)(2,1)} %get-tuple-element.32), calls=%async_computation | async-start | bytes 2359296 | tf_op jit(solution)/shard_map/all_to_all | solution.py:282
  19.3 20.3 %copy-start.4 = (f32[256]{0:T(256)S(1)}, f32[256]{0:T(256)}, u32[]{:S(2)}) copy-start(f32[256]{0:T(256)} %param.9) | copy-start | bytes 3076
  19.3 20.4 %copy-start.6 = (s32[128,3]{0,1:T(4,128)S(1)}, s32[128,3]{0,1:T(4,128)}, u32[]{:S(2)}) copy-start(s32[128,3]{0,1:T(4,128)} %param.11) | copy-start | bytes 4612
  19.3 20.5 %copy-start.7 = (f32[128]{0:T(128)S(1)}, f32[128]{0:T(128)}, u32[]{:S(2)}) copy-start(f32[128]{0:T(128)} %param.12) | copy-start | bytes 1540
  19.3 49.0 %copy-start = (bf16[128,128]{1,0:T(8,128)(2,1)S(1)}, bf16[128,128]{1,0:T(8,128)(2,1)}, u32[]{:S(2)}) copy-start(bf16[128,128]{1,0:T(8,128)(2,1)} %mixing_ref.1) | copy-start | bytes 98308
  19.3 95.3 %copy-start.2 = (s32[2048,4]{0,1:T(4,128)S(1)}, s32[2048,4]{0,1:T(4,128)}, u32[]{:S(2)}) copy-start(s32[2048,4]{0,1:T(4,128)} %param.8) | copy-start | bytes 98308
  19.3 108.5 %copy-start.5 = (f32[128]{0:T(128)S(1)}, f32[128]{0:T(128)}, u32[]{:S(2)}) copy-start(f32[128]{0:T(128)} %param.13) | copy-start | bytes 1540
  32.7 21.8 %all-to-all-start.1 = ((bf16[8,4,128,128]{3,2,1,0:T(8,128)(2,1)}), bf16[8,4,128,128]{3,2,1,0:T(8,128)(2,1)S(1)}, u32[]{:S(2)}, u32[]{:S(2)}) async-start(bf16[8,4,128,128]{3,2,1,0:T(8,128)(2,1)} %shard_map.74), calls=%async_computation.1 | async-start | bytes 2097152 | tf_op jit(solution)/shard_map/all_to_all | solution.py:285
  40.4 7.3 %collective-permute-start = (bf16[4,144,128]{2,1,0:T(8,128)(2,1)S(1)}, bf16[4,144,128]{2,1,0:T(8,128)(2,1)S(1)}, u32[]{:S(2)}, u32[]{:S(2)}) collective-permute-start(bf16[4,144,128]{2,1,0:T(8,128)(2,1)S(1)} %get-tuple-element.36), channel_id=1, source_target_pairs={{0,8},{8,16},{16,24},{24,0},{1,9},{9,17},{17,25},{25,1},{2,10},{10... | collective-permute-start | bytes 442376 | tf_op jit(solution)/shard_map/ppermute | solution.py:453
  41.8 12.7 %collective-permute-start.1 = (bf16[4,144,128]{2,1,0:T(8,128)(2,1)S(1)}, bf16[4,144,128]{2,1,0:T(8,128)(2,1)S(1)}, u32[]{:S(2)}, u32[]{:S(2)}) collective-permute-start(bf16[4,144,128]{2,1,0:T(8,128)(2,1)S(1)} %get-tuple-element.37), channel_id=1, source_target_pairs={{0,16},{8,24},{16,0},{24,8},{1,17},{9,25},{17,1},{25,9},{2,18},{10... | collective-permute-start | bytes 442376 | tf_op jit(solution)/shard_map/ppermute | solution.py:453
  44.1 10.4 %collective-permute-start.2 = (bf16[4,144,128]{2,1,0:T(8,128)(2,1)S(1)}, bf16[4,144,128]{2,1,0:T(8,128)(2,1)S(1)}, u32[]{:S(2)}, u32[]{:S(2)}) collective-permute-start(bf16[4,144,128]{2,1,0:T(8,128)(2,1)S(1)} %get-tuple-element.38), channel_id=1, source_target_pairs={{0,24},{8,0},{16,8},{24,16},{1,25},{9,1},{17,9},{25,17},{2,26},{10... | collective-permute-start | bytes 442376 | tf_op jit(solution)/shard_map/ppermute | solution.py:453
  54.6 7.0 %collective-permute-start.3 = (bf16[4,128,128]{2,1,0:T(8,128)(2,1)S(1)}, bf16[4,128,128]{2,1,0:T(8,128)(2,1)S(1)}, u32[]{:S(2)}, u32[]{:S(2)}) collective-permute-start(bf16[4,128,128]{2,1,0:T(8,128)(2,1)S(1)} %get-tuple-element.41), channel_id=1, source_target_pairs={{0,8},{8,16},{16,24},{24,0},{1,9},{9,17},{17,25},{25,1},{2,10},{10... | collective-permute-start | bytes 393224 | tf_op jit(solution)/shard_map/ppermute | solution.py:453
  58.1 10.2 %collective-permute-start.4 = (bf16[4,128,128]{2,1,0:T(8,128)(2,1)S(1)}, bf16[4,128,128]{2,1,0:T(8,128)(2,1)S(1)}, u32[]{:S(2)}, u32[]{:S(2)}) collective-permute-start(bf16[4,128,128]{2,1,0:T(8,128)(2,1)S(1)} %get-tuple-element.42), channel_id=1, source_target_pairs={{0,16},{8,24},{16,0},{24,8},{1,17},{9,25},{17,1},{25,9},{2,18},{10... | collective-permute-start | bytes 393224 | tf_op jit(solution)/shard_map/ppermute | solution.py:453
  59.0 9.3 %collective-permute-start.5 = (bf16[4,128,128]{2,1,0:T(8,128)(2,1)S(1)}, bf16[4,128,128]{2,1,0:T(8,128)(2,1)S(1)}, u32[]{:S(2)}, u32[]{:S(2)}) collective-permute-start(bf16[4,128,128]{2,1,0:T(8,128)(2,1)S(1)} %get-tuple-element.43), channel_id=1, source_target_pairs={{0,24},{8,0},{16,8},{24,16},{1,25},{9,1},{17,9},{25,17},{2,26},{10... | collective-permute-start | bytes 393224 | tf_op jit(solution)/shard_map/ppermute | solution.py:453
  68.9 1.6 %collective-permute-start.6 = (bf16[8,64,128]{2,1,0:T(8,128)(2,1)S(1)}, bf16[8,64,128]{2,1,0:T(8,128)(2,1)S(1)}, u32[]{:S(2)}, u32[]{:S(2)}) collective-permute-start(bf16[8,64,128]{2,1,0:T(8,128)(2,1)S(1)} %get-tuple-element.49), channel_id=1, source_target_pairs={{0,1},{1,0},{2,3},{3,2},{4,5},{5,4},{6,7},{7,6},{8,9},{9,8},{10,11... | collective-permute-start | bytes 393224 | tf_op jit(solution)/shard_map/ppermute | solution.py:469
  70.6 7.3 %collective-permute-start.9 = (bf16[16,16,128]{2,1,0:T(8,128)(2,1)S(1)}, bf16[16,16,128]{2,1,0:T(8,128)(2,1)S(1)}, u32[]{:S(2)}, u32[]{:S(2)}) collective-permute-start(bf16[16,16,128]{2,1,0:T(8,128)(2,1)S(1)} %slice.18), channel_id=1, source_target_pairs={{0,6},{1,7},{2,4},{3,5},{4,2},{5,3},{6,0},{7,1},{8,14},{9,15},{10,... | collective-permute-start | bytes 196616 | tf_op jit(solution)/shard_map/ppermute | solution.py:465
  72.8 8.6 %collective-permute-start.12 = (bf16[16,48,128]{2,1,0:T(8,128)(2,1)S(1)}, bf16[16,48,128]{2,1,0:T(8,128)(2,1)S(1)}, u32[]{:S(2)}, u32[]{:S(2)}) collective-permute-start(bf16[16,48,128]{2,1,0:T(8,128)(2,1)S(1)} %slice.19), channel_id=1, source_target_pairs={{0,24},{8,0},{16,8},{24,16},{1,25},{9,1},{17,9},{25,17},{2,26},{10... | collective-permute-start | bytes 589832 | tf_op jit(solution)/shard_map/ppermute | solution.py:453
  77.2 16.7 %collective-permute-start.11 = (bf16[16,48,128]{2,1,0:T(8,128)(2,1)S(1)}, bf16[16,48,128]{2,1,0:T(8,128)(2,1)S(1)}, u32[]{:S(2)}, u32[]{:S(2)}) collective-permute-start(bf16[16,48,128]{2,1,0:T(8,128)(2,1)S(1)} %slice.19), channel_id=1, source_target_pairs={{0,16},{8,24},{16,0},{24,8},{1,17},{9,25},{17,1},{25,9},{2,18},{10... | collective-permute-start | bytes 589832 | tf_op jit(solution)/shard_map/ppermute | solution.py:453
  77.2 16.7 %collective-permute-start.10 = (bf16[16,48,128]{2,1,0:T(8,128)(2,1)S(1)}, bf16[16,48,128]{2,1,0:T(8,128)(2,1)S(1)}, u32[]{:S(2)}, u32[]{:S(2)}) collective-permute-start(bf16[16,48,128]{2,1,0:T(8,128)(2,1)S(1)} %slice.19), channel_id=1, source_target_pairs={{0,8},{8,16},{16,24},{24,0},{1,9},{9,17},{17,25},{25,1},{2,10},{10... | collective-permute-start | bytes 589832 | tf_op jit(solution)/shard_map/ppermute | solution.py:453
  77.6 3.4 %collective-permute-start.8 = (bf16[16,16,128]{2,1,0:T(8,128)(2,1)S(1)}, bf16[16,16,128]{2,1,0:T(8,128)(2,1)S(1)}, u32[]{:S(2)}, u32[]{:S(2)}) collective-permute-start(bf16[16,16,128]{2,1,0:T(8,128)(2,1)S(1)} %slice.18), channel_id=1, source_target_pairs={{0,4},{1,3},{2,6},{3,1},{4,0},{5,7},{6,2},{7,5},{8,12},{9,11},{10,... | collective-permute-start | bytes 196616 | tf_op jit(solution)/shard_map/ppermute | solution.py:461
  77.9 3.4 %collective-permute-start.7 = (bf16[16,16,128]{2,1,0:T(8,128)(2,1)S(1)}, bf16[16,16,128]{2,1,0:T(8,128)(2,1)S(1)}, u32[]{:S(2)}, u32[]{:S(2)}) collective-permute-start(bf16[16,16,128]{2,1,0:T(8,128)(2,1)S(1)} %slice.18), channel_id=1, source_target_pairs={{0,2},{1,5},{2,0},{3,7},{4,6},{5,1},{6,4},{7,3},{8,10},{9,13},{10,... | collective-permute-start | bytes 196616 | tf_op jit(solution)/shard_map/ppermute | solution.py:461
  94.1 20.5 %collective-permute-start.14 = (bf16[64,48,128]{2,1,0:T(8,128)(2,1)S(1)}, bf16[64,48,128]{2,1,0:T(8,128)(2,1)S(1)}, u32[]{:S(2)}, u32[]{:S(2)}) collective-permute-start(bf16[64,48,128]{2,1,0:T(8,128)(2,1)S(1)} %pad_maximum_fusion.refs_0_), channel_id=1, source_target_pairs={{0,2},{1,5},{2,0},{3,7},{4,6},{5,1},{6,4},{7,3},{8,10},{9,13},{10,... | collective-permute-start | bytes 2359304 | tf_op jit(solution)/shard_map/ppermute | solution.py:461
  94.4 20.2 %collective-permute-start.16 = (bf16[64,16,128]{2,1,0:T(8,128)(2,1)S(1)}, bf16[64,16,128]{2,1,0:T(8,128)(2,1)S(1)}, u32[]{:S(2)}, u32[]{:S(2)}) collective-permute-start(bf16[64,16,128]{2,1,0:T(8,128)(2,1)S(1)} %pad_maximum_fusion.1.refs_4_), channel_id=1, source_target_pairs={{0,16},{8,24},{16,0},{24,8},{1,17},{9,25},{17,1},{25,9},{2,18},{10... | collective-permute-start | bytes 786440 | tf_op jit(solution)/shard_map/ppermute | solution.py:453
  96.4 18.2 %collective-permute-start.15 = (bf16[64,16,128]{2,1,0:T(8,128)(2,1)S(1)}, bf16[64,16,128]{2,1,0:T(8,128)(2,1)S(1)}, u32[]{:S(2)}, u32[]{:S(2)}) collective-permute-start(bf16[64,16,128]{2,1,0:T(8,128)(2,1)S(1)} %pad_maximum_fusion.1.refs_4_), channel_id=1, source_target_pairs={{0,8},{8,16},{16,24},{24,0},{1,9},{9,17},{17,25},{25,1},{2,10},{10... | collective-permute-start | bytes 786440 | tf_op jit(solution)/shard_map/ppermute | solution.py:453
  96.4 28.9 %collective-permute-start.18 = (bf16[64,48,128]{2,1,0:T(8,128)(2,1)S(1)}, bf16[64,48,128]{2,1,0:T(8,128)(2,1)}, u32[]{:S(2)}, u32[]{:S(2)}) collective-permute-start(bf16[64,48,128]{2,1,0:T(8,128)(2,1)S(1)} %pad_maximum_fusion.refs_0_), channel_id=1, source_target_pairs={{0,4},{1,3},{2,6},{3,1},{4,0},{5,7},{6,2},{7,5},{8,12},{9,11},{10,... | collective-permute-start | bytes 2359304 | tf_op jit(solution)/shard_map/ppermute | solution.py:461
  96.5 29.0 %collective-permute-start.13 = (bf16[64,48,128]{2,1,0:T(8,128)(2,1)S(1)}, bf16[64,48,128]{2,1,0:T(8,128)(2,1)S(1)}, u32[]{:S(2)}, u32[]{:S(2)}) collective-permute-start(bf16[64,48,128]{2,1,0:T(8,128)(2,1)S(1)} %pad_maximum_fusion.refs_0_), channel_id=1, source_target_pairs={{0,1},{1,0},{2,3},{3,2},{4,5},{5,4},{6,7},{7,6},{8,9},{9,8},{10,11... | collective-permute-start | bytes 2359304 | tf_op jit(solution)/shard_map/ppermute | solution.py:469
  114.6 11.3 %collective-permute-start.20 = (bf16[64,48,128]{2,1,0:T(8,128)(2,1)S(1)}, bf16[64,48,128]{2,1,0:T(8,128)(2,1)}, u32[]{:S(2)}, u32[]{:S(2)}) collective-permute-start(bf16[64,48,128]{2,1,0:T(8,128)(2,1)S(1)} %collective-permute-done.14.refs_1_), channel_id=1, source_target_pairs={{0,4},{1,3},{2,6},{3,1},{4,0},{5,7},{6,2},{7,5},{8,12},{9,11},{10,... | collective-permute-start | bytes 2359304 | tf_op jit(solution)/shard_map/ppermute | solution.py:461
  114.6 6.0 %collective-permute-start.25 = (bf16[64,16,128]{2,1,0:T(8,128)(2,1)S(1)}, bf16[64,16,128]{2,1,0:T(8,128)(2,1)}, u32[]{:S(2)}, u32[]{:S(2)}) collective-permute-start(bf16[64,16,128]{2,1,0:T(8,128)(2,1)S(1)} %pad_maximum_fusion.1.refs_4_), channel_id=1, source_target_pairs={{0,24},{8,0},{16,8},{24,16},{1,25},{9,1},{17,9},{25,17},{2,26},{10... | collective-permute-start | bytes 786440 | tf_op jit(solution)/shard_map/ppermute | solution.py:453
  114.8 8.8 %collective-permute-start.22 = (bf16[64,16,128]{2,1,0:T(8,128)(2,1)S(1)}, bf16[64,16,128]{2,1,0:T(8,128)(2,1)S(1)}, u32[]{:S(2)}, u32[]{:S(2)}) collective-permute-start(bf16[64,16,128]{2,1,0:T(8,128)(2,1)S(1)} %pad_maximum_fusion.1.refs_4_), channel_id=1, source_target_pairs={{0,1},{1,0},{2,3},{3,2},{4,5},{5,4},{6,7},{7,6},{8,9},{9,8},{10,11... | collective-permute-start | bytes 786440 | tf_op jit(solution)/shard_map/ppermute | solution.py:469
  120.6 4.4 %collective-permute-start.26 = (bf16[64,16,128]{2,1,0:T(8,128)(2,1)}, bf16[64,16,128]{2,1,0:T(8,128)(2,1)}, u32[]{:S(2)}, u32[]{:S(2)}) collective-permute-start(bf16[64,16,128]{2,1,0:T(8,128)(2,1)} %collective-permute-done.25.refs_7_), channel_id=1, source_target_pairs={{0,1},{1,0},{2,3},{3,2},{4,5},{5,4},{6,7},{7,6},{8,9},{9,8},{10,11... | collective-permute-start | bytes 786440 | tf_op jit(solution)/shard_map/ppermute | solution.py:469
  123.6 14.1 %collective-permute-start.17 = (bf16[64,48,128]{2,1,0:T(8,128)(2,1)S(1)}, bf16[64,48,128]{2,1,0:T(8,128)(2,1)S(1)}, u32[]{:S(2)}, u32[]{:S(2)}) collective-permute-start(bf16[64,48,128]{2,1,0:T(8,128)(2,1)S(1)} %collective-permute-done.14.refs_1_), channel_id=1, source_target_pairs={{0,1},{1,0},{2,3},{3,2},{4,5},{5,4},{6,7},{7,6},{8,9},{9,8},{10,11... | collective-permute-start | bytes 2359304 | tf_op jit(solution)/shard_map/ppermute | solution.py:469
  125.0 12.7 %collective-permute-start.23 = (bf16[64,16,128]{2,1,0:T(8,128)(2,1)S(1)}, bf16[64,16,128]{2,1,0:T(8,128)(2,1)S(1)}, u32[]{:S(2)}, u32[]{:S(2)}) collective-permute-start(bf16[64,16,128]{2,1,0:T(8,128)(2,1)S(1)} %collective-permute-done.15.refs_5_), channel_id=1, source_target_pairs={{0,1},{1,0},{2,3},{3,2},{4,5},{5,4},{6,7},{7,6},{8,9},{9,8},{10,11... | collective-permute-start | bytes 786440 | tf_op jit(solution)/shard_map/ppermute | solution.py:469
  125.3 12.3 %collective-permute-start.24 = (bf16[64,16,128]{2,1,0:T(8,128)(2,1)S(1)}, bf16[64,16,128]{2,1,0:T(8,128)(2,1)S(1)}, u32[]{:S(2)}, u32[]{:S(2)}) collective-permute-start(bf16[64,16,128]{2,1,0:T(8,128)(2,1)S(1)} %collective-permute-done.16.refs_6_), channel_id=1, source_target_pairs={{0,1},{1,0},{2,3},{3,2},{4,5},{5,4},{6,7},{7,6},{8,9},{9,8},{10,11... | collective-permute-start | bytes 786440 | tf_op jit(solution)/shard_map/ppermute | solution.py:469
  125.5 12.2 %collective-permute-start.19 = (bf16[64,48,128]{2,1,0:T(8,128)(2,1)}, bf16[64,48,128]{2,1,0:T(8,128)(2,1)S(1)}, u32[]{:S(2)}, u32[]{:S(2)}) collective-permute-start(bf16[64,48,128]{2,1,0:T(8,128)(2,1)} %collective-permute-done.18.refs_2_), channel_id=1, source_target_pairs={{0,1},{1,0},{2,3},{3,2},{4,5},{5,4},{6,7},{7,6},{8,9},{9,8},{10,11... | collective-permute-start | bytes 2359304 | tf_op jit(solution)/shard_map/ppermute | solution.py:469
  125.9 11.8 %collective-permute-start.21 = (bf16[64,48,128]{2,1,0:T(8,128)(2,1)}, bf16[64,48,128]{2,1,0:T(8,128)(2,1)S(1)}, u32[]{:S(2)}, u32[]{:S(2)}) collective-permute-start(bf16[64,48,128]{2,1,0:T(8,128)(2,1)} %collective-permute-done.20.refs_3_), channel_id=1, source_target_pairs={{0,1},{1,0},{2,3},{3,2},{4,5},{5,4},{6,7},{7,6},{8,9},{9,8},{10,11... | collective-permute-start | bytes 2359304 | tf_op jit(solution)/shard_map/ppermute | solution.py:469

commit v13 on v11

--- a/solution.py
+++ b/solution.py
@@ -252,11 +252,12 @@
     seconds, roots, weighted = second_sums(line, cells, edges_t, edge_weight, plan)
     seconds = [shifted(part, shift) if shift else part for shift, part in enumerate(seconds)]
     first = first_sums(line, cells, weighted, plan)
-    first, *seconds[1::2] = lax.optimization_barrier((first, *seconds[1::2]))
+    first, seconds[1] = lax.optimization_barrier((first, seconds[1]))
     first = lax.all_to_all(first, SQUARE, split_axis=0, concat_axis=0, tiled=True)
-    second = fold(fold_second_kernel, plan, seconds, [(8, plan.rest, plan.second_rows, lanes)])[0]
     firsts = fold(fold_first_kernel, plan, [first], [(4, plan.first_rows, lanes)] * plan.line)
     firsts = [shifted(part, shift) if shift else part for shift, part in enumerate(firsts)]
+    *firsts[1:3], seconds[2] = lax.optimization_barrier((*firsts[1:3], seconds[2]))
+    second = fold(fold_second_kernel, plan, seconds, [(8, plan.rest, plan.second_rows, lanes)])[0]
     second = lax.all_to_all(second, SQUARE, split_axis=0, concat_axis=0, tiled=True)
     return firsts, second, roots
 
@@ -391,7 +392,7 @@
     zones = 2 * (longs[0].shape[1] + shorts[0].shape[1])
     edges = len(longs) * longs[0].shape[0]
     rows = min(16, anchors // 8)
-    slots = min(8, anchors // rows)
+    slots = min(4, anchors // rows)
     smem = pl.BlockSpec(memory_space=pltpu.SMEM)
     anywhere = pl.BlockSpec(memory_space=pltpu.HBM)
     pieces = longs + shorts + far[0] + far[1]
@@ -406,7 +407,7 @@
             pltpu.SemaphoreType.DMA((2 * len(longs) * (1 + len(shorts)),)),
             pltpu.SemaphoreType.DMA((slots,)),
         ],
-        compiler_params=pltpu.CompilerParams(vmem_limit_bytes=32 * 1024 * 1024),
+        compiler_params=pltpu.CompilerParams(vmem_limit_bytes=12 * 1024 * 1024),
         cost_estimate=pl.CostEstimate(
             flops=4096 * anchors * zones * lanes, bytes_accessed=4 * anchors * zones * lanes, transcendentals=0
         ),

time: 156 us -> 156 us (level)
  the two profiles are of different devices: /device:TPU:0 before, /device:TPU:13 now
where the time goes in v13:
time: 156 us; the launch traced here: 154 us
  waiting for transfers between devices  56 us (36%)
  starting transfers between devices  46.8 us (30%)
  Pallas kernels  34.9 us (22%)
  local copies, waits for them, and re-layouts  14.2 us (9%)
    ppermute x12, waiting for transfers between devices, shifted(): lax.ppermute(x, LINE, [(i, (i + amount) % size) for i in range(size)])  40.2 us
    ppermute x12, starting transfers between devices, shifted(): lax.ppermute(x, LINE, [(i, (i + amount) % size) for i in range(size)])  23.8 us
    pallas_call x2, Pallas kernels, half_sums(): pl.pallas_call(functools.partial(kernel, plan, begin, half, pitch), grid=...  17.3 us
    pallas_call x1, Pallas kernels, spread(): pl.pallas_call(functools.partial(spread_kernel, len(longs), len(shorts)),...  16 us
    unnamed x42, local copies, waits for them, and re-layouts  14.1 us
    all_to_all x1, waiting for transfers between devices, org_sums(): lax.all_to_all(first, SQUARE, split_axis=0, concat_axis=0, tiled=True)  8.91 us
    ppermute x9, starting transfers between devices, swapped(): return lax.ppermute(x, 'core', [(0, 1), (1, 0)])  7.84 us
    all_to_all x1, starting transfers between devices, org_sums(): lax.all_to_all(second, SQUARE, split_axis=0, concat_axis=0, tiled=True)  5.03 us
  transfers between devices with their start and end apart: 29, of which 17 were waited for; matrix products, arithmetic and copies ran while one was open for 1% of the time, Pallas kernels for 6%

profile of v13, /device:TPU:13, one launch (start us, length us, event | category | flops | bytes accessed | tf_op | source)
XLA Modules:
  0.0 153.6 jit_solution(18422291343501371601)
XLA Ops:
  1.4 8.8 %shard_map.73 = (bf16[8,144,128]{2,1,0:T(8,128)(2,1)S(1)}, bf16[8,144,128]{2,1,0:T(8,128)(2,1)S(1)}, bf16[8,144,128]{2,1,0:T(8,128)(2,1)S(1)}, bf16[8,144,128]{2...) custom-call(s32[1]{0:T(128)} %bitcast.2.line_ref, s32[4,2048]{1,0:T(4,128)S(1)} %bitcast.23, ...), custom_call_target="tpu_custom_call" | custom-call | flops 8589934592 | bytes 16777216 | tf_op jit(solution)/shard_map/pallas_call | solution.py:171
  10.3 1.4 collective-permute-start
  11.6 8.5 %shard_map.74 = bf16[8,4,128,128]{3,2,1,0:T(8,128)(2,1)} custom-call(s32[1]{0:T(128)} %bitcast.2.line_ref, bf16[256,2048]{1,0:T(8,128)(2,1)S(1)} %get-tuple-element.37.weighted_ref, bf16[2048,32,128]{2,1,0:T(8,128)(2,1)} %cells_ref.3), custom_call_target="tpu_custom_call" | custom-call | flops 8589934592 | bytes 16777216 | tf_op jit(solution)/shard_map/pallas_call | solution.py:171
  20.1 4.8 %all-to-all-start = ((bf16[8,4,128,128]{3,2,1,0:T(8,128)(2,1)}), bf16[8,4,128,128]{3,2,1,0:T(8,128)(2,1)S(1)}, u32[]{:S(2)}, u32[]{:S(2)}) async-start(bf16[8,4,128,128]{3,2,1,0:T(8,128)(2,1)} %shard_map.74), calls=%async_computation | async-start | bytes 2097152 | tf_op jit(solution)/shard_map/all_to_all | solution.py:256
  25.0 0.9 collective-permute-start.3
  25.9 1.5 %collective-permute-start.5 = (bf16[8,144,128]{2,1,0:T(8,128)(2,1)S(1)}, bf16[8,144,128]{2,1,0:T(8,128)(2,1)S(1)}, u32[]{:S(2)}, u32[]{:S(2)}) collective-permute-start(bf16[8,144,128]{2,1,0:T(8,128)(2,1)S(1)} %get-tuple-element.50), channel_id=1, source_target_pairs={{0,24},{8,0},{16,8},{24,16},{1,25},{9,1},{17,9},{25,17},{2,26},{10... | collective-permute-start | bytes 884744 | tf_op jit(solution)/shard_map/ppermute | solution.py:423
  27.7 8.9 %all-to-all-done.part_ref = bf16[8,4,128,128]{3,2,1,0:T(8,128)(2,1)S(1)} async-done(((bf16[8,4,128,128]{3,2,1,0:T(8,128)(2,1)}), bf16[8,4,128,128]{3,2,1,0:T(8,128)(2,1)S(1)}, u32[]{:S(2)}, u32[]{:S(2)}) %all-to-all-start) | async-done | bytes 1048608 | tf_op jit(solution)/shard_map/all_to_all | solution.py:256
  36.8 1.4 collective-permute-start.1
  38.1 1.4 collective-permute-start.2
  39.9 7.5 %collective-permute-done.3.refs_2_ = bf16[8,144,128]{2,1,0:T(8,128)(2,1)S(1)} collective-permute-done((bf16[8,144,128]{2,1,0:T(8,128)(2,1)S(1)}, bf16[8,144,128]{2,1,0:T(8,128)(2,1)S(1)}, u32[]{:S(2)}, u32[]{:S(2)}) %collective-permute-start.3) | collective-permute-done | bytes 294944 | tf_op jit(solution)/shard_map/ppermute | solution.py:423
  47.4 2.8 %collective-permute-done.1.refs_1_ = bf16[4,128,128]{2,1,0:T(8,128)(2,1)S(1)} collective-permute-done((bf16[4,128,128]{2,1,0:T(8,128)(2,1)S(1)}, bf16[4,128,128]{2,1,0:T(8,128)(2,1)S(1)}, u32[]{:S(2)}, u32[]{:S(2)}) %collective-permute-start.1) | collective-permute-done | bytes 131104 | tf_op jit(solution)/shard_map/ppermute | solution.py:423
  50.2 2.8 %collective-permute-done.2.refs_2_ = bf16[4,128,128]{2,1,0:T(8,128)(2,1)S(1)} collective-permute-done((bf16[4,128,128]{2,1,0:T(8,128)(2,1)S(1)}, bf16[4,128,128]{2,1,0:T(8,128)(2,1)S(1)}, u32[]{:S(2)}, u32[]{:S(2)}) %collective-permute-start.2) | collective-permute-done | bytes 131104 | tf_op jit(solution)/shard_map/ppermute | solution.py:423
  53.9 5.0 %all-to-all-start.1 = ((bf16[8,1,144,128]{3,2,1,0:T(8,128)(2,1)}), bf16[8,1,144,128]{3,2,1,0:T(8,128)(2,1)S(1)}, u32[]{:S(2)}, u32[]{:S(2)}) async-start(bf16[8,1,144,128]{3,2,1,0:T(8,128)(2,1)} %shard_map.76), calls=%async_computation.1 | async-start | bytes 589824 | tf_op jit(solution)/shard_map/all_to_all | solution.py:261
  59.0 2.8 %collective-permute-start.4 = (bf16[4,128,128]{2,1,0:T(8,128)(2,1)S(1)}, bf16[4,128,128]{2,1,0:T(8,128)(2,1)S(1)}, u32[]{:S(2)}, u32[]{:S(2)}) collective-permute-start(bf16[4,128,128]{2,1,0:T(8,128)(2,1)S(1)} %get-tuple-element.46), channel_id=1, source_target_pairs={{0,24},{8,0},{16,8},{24,16},{1,25},{9,1},{17,9},{25,17},{2,26},{10... | collective-permute-start | bytes 393224 | tf_op jit(solution)/shard_map/ppermute | solution.py:423
  61.9 2.5 %collective-permute-done.4.refs_3_ = bf16[4,128,128]{2,1,0:T(8,128)(2,1)S(1)} collective-permute-done((bf16[4,128,128]{2,1,0:T(8,128)(2,1)S(1)}, bf16[4,128,128]{2,1,0:T(8,128)(2,1)S(1)}, u32[]{:S(2)}, u32[]{:S(2)}) %collective-permute-start.4) | collective-permute-done | bytes 131104 | tf_op jit(solution)/shard_map/ppermute | solution.py:423
  65.0 1.2 collective-permute-start.6
  66.3 1.0 collective-permute-done.6
  67.3 1.2 collective-permute-start.9
  68.6 2.4 %collective-permute-start.12 = (bf16[16,48,128]{2,1,0:T(8,128)(2,1)S(1)}, bf16[16,48,128]{2,1,0:T(8,128)(2,1)S(1)}, u32[]{:S(2)}, u32[]{:S(2)}) collective-permute-start(bf16[16,48,128]{2,1,0:T(8,128)(2,1)S(1)} %pad_maximum_fusion.2), channel_id=1, source_target_pairs={{0,24},{8,0},{16,8},{24,16},{1,25},{9,1},{17,9},{25,17},{2,26},{10... | collective-permute-start | bytes 589832 | tf_op jit(solution)/shard_map/ppermute | solution.py:423
  71.0 2.0 %collective-permute-start.11 = (bf16[16,48,128]{2,1,0:T(8,128)(2,1)S(1)}, bf16[16,48,128]{2,1,0:T(8,128)(2,1)S(1)}, u32[]{:S(2)}, u32[]{:S(2)}) collective-permute-start(bf16[16,48,128]{2,1,0:T(8,128)(2,1)S(1)} %pad_maximum_fusion.2), channel_id=1, source_target_pairs={{0,16},{8,24},{16,0},{24,8},{1,17},{9,25},{17,1},{25,9},{2,18},{10... | collective-permute-start | bytes 589832 | tf_op jit(solution)/shard_map/ppermute | solution.py:423
  73.0 2.3 %collective-permute-start.10 = (bf16[16,48,128]{2,1,0:T(8,128)(2,1)S(1)}, bf16[16,48,128]{2,1,0:T(8,128)(2,1)S(1)}, u32[]{:S(2)}, u32[]{:S(2)}) collective-permute-start(bf16[16,48,128]{2,1,0:T(8,128)(2,1)S(1)} %pad_maximum_fusion.2), channel_id=1, source_target_pairs={{0,8},{8,16},{16,24},{24,0},{1,9},{9,17},{17,25},{25,1},{2,10},{10... | collective-permute-start | bytes 589832 | tf_op jit(solution)/shard_map/ppermute | solution.py:423
  75.3 1.2 collective-permute-start.8
  76.7 1.7 %collective-permute-done.8 = bf16[16,16,128]{2,1,0:T(8,128)(2,1)S(1)} collective-permute-done((bf16[16,16,128]{2,1,0:T(8,128)(2,1)S(1)}, bf16[16,16,128]{2,1,0:T(8,128)(2,1)S(1)}, u32[]{:S(2)}, u32[]{:S(2)}) %collective-permute-start.8) | collective-permute-done | bytes 65568 | tf_op jit(solution)/shard_map/ppermute | solution.py:435
  78.4 1.5 collective-permute-done.7
  79.9 5.3 %collective-permute-done.11 = bf16[16,48,128]{2,1,0:T(8,128)(2,1)S(1)} collective-permute-done((bf16[16,48,128]{2,1,0:T(8,128)(2,1)S(1)}, bf16[16,48,128]{2,1,0:T(8,128)(2,1)S(1)}, u32[]{:S(2)}, u32[]{:S(2)}) %collective-permute-start.11) | collective-permute-done | bytes 196640 | tf_op jit(solution)/shard_map/ppermute | solution.py:423
  85.2 4.2 %collective-permute-done.10 = bf16[16,48,128]{2,1,0:T(8,128)(2,1)S(1)} collective-permute-done((bf16[16,48,128]{2,1,0:T(8,128)(2,1)S(1)}, bf16[16,48,128]{2,1,0:T(8,128)(2,1)S(1)}, u32[]{:S(2)}, u32[]{:S(2)}) %collective-permute-start.10) | collective-permute-done | bytes 196640 | tf_op jit(solution)/shard_map/ppermute | solution.py:423
  89.6 1.4 collective-permute-start.14
  90.9 1.2 collective-permute-start.13
  92.4 2.2 %collective-permute-start.16 = (bf16[64,16,128]{2,1,0:T(8,128)(2,1)S(1)}, bf16[64,16,128]{2,1,0:T(8,128)(2,1)S(1)}, u32[]{:S(2)}, u32[]{:S(2)}) collective-permute-start(bf16[64,16,128]{2,1,0:T(8,128)(2,1)S(1)} %pad_maximum_fusion.1.refs_4_), channel_id=1, source_target_pairs={{0,8},{8,16},{16,24},{24,0},{1,9},{9,17},{17,25},{25,1},{2,10},{10... | collective-permute-start | bytes 786440 | tf_op jit(solution)/shard_map/ppermute | solution.py:423
  94.6 8.5 %collective-permute-done.17.refs_6_ = bf16[64,16,128]{2,1,0:T(8,128)(2,1)S(1)} collective-permute-done((bf16[64,16,128]{2,1,0:T(8,128)(2,1)S(1)}, bf16[64,16,128]{2,1,0:T(8,128)(2,1)S(1)}, u32[]{:S(2)}, u32[]{:S(2)}) %collective-permute-start.17) | collective-permute-done | bytes 262176 | tf_op jit(solution)/shard_map/ppermute | solution.py:423
  103.1 2.3 %collective-permute-start.15 = (bf16[64,16,128]{2,1,0:T(8,128)(2,1)S(1)}, bf16[64,16,128]{2,1,0:T(8,128)(2,1)S(1)}, u32[]{:S(2)}, u32[]{:S(2)}) collective-permute-start(bf16[64,16,128]{2,1,0:T(8,128)(2,1)S(1)} %pad_maximum_fusion.1.refs_4_), channel_id=1, source_target_pairs={{0,1},{1,0},{2,3},{3,2},{4,5},{5,4},{6,7},{7,6},{8,9},{9,8},{10,11... | collective-permute-start | bytes 786440 | tf_op jit(solution)/shard_map/ppermute | solution.py:439
  105.5 3.4 %collective-permute-done.16.refs_5_ = bf16[64,16,128]{2,1,0:T(8,128)(2,1)S(1)} collective-permute-done((bf16[64,16,128]{2,1,0:T(8,128)(2,1)S(1)}, bf16[64,16,128]{2,1,0:T(8,128)(2,1)S(1)}, u32[]{:S(2)}, u32[]{:S(2)}) %collective-permute-start.16) | collective-permute-done | bytes 262176 | tf_op jit(solution)/shard_map/ppermute | solution.py:423
  108.9 5.4 %collective-permute-start.24 = (bf16[64,16,128]{2,1,0:T(8,128)(2,1)S(1)}, bf16[64,16,128]{2,1,0:T(8,128)(2,1)S(1)}, u32[]{:S(2)}, u32[]{:S(2)}) collective-permute-start(bf16[64,16,128]{2,1,0:T(8,128)(2,1)S(1)} %pad_maximum_fusion.1.refs_4_), channel_id=1, source_target_pairs={{0,24},{8,0},{16,8},{24,16},{1,25},{9,1},{17,9},{25,17},{2,26},{10... | collective-permute-start | bytes 786440 | tf_op jit(solution)/shard_map/ppermute | solution.py:423
  114.7 0.9 copy-done.2
  115.8 1.2 collective-permute-start.19
  116.9 3.1 %collective-permute-done.24.refs_7_ = bf16[64,16,128]{2,1,0:T(8,128)(2,1)S(1)} collective-permute-done((bf16[64,16,128]{2,1,0:T(8,128)(2,1)S(1)}, bf16[64,16,128]{2,1,0:T(8,128)(2,1)S(1)}, u32[]{:S(2)}, u32[]{:S(2)}) %collective-permute-start.24) | collective-permute-done | bytes 262176 | tf_op jit(solution)/shard_map/ppermute | solution.py:423
  124.9 0.9 copy-done.4
  125.8 0.9 copy-done.6
  127.0 1.1 collective-permute-start.26
  128.9 1.5 collective-permute-done.26.refs_11_
  130.4 1.1 copy-done.3
  131.5 1.1 copy-done.5
  132.7 1.1 copy-done.7
  133.8 0.9 copy-done.9
  134.8 0.9 copy-done.11
  135.7 0.9 copy-done.13
  136.7 0.9 copy-done.15
  137.6 16.0 %shard_map.78 = bf16[512,128,128]{2,1,0:T(8,128)(2,1)} custom-call(s32[1]{0:T(128)} %bitcast.core_ref, s32[4,512]{1,0:T(4,128)S(1)} %fusion.13.places_ref, f32[1,512]{1,0:T(1,128)S(1)} %constant_dynamic-slice_fusion.root_ref, f32[1,128]{1,0:T(1,128)S(1)} %bitcast.25, bf16[64,48,128]{2,1,0:T(8,128)(2,1)S(1)} %pad_maximum_fusion.refs_0_, ...), custom_call_target="tpu_custom_call" | custom-call | flops 34359738368 | bytes 33554432 | tf_op jit(solution)/shard_map/pallas_call | solution.py:399
  (74 shorter events, 11.1 us)
Async XLA Ops:
  0.0 0.8 copy-start.1
  10.3 9.9 %collective-permute-start = (bf16[8,144,128]{2,1,0:T(8,128)(2,1)S(1)}, bf16[8,144,128]{2,1,0:T(8,128)(2,1)S(1)}, u32[]{:S(2)}, u32[]{:S(2)}) collective-permute-start(bf16[8,144,128]{2,1,0:T(8,128)(2,1)S(1)} %get-tuple-element.38), channel_id=1, source_target_pairs={{0,8},{8,16},{16,24},{24,0},{1,9},{9,17},{17,25},{25,1},{2,10},{10... | collective-permute-start | bytes 884744 | tf_op jit(solution)/shard_map/ppermute | solution.py:423
  11.6 15.8 %copy-start.19 = (s32[128,3]{0,1:T(4,128)S(1)}, s32[128,3]{0,1:T(4,128)}, u32[]{:S(2)}) copy-start(s32[128,3]{0,1:T(4,128)} %param.11) | copy-start | bytes 4612
  11.6 16.0 %copy-start.20 = (f32[128]{0:T(128)S(1)}, f32[128]{0:T(128)}, u32[]{:S(2)}) copy-start(f32[128]{0:T(128)} %param.12) | copy-start | bytes 1540
  11.6 47.3 %copy-start.17 = (f32[256]{0:T(256)S(1)}, f32[256]{0:T(256)}, u32[]{:S(2)}) copy-start(f32[256]{0:T(256)} %param.9) | copy-start | bytes 3076
  11.6 52.8 %copy-start = (bf16[128,128]{1,0:T(8,128)(2,1)S(1)}, bf16[128,128]{1,0:T(8,128)(2,1)}, u32[]{:S(2)}) copy-start(bf16[128,128]{1,0:T(8,128)(2,1)} %mixing_ref.1) | copy-start | bytes 98308
  11.6 118.8 %copy-start.18 = (f32[128]{0:T(128)S(1)}, f32[128]{0:T(128)}, u32[]{:S(2)}) copy-start(f32[128]{0:T(128)} %param.13) | copy-start | bytes 1540
  20.1 16.5 %all-to-all-start = ((bf16[8,4,128,128]{3,2,1,0:T(8,128)(2,1)}), bf16[8,4,128,128]{3,2,1,0:T(8,128)(2,1)S(1)}, u32[]{:S(2)}, u32[]{:S(2)}) async-start(bf16[8,4,128,128]{3,2,1,0:T(8,128)(2,1)} %shard_map.74), calls=%async_computation | async-start | bytes 2097152 | tf_op jit(solution)/shard_map/all_to_all | solution.py:256
  25.0 22.5 %collective-permute-start.3 = (bf16[8,144,128]{2,1,0:T(8,128)(2,1)S(1)}, bf16[8,144,128]{2,1,0:T(8,128)(2,1)S(1)}, u32[]{:S(2)}, u32[]{:S(2)}) collective-permute-start(bf16[8,144,128]{2,1,0:T(8,128)(2,1)S(1)} %get-tuple-element.43), channel_id=1, source_target_pairs={{0,16},{8,24},{16,0},{24,8},{1,17},{9,25},{17,1},{25,9},{2,18},{10... | collective-permute-start | bytes 884744 | tf_op jit(solution)/shard_map/ppermute | solution.py:423
  25.9 27.1 %collective-permute-start.5 = (bf16[8,144,128]{2,1,0:T(8,128)(2,1)S(1)}, bf16[8,144,128]{2,1,0:T(8,128)(2,1)S(1)}, u32[]{:S(2)}, u32[]{:S(2)}) collective-permute-start(bf16[8,144,128]{2,1,0:T(8,128)(2,1)S(1)} %get-tuple-element.50), channel_id=1, source_target_pairs={{0,24},{8,0},{16,8},{24,16},{1,25},{9,1},{17,9},{25,17},{2,26},{10... | collective-permute-start | bytes 884744 | tf_op jit(solution)/shard_map/ppermute | solution.py:423
  36.8 13.5 %collective-permute-start.1 = (bf16[4,128,128]{2,1,0:T(8,128)(2,1)S(1)}, bf16[4,128,128]{2,1,0:T(8,128)(2,1)S(1)}, u32[]{:S(2)}, u32[]{:S(2)}) collective-permute-start(bf16[4,128,128]{2,1,0:T(8,128)(2,1)S(1)} %get-tuple-element.41), channel_id=1, source_target_pairs={{0,8},{8,16},{16,24},{24,0},{1,9},{9,17},{17,25},{25,1},{2,10},{10... | collective-permute-start | bytes 393224 | tf_op jit(solution)/shard_map/ppermute | solution.py:423
  38.1 14.9 %collective-permute-start.2 = (bf16[4,128,128]{2,1,0:T(8,128)(2,1)S(1)}, bf16[4,128,128]{2,1,0:T(8,128)(2,1)S(1)}, u32[]{:S(2)}, u32[]{:S(2)}) collective-permute-start(bf16[4,128,128]{2,1,0:T(8,128)(2,1)S(1)} %get-tuple-element.42), channel_id=1, source_target_pairs={{0,16},{8,24},{16,0},{24,8},{1,17},{9,25},{17,1},{25,9},{2,18},{10... | collective-permute-start | bytes 393224 | tf_op jit(solution)/shard_map/ppermute | solution.py:423
  53.9 10.5 %all-to-all-start.1 = ((bf16[8,1,144,128]{3,2,1,0:T(8,128)(2,1)}), bf16[8,1,144,128]{3,2,1,0:T(8,128)(2,1)S(1)}, u32[]{:S(2)}, u32[]{:S(2)}) async-start(bf16[8,1,144,128]{3,2,1,0:T(8,128)(2,1)} %shard_map.76), calls=%async_computation.1 | async-start | bytes 589824 | tf_op jit(solution)/shard_map/all_to_all | solution.py:261
  59.0 5.3 %collective-permute-start.4 = (bf16[4,128,128]{2,1,0:T(8,128)(2,1)S(1)}, bf16[4,128,128]{2,1,0:T(8,128)(2,1)S(1)}, u32[]{:S(2)}, u32[]{:S(2)}) collective-permute-start(bf16[4,128,128]{2,1,0:T(8,128)(2,1)S(1)} %get-tuple-element.46), channel_id=1, source_target_pairs={{0,24},{8,0},{16,8},{24,16},{1,25},{9,1},{17,9},{25,17},{2,26},{10... | collective-permute-start | bytes 393224 | tf_op jit(solution)/shard_map/ppermute | solution.py:423
  65.0 2.2 %collective-permute-start.6 = (bf16[8,64,128]{2,1,0:T(8,128)(2,1)S(1)}, bf16[8,64,128]{2,1,0:T(8,128)(2,1)S(1)}, u32[]{:S(2)}, u32[]{:S(2)}) collective-permute-start(bf16[8,64,128]{2,1,0:T(8,128)(2,1)S(1)} %get-tuple-element.52), channel_id=1, source_target_pairs={{0,1},{1,0},{2,3},{3,2},{4,5},{5,4},{6,7},{7,6},{8,9},{9,8},{10,11... | collective-permute-start | bytes 393224 | tf_op jit(solution)/shard_map/ppermute | solution.py:439
  67.3 9.1 %collective-permute-start.9 = (bf16[16,16,128]{2,1,0:T(8,128)(2,1)S(1)}, bf16[16,16,128]{2,1,0:T(8,128)(2,1)S(1)}, u32[]{:S(2)}, u32[]{:S(2)}) collective-permute-start(bf16[16,16,128]{2,1,0:T(8,128)(2,1)S(1)} %pad_maximum_fusion.3), channel_id=1, source_target_pairs={{0,6},{1,7},{2,4},{3,5},{4,2},{5,3},{6,0},{7,1},{8,14},{9,15},{10,... | collective-permute-start | bytes 196616 | tf_op jit(solution)/shard_map/ppermute | solution.py:435
  68.6 11.3 %collective-permute-start.12 = (bf16[16,48,128]{2,1,0:T(8,128)(2,1)S(1)}, bf16[16,48,128]{2,1,0:T(8,128)(2,1)S(1)}, u32[]{:S(2)}, u32[]{:S(2)}) collective-permute-start(bf16[16,48,128]{2,1,0:T(8,128)(2,1)S(1)} %pad_maximum_fusion.2), channel_id=1, source_target_pairs={{0,24},{8,0},{16,8},{24,16},{1,25},{9,1},{17,9},{25,17},{2,26},{10... | collective-permute-start | bytes 589832 | tf_op jit(solution)/shard_map/ppermute | solution.py:423
  71.0 14.2 %collective-permute-start.11 = (bf16[16,48,128]{2,1,0:T(8,128)(2,1)S(1)}, bf16[16,48,128]{2,1,0:T(8,128)(2,1)S(1)}, u32[]{:S(2)}, u32[]{:S(2)}) collective-permute-start(bf16[16,48,128]{2,1,0:T(8,128)(2,1)S(1)} %pad_maximum_fusion.2), channel_id=1, source_target_pairs={{0,16},{8,24},{16,0},{24,8},{1,17},{9,25},{17,1},{25,9},{2,18},{10... | collective-permute-start | bytes 589832 | tf_op jit(solution)/shard_map/ppermute | solution.py:423
  73.0 16.5 %collective-permute-start.10 = (bf16[16,48,128]{2,1,0:T(8,128)(2,1)S(1)}, bf16[16,48,128]{2,1,0:T(8,128)(2,1)S(1)}, u32[]{:S(2)}, u32[]{:S(2)}) collective-permute-start(bf16[16,48,128]{2,1,0:T(8,128)(2,1)S(1)} %pad_maximum_fusion.2), channel_id=1, source_target_pairs={{0,8},{8,16},{16,24},{24,0},{1,9},{9,17},{17,25},{25,1},{2,10},{10... | collective-permute-start | bytes 589832 | tf_op jit(solution)/shard_map/ppermute | solution.py:423
  75.3 3.1 %collective-permute-start.8 = (bf16[16,16,128]{2,1,0:T(8,128)(2,1)S(1)}, bf16[16,16,128]{2,1,0:T(8,128)(2,1)S(1)}, u32[]{:S(2)}, u32[]{:S(2)}) collective-permute-start(bf16[16,16,128]{2,1,0:T(8,128)(2,1)S(1)} %pad_maximum_fusion.3), channel_id=1, source_target_pairs={{0,4},{1,5},{2,6},{3,7},{4,0},{5,1},{6,2},{7,3},{8,12},{9,13},{10,... | collective-permute-start | bytes 196616 | tf_op jit(solution)/shard_map/ppermute | solution.py:435
  76.4 3.4 %collective-permute-start.7 = (bf16[16,16,128]{2,1,0:T(8,128)(2,1)S(1)}, bf16[16,16,128]{2,1,0:T(8,128)(2,1)S(1)}, u32[]{:S(2)}, u32[]{:S(2)}) collective-permute-start(bf16[16,16,128]{2,1,0:T(8,128)(2,1)S(1)} %pad_maximum_fusion.3), channel_id=1, source_target_pairs={{0,2},{1,3},{2,0},{3,1},{4,6},{5,7},{6,4},{7,5},{8,10},{9,11},{10,... | collective-permute-start | bytes 196616 | tf_op jit(solution)/shard_map/ppermute | solution.py:435
  89.6 24.7 %collective-permute-start.14 = (bf16[64,48,128]{2,1,0:T(8,128)(2,1)S(1)}, bf16[64,48,128]{2,1,0:T(8,128)(2,1)S(1)}, u32[]{:S(2)}, u32[]{:S(2)}) collective-permute-start(bf16[64,48,128]{2,1,0:T(8,128)(2,1)S(1)} %pad_maximum_fusion.refs_0_), channel_id=1, source_target_pairs={{0,1},{1,0},{2,3},{3,2},{4,5},{5,4},{6,7},{7,6},{8,9},{9,8},{10,11... | collective-permute-start | bytes 2359304 | tf_op jit(solution)/shard_map/ppermute | solution.py:439
  90.9 23.4 %collective-permute-start.13 = (bf16[64,48,128]{2,1,0:T(8,128)(2,1)S(1)}, bf16[64,48,128]{2,1,0:T(8,128)(2,1)S(1)}, u32[]{:S(2)}, u32[]{:S(2)}) collective-permute-start(bf16[64,48,128]{2,1,0:T(8,128)(2,1)S(1)} %pad_maximum_fusion.refs_0_), channel_id=1, source_target_pairs={{0,2},{1,5},{2,0},{3,7},{4,6},{5,1},{6,4},{7,3},{8,10},{9,13},{10,... | collective-permute-start | bytes 2359304 | tf_op jit(solution)/shard_map/ppermute | solution.py:431
  92.1 22.2 %collective-permute-start.18 = (bf16[64,48,128]{2,1,0:T(8,128)(2,1)S(1)}, bf16[64,48,128]{2,1,0:T(8,128)(2,1)S(1)}, u32[]{:S(2)}, u32[]{:S(2)}) collective-permute-start(bf16[64,48,128]{2,1,0:T(8,128)(2,1)S(1)} %pad_maximum_fusion.refs_0_), channel_id=1, source_target_pairs={{0,4},{1,3},{2,6},{3,1},{4,0},{5,7},{6,2},{7,5},{8,12},{9,11},{10,... | collective-permute-start | bytes 2359304 | tf_op jit(solution)/shard_map/ppermute | solution.py:431
  92.4 10.7 %collective-permute-start.17 = (bf16[64,16,128]{2,1,0:T(8,128)(2,1)S(1)}, bf16[64,16,128]{2,1,0:T(8,128)(2,1)S(1)}, u32[]{:S(2)}, u32[]{:S(2)}) collective-permute-start(bf16[64,16,128]{2,1,0:T(8,128)(2,1)S(1)} %pad_maximum_fusion.1.refs_4_), channel_id=1, source_target_pairs={{0,16},{8,24},{16,0},{24,8},{1,17},{9,25},{17,1},{25,9},{2,18},{10... | collective-permute-start | bytes 786440 | tf_op jit(solution)/shard_map/ppermute | solution.py:423
  92.4 16.5 %collective-permute-start.16 = (bf16[64,16,128]{2,1,0:T(8,128)(2,1)S(1)}, bf16[64,16,128]{2,1,0:T(8,128)(2,1)S(1)}, u32[]{:S(2)}, u32[]{:S(2)}) collective-permute-start(bf16[64,16,128]{2,1,0:T(8,128)(2,1)S(1)} %pad_maximum_fusion.1.refs_4_), channel_id=1, source_target_pairs={{0,8},{8,16},{16,24},{24,0},{1,9},{9,17},{17,25},{25,1},{2,10},{10... | collective-permute-start | bytes 786440 | tf_op jit(solution)/shard_map/ppermute | solution.py:423
  103.1 11.2 %collective-permute-start.15 = (bf16[64,16,128]{2,1,0:T(8,128)(2,1)S(1)}, bf16[64,16,128]{2,1,0:T(8,128)(2,1)S(1)}, u32[]{:S(2)}, u32[]{:S(2)}) collective-permute-start(bf16[64,16,128]{2,1,0:T(8,128)(2,1)S(1)} %pad_maximum_fusion.1.refs_4_), channel_id=1, source_target_pairs={{0,1},{1,0},{2,3},{3,2},{4,5},{5,4},{6,7},{7,6},{8,9},{9,8},{10,11... | collective-permute-start | bytes 786440 | tf_op jit(solution)/shard_map/ppermute | solution.py:439
  108.9 11.1 %collective-permute-start.24 = (bf16[64,16,128]{2,1,0:T(8,128)(2,1)S(1)}, bf16[64,16,128]{2,1,0:T(8,128)(2,1)S(1)}, u32[]{:S(2)}, u32[]{:S(2)}) collective-permute-start(bf16[64,16,128]{2,1,0:T(8,128)(2,1)S(1)} %pad_maximum_fusion.1.refs_4_), channel_id=1, source_target_pairs={{0,24},{8,0},{16,8},{24,16},{1,25},{9,1},{17,9},{25,17},{2,26},{10... | collective-permute-start | bytes 786440 | tf_op jit(solution)/shard_map/ppermute | solution.py:423
  114.3 10.6 %collective-permute-start.21 = (bf16[64,48,128]{2,1,0:T(8,128)(2,1)S(1)}, bf16[64,48,128]{2,1,0:T(8,128)(2,1)S(1)}, u32[]{:S(2)}, u32[]{:S(2)}) collective-permute-start(bf16[64,48,128]{2,1,0:T(8,128)(2,1)S(1)} %collective-permute-done.18.refs_2_), channel_id=1, source_target_pairs={{0,1},{1,0},{2,3},{3,2},{4,5},{5,4},{6,7},{7,6},{8,9},{9,8},{10,11... | collective-permute-start | bytes 2359304 | tf_op jit(solution)/shard_map/ppermute | solution.py:439
  114.7 0.9 copy-start.2
  115.5 10.2 %collective-permute-start.20 = (bf16[64,48,128]{2,1,0:T(8,128)(2,1)S(1)}, bf16[64,48,128]{2,1,0:T(8,128)(2,1)S(1)}, u32[]{:S(2)}, u32[]{:S(2)}) collective-permute-start(bf16[64,48,128]{2,1,0:T(8,128)(2,1)S(1)} %collective-permute-done.13.refs_1_), channel_id=1, source_target_pairs={{0,1},{1,0},{2,3},{3,2},{4,5},{5,4},{6,7},{7,6},{8,9},{9,8},{10,11... | collective-permute-start | bytes 2359304 | tf_op jit(solution)/shard_map/ppermute | solution.py:439
  115.8 11.2 %collective-permute-start.19 = (bf16[64,48,128]{2,1,0:T(8,128)(2,1)S(1)}, bf16[64,48,128]{2,1,0:T(8,128)(2,1)}, u32[]{:S(2)}, u32[]{:S(2)}) collective-permute-start(bf16[64,48,128]{2,1,0:T(8,128)(2,1)S(1)} %collective-permute-done.13.refs_1_), channel_id=1, source_target_pairs={{0,4},{1,3},{2,6},{3,1},{4,0},{5,7},{6,2},{7,5},{8,12},{9,11},{10,... | collective-permute-start | bytes 2359304 | tf_op jit(solution)/shard_map/ppermute | solution.py:431
  120.0 1.9 %collective-permute-start.25 = (bf16[64,16,128]{2,1,0:T(8,128)(2,1)S(1)}, bf16[64,16,128]{2,1,0:T(8,128)(2,1)S(1)}, u32[]{:S(2)}, u32[]{:S(2)}) collective-permute-start(bf16[64,16,128]{2,1,0:T(8,128)(2,1)S(1)} %collective-permute-done.24.refs_7_), channel_id=1, source_target_pairs={{0,1},{1,0},{2,3},{3,2},{4,5},{5,4},{6,7},{7,6},{8,9},{9,8},{10,11... | collective-permute-start | bytes 786440 | tf_op jit(solution)/shard_map/ppermute | solution.py:439
  120.8 0.7 copy-start.8
  121.5 1.5 %collective-permute-start.22 = (bf16[64,16,128]{2,1,0:T(8,128)(2,1)S(1)}, bf16[64,16,128]{2,1,0:T(8,128)(2,1)S(1)}, u32[]{:S(2)}, u32[]{:S(2)}) collective-permute-start(bf16[64,16,128]{2,1,0:T(8,128)(2,1)S(1)} %collective-permute-done.16.refs_5_), channel_id=1, source_target_pairs={{0,1},{1,0},{2,3},{3,2},{4,5},{5,4},{6,7},{7,6},{8,9},{9,8},{10,11... | collective-permute-start | bytes 786440 | tf_op jit(solution)/shard_map/ppermute | solution.py:439
  122.0 0.7 copy-start.10
  122.7 1.5 %collective-permute-start.23 = (bf16[64,16,128]{2,1,0:T(8,128)(2,1)S(1)}, bf16[64,16,128]{2,1,0:T(8,128)(2,1)S(1)}, u32[]{:S(2)}, u32[]{:S(2)}) collective-permute-start(bf16[64,16,128]{2,1,0:T(8,128)(2,1)S(1)} %collective-permute-done.17.refs_6_), channel_id=1, source_target_pairs={{0,1},{1,0},{2,3},{3,2},{4,5},{5,4},{6,7},{7,6},{8,9},{9,8},{10,11... | collective-permute-start | bytes 786440 | tf_op jit(solution)/shard_map/ppermute | solution.py:439
  124.2 0.7 copy-start.14
  124.9 0.9 copy-start.4
  125.8 0.9 copy-start.6
  127.0 3.4 %collective-permute-start.26 = (bf16[64,48,128]{2,1,0:T(8,128)(2,1)}, bf16[64,48,128]{2,1,0:T(8,128)(2,1)}, u32[]{:S(2)}, u32[]{:S(2)}) collective-permute-start(bf16[64,48,128]{2,1,0:T(8,128)(2,1)} %collective-permute-done.19.refs_3_), channel_id=1, source_target_pairs={{0,1},{1,0},{2,3},{3,2},{4,5},{5,4},{6,7},{7,6},{8,9},{9,8},{10,11... | collective-permute-start | bytes 2359304 | tf_op jit(solution)/shard_map/ppermute | solution.py:439
  130.4 1.1 copy-start.3
  131.5 1.1 copy-start.5
  132.7 1.1 copy-start.7
  133.8 0.9 copy-start.9
  134.8 0.9 copy-start.11
  135.7 0.9 copy-start.13
  136.7 0.9 copy-start.15
  (2 other events, 1.4 us)

commit v14 on v9

--- a/solution.py
+++ b/solution.py
@@ -252,11 +252,12 @@
     seconds, roots, weighted = second_sums(line, cells, edges_t, edge_weight, plan)
     seconds = [shifted(part, shift) if shift else part for shift, part in enumerate(seconds)]
     first = first_sums(line, cells, weighted, plan)
-    first, *seconds[1::2] = lax.optimization_barrier((first, *seconds[1::2]))
+    first, seconds[1] = lax.optimization_barrier((first, seconds[1]))
     first = lax.all_to_all(first, SQUARE, split_axis=0, concat_axis=0, tiled=True)
-    second = fold(fold_second_kernel, plan, seconds, [(8, plan.rest, plan.second_rows, lanes)])[0]
     firsts = fold(fold_first_kernel, plan, [first], [(4, plan.first_rows, lanes)] * plan.line)
     firsts = [shifted(part, shift) if shift else part for shift, part in enumerate(firsts)]
+    *firsts[1:3], seconds[2] = lax.optimization_barrier((*firsts[1:3], seconds[2]))
+    second = fold(fold_second_kernel, plan, seconds, [(8, plan.rest, plan.second_rows, lanes)])[0]
     second = lax.all_to_all(second, SQUARE, split_axis=0, concat_axis=0, tiled=True)
     return firsts, second, roots
 
@@ -313,16 +314,20 @@
     )(weight_rows, mixing, matrix, *firsts, second)
 
 
-def spread_kernel(n_pieces, stride, offset, half_ref, places_ref, root_ref, bias_ref, *refs):
-    out_ref, table_ref, ring_ref, sems, ring_sems = refs[-5:]
-    slots, rows, zones, lanes = ring_ref.shape
+def spread_kernel(sides, n_pieces, stride, offset, halves_ref, places_ref, root_ref, bias_ref, *refs):
+    pieces = refs[: len(refs) - 4 - sides]
+    tables = refs[len(refs) - 3 - sides : len(refs) - 3]
+    out_ref = refs[len(refs) - 4 - sides]
+    ring_ref, sems, ring_sems = refs[-3:]
+    slots, _, rows, zones, lanes = ring_ref.shape
     steps = out_ref.shape[0] // rows
-    first_zone = pl.multiple_of(half_ref[0] * stride + offset, 16)
 
     copies = []
-    for i, source in enumerate(refs[:n_pieces]):
-        size = source.shape[0]
-        copies.append(pltpu.make_async_copy(source, table_ref.at[pl.ds(i * size, size)], sems.at[i]))
+    for side in range(sides):
+        for i, source in enumerate(pieces[side * n_pieces :][:n_pieces]):
+            size = source.shape[0]
+            place = tables[side].at[pl.ds(i * size, size)]
+            copies.append(pltpu.make_async_copy(source, place, sems.at[len(copies)]))
     for copy in copies:
         copy.start()
     for copy in copies:
@@ -331,19 +336,21 @@
     bias = bias_ref[...]
     count = places_ref.shape[0]
     tile = 16
-    batch = min(8 if zones > tile else 16, rows)
+    batch = min(8, rows)
     tiles = zones // tile
 
-    def leaving(step, slot):
+    def leaving(step, slot, side):
+        first_zone = pl.multiple_of(halves_ref[side] * stride + offset, 16)
         place = out_ref.at[pl.ds(step * rows, rows), pl.ds(first_zone, zones), :]
-        return pltpu.make_async_copy(ring_ref.at[slot], place, ring_sems.at[slot])
+        return pltpu.make_async_copy(ring_ref.at[slot, side], place, ring_sems.at[slot, side])
 
     def one_step(step, carry):
         slot = lax.rem(step, slots)
 
         @pl.when(step >= slots)
         def _():
-            leaving(step - slots, slot).wait()
+            for side in range(sides):
+                leaving(step - slots, slot, side).wait()
 
         def several(group, inner):
             values = []
@@ -351,50 +358,55 @@
                 at = step * rows + group * batch + i
                 scale = root_ref[0, at]
                 spots = [places_ref[j, at] for j in range(count)]
-                for first in range(0, zones, tile):
-                    pieces = [table_ref[spot, first : first + tile, :] for spot in spots]
-                    pieces = [(a + b).astype(F32) for a, b in zip(pieces[0::2], pieces[1::2])]
-                    total = sum(pieces[1:], pieces[0])
-                    values.append(jnp.maximum((total * scale + bias).astype(BF16), BF16(0.0)))
+                for side in range(sides):
+                    for first in range(0, zones, tile):
+                        parts = [tables[side][spot, first : first + tile, :] for spot in spots]
+                        parts = [(a + b).astype(F32) for a, b in zip(parts[0::2], parts[1::2])]
+                        total = sum(parts[1:], parts[0])
+                        values.append(jnp.maximum((total * scale + bias).astype(BF16), BF16(0.0)))
             for n, value in enumerate(values):
-                start = n % tiles * tile
-                ring_ref[slot, group * batch + n // tiles, start : start + tile, :] = value
+                i, side, start = n // (sides * tiles), n // tiles % sides, n % tiles * tile
+                ring_ref[slot, side, group * batch + i, start : start + tile, :] = value
             return inner
 
         lax.fori_loop(0, rows // batch, several, 0)
-        leaving(step, slot).start()
+        for side in range(sides):
+            leaving(step, slot, side).start()
         return carry
 
     lax.fori_loop(0, steps, one_step, 0)
     for step in range(steps - slots, steps):
-        leaving(step, step % slots).wait()
-
-
-def spread(half, places, root, bias, pieces, offset, stride, before=None):
+        for side in range(sides):
+            leaving(step, step % slots, side).wait()
+
+
+def spread(halves, places, root, bias, pieces, offset, stride, before=None):
+    sides = len(pieces)
     anchors = places.shape[1]
     lanes = bias.shape[1]
-    zones = pieces[0].shape[1]
+    count, zones = len(pieces[0]), pieces[0][0].shape[1]
+    edges = count * pieces[0][0].shape[0]
     rows = min(16, anchors // 8)
     slots = min(8, anchors // rows)
     smem = pl.BlockSpec(memory_space=pltpu.SMEM)
     anywhere = pl.BlockSpec(memory_space=pltpu.HBM)
-    operands = [half, places, root, bias] + pieces
-    specs = [smem, smem, smem, pl.BlockSpec(memory_space=pltpu.VMEM)] + [anywhere] * len(pieces)
+    operands = [halves, places, root, bias] + [piece for side in pieces for piece in side]
+    specs = [smem, smem, smem, pl.BlockSpec(memory_space=pltpu.VMEM)] + [anywhere] * (sides * count)
     aliases = {}
     if before is not None:
         aliases = {len(operands): 0}
         operands.append(before)
         specs.append(anywhere)
     return pl.pallas_call(
-        functools.partial(spread_kernel, len(pieces), stride, offset),
+        functools.partial(spread_kernel, sides, count, stride, offset),
         in_specs=specs,
         out_specs=anywhere,
         out_shape=jax.ShapeDtypeStruct((anchors, 2 * stride, lanes), BF16),
-        scratch_shapes=[
-            pltpu.VMEM((len(pieces) * pieces[0].shape[0], zones, lanes), BF16),
-            pltpu.VMEM((slots, rows, zones, lanes), BF16),
-            pltpu.SemaphoreType.DMA((len(pieces),)),
-            pltpu.SemaphoreType.DMA((slots,)),
+        scratch_shapes=[pltpu.VMEM((edges, zones, lanes), BF16)] * sides
+        + [
+            pltpu.VMEM((slots, sides, rows, zones, lanes), BF16),
+            pltpu.SemaphoreType.DMA((sides * count,)),
+            pltpu.SemaphoreType.DMA((slots, sides)),
         ],
         input_output_aliases=aliases,
         compiler_params=pltpu.CompilerParams(vmem_limit_bytes=24 * 1024 * 1024),
@@ -429,33 +441,34 @@
     return lax.ppermute(x, "core", [(0, 1), (1, 0)])
 
 
-def gather_table(keep, give):
+def gather_table(keep, give, core):
     size = lax.axis_size(LINE)
-    block = jnp.concatenate([keep, swapped(give)], axis=0)
+    got = swapped(give)
+    block = jnp.concatenate([jnp.where(core == 0, keep, got), jnp.where(core == 0, got, keep)], axis=0)
     split = block.shape[1] * 3 // 4
     long, short = block[:, :split], block[:, split:]
     line = [long] + [shifted(long, k) for k in range(1, size)]
-    short = jnp.concatenate([short, crossed(short, 0), crossed(short, 1), masked(short, 6)], axis=0)
+    short = jnp.concatenate([short, masked(short, 2), masked(short, 4), masked(short, 6)], axis=0)
     long = jnp.concatenate(line, axis=0)
     short, long = lax.optimization_barrier((short, long))
     first = crossed(long, 0)
     second = crossed(long, 1)
     shorts = [short] + [shifted(short, k) for k in range(1, size)]
-    first, *shorts[1:-1] = lax.optimization_barrier((first, *shorts[1:-1]))
-    both = crossed(first, 1)
-    return [long, first, second, both], shorts
+    first, shorts[1] = lax.optimization_barrier((first, shorts[1]))
+    return [long, first, second, crossed(first, 1)], shorts
 
 
 def places_of(ids, core, own):
     rest, size = lax.axis_size("rest"), lax.axis_size(LINE)
     owner = ids // own
-    slot = jnp.where(owner % 2 == core, 0, own) + ids % own
+    slot = owner % 2 * own + ids % own
     near = jnp.bitwise_xor(owner // 2 % 2, lax.axis_index("near"))
     mid = jnp.bitwise_xor(owner // (4 * rest) % 2, lax.axis_index("mid"))
     line = owner // (8 * rest) * rest + owner // 4 % rest
     line = lax.rem(lax.axis_index(LINE) - line + size, size)
     square = jnp.where(core == 0, 2 * mid + near, 2 * near + mid)
-    return (square * size + line) * (2 * own) + slot, (line * 4 + square) * (2 * own) + slot
+    short = (line * 4 + 2 * mid + near) * (2 * own) + slot
+    return (square * size + line) * (2 * own) + slot, short
 
 
 def relative_columns(matrix):
@@ -482,7 +495,7 @@
     half = matrix.shape[0] // 2
     matrix = jnp.where(core == 0, matrix, jnp.concatenate([matrix[half:], matrix[:half]], axis=0))
     keep, give = table_rows(firsts, second, weight_rows, mixing, matrix, plan)
-    longs, shorts = gather_table(keep, give)
+    longs, shorts = gather_table(keep, give, core)
     rows = anchor_edges.shape[0] // n_dst
     start = lax.axis_index(("rest", "near", "core")) * rows
     ids = lax.dynamic_slice_in_dim(edges_t, start, rows, 1)
@@ -490,15 +503,13 @@
     bias = out_bias[None, :]
     other = 1 - core
     long_places, short_places = places_of(ids, core, own)
-    far_long_places, far_short_places = places_of(ids, other, own)
+    far_long_places, _ = places_of(ids, other, own)
     split = longs[0].shape[1]
-    here, there = core[None], other[None]
-    result = spread(here, short_places, own_root, bias, shorts, split, half)
     far = [swapped(x) for x in shorts]
-    result = spread(there, far_short_places, own_root, bias, far, split, half, result)
-    result = spread(here, long_places, own_root, bias, longs, 0, half, result)
+    result = spread(jnp.stack([core, other]), short_places, own_root, bias, [shorts, far], split, half)
+    result = spread(core[None], long_places, own_root, bias, [longs], 0, half, result)
     far = [swapped(x) for x in longs]
-    return spread(there, far_long_places, own_root, bias, far, 0, half, result)
+    return spread(other[None], far_long_places, own_root, bias, [far], 0, half, result)
 
 
 def solution(mesh):

time: 144 us -> 142 us (0.986)
  waiting for transfers between devices: 62.5 us -> 55 us
  starting transfers between devices: 33.5 us -> 40.2 us
  Pallas kernels: 44.5 us -> 41.4 us
    ppermute x12, waiting for transfers between devices: 58.7 us -> 35 us  [shifted(): lax.ppermute(x, LINE, [(i, (i + amount) % size) for i in range(size)])]
    all_to_all x1, waiting for transfers between devices: 0.01 us -> 8.91 us  [org_sums(): lax.all_to_all(first, SQUARE, split_axis=0, concat_axis=0, tiled=True)]
    ppermute x5 -> x3, waiting for transfers between devices: 0.86 us -> 6.65 us  [crossed(): return lax.ppermute(x, SQUARE, pairs)]
    ppermute x12, starting transfers between devices: 11.9 us -> 16.6 us  [shifted(): lax.ppermute(x, LINE, [(i, (i + amount) % size) for i in range(size)])]
    pallas_call x4 -> x3, Pallas kernels: 25.6 us -> 22.6 us  [spread(): pl.pallas_call(functools.partial(spread_kernel, sides, count, stride, off...]
    ppermute x5 -> x3, starting transfers between devices: 5.57 us -> 3.75 us  [crossed(): return lax.ppermute(x, SQUARE, pairs)]
    ppermute x1 -> x3, starting transfers between devices: 1.17 us -> 2.71 us  [masked(): lax.ppermute(x, SQUARE, [(device, device ^ mask) for device in range(8)])]
  transfers between devices with their start and end apart: 29 -> 29, of which waited for: 12 -> 14; matrix products, arithmetic and copies ran while one was open for 1% -> 1% of each run, Pallas kernels for 20% -> 17%
where the time goes in v14:
time: 142 us; the launch traced here: 140 us
  waiting for transfers between devices  55 us (39%)
  Pallas kernels  41.4 us (29%)
  starting transfers between devices  40.2 us (28%)
  local copies, waits for them, and re-layouts  1.61 us (1%)
    ppermute x12, waiting for transfers between devices, shifted(): lax.ppermute(x, LINE, [(i, (i + amount) % size) for i in range(size)])  35 us
    pallas_call x3, Pallas kernels, spread(): pl.pallas_call(functools.partial(spread_kernel, sides, count, stride, off...  22.6 us
    pallas_call x2, Pallas kernels, half_sums(): pl.pallas_call(functools.partial(kernel, plan, begin, half, pitch), grid=...  17.3 us
    ppermute x12, starting transfers between devices, shifted(): lax.ppermute(x, LINE, [(i, (i + amount) % size) for i in range(size)])  16.6 us
    all_to_all x1, waiting for transfers between devices, org_sums(): lax.all_to_all(first, SQUARE, split_axis=0, concat_axis=0, tiled=True)  8.91 us
    ppermute x9, starting transfers between devices, swapped(): return lax.ppermute(x, 'core', [(0, 1), (1, 0)])  7.26 us
    ppermute x3, waiting for transfers between devices, crossed(): return lax.ppermute(x, SQUARE, pairs)  6.65 us
    all_to_all x1, starting transfers between devices, org_sums(): lax.all_to_all(second, SQUARE, split_axis=0, concat_axis=0, tiled=True)  5.03 us
  transfers between devices with their start and end apart: 29, of which 14 were waited for; matrix products, arithmetic and copies ran while one was open for 1% of the time, Pallas kernels for 17%

profile of v14, /device:TPU:13, one launch (start us, length us, event | category | flops | bytes accessed | tf_op | source)
XLA Modules:
  0.0 140.1 jit_solution(14742137281222545149)
XLA Ops:
  0.0 0.8 copy-done.1
  0.8 0.7 copy-done.3
  1.4 8.8 %shard_map.73 = (bf16[8,144,128]{2,1,0:T(8,128)(2,1)S(1)}, bf16[8,144,128]{2,1,0:T(8,128)(2,1)S(1)}, bf16[8,144,128]{2,1,0:T(8,128)(2,1)S(1)}, bf16[8,144,128]{2...) custom-call(s32[1]{0:T(128)} %bitcast.2.line_ref, s32[4,2048]{1,0:T(4,128)S(1)} %bitcast.26, ...), custom_call_target="tpu_custom_call" | custom-call | flops 8589934592 | bytes 16777216 | tf_op jit(solution)/shard_map/pallas_call | solution.py:171
  10.3 1.4 collective-permute-start
  11.6 8.5 %shard_map.74 = bf16[8,4,128,128]{3,2,1,0:T(8,128)(2,1)} custom-call(s32[1]{0:T(128)} %bitcast.2.line_ref, bf16[256,2048]{1,0:T(8,128)(2,1)S(1)} %get-tuple-element.27.weighted_ref, bf16[2048,32,128]{2,1,0:T(8,128)(2,1)} %cells_ref.3), custom_call_target="tpu_custom_call" | custom-call | flops 8589934592 | bytes 16777216 | tf_op jit(solution)/shard_map/pallas_call | solution.py:171
  20.1 4.8 %all-to-all-start = ((bf16[8,4,128,128]{3,2,1,0:T(8,128)(2,1)}), bf16[8,4,128,128]{3,2,1,0:T(8,128)(2,1)S(1)}, u32[]{:S(2)}, u32[]{:S(2)}) async-start(bf16[8,4,128,128]{3,2,1,0:T(8,128)(2,1)} %shard_map.74), calls=%async_computation | async-start | bytes 2097152 | tf_op jit(solution)/shard_map/all_to_all | solution.py:256
  25.0 0.9 collective-permute-start.3
  25.9 1.5 %collective-permute-start.5 = (bf16[8,144,128]{2,1,0:T(8,128)(2,1)S(1)}, bf16[8,144,128]{2,1,0:T(8,128)(2,1)S(1)}, u32[]{:S(2)}, u32[]{:S(2)}) collective-permute-start(bf16[8,144,128]{2,1,0:T(8,128)(2,1)S(1)} %get-tuple-element.40), channel_id=1, source_target_pairs={{0,24},{8,0},{16,8},{24,16},{1,25},{9,1},{17,9},{25,17},{2,26},{10... | collective-permute-start | bytes 884744 | tf_op jit(solution)/shard_map/ppermute | solution.py:425
  27.7 8.9 %all-to-all-done.part_ref = bf16[8,4,128,128]{3,2,1,0:T(8,128)(2,1)S(1)} async-done(((bf16[8,4,128,128]{3,2,1,0:T(8,128)(2,1)}), bf16[8,4,128,128]{3,2,1,0:T(8,128)(2,1)S(1)}, u32[]{:S(2)}, u32[]{:S(2)}) %all-to-all-start) | async-done | bytes 1048608 | tf_op jit(solution)/shard_map/all_to_all | solution.py:256
  36.8 1.4 collective-permute-start.1
  38.1 1.4 %collective-permute-start.2 = (bf16[4,128,128]{2,1,0:T(8,128)(2,1)S(1)}, bf16[4,128,128]{2,1,0:T(8,128)(2,1)S(1)}, u32[]{:S(2)}, u32[]{:S(2)}) collective-permute-start(bf16[4,128,128]{2,1,0:T(8,128)(2,1)S(1)} %get-tuple-element.32), channel_id=1, source_target_pairs={{0,16},{8,24},{16,0},{24,8},{1,17},{9,25},{17,1},{25,9},{2,18},{10... | collective-permute-start | bytes 393224 | tf_op jit(solution)/shard_map/ppermute | solution.py:425
  39.6 0.3 convolution_convert_fusion
  39.9 7.5 %collective-permute-done.3.refs_2_ = bf16[8,144,128]{2,1,0:T(8,128)(2,1)S(1)} collective-permute-done((bf16[8,144,128]{2,1,0:T(8,128)(2,1)S(1)}, bf16[8,144,128]{2,1,0:T(8,128)(2,1)S(1)}, u32[]{:S(2)}, u32[]{:S(2)}) %collective-permute-start.3) | collective-permute-done | bytes 294944 | tf_op jit(solution)/shard_map/ppermute | solution.py:425
  47.4 2.8 %collective-permute-done.1.refs_1_ = bf16[4,128,128]{2,1,0:T(8,128)(2,1)S(1)} collective-permute-done((bf16[4,128,128]{2,1,0:T(8,128)(2,1)S(1)}, bf16[4,128,128]{2,1,0:T(8,128)(2,1)S(1)}, u32[]{:S(2)}, u32[]{:S(2)}) %collective-permute-start.1) | collective-permute-done | bytes 131104 | tf_op jit(solution)/shard_map/ppermute | solution.py:425
  50.2 2.8 %collective-permute-done.2.refs_2_ = bf16[4,128,128]{2,1,0:T(8,128)(2,1)S(1)} collective-permute-done((bf16[4,128,128]{2,1,0:T(8,128)(2,1)S(1)}, bf16[4,128,128]{2,1,0:T(8,128)(2,1)S(1)}, u32[]{:S(2)}, u32[]{:S(2)}) %collective-permute-start.2) | collective-permute-done | bytes 131104 | tf_op jit(solution)/shard_map/ppermute | solution.py:425
  53.1 0.9 shard_map.76
  53.9 5.0 %all-to-all-start.1 = ((bf16[8,1,144,128]{3,2,1,0:T(8,128)(2,1)}), bf16[8,1,144,128]{3,2,1,0:T(8,128)(2,1)S(1)}, u32[]{:S(2)}, u32[]{:S(2)}) async-start(bf16[8,1,144,128]{3,2,1,0:T(8,128)(2,1)} %shard_map.76), calls=%async_computation.1 | async-start | bytes 589824 | tf_op jit(solution)/shard_map/all_to_all | solution.py:261
  59.0 2.8 %collective-permute-start.4 = (bf16[4,128,128]{2,1,0:T(8,128)(2,1)S(1)}, bf16[4,128,128]{2,1,0:T(8,128)(2,1)S(1)}, u32[]{:S(2)}, u32[]{:S(2)}) collective-permute-start(bf16[4,128,128]{2,1,0:T(8,128)(2,1)S(1)} %get-tuple-element.36), channel_id=1, source_target_pairs={{0,24},{8,0},{16,8},{24,16},{1,25},{9,1},{17,9},{25,17},{2,26},{10... | collective-permute-start | bytes 393224 | tf_op jit(solution)/shard_map/ppermute | solution.py:425
  61.9 2.5 %collective-permute-done.4.refs_3_ = bf16[4,128,128]{2,1,0:T(8,128)(2,1)S(1)} collective-permute-done((bf16[4,128,128]{2,1,0:T(8,128)(2,1)S(1)}, bf16[4,128,128]{2,1,0:T(8,128)(2,1)S(1)}, u32[]{:S(2)}, u32[]{:S(2)}) %collective-permute-start.4) | collective-permute-done | bytes 131104 | tf_op jit(solution)/shard_map/ppermute | solution.py:425
  64.5 0.5 shard_map.77
  65.0 1.3 collective-permute-start.6
  66.3 1.0 collective-permute-done.6
  67.3 1.2 collective-permute-start.7
  68.6 1.4 collective-permute-start.10
  69.9 3.1 %collective-permute-start.11 = (bf16[16,48,128]{2,1,0:T(8,128)(2,1)S(1)}, bf16[16,48,128]{2,1,0:T(8,128)(2,1)S(1)}, u32[]{:S(2)}, u32[]{:S(2)}) collective-permute-start(bf16[16,48,128]{2,1,0:T(8,128)(2,1)S(1)} %pad_maximum_fusion.2), channel_id=1, source_target_pairs={{0,16},{8,24},{16,0},{24,8},{1,17},{9,25},{17,1},{25,9},{2,18},{10... | collective-permute-start | bytes 589832 | tf_op jit(solution)/shard_map/ppermute | solution.py:425
  73.0 1.4 collective-permute-start.12
  74.6 1.2 collective-permute-start.9
  75.8 1.6 %collective-permute-done.8 = bf16[16,16,128]{2,1,0:T(8,128)(2,1)S(1)} collective-permute-done((bf16[16,16,128]{2,1,0:T(8,128)(2,1)S(1)}, bf16[16,16,128]{2,1,0:T(8,128)(2,1)S(1)}, u32[]{:S(2)}, u32[]{:S(2)}) %collective-permute-start.8) | collective-permute-done | bytes 65568 | tf_op jit(solution)/shard_map/ppermute | solution.py:437
  77.5 1.2 collective-permute-done.9
  78.7 7.4 %collective-permute-done.11 = bf16[16,48,128]{2,1,0:T(8,128)(2,1)S(1)} collective-permute-done((bf16[16,48,128]{2,1,0:T(8,128)(2,1)S(1)}, bf16[16,48,128]{2,1,0:T(8,128)(2,1)S(1)}, u32[]{:S(2)}, u32[]{:S(2)}) %collective-permute-start.11) | collective-permute-done | bytes 196640 | tf_op jit(solution)/shard_map/ppermute | solution.py:425
  86.2 4.7 %collective-permute-done.12 = bf16[16,48,128]{2,1,0:T(8,128)(2,1)S(1)} collective-permute-done((bf16[16,48,128]{2,1,0:T(8,128)(2,1)S(1)}, bf16[16,48,128]{2,1,0:T(8,128)(2,1)S(1)}, u32[]{:S(2)}, u32[]{:S(2)}) %collective-permute-start.12) | collective-permute-done | bytes 196640 | tf_op jit(solution)/shard_map/ppermute | solution.py:425
  91.0 0.5 collective-permute-start.14
  91.7 1.4 collective-permute-start.22
  93.1 5.6 %collective-permute-done.15.refs_1_ = bf16[64,16,128]{2,1,0:T(8,128)(2,1)S(1)} collective-permute-done((bf16[64,16,128]{2,1,0:T(8,128)(2,1)S(1)}, bf16[64,16,128]{2,1,0:T(8,128)(2,1)S(1)}, u32[]{:S(2)}, u32[]{:S(2)}) %collective-permute-start.15) | collective-permute-done | bytes 262176 | tf_op jit(solution)/shard_map/ppermute | solution.py:425
  98.7 2.8 %collective-permute-start.23 = (bf16[64,16,128]{2,1,0:T(8,128)(2,1)S(1)}, bf16[64,16,128]{2,1,0:T(8,128)(2,1)S(1)}, u32[]{:S(2)}, u32[]{:S(2)}) collective-permute-start(bf16[64,16,128]{2,1,0:T(8,128)(2,1)S(1)} %pad_maximum_fusion.1.refs_0_), channel_id=1, source_target_pairs={{0,1},{1,0},{2,3},{3,2},{4,5},{5,4},{6,7},{7,6},{8,9},{9,8},{10,11... | collective-permute-start | bytes 786440 | tf_op jit(solution)/shard_map/ppermute | solution.py:441
  101.5 0.8 multiply_add_fusion
  102.3 6.6 %collective-permute-done.14.refs_1_ = bf16[64,48,128]{2,1,0:T(8,128)(2,1)} collective-permute-done((bf16[64,48,128]{2,1,0:T(8,128)(2,1)S(1)}, bf16[64,48,128]{2,1,0:T(8,128)(2,1)}, u32[]{:S(2)}, u32[]{:S(2)}) %collective-permute-start.14) | collective-permute-done | bytes 786464 | tf_op jit(solution)/shard_map/ppermute | solution.py:433
  109.0 3.1 %collective-permute-start.19 = (bf16[64,48,128]{2,1,0:T(8,128)(2,1)}, bf16[64,48,128]{2,1,0:T(8,128)(2,1)}, u32[]{:S(2)}, u32[]{:S(2)}) collective-permute-start(bf16[64,48,128]{2,1,0:T(8,128)(2,1)} %collective-permute-done.14.refs_1_), channel_id=1, source_target_pairs={{0,4},{1,3},{2,6},{3,1},{4,0},{5,7},{6,2},{7,5},{8,12},{9,11},{10,... | collective-permute-start | bytes 2359304 | tf_op jit(solution)/shard_map/ppermute | solution.py:433
  112.0 1.6 %collective-permute-done.21.refs_2_ = bf16[64,16,128]{2,1,0:T(8,128)(2,1)S(1)} collective-permute-done((bf16[64,16,128]{2,1,0:T(8,128)(2,1)S(1)}, bf16[64,16,128]{2,1,0:T(8,128)(2,1)S(1)}, u32[]{:S(2)}, u32[]{:S(2)}) %collective-permute-start.21) | collective-permute-done | bytes 262176 | tf_op jit(solution)/shard_map/ppermute | solution.py:425
  113.6 1.3 collective-permute-start.25
  114.9 0.5 collective-permute-start.24
  115.6 0.5 collective-permute-done.25.refs_6_
  116.1 0.4 collective-permute-start.13
  116.5 0.4 collective-permute-start.16
  117.0 6.9 %shard_map.78.refs_4_ = bf16[512,128,128]{2,1,0:T(8,128)(2,1)} custom-call(s32[2]{0:T(128)S(1)} %pad_add_fusion.halves_ref, s32[4,512]{1,0:T(4,128)S(1)} %get-tuple-element.49.places_ref, f32[1,512]{1,0:T(1,128)S(1)} %constant_dynamic-slice_fusion.root_ref, f32[1,128]{1,0:T(1,128)S(1)} %bitcast.27, bf16[64,16,128]{2,1,0:T(8,128)(2,1)S(1)} %pad_maximum_fusion.1.refs_0_, ...), custom_call_target="tpu_custom_call" | custom-call | flops 4294967296 | bytes 4194304 | tf_op jit(solution)/shard_map/pallas_call | solution.py:400
  123.9 0.4 collective-permute-start.20
  124.3 8.5 %shard_map.79.refs_4_ = bf16[512,128,128]{2,1,0:T(8,128)(2,1)} custom-call(s32[1]{0:T(128)} %bitcast.6.halves_ref, s32[4,512]{1,0:T(4,128)S(1)} %get-tuple-element.56.places_ref, f32[1,512]{1,0:T(1,128)S(1)} %constant_dynamic-slice_fusion.root_ref, f32[1,128]{1,0:T(1,128)S(1)} %bitcast.28, ...), custom_call_target="tpu_custom_call", output_to_operand_aliasing={{}: (8, {})} | custom-call | flops 12884901888 | bytes 12582912 | tf_op jit(solution)/shard_map/pallas_call | solution.py:400
  132.9 7.1 %shard_map.80 = bf16[512,128,128]{2,1,0:T(8,128)(2,1)} custom-call(s32[1]{0:T(128)} %bitcast.halves_ref, s32[4,512]{1,0:T(4,128)S(1)} %get-tuple-element.57.places_ref, f32[1,512]{1,0:T(1,128)S(1)} %constant_dynamic-slice_fusion.root_ref, f32[1,128]{1,0:T(1,128)S(1)} %bitcast.29, ...), custom_call_target="tpu_custom_call", output_to_operand_aliasing={{}: (8, {})} | custom-call | flops 12884901888 | bytes 12582912 | tf_op jit(solution)/shard_map/pallas_call | solution.py:400
  (50 shorter events, 1.5 us)
Async XLA Ops:
  0.0 0.8 copy-start.1
  0.8 0.7 copy-start.3
  10.3 9.9 %collective-permute-start = (bf16[8,144,128]{2,1,0:T(8,128)(2,1)S(1)}, bf16[8,144,128]{2,1,0:T(8,128)(2,1)S(1)}, u32[]{:S(2)}, u32[]{:S(2)}) collective-permute-start(bf16[8,144,128]{2,1,0:T(8,128)(2,1)S(1)} %get-tuple-element.28), channel_id=1, source_target_pairs={{0,8},{8,16},{16,24},{24,0},{1,9},{9,17},{17,25},{25,1},{2,10},{10... | collective-permute-start | bytes 884744 | tf_op jit(solution)/shard_map/ppermute | solution.py:425
  11.6 15.8 %copy-start.5 = (s32[128,3]{0,1:T(4,128)S(1)}, s32[128,3]{0,1:T(4,128)}, u32[]{:S(2)}) copy-start(s32[128,3]{0,1:T(4,128)} %param.11) | copy-start | bytes 4612
  11.6 16.0 %copy-start.6 = (f32[128]{0:T(128)S(1)}, f32[128]{0:T(128)}, u32[]{:S(2)}) copy-start(f32[128]{0:T(128)} %param.12) | copy-start | bytes 1540
  11.6 47.3 %copy-start.4 = (f32[256]{0:T(256)S(1)}, f32[256]{0:T(256)}, u32[]{:S(2)}) copy-start(f32[256]{0:T(256)} %param.9) | copy-start | bytes 3076
  11.6 52.8 %copy-start = (bf16[128,128]{1,0:T(8,128)(2,1)S(1)}, bf16[128,128]{1,0:T(8,128)(2,1)}, u32[]{:S(2)}) copy-start(bf16[128,128]{1,0:T(8,128)(2,1)} %mixing_ref.1) | copy-start | bytes 98308
  11.6 105.4 %copy-start.2 = (f32[128]{0:T(128)S(1)}, f32[128]{0:T(128)}, u32[]{:S(2)}) copy-start(f32[128]{0:T(128)} %param.13) | copy-start | bytes 1540
  20.1 16.5 %all-to-all-start = ((bf16[8,4,128,128]{3,2,1,0:T(8,128)(2,1)}), bf16[8,4,128,128]{3,2,1,0:T(8,128)(2,1)S(1)}, u32[]{:S(2)}, u32[]{:S(2)}) async-start(bf16[8,4,128,128]{3,2,1,0:T(8,128)(2,1)} %shard_map.74), calls=%async_computation | async-start | bytes 2097152 | tf_op jit(solution)/shard_map/all_to_all | solution.py:256
  25.0 22.5 %collective-permute-start.3 = (bf16[8,144,128]{2,1,0:T(8,128)(2,1)S(1)}, bf16[8,144,128]{2,1,0:T(8,128)(2,1)S(1)}, u32[]{:S(2)}, u32[]{:S(2)}) collective-permute-start(bf16[8,144,128]{2,1,0:T(8,128)(2,1)S(1)} %get-tuple-element.33), channel_id=1, source_target_pairs={{0,16},{8,24},{16,0},{24,8},{1,17},{9,25},{17,1},{25,9},{2,18},{10... | collective-permute-start | bytes 884744 | tf_op jit(solution)/shard_map/ppermute | solution.py:425
  25.9 27.1 %collective-permute-start.5 = (bf16[8,144,128]{2,1,0:T(8,128)(2,1)S(1)}, bf16[8,144,128]{2,1,0:T(8,128)(2,1)S(1)}, u32[]{:S(2)}, u32[]{:S(2)}) collective-permute-start(bf16[8,144,128]{2,1,0:T(8,128)(2,1)S(1)} %get-tuple-element.40), channel_id=1, source_target_pairs={{0,24},{8,0},{16,8},{24,16},{1,25},{9,1},{17,9},{25,17},{2,26},{10... | collective-permute-start | bytes 884744 | tf_op jit(solution)/shard_map/ppermute | solution.py:425
  36.8 13.5 %collective-permute-start.1 = (bf16[4,128,128]{2,1,0:T(8,128)(2,1)S(1)}, bf16[4,128,128]{2,1,0:T(8,128)(2,1)S(1)}, u32[]{:S(2)}, u32[]{:S(2)}) collective-permute-start(bf16[4,128,128]{2,1,0:T(8,128)(2,1)S(1)} %get-tuple-element.31), channel_id=1, source_target_pairs={{0,8},{8,16},{16,24},{24,0},{1,9},{9,17},{17,25},{25,1},{2,10},{10... | collective-permute-start | bytes 393224 | tf_op jit(solution)/shard_map/ppermute | solution.py:425
  38.1 14.9 %collective-permute-start.2 = (bf16[4,128,128]{2,1,0:T(8,128)(2,1)S(1)}, bf16[4,128,128]{2,1,0:T(8,128)(2,1)S(1)}, u32[]{:S(2)}, u32[]{:S(2)}) collective-permute-start(bf16[4,128,128]{2,1,0:T(8,128)(2,1)S(1)} %get-tuple-element.32), channel_id=1, source_target_pairs={{0,16},{8,24},{16,0},{24,8},{1,17},{9,25},{17,1},{25,9},{2,18},{10... | collective-permute-start | bytes 393224 | tf_op jit(solution)/shard_map/ppermute | solution.py:425
  53.9 10.5 %all-to-all-start.1 = ((bf16[8,1,144,128]{3,2,1,0:T(8,128)(2,1)}), bf16[8,1,144,128]{3,2,1,0:T(8,128)(2,1)S(1)}, u32[]{:S(2)}, u32[]{:S(2)}) async-start(bf16[8,1,144,128]{3,2,1,0:T(8,128)(2,1)} %shard_map.76), calls=%async_computation.1 | async-start | bytes 589824 | tf_op jit(solution)/shard_map/all_to_all | solution.py:261
  59.0 5.3 %collective-permute-start.4 = (bf16[4,128,128]{2,1,0:T(8,128)(2,1)S(1)}, bf16[4,128,128]{2,1,0:T(8,128)(2,1)S(1)}, u32[]{:S(2)}, u32[]{:S(2)}) collective-permute-start(bf16[4,128,128]{2,1,0:T(8,128)(2,1)S(1)} %get-tuple-element.36), channel_id=1, source_target_pairs={{0,24},{8,0},{16,8},{24,16},{1,25},{9,1},{17,9},{25,17},{2,26},{10... | collective-permute-start | bytes 393224 | tf_op jit(solution)/shard_map/ppermute | solution.py:425
  65.0 2.2 %collective-permute-start.6 = (bf16[8,64,128]{2,1,0:T(8,128)(2,1)S(1)}, bf16[8,64,128]{2,1,0:T(8,128)(2,1)S(1)}, u32[]{:S(2)}, u32[]{:S(2)}) collective-permute-start(bf16[8,64,128]{2,1,0:T(8,128)(2,1)S(1)} %get-tuple-element.42), channel_id=1, source_target_pairs={{0,1},{1,0},{2,3},{3,2},{4,5},{5,4},{6,7},{7,6},{8,9},{9,8},{10,11... | collective-permute-start | bytes 393224 | tf_op jit(solution)/shard_map/ppermute | solution.py:441
  67.3 7.4 %collective-permute-start.7 = (bf16[16,16,128]{2,1,0:T(8,128)(2,1)S(1)}, bf16[16,16,128]{2,1,0:T(8,128)(2,1)S(1)}, u32[]{:S(2)}, u32[]{:S(2)}) collective-permute-start(bf16[16,16,128]{2,1,0:T(8,128)(2,1)S(1)} %pad_maximum_fusion.3), channel_id=1, source_target_pairs={{0,2},{1,3},{2,0},{3,1},{4,6},{5,7},{6,4},{7,5},{8,10},{9,11},{10,... | collective-permute-start | bytes 196616 | tf_op jit(solution)/shard_map/ppermute | solution.py:437
  68.6 10.1 %collective-permute-start.10 = (bf16[16,48,128]{2,1,0:T(8,128)(2,1)S(1)}, bf16[16,48,128]{2,1,0:T(8,128)(2,1)S(1)}, u32[]{:S(2)}, u32[]{:S(2)}) collective-permute-start(bf16[16,48,128]{2,1,0:T(8,128)(2,1)S(1)} %pad_maximum_fusion.2), channel_id=1, source_target_pairs={{0,8},{8,16},{16,24},{24,0},{1,9},{9,17},{17,25},{25,1},{2,10},{10... | collective-permute-start | bytes 589832 | tf_op jit(solution)/shard_map/ppermute | solution.py:425
  69.9 16.2 %collective-permute-start.11 = (bf16[16,48,128]{2,1,0:T(8,128)(2,1)S(1)}, bf16[16,48,128]{2,1,0:T(8,128)(2,1)S(1)}, u32[]{:S(2)}, u32[]{:S(2)}) collective-permute-start(bf16[16,48,128]{2,1,0:T(8,128)(2,1)S(1)} %pad_maximum_fusion.2), channel_id=1, source_target_pairs={{0,16},{8,24},{16,0},{24,8},{1,17},{9,25},{17,1},{25,9},{2,18},{10... | collective-permute-start | bytes 589832 | tf_op jit(solution)/shard_map/ppermute | solution.py:425
  73.0 17.9 %collective-permute-start.12 = (bf16[16,48,128]{2,1,0:T(8,128)(2,1)S(1)}, bf16[16,48,128]{2,1,0:T(8,128)(2,1)S(1)}, u32[]{:S(2)}, u32[]{:S(2)}) collective-permute-start(bf16[16,48,128]{2,1,0:T(8,128)(2,1)S(1)} %pad_maximum_fusion.2), channel_id=1, source_target_pairs={{0,24},{8,0},{16,8},{24,16},{1,25},{9,1},{17,9},{25,17},{2,26},{10... | collective-permute-start | bytes 589832 | tf_op jit(solution)/shard_map/ppermute | solution.py:425
  74.4 3.1 %collective-permute-start.8 = (bf16[16,16,128]{2,1,0:T(8,128)(2,1)S(1)}, bf16[16,16,128]{2,1,0:T(8,128)(2,1)S(1)}, u32[]{:S(2)}, u32[]{:S(2)}) collective-permute-start(bf16[16,16,128]{2,1,0:T(8,128)(2,1)S(1)} %pad_maximum_fusion.3), channel_id=1, source_target_pairs={{0,4},{1,5},{2,6},{3,7},{4,0},{5,1},{6,2},{7,3},{8,12},{9,13},{10,... | collective-permute-start | bytes 196616 | tf_op jit(solution)/shard_map/ppermute | solution.py:437
  74.6 4.0 %collective-permute-start.9 = (bf16[16,16,128]{2,1,0:T(8,128)(2,1)S(1)}, bf16[16,16,128]{2,1,0:T(8,128)(2,1)S(1)}, u32[]{:S(2)}, u32[]{:S(2)}) collective-permute-start(bf16[16,16,128]{2,1,0:T(8,128)(2,1)S(1)} %pad_maximum_fusion.3), channel_id=1, source_target_pairs={{0,6},{1,7},{2,4},{3,5},{4,2},{5,3},{6,0},{7,1},{8,14},{9,15},{10,... | collective-permute-start | bytes 196616 | tf_op jit(solution)/shard_map/ppermute | solution.py:437
  91.0 17.9 %collective-permute-start.14 = (bf16[64,48,128]{2,1,0:T(8,128)(2,1)S(1)}, bf16[64,48,128]{2,1,0:T(8,128)(2,1)}, u32[]{:S(2)}, u32[]{:S(2)}) collective-permute-start(bf16[64,48,128]{2,1,0:T(8,128)(2,1)S(1)} %pad_maximum_fusion.refs_0_), channel_id=1, source_target_pairs={{0,2},{1,5},{2,0},{3,7},{4,6},{5,1},{6,4},{7,3},{8,10},{9,13},{10,... | collective-permute-start | bytes 2359304 | tf_op jit(solution)/shard_map/ppermute | solution.py:433
  91.5 7.2 %collective-permute-start.15 = (bf16[64,16,128]{2,1,0:T(8,128)(2,1)S(1)}, bf16[64,16,128]{2,1,0:T(8,128)(2,1)S(1)}, u32[]{:S(2)}, u32[]{:S(2)}) collective-permute-start(bf16[64,16,128]{2,1,0:T(8,128)(2,1)S(1)} %pad_maximum_fusion.1.refs_0_), channel_id=1, source_target_pairs={{0,8},{8,16},{16,24},{24,0},{1,9},{9,17},{17,25},{25,1},{2,10},{10... | collective-permute-start | bytes 786440 | tf_op jit(solution)/shard_map/ppermute | solution.py:425
  91.6 25.3 %collective-permute-start.17 = (bf16[64,48,128]{2,1,0:T(8,128)(2,1)S(1)}, bf16[64,48,128]{2,1,0:T(8,128)(2,1)}, u32[]{:S(2)}, u32[]{:S(2)}) collective-permute-start(bf16[64,48,128]{2,1,0:T(8,128)(2,1)S(1)} %pad_maximum_fusion.refs_0_), channel_id=1, source_target_pairs={{0,4},{1,3},{2,6},{3,1},{4,0},{5,7},{6,2},{7,5},{8,12},{9,11},{10,... | collective-permute-start | bytes 2359304 | tf_op jit(solution)/shard_map/ppermute | solution.py:433
  91.7 21.9 %collective-permute-start.21 = (bf16[64,16,128]{2,1,0:T(8,128)(2,1)S(1)}, bf16[64,16,128]{2,1,0:T(8,128)(2,1)S(1)}, u32[]{:S(2)}, u32[]{:S(2)}) collective-permute-start(bf16[64,16,128]{2,1,0:T(8,128)(2,1)S(1)} %pad_maximum_fusion.1.refs_0_), channel_id=1, source_target_pairs={{0,16},{8,24},{16,0},{24,8},{1,17},{9,25},{17,1},{25,9},{2,18},{10... | collective-permute-start | bytes 786440 | tf_op jit(solution)/shard_map/ppermute | solution.py:425
  91.7 23.2 %collective-permute-start.22 = (bf16[64,16,128]{2,1,0:T(8,128)(2,1)S(1)}, bf16[64,16,128]{2,1,0:T(8,128)(2,1)S(1)}, u32[]{:S(2)}, u32[]{:S(2)}) collective-permute-start(bf16[64,16,128]{2,1,0:T(8,128)(2,1)S(1)} %pad_maximum_fusion.1.refs_0_), channel_id=1, source_target_pairs={{0,24},{8,0},{16,8},{24,16},{1,25},{9,1},{17,9},{25,17},{2,26},{10... | collective-permute-start | bytes 786440 | tf_op jit(solution)/shard_map/ppermute | solution.py:425
  98.7 16.2 %collective-permute-start.23 = (bf16[64,16,128]{2,1,0:T(8,128)(2,1)S(1)}, bf16[64,16,128]{2,1,0:T(8,128)(2,1)S(1)}, u32[]{:S(2)}, u32[]{:S(2)}) collective-permute-start(bf16[64,16,128]{2,1,0:T(8,128)(2,1)S(1)} %pad_maximum_fusion.1.refs_0_), channel_id=1, source_target_pairs={{0,1},{1,0},{2,3},{3,2},{4,5},{5,4},{6,7},{7,6},{8,9},{9,8},{10,11... | collective-permute-start | bytes 786440 | tf_op jit(solution)/shard_map/ppermute | solution.py:441
  109.0 15.0 %collective-permute-start.19 = (bf16[64,48,128]{2,1,0:T(8,128)(2,1)}, bf16[64,48,128]{2,1,0:T(8,128)(2,1)}, u32[]{:S(2)}, u32[]{:S(2)}) collective-permute-start(bf16[64,48,128]{2,1,0:T(8,128)(2,1)} %collective-permute-done.14.refs_1_), channel_id=1, source_target_pairs={{0,4},{1,3},{2,6},{3,1},{4,0},{5,7},{6,2},{7,5},{8,12},{9,11},{10,... | collective-permute-start | bytes 2359304 | tf_op jit(solution)/shard_map/ppermute | solution.py:433
  113.6 2.5 %collective-permute-start.25 = (bf16[64,16,128]{2,1,0:T(8,128)(2,1)S(1)}, bf16[64,16,128]{2,1,0:T(8,128)(2,1)S(1)}, u32[]{:S(2)}, u32[]{:S(2)}) collective-permute-start(bf16[64,16,128]{2,1,0:T(8,128)(2,1)S(1)} %collective-permute-done.21.refs_2_), channel_id=1, source_target_pairs={{0,1},{1,0},{2,3},{3,2},{4,5},{5,4},{6,7},{7,6},{8,9},{9,8},{10,11... | collective-permute-start | bytes 786440 | tf_op jit(solution)/shard_map/ppermute | solution.py:441
  114.9 1.5 %collective-permute-start.26 = (bf16[64,16,128]{2,1,0:T(8,128)(2,1)S(1)}, bf16[64,16,128]{2,1,0:T(8,128)(2,1)S(1)}, u32[]{:S(2)}, u32[]{:S(2)}) collective-permute-start(bf16[64,16,128]{2,1,0:T(8,128)(2,1)S(1)} %collective-permute-done.22.refs_3_), channel_id=1, source_target_pairs={{0,1},{1,0},{2,3},{3,2},{4,5},{5,4},{6,7},{7,6},{8,9},{9,8},{10,11... | collective-permute-start | bytes 786440 | tf_op jit(solution)/shard_map/ppermute | solution.py:441
  114.9 2.0 %collective-permute-start.24 = (bf16[64,16,128]{2,1,0:T(8,128)(2,1)S(1)}, bf16[64,16,128]{2,1,0:T(8,128)(2,1)S(1)}, u32[]{:S(2)}, u32[]{:S(2)}) collective-permute-start(bf16[64,16,128]{2,1,0:T(8,128)(2,1)S(1)} %collective-permute-done.15.refs_1_), channel_id=1, source_target_pairs={{0,1},{1,0},{2,3},{3,2},{4,5},{5,4},{6,7},{7,6},{8,9},{9,8},{10,11... | collective-permute-start | bytes 786440 | tf_op jit(solution)/shard_map/ppermute | solution.py:441
  116.1 16.8 %collective-permute-start.13 = (bf16[64,48,128]{2,1,0:T(8,128)(2,1)S(1)}, bf16[64,48,128]{2,1,0:T(8,128)(2,1)S(1)}, u32[]{:S(2)}, u32[]{:S(2)}) collective-permute-start(bf16[64,48,128]{2,1,0:T(8,128)(2,1)S(1)} %pad_maximum_fusion.refs_0_), channel_id=1, source_target_pairs={{0,1},{1,0},{2,3},{3,2},{4,5},{5,4},{6,7},{7,6},{8,9},{9,8},{10,11... | collective-permute-start | bytes 2359304 | tf_op jit(solution)/shard_map/ppermute | solution.py:441
  116.5 16.4 %collective-permute-start.16 = (bf16[64,48,128]{2,1,0:T(8,128)(2,1)}, bf16[64,48,128]{2,1,0:T(8,128)(2,1)S(1)}, u32[]{:S(2)}, u32[]{:S(2)}) collective-permute-start(bf16[64,48,128]{2,1,0:T(8,128)(2,1)} %collective-permute-done.14.refs_1_), channel_id=1, source_target_pairs={{0,1},{1,0},{2,3},{3,2},{4,5},{5,4},{6,7},{7,6},{8,9},{9,8},{10,11... | collective-permute-start | bytes 2359304 | tf_op jit(solution)/shard_map/ppermute | solution.py:441
  116.8 16.1 %collective-permute-start.18 = (bf16[64,48,128]{2,1,0:T(8,128)(2,1)}, bf16[64,48,128]{2,1,0:T(8,128)(2,1)S(1)}, u32[]{:S(2)}, u32[]{:S(2)}) collective-permute-start(bf16[64,48,128]{2,1,0:T(8,128)(2,1)} %collective-permute-done.17.refs_2_), channel_id=1, source_target_pairs={{0,1},{1,0},{2,3},{3,2},{4,5},{5,4},{6,7},{7,6},{8,9},{9,8},{10,11... | collective-permute-start | bytes 2359304 | tf_op jit(solution)/shard_map/ppermute | solution.py:441
  123.9 9.0 %collective-permute-start.20 = (bf16[64,48,128]{2,1,0:T(8,128)(2,1)}, bf16[64,48,128]{2,1,0:T(8,128)(2,1)S(1)}, u32[]{:S(2)}, u32[]{:S(2)}) collective-permute-start(bf16[64,48,128]{2,1,0:T(8,128)(2,1)} %collective-permute-done.19.refs_3_), channel_id=1, source_target_pairs={{0,1},{1,0},{2,3},{3,2},{4,5},{5,4},{6,7},{7,6},{8,9},{9,8},{10,11... | collective-permute-start | bytes 2359304 | tf_op jit(solution)/shard_map/ppermute | solution.py:441

commit v15 on v14

--- a/solution.py
+++ b/solution.py
@@ -89,7 +89,7 @@
             wide_ref[pl.ds(pl.multiple_of((first + j) * pitch, 8), zones), :] = piece[j]
         return carry
 
-    lax.fori_loop(0, rows // part, widen, 0)
+    lax.fori_loop(0, rows // part, widen, 0, unroll=4)
     for pair in range(zones // 2):
         left = wide_ref[pl.ds(2 * pair, rows, stride=pitch), :].astype(BF16)
         right = wide_ref[pl.ds(2 * pair + 1, rows, stride=pitch), :].astype(BF16)
@@ -361,8 +361,9 @@
                 for side in range(sides):
                     for first in range(0, zones, tile):
                         parts = [tables[side][spot, first : first + tile, :] for spot in spots]
-                        parts = [(a + b).astype(F32) for a, b in zip(parts[0::2], parts[1::2])]
-                        total = sum(parts[1:], parts[0])
+                        while len(parts) > 1:
+                            parts = [sum(parts[n + 1 : n + 2], parts[n]) for n in range(0, len(parts), 2)]
+                        total = parts[0].astype(F32)
                         values.append(jnp.maximum((total * scale + bias).astype(BF16), BF16(0.0)))
             for n, value in enumerate(values):
                 i, side, start = n // (sides * tiles), n // tiles % sides, n % tiles * tile

time: 142 us -> 142 us (level)
  no operation moved by 1% of the time
where the time goes in v15:
time: 142 us; the launch traced here: 140 us
  waiting for transfers between devices  55 us (39%)
  Pallas kernels  41.4 us (29%)
  starting transfers between devices  40.3 us (28%)
  local copies, waits for them, and re-layouts  1.61 us (1%)
    ppermute x12, waiting for transfers between devices, shifted(): lax.ppermute(x, LINE, [(i, (i + amount) % size) for i in range(size)])  35.1 us
    pallas_call x3, Pallas kernels, spread(): pl.pallas_call(functools.partial(spread_kernel, sides, count, stride, off...  22.8 us
    pallas_call x2, Pallas kernels, half_sums(): pl.pallas_call(functools.partial(kernel, plan, begin, half, pitch), grid=...  17 us
    ppermute x12, starting transfers between devices, shifted(): lax.ppermute(x, LINE, [(i, (i + amount) % size) for i in range(size)])  16.7 us
    all_to_all x1, waiting for transfers between devices, org_sums(): lax.all_to_all(first, SQUARE, split_axis=0, concat_axis=0, tiled=True)  8.91 us
    ppermute x9, starting transfers between devices, swapped(): return lax.ppermute(x, 'core', [(0, 1), (1, 0)])  7.23 us
    ppermute x3, waiting for transfers between devices, crossed(): return lax.ppermute(x, SQUARE, pairs)  6.67 us
    all_to_all x1, starting transfers between devices, org_sums(): lax.all_to_all(second, SQUARE, split_axis=0, concat_axis=0, tiled=True)  5.03 us
  transfers between devices with their start and end apart: 29, of which 14 were waited for; matrix products, arithmetic and copies ran while one was open for 1% of the time, Pallas kernels for 17%

profile of v15, /device:TPU:13, one launch (start us, length us, event | category | flops | bytes accessed | tf_op | source)
XLA Modules:
  0.0 140.2 jit_solution(682014278550963409)
XLA Ops:
  0.0 0.8 copy-done.1
  0.8 0.7 copy-done.3
  1.4 8.6 %shard_map.73 = (bf16[8,144,128]{2,1,0:T(8,128)(2,1)S(1)}, bf16[8,144,128]{2,1,0:T(8,128)(2,1)S(1)}, bf16[8,144,128]{2,1,0:T(8,128)(2,1)S(1)}, bf16[8,144,128]{2...) custom-call(s32[1]{0:T(128)} %bitcast.2.line_ref, s32[4,2048]{1,0:T(4,128)S(1)} %bitcast.26, ...), custom_call_target="tpu_custom_call" | custom-call | flops 8589934592 | bytes 16777216 | tf_op jit(solution)/shard_map/pallas_call | solution.py:171
  10.1 1.4 collective-permute-start
  11.5 8.4 %shard_map.74 = bf16[8,4,128,128]{3,2,1,0:T(8,128)(2,1)} custom-call(s32[1]{0:T(128)} %bitcast.2.line_ref, bf16[256,2048]{1,0:T(8,128)(2,1)S(1)} %get-tuple-element.27.weighted_ref, bf16[2048,32,128]{2,1,0:T(8,128)(2,1)} %cells_ref.3), custom_call_target="tpu_custom_call" | custom-call | flops 8589934592 | bytes 16777216 | tf_op jit(solution)/shard_map/pallas_call | solution.py:171
  19.9 4.8 %all-to-all-start = ((bf16[8,4,128,128]{3,2,1,0:T(8,128)(2,1)}), bf16[8,4,128,128]{3,2,1,0:T(8,128)(2,1)S(1)}, u32[]{:S(2)}, u32[]{:S(2)}) async-start(bf16[8,4,128,128]{3,2,1,0:T(8,128)(2,1)} %shard_map.74), calls=%async_computation | async-start | bytes 2097152 | tf_op jit(solution)/shard_map/all_to_all | solution.py:256
  24.7 1.0 collective-permute-start.3
  25.7 1.5 %collective-permute-start.5 = (bf16[8,144,128]{2,1,0:T(8,128)(2,1)S(1)}, bf16[8,144,128]{2,1,0:T(8,128)(2,1)S(1)}, u32[]{:S(2)}, u32[]{:S(2)}) collective-permute-start(bf16[8,144,128]{2,1,0:T(8,128)(2,1)S(1)} %get-tuple-element.40), channel_id=1, source_target_pairs={{0,24},{8,0},{16,8},{24,16},{1,25},{9,1},{17,9},{25,17},{2,26},{10... | collective-permute-start | bytes 884744 | tf_op jit(solution)/shard_map/ppermute | solution.py:426
  27.5 8.9 %all-to-all-done.part_ref = bf16[8,4,128,128]{3,2,1,0:T(8,128)(2,1)S(1)} async-done(((bf16[8,4,128,128]{3,2,1,0:T(8,128)(2,1)}), bf16[8,4,128,128]{3,2,1,0:T(8,128)(2,1)S(1)}, u32[]{:S(2)}, u32[]{:S(2)}) %all-to-all-start) | async-done | bytes 1048608 | tf_op jit(solution)/shard_map/all_to_all | solution.py:256
  36.5 1.4 collective-permute-start.1
  37.8 1.5 %collective-permute-start.2 = (bf16[4,128,128]{2,1,0:T(8,128)(2,1)S(1)}, bf16[4,128,128]{2,1,0:T(8,128)(2,1)S(1)}, u32[]{:S(2)}, u32[]{:S(2)}) collective-permute-start(bf16[4,128,128]{2,1,0:T(8,128)(2,1)S(1)} %get-tuple-element.32), channel_id=1, source_target_pairs={{0,16},{8,24},{16,0},{24,8},{1,17},{9,25},{17,1},{25,9},{2,18},{10... | collective-permute-start | bytes 393224 | tf_op jit(solution)/shard_map/ppermute | solution.py:426
  39.4 0.3 convolution_convert_fusion
  39.7 7.5 %collective-permute-done.3.refs_2_ = bf16[8,144,128]{2,1,0:T(8,128)(2,1)S(1)} collective-permute-done((bf16[8,144,128]{2,1,0:T(8,128)(2,1)S(1)}, bf16[8,144,128]{2,1,0:T(8,128)(2,1)S(1)}, u32[]{:S(2)}, u32[]{:S(2)}) %collective-permute-start.3) | collective-permute-done | bytes 294944 | tf_op jit(solution)/shard_map/ppermute | solution.py:426
  47.2 2.8 %collective-permute-done.1.refs_1_ = bf16[4,128,128]{2,1,0:T(8,128)(2,1)S(1)} collective-permute-done((bf16[4,128,128]{2,1,0:T(8,128)(2,1)S(1)}, bf16[4,128,128]{2,1,0:T(8,128)(2,1)S(1)}, u32[]{:S(2)}, u32[]{:S(2)}) %collective-permute-start.1) | collective-permute-done | bytes 131104 | tf_op jit(solution)/shard_map/ppermute | solution.py:426
  50.1 2.8 %collective-permute-done.2.refs_2_ = bf16[4,128,128]{2,1,0:T(8,128)(2,1)S(1)} collective-permute-done((bf16[4,128,128]{2,1,0:T(8,128)(2,1)S(1)}, bf16[4,128,128]{2,1,0:T(8,128)(2,1)S(1)}, u32[]{:S(2)}, u32[]{:S(2)}) %collective-permute-start.2) | collective-permute-done | bytes 131104 | tf_op jit(solution)/shard_map/ppermute | solution.py:426
  52.9 0.9 shard_map.76
  53.7 5.0 %all-to-all-start.1 = ((bf16[8,1,144,128]{3,2,1,0:T(8,128)(2,1)}), bf16[8,1,144,128]{3,2,1,0:T(8,128)(2,1)S(1)}, u32[]{:S(2)}, u32[]{:S(2)}) async-start(bf16[8,1,144,128]{3,2,1,0:T(8,128)(2,1)} %shard_map.76), calls=%async_computation.1 | async-start | bytes 589824 | tf_op jit(solution)/shard_map/all_to_all | solution.py:261
  58.9 2.8 %collective-permute-start.4 = (bf16[4,128,128]{2,1,0:T(8,128)(2,1)S(1)}, bf16[4,128,128]{2,1,0:T(8,128)(2,1)S(1)}, u32[]{:S(2)}, u32[]{:S(2)}) collective-permute-start(bf16[4,128,128]{2,1,0:T(8,128)(2,1)S(1)} %get-tuple-element.36), channel_id=1, source_target_pairs={{0,24},{8,0},{16,8},{24,16},{1,25},{9,1},{17,9},{25,17},{2,26},{10... | collective-permute-start | bytes 393224 | tf_op jit(solution)/shard_map/ppermute | solution.py:426
  61.7 2.5 %collective-permute-done.4.refs_3_ = bf16[4,128,128]{2,1,0:T(8,128)(2,1)S(1)} collective-permute-done((bf16[4,128,128]{2,1,0:T(8,128)(2,1)S(1)}, bf16[4,128,128]{2,1,0:T(8,128)(2,1)S(1)}, u32[]{:S(2)}, u32[]{:S(2)}) %collective-permute-start.4) | collective-permute-done | bytes 131104 | tf_op jit(solution)/shard_map/ppermute | solution.py:426
  64.3 0.5 shard_map.77
  64.8 1.3 collective-permute-start.6
  66.1 1.0 collective-permute-done.6
  67.1 1.2 collective-permute-start.7
  68.4 1.4 collective-permute-start.10
  69.7 3.1 %collective-permute-start.11 = (bf16[16,48,128]{2,1,0:T(8,128)(2,1)S(1)}, bf16[16,48,128]{2,1,0:T(8,128)(2,1)S(1)}, u32[]{:S(2)}, u32[]{:S(2)}) collective-permute-start(bf16[16,48,128]{2,1,0:T(8,128)(2,1)S(1)} %pad_maximum_fusion.2), channel_id=1, source_target_pairs={{0,16},{8,24},{16,0},{24,8},{1,17},{9,25},{17,1},{25,9},{2,18},{10... | collective-permute-start | bytes 589832 | tf_op jit(solution)/shard_map/ppermute | solution.py:426
  72.8 1.4 collective-permute-start.12
  74.5 1.2 collective-permute-start.9
  75.6 1.6 %collective-permute-done.8 = bf16[16,16,128]{2,1,0:T(8,128)(2,1)S(1)} collective-permute-done((bf16[16,16,128]{2,1,0:T(8,128)(2,1)S(1)}, bf16[16,16,128]{2,1,0:T(8,128)(2,1)S(1)}, u32[]{:S(2)}, u32[]{:S(2)}) %collective-permute-start.8) | collective-permute-done | bytes 65568 | tf_op jit(solution)/shard_map/ppermute | solution.py:438
  77.3 1.2 collective-permute-done.9
  78.5 7.4 %collective-permute-done.11 = bf16[16,48,128]{2,1,0:T(8,128)(2,1)S(1)} collective-permute-done((bf16[16,48,128]{2,1,0:T(8,128)(2,1)S(1)}, bf16[16,48,128]{2,1,0:T(8,128)(2,1)S(1)}, u32[]{:S(2)}, u32[]{:S(2)}) %collective-permute-start.11) | collective-permute-done | bytes 196640 | tf_op jit(solution)/shard_map/ppermute | solution.py:426
  86.0 4.7 %collective-permute-done.12 = bf16[16,48,128]{2,1,0:T(8,128)(2,1)S(1)} collective-permute-done((bf16[16,48,128]{2,1,0:T(8,128)(2,1)S(1)}, bf16[16,48,128]{2,1,0:T(8,128)(2,1)S(1)}, u32[]{:S(2)}, u32[]{:S(2)}) %collective-permute-start.12) | collective-permute-done | bytes 196640 | tf_op jit(solution)/shard_map/ppermute | solution.py:426
  90.8 0.5 collective-permute-start.14
  91.5 1.4 collective-permute-start.22
  92.9 5.6 %collective-permute-done.15.refs_1_ = bf16[64,16,128]{2,1,0:T(8,128)(2,1)S(1)} collective-permute-done((bf16[64,16,128]{2,1,0:T(8,128)(2,1)S(1)}, bf16[64,16,128]{2,1,0:T(8,128)(2,1)S(1)}, u32[]{:S(2)}, u32[]{:S(2)}) %collective-permute-start.15) | collective-permute-done | bytes 262176 | tf_op jit(solution)/shard_map/ppermute | solution.py:426
  98.5 2.8 %collective-permute-start.23 = (bf16[64,16,128]{2,1,0:T(8,128)(2,1)S(1)}, bf16[64,16,128]{2,1,0:T(8,128)(2,1)S(1)}, u32[]{:S(2)}, u32[]{:S(2)}) collective-permute-start(bf16[64,16,128]{2,1,0:T(8,128)(2,1)S(1)} %pad_maximum_fusion.1.refs_0_), channel_id=1, source_target_pairs={{0,1},{1,0},{2,3},{3,2},{4,5},{5,4},{6,7},{7,6},{8,9},{9,8},{10,11... | collective-permute-start | bytes 786440 | tf_op jit(solution)/shard_map/ppermute | solution.py:442
  101.3 0.8 multiply_add_fusion
  102.1 6.7 %collective-permute-done.14.refs_1_ = bf16[64,48,128]{2,1,0:T(8,128)(2,1)} collective-permute-done((bf16[64,48,128]{2,1,0:T(8,128)(2,1)S(1)}, bf16[64,48,128]{2,1,0:T(8,128)(2,1)}, u32[]{:S(2)}, u32[]{:S(2)}) %collective-permute-start.14) | collective-permute-done | bytes 786464 | tf_op jit(solution)/shard_map/ppermute | solution.py:434
  108.8 3.1 %collective-permute-start.19 = (bf16[64,48,128]{2,1,0:T(8,128)(2,1)}, bf16[64,48,128]{2,1,0:T(8,128)(2,1)}, u32[]{:S(2)}, u32[]{:S(2)}) collective-permute-start(bf16[64,48,128]{2,1,0:T(8,128)(2,1)} %collective-permute-done.14.refs_1_), channel_id=1, source_target_pairs={{0,4},{1,3},{2,6},{3,1},{4,0},{5,7},{6,2},{7,5},{8,12},{9,11},{10,... | collective-permute-start | bytes 2359304 | tf_op jit(solution)/shard_map/ppermute | solution.py:434
  111.8 1.6 %collective-permute-done.21.refs_2_ = bf16[64,16,128]{2,1,0:T(8,128)(2,1)S(1)} collective-permute-done((bf16[64,16,128]{2,1,0:T(8,128)(2,1)S(1)}, bf16[64,16,128]{2,1,0:T(8,128)(2,1)S(1)}, u32[]{:S(2)}, u32[]{:S(2)}) %collective-permute-start.21) | collective-permute-done | bytes 262176 | tf_op jit(solution)/shard_map/ppermute | solution.py:426
  113.4 1.3 collective-permute-start.25
  114.8 0.5 collective-permute-start.24
  115.4 0.5 collective-permute-done.25.refs_6_
  115.9 0.4 collective-permute-start.13
  116.3 0.4 collective-permute-start.16
  116.8 6.9 %shard_map.78.refs_4_ = bf16[512,128,128]{2,1,0:T(8,128)(2,1)} custom-call(s32[2]{0:T(128)S(1)} %pad_add_fusion.halves_ref, s32[4,512]{1,0:T(4,128)S(1)} %get-tuple-element.49.places_ref, f32[1,512]{1,0:T(1,128)S(1)} %constant_dynamic-slice_fusion.root_ref, f32[1,128]{1,0:T(1,128)S(1)} %bitcast.27, bf16[64,16,128]{2,1,0:T(8,128)(2,1)S(1)} %pad_maximum_fusion.1.refs_0_, ...), custom_call_target="tpu_custom_call" | custom-call | flops 4294967296 | bytes 4194304 | tf_op jit(solution)/shard_map/pallas_call | solution.py:401
  123.7 0.4 collective-permute-start.20
  124.2 8.7 %shard_map.79.refs_4_ = bf16[512,128,128]{2,1,0:T(8,128)(2,1)} custom-call(s32[1]{0:T(128)} %bitcast.6.halves_ref, s32[4,512]{1,0:T(4,128)S(1)} %get-tuple-element.56.places_ref, f32[1,512]{1,0:T(1,128)S(1)} %constant_dynamic-slice_fusion.root_ref, f32[1,128]{1,0:T(1,128)S(1)} %bitcast.28, ...), custom_call_target="tpu_custom_call", output_to_operand_aliasing={{}: (8, {})} | custom-call | flops 12884901888 | bytes 12582912 | tf_op jit(solution)/shard_map/pallas_call | solution.py:401
  132.9 7.3 %shard_map.80 = bf16[512,128,128]{2,1,0:T(8,128)(2,1)} custom-call(s32[1]{0:T(128)} %bitcast.halves_ref, s32[4,512]{1,0:T(4,128)S(1)} %get-tuple-element.57.places_ref, f32[1,512]{1,0:T(1,128)S(1)} %constant_dynamic-slice_fusion.root_ref, f32[1,128]{1,0:T(1,128)S(1)} %bitcast.29, ...), custom_call_target="tpu_custom_call", output_to_operand_aliasing={{}: (8, {})} | custom-call | flops 12884901888 | bytes 12582912 | tf_op jit(solution)/shard_map/pallas_call | solution.py:401
  (50 shorter events, 1.5 us)
Async XLA Ops:
  0.0 0.8 copy-start.1
  0.8 0.7 copy-start.3
  10.1 9.8 %collective-permute-start = (bf16[8,144,128]{2,1,0:T(8,128)(2,1)S(1)}, bf16[8,144,128]{2,1,0:T(8,128)(2,1)S(1)}, u32[]{:S(2)}, u32[]{:S(2)}) collective-permute-start(bf16[8,144,128]{2,1,0:T(8,128)(2,1)S(1)} %get-tuple-element.28), channel_id=1, source_target_pairs={{0,8},{8,16},{16,24},{24,0},{1,9},{9,17},{17,25},{25,1},{2,10},{10... | collective-permute-start | bytes 884744 | tf_op jit(solution)/shard_map/ppermute | solution.py:426
  11.4 15.7 %copy-start.5 = (s32[128,3]{0,1:T(4,128)S(1)}, s32[128,3]{0,1:T(4,128)}, u32[]{:S(2)}) copy-start(s32[128,3]{0,1:T(4,128)} %param.11) | copy-start | bytes 4612
  11.4 15.9 %copy-start.6 = (f32[128]{0:T(128)S(1)}, f32[128]{0:T(128)}, u32[]{:S(2)}) copy-start(f32[128]{0:T(128)} %param.12) | copy-start | bytes 1540
  11.4 47.3 %copy-start.4 = (f32[256]{0:T(256)S(1)}, f32[256]{0:T(256)}, u32[]{:S(2)}) copy-start(f32[256]{0:T(256)} %param.9) | copy-start | bytes 3076
  11.4 52.8 %copy-start = (bf16[128,128]{1,0:T(8,128)(2,1)S(1)}, bf16[128,128]{1,0:T(8,128)(2,1)}, u32[]{:S(2)}) copy-start(bf16[128,128]{1,0:T(8,128)(2,1)} %mixing_ref.1) | copy-start | bytes 98308
  11.4 105.4 %copy-start.2 = (f32[128]{0:T(128)S(1)}, f32[128]{0:T(128)}, u32[]{:S(2)}) copy-start(f32[128]{0:T(128)} %param.13) | copy-start | bytes 1540
  19.9 16.5 %all-to-all-start = ((bf16[8,4,128,128]{3,2,1,0:T(8,128)(2,1)}), bf16[8,4,128,128]{3,2,1,0:T(8,128)(2,1)S(1)}, u32[]{:S(2)}, u32[]{:S(2)}) async-start(bf16[8,4,128,128]{3,2,1,0:T(8,128)(2,1)} %shard_map.74), calls=%async_computation | async-start | bytes 2097152 | tf_op jit(solution)/shard_map/all_to_all | solution.py:256
  24.7 22.6 %collective-permute-start.3 = (bf16[8,144,128]{2,1,0:T(8,128)(2,1)S(1)}, bf16[8,144,128]{2,1,0:T(8,128)(2,1)S(1)}, u32[]{:S(2)}, u32[]{:S(2)}) collective-permute-start(bf16[8,144,128]{2,1,0:T(8,128)(2,1)S(1)} %get-tuple-element.33), channel_id=1, source_target_pairs={{0,16},{8,24},{16,0},{24,8},{1,17},{9,25},{17,1},{25,9},{2,18},{10... | collective-permute-start | bytes 884744 | tf_op jit(solution)/shard_map/ppermute | solution.py:426
  25.7 27.1 %collective-permute-start.5 = (bf16[8,144,128]{2,1,0:T(8,128)(2,1)S(1)}, bf16[8,144,128]{2,1,0:T(8,128)(2,1)S(1)}, u32[]{:S(2)}, u32[]{:S(2)}) collective-permute-start(bf16[8,144,128]{2,1,0:T(8,128)(2,1)S(1)} %get-tuple-element.40), channel_id=1, source_target_pairs={{0,24},{8,0},{16,8},{24,16},{1,25},{9,1},{17,9},{25,17},{2,26},{10... | collective-permute-start | bytes 884744 | tf_op jit(solution)/shard_map/ppermute | solution.py:426
  36.5 13.6 %collective-permute-start.1 = (bf16[4,128,128]{2,1,0:T(8,128)(2,1)S(1)}, bf16[4,128,128]{2,1,0:T(8,128)(2,1)S(1)}, u32[]{:S(2)}, u32[]{:S(2)}) collective-permute-start(bf16[4,128,128]{2,1,0:T(8,128)(2,1)S(1)} %get-tuple-element.31), channel_id=1, source_target_pairs={{0,8},{8,16},{16,24},{24,0},{1,9},{9,17},{17,25},{25,1},{2,10},{10... | collective-permute-start | bytes 393224 | tf_op jit(solution)/shard_map/ppermute | solution.py:426
  37.8 15.0 %collective-permute-start.2 = (bf16[4,128,128]{2,1,0:T(8,128)(2,1)S(1)}, bf16[4,128,128]{2,1,0:T(8,128)(2,1)S(1)}, u32[]{:S(2)}, u32[]{:S(2)}) collective-permute-start(bf16[4,128,128]{2,1,0:T(8,128)(2,1)S(1)} %get-tuple-element.32), channel_id=1, source_target_pairs={{0,16},{8,24},{16,0},{24,8},{1,17},{9,25},{17,1},{25,9},{2,18},{10... | collective-permute-start | bytes 393224 | tf_op jit(solution)/shard_map/ppermute | solution.py:426
  53.7 10.5 %all-to-all-start.1 = ((bf16[8,1,144,128]{3,2,1,0:T(8,128)(2,1)}), bf16[8,1,144,128]{3,2,1,0:T(8,128)(2,1)S(1)}, u32[]{:S(2)}, u32[]{:S(2)}) async-start(bf16[8,1,144,128]{3,2,1,0:T(8,128)(2,1)} %shard_map.76), calls=%async_computation.1 | async-start | bytes 589824 | tf_op jit(solution)/shard_map/all_to_all | solution.py:261
  58.9 5.3 %collective-permute-start.4 = (bf16[4,128,128]{2,1,0:T(8,128)(2,1)S(1)}, bf16[4,128,128]{2,1,0:T(8,128)(2,1)S(1)}, u32[]{:S(2)}, u32[]{:S(2)}) collective-permute-start(bf16[4,128,128]{2,1,0:T(8,128)(2,1)S(1)} %get-tuple-element.36), channel_id=1, source_target_pairs={{0,24},{8,0},{16,8},{24,16},{1,25},{9,1},{17,9},{25,17},{2,26},{10... | collective-permute-start | bytes 393224 | tf_op jit(solution)/shard_map/ppermute | solution.py:426
  64.8 2.2 %collective-permute-start.6 = (bf16[8,64,128]{2,1,0:T(8,128)(2,1)S(1)}, bf16[8,64,128]{2,1,0:T(8,128)(2,1)S(1)}, u32[]{:S(2)}, u32[]{:S(2)}) collective-permute-start(bf16[8,64,128]{2,1,0:T(8,128)(2,1)S(1)} %get-tuple-element.42), channel_id=1, source_target_pairs={{0,1},{1,0},{2,3},{3,2},{4,5},{5,4},{6,7},{7,6},{8,9},{9,8},{10,11... | collective-permute-start | bytes 393224 | tf_op jit(solution)/shard_map/ppermute | solution.py:442
  67.1 7.4 %collective-permute-start.7 = (bf16[16,16,128]{2,1,0:T(8,128)(2,1)S(1)}, bf16[16,16,128]{2,1,0:T(8,128)(2,1)S(1)}, u32[]{:S(2)}, u32[]{:S(2)}) collective-permute-start(bf16[16,16,128]{2,1,0:T(8,128)(2,1)S(1)} %pad_maximum_fusion.3), channel_id=1, source_target_pairs={{0,2},{1,3},{2,0},{3,1},{4,6},{5,7},{6,4},{7,5},{8,10},{9,11},{10,... | collective-permute-start | bytes 196616 | tf_op jit(solution)/shard_map/ppermute | solution.py:438
  68.4 10.1 %collective-permute-start.10 = (bf16[16,48,128]{2,1,0:T(8,128)(2,1)S(1)}, bf16[16,48,128]{2,1,0:T(8,128)(2,1)S(1)}, u32[]{:S(2)}, u32[]{:S(2)}) collective-permute-start(bf16[16,48,128]{2,1,0:T(8,128)(2,1)S(1)} %pad_maximum_fusion.2), channel_id=1, source_target_pairs={{0,8},{8,16},{16,24},{24,0},{1,9},{9,17},{17,25},{25,1},{2,10},{10... | collective-permute-start | bytes 589832 | tf_op jit(solution)/shard_map/ppermute | solution.py:426
  69.7 16.2 %collective-permute-start.11 = (bf16[16,48,128]{2,1,0:T(8,128)(2,1)S(1)}, bf16[16,48,128]{2,1,0:T(8,128)(2,1)S(1)}, u32[]{:S(2)}, u32[]{:S(2)}) collective-permute-start(bf16[16,48,128]{2,1,0:T(8,128)(2,1)S(1)} %pad_maximum_fusion.2), channel_id=1, source_target_pairs={{0,16},{8,24},{16,0},{24,8},{1,17},{9,25},{17,1},{25,9},{2,18},{10... | collective-permute-start | bytes 589832 | tf_op jit(solution)/shard_map/ppermute | solution.py:426
  72.8 17.9 %collective-permute-start.12 = (bf16[16,48,128]{2,1,0:T(8,128)(2,1)S(1)}, bf16[16,48,128]{2,1,0:T(8,128)(2,1)S(1)}, u32[]{:S(2)}, u32[]{:S(2)}) collective-permute-start(bf16[16,48,128]{2,1,0:T(8,128)(2,1)S(1)} %pad_maximum_fusion.2), channel_id=1, source_target_pairs={{0,24},{8,0},{16,8},{24,16},{1,25},{9,1},{17,9},{25,17},{2,26},{10... | collective-permute-start | bytes 589832 | tf_op jit(solution)/shard_map/ppermute | solution.py:426
  74.2 3.1 %collective-permute-start.8 = (bf16[16,16,128]{2,1,0:T(8,128)(2,1)S(1)}, bf16[16,16,128]{2,1,0:T(8,128)(2,1)S(1)}, u32[]{:S(2)}, u32[]{:S(2)}) collective-permute-start(bf16[16,16,128]{2,1,0:T(8,128)(2,1)S(1)} %pad_maximum_fusion.3), channel_id=1, source_target_pairs={{0,4},{1,5},{2,6},{3,7},{4,0},{5,1},{6,2},{7,3},{8,12},{9,13},{10,... | collective-permute-start | bytes 196616 | tf_op jit(solution)/shard_map/ppermute | solution.py:438
  74.5 4.0 %collective-permute-start.9 = (bf16[16,16,128]{2,1,0:T(8,128)(2,1)S(1)}, bf16[16,16,128]{2,1,0:T(8,128)(2,1)S(1)}, u32[]{:S(2)}, u32[]{:S(2)}) collective-permute-start(bf16[16,16,128]{2,1,0:T(8,128)(2,1)S(1)} %pad_maximum_fusion.3), channel_id=1, source_target_pairs={{0,6},{1,7},{2,4},{3,5},{4,2},{5,3},{6,0},{7,1},{8,14},{9,15},{10,... | collective-permute-start | bytes 196616 | tf_op jit(solution)/shard_map/ppermute | solution.py:438
  90.8 18.0 %collective-permute-start.14 = (bf16[64,48,128]{2,1,0:T(8,128)(2,1)S(1)}, bf16[64,48,128]{2,1,0:T(8,128)(2,1)}, u32[]{:S(2)}, u32[]{:S(2)}) collective-permute-start(bf16[64,48,128]{2,1,0:T(8,128)(2,1)S(1)} %pad_maximum_fusion.refs_0_), channel_id=1, source_target_pairs={{0,2},{1,5},{2,0},{3,7},{4,6},{5,1},{6,4},{7,3},{8,10},{9,13},{10,... | collective-permute-start | bytes 2359304 | tf_op jit(solution)/shard_map/ppermute | solution.py:434
  91.4 7.2 %collective-permute-start.15 = (bf16[64,16,128]{2,1,0:T(8,128)(2,1)S(1)}, bf16[64,16,128]{2,1,0:T(8,128)(2,1)S(1)}, u32[]{:S(2)}, u32[]{:S(2)}) collective-permute-start(bf16[64,16,128]{2,1,0:T(8,128)(2,1)S(1)} %pad_maximum_fusion.1.refs_0_), channel_id=1, source_target_pairs={{0,8},{8,16},{16,24},{24,0},{1,9},{9,17},{17,25},{25,1},{2,10},{10... | collective-permute-start | bytes 786440 | tf_op jit(solution)/shard_map/ppermute | solution.py:426
  91.4 25.3 %collective-permute-start.17 = (bf16[64,48,128]{2,1,0:T(8,128)(2,1)S(1)}, bf16[64,48,128]{2,1,0:T(8,128)(2,1)}, u32[]{:S(2)}, u32[]{:S(2)}) collective-permute-start(bf16[64,48,128]{2,1,0:T(8,128)(2,1)S(1)} %pad_maximum_fusion.refs_0_), channel_id=1, source_target_pairs={{0,4},{1,3},{2,6},{3,1},{4,0},{5,7},{6,2},{7,5},{8,12},{9,11},{10,... | collective-permute-start | bytes 2359304 | tf_op jit(solution)/shard_map/ppermute | solution.py:434
  91.5 21.9 %collective-permute-start.21 = (bf16[64,16,128]{2,1,0:T(8,128)(2,1)S(1)}, bf16[64,16,128]{2,1,0:T(8,128)(2,1)S(1)}, u32[]{:S(2)}, u32[]{:S(2)}) collective-permute-start(bf16[64,16,128]{2,1,0:T(8,128)(2,1)S(1)} %pad_maximum_fusion.1.refs_0_), channel_id=1, source_target_pairs={{0,16},{8,24},{16,0},{24,8},{1,17},{9,25},{17,1},{25,9},{2,18},{10... | collective-permute-start | bytes 786440 | tf_op jit(solution)/shard_map/ppermute | solution.py:426
  91.5 23.2 %collective-permute-start.22 = (bf16[64,16,128]{2,1,0:T(8,128)(2,1)S(1)}, bf16[64,16,128]{2,1,0:T(8,128)(2,1)S(1)}, u32[]{:S(2)}, u32[]{:S(2)}) collective-permute-start(bf16[64,16,128]{2,1,0:T(8,128)(2,1)S(1)} %pad_maximum_fusion.1.refs_0_), channel_id=1, source_target_pairs={{0,24},{8,0},{16,8},{24,16},{1,25},{9,1},{17,9},{25,17},{2,26},{10... | collective-permute-start | bytes 786440 | tf_op jit(solution)/shard_map/ppermute | solution.py:426
  98.5 16.2 %collective-permute-start.23 = (bf16[64,16,128]{2,1,0:T(8,128)(2,1)S(1)}, bf16[64,16,128]{2,1,0:T(8,128)(2,1)S(1)}, u32[]{:S(2)}, u32[]{:S(2)}) collective-permute-start(bf16[64,16,128]{2,1,0:T(8,128)(2,1)S(1)} %pad_maximum_fusion.1.refs_0_), channel_id=1, source_target_pairs={{0,1},{1,0},{2,3},{3,2},{4,5},{5,4},{6,7},{7,6},{8,9},{9,8},{10,11... | collective-permute-start | bytes 786440 | tf_op jit(solution)/shard_map/ppermute | solution.py:442
  108.8 14.9 %collective-permute-start.19 = (bf16[64,48,128]{2,1,0:T(8,128)(2,1)}, bf16[64,48,128]{2,1,0:T(8,128)(2,1)}, u32[]{:S(2)}, u32[]{:S(2)}) collective-permute-start(bf16[64,48,128]{2,1,0:T(8,128)(2,1)} %collective-permute-done.14.refs_1_), channel_id=1, source_target_pairs={{0,4},{1,3},{2,6},{3,1},{4,0},{5,7},{6,2},{7,5},{8,12},{9,11},{10,... | collective-permute-start | bytes 2359304 | tf_op jit(solution)/shard_map/ppermute | solution.py:434
  113.4 2.5 %collective-permute-start.25 = (bf16[64,16,128]{2,1,0:T(8,128)(2,1)S(1)}, bf16[64,16,128]{2,1,0:T(8,128)(2,1)S(1)}, u32[]{:S(2)}, u32[]{:S(2)}) collective-permute-start(bf16[64,16,128]{2,1,0:T(8,128)(2,1)S(1)} %collective-permute-done.21.refs_2_), channel_id=1, source_target_pairs={{0,1},{1,0},{2,3},{3,2},{4,5},{5,4},{6,7},{7,6},{8,9},{9,8},{10,11... | collective-permute-start | bytes 786440 | tf_op jit(solution)/shard_map/ppermute | solution.py:442
  114.7 1.5 %collective-permute-start.26 = (bf16[64,16,128]{2,1,0:T(8,128)(2,1)S(1)}, bf16[64,16,128]{2,1,0:T(8,128)(2,1)S(1)}, u32[]{:S(2)}, u32[]{:S(2)}) collective-permute-start(bf16[64,16,128]{2,1,0:T(8,128)(2,1)S(1)} %collective-permute-done.22.refs_3_), channel_id=1, source_target_pairs={{0,1},{1,0},{2,3},{3,2},{4,5},{5,4},{6,7},{7,6},{8,9},{9,8},{10,11... | collective-permute-start | bytes 786440 | tf_op jit(solution)/shard_map/ppermute | solution.py:442
  114.8 2.0 %collective-permute-start.24 = (bf16[64,16,128]{2,1,0:T(8,128)(2,1)S(1)}, bf16[64,16,128]{2,1,0:T(8,128)(2,1)S(1)}, u32[]{:S(2)}, u32[]{:S(2)}) collective-permute-start(bf16[64,16,128]{2,1,0:T(8,128)(2,1)S(1)} %collective-permute-done.15.refs_1_), channel_id=1, source_target_pairs={{0,1},{1,0},{2,3},{3,2},{4,5},{5,4},{6,7},{7,6},{8,9},{9,8},{10,11... | collective-permute-start | bytes 786440 | tf_op jit(solution)/shard_map/ppermute | solution.py:442
  115.9 16.9 %collective-permute-start.13 = (bf16[64,48,128]{2,1,0:T(8,128)(2,1)S(1)}, bf16[64,48,128]{2,1,0:T(8,128)(2,1)S(1)}, u32[]{:S(2)}, u32[]{:S(2)}) collective-permute-start(bf16[64,48,128]{2,1,0:T(8,128)(2,1)S(1)} %pad_maximum_fusion.refs_0_), channel_id=1, source_target_pairs={{0,1},{1,0},{2,3},{3,2},{4,5},{5,4},{6,7},{7,6},{8,9},{9,8},{10,11... | collective-permute-start | bytes 2359304 | tf_op jit(solution)/shard_map/ppermute | solution.py:442
  116.3 16.6 %collective-permute-start.16 = (bf16[64,48,128]{2,1,0:T(8,128)(2,1)}, bf16[64,48,128]{2,1,0:T(8,128)(2,1)S(1)}, u32[]{:S(2)}, u32[]{:S(2)}) collective-permute-start(bf16[64,48,128]{2,1,0:T(8,128)(2,1)} %collective-permute-done.14.refs_1_), channel_id=1, source_target_pairs={{0,1},{1,0},{2,3},{3,2},{4,5},{5,4},{6,7},{7,6},{8,9},{9,8},{10,11... | collective-permute-start | bytes 2359304 | tf_op jit(solution)/shard_map/ppermute | solution.py:442
  116.7 16.2 %collective-permute-start.18 = (bf16[64,48,128]{2,1,0:T(8,128)(2,1)}, bf16[64,48,128]{2,1,0:T(8,128)(2,1)S(1)}, u32[]{:S(2)}, u32[]{:S(2)}) collective-permute-start(bf16[64,48,128]{2,1,0:T(8,128)(2,1)} %collective-permute-done.17.refs_2_), channel_id=1, source_target_pairs={{0,1},{1,0},{2,3},{3,2},{4,5},{5,4},{6,7},{7,6},{8,9},{9,8},{10,11... | collective-permute-start | bytes 2359304 | tf_op jit(solution)/shard_map/ppermute | solution.py:442
  123.7 9.2 %collective-permute-start.20 = (bf16[64,48,128]{2,1,0:T(8,128)(2,1)}, bf16[64,48,128]{2,1,0:T(8,128)(2,1)S(1)}, u32[]{:S(2)}, u32[]{:S(2)}) collective-permute-start(bf16[64,48,128]{2,1,0:T(8,128)(2,1)} %collective-permute-done.19.refs_3_), channel_id=1, source_target_pairs={{0,1},{1,0},{2,3},{3,2},{4,5},{5,4},{6,7},{7,6},{8,9},{9,8},{10,11... | collective-permute-start | bytes 2359304 | tf_op jit(solution)/shard_map/ppermute | solution.py:442

commit v16 on v14

--- a/solution.py
+++ b/solution.py
@@ -175,7 +175,7 @@
         out_specs=out_specs,
         out_shape=outs,
         scratch_shapes=[pltpu.VMEM((half // 2, edges, 2 * lanes), F32)] + counts + [pltpu.VMEM((rows * pitch, lanes), F32)],
-        compiler_params=pltpu.CompilerParams(vmem_limit_bytes=40 * 1024 * 1024),
+        compiler_params=pltpu.CompilerParams(vmem_limit_bytes=60 * 1024 * 1024),
         cost_estimate=pl.CostEstimate(
             flops=4 * anchors * edges * zones * lanes, bytes_accessed=2 * anchors * zones * lanes, transcendentals=0
         ),

time: 142 us -> 142 us (level)
  transfers between devices with their start and end apart: 29 -> 29, of which waited for: 14 -> 14; matrix products, arithmetic and copies ran while one was open for 1% -> 2% of each run, Pallas kernels for 17% -> 17%
where the time goes in v16:
time: 142 us; the launch traced here: 140 us
  waiting for transfers between devices  54.3 us (38%)
  Pallas kernels  42.6 us (30%)
  starting transfers between devices  40.1 us (28%)
    ppermute x12, waiting for transfers between devices, shifted(): lax.ppermute(x, LINE, [(i, (i + amount) % size) for i in range(size)])  34.4 us
    pallas_call x3, Pallas kernels, spread(): pl.pallas_call(functools.partial(spread_kernel, sides, count, stride, off...  22.6 us
    pallas_call x2, Pallas kernels, half_sums(): pl.pallas_call(functools.partial(kernel, plan, begin, half, pitch), grid=...  18.5 us
    ppermute x12, starting transfers between devices, shifted(): lax.ppermute(x, LINE, [(i, (i + amount) % size) for i in range(size)])  16.6 us
    all_to_all x1, waiting for transfers between devices, org_sums(): lax.all_to_all(first, SQUARE, split_axis=0, concat_axis=0, tiled=True)  8.92 us
    ppermute x9, starting transfers between devices, swapped(): return lax.ppermute(x, 'core', [(0, 1), (1, 0)])  7.26 us
    ppermute x3, waiting for transfers between devices, crossed(): return lax.ppermute(x, SQUARE, pairs)  6.69 us
    all_to_all x1, starting transfers between devices, org_sums(): lax.all_to_all(second, SQUARE, split_axis=0, concat_axis=0, tiled=True)  5.03 us
  transfers between devices with their start and end apart: 29, of which 14 were waited for; matrix products, arithmetic and copies ran while one was open for 2% of the time, Pallas kernels for 17%

profile of v16, /device:TPU:13, one launch (start us, length us, event | category | flops | bytes accessed | tf_op | source)
XLA Modules:
  0.0 139.8 jit_solution(18316249368844604172)
XLA Ops:
  0.0 9.8 %shard_map.73 = (bf16[8,144,128]{2,1,0:T(8,128)(2,1)}, bf16[8,144,128]{2,1,0:T(8,128)(2,1)}, bf16[8,144,128]{2,1,0:T(8,128)(2,1)}, bf16[8,144,128]{2,1,0:T(8,128...) custom-call(s32[1]{0:T(128)} %bitcast.2.line_ref, s32[4,2048]{1,0:T(4,128)} %bitcast.29, f32[1,256]{1,0:T(1,128)} %bitcast.30, ...), custom_call_target="tpu_custom_call" | custom-call | flops 8589934592 | bytes 16777216 | tf_op jit(solution)/shard_map/pallas_call | solution.py:171
  9.8 1.3 collective-permute-start
  11.2 8.7 %shard_map.74 = bf16[8,4,128,128]{3,2,1,0:T(8,128)(2,1)} custom-call(s32[1]{0:T(128)} %bitcast.2.line_ref, bf16[256,2048]{1,0:T(8,128)(2,1)} %get-tuple-element.27.weighted_ref, bf16[2048,32,128]{2,1,0:T(8,128)(2,1)} %cells_ref.3), custom_call_target="tpu_custom_call" | custom-call | flops 8589934592 | bytes 16777216 | tf_op jit(solution)/shard_map/pallas_call | solution.py:171
  19.9 4.8 %all-to-all-start = ((bf16[8,4,128,128]{3,2,1,0:T(8,128)(2,1)}), bf16[8,4,128,128]{3,2,1,0:T(8,128)(2,1)S(1)}, u32[]{:S(2)}, u32[]{:S(2)}) async-start(bf16[8,4,128,128]{3,2,1,0:T(8,128)(2,1)} %shard_map.74), calls=%async_computation | async-start | bytes 2097152 | tf_op jit(solution)/shard_map/all_to_all | solution.py:256
  24.7 1.0 collective-permute-start.3
  25.7 1.5 %collective-permute-start.5 = (bf16[8,144,128]{2,1,0:T(8,128)(2,1)S(1)}, bf16[8,144,128]{2,1,0:T(8,128)(2,1)S(1)}, u32[]{:S(2)}, u32[]{:S(2)}) collective-permute-start(bf16[8,144,128]{2,1,0:T(8,128)(2,1)S(1)} %copy-done.5), channel_id=1, source_target_pairs={{0,24},{8,0},{16,8},{24,16},{1,25},{9,1},{17,9},{25,17},{2,26},{10... | collective-permute-start | bytes 884744 | tf_op jit(solution)/shard_map/ppermute | solution.py:425
  27.5 8.9 %all-to-all-done.part_ref = bf16[8,4,128,128]{3,2,1,0:T(8,128)(2,1)S(1)} async-done(((bf16[8,4,128,128]{3,2,1,0:T(8,128)(2,1)}), bf16[8,4,128,128]{3,2,1,0:T(8,128)(2,1)S(1)}, u32[]{:S(2)}, u32[]{:S(2)}) %all-to-all-start) | async-done | bytes 1048608 | tf_op jit(solution)/shard_map/all_to_all | solution.py:256
  36.5 1.3 collective-permute-start.1
  37.8 1.4 %collective-permute-start.2 = (bf16[4,128,128]{2,1,0:T(8,128)(2,1)S(1)}, bf16[4,128,128]{2,1,0:T(8,128)(2,1)S(1)}, u32[]{:S(2)}, u32[]{:S(2)}) collective-permute-start(bf16[4,128,128]{2,1,0:T(8,128)(2,1)S(1)} %get-tuple-element.32), channel_id=1, source_target_pairs={{0,16},{8,24},{16,0},{24,8},{1,17},{9,25},{17,1},{25,9},{2,18},{10... | collective-permute-start | bytes 393224 | tf_op jit(solution)/shard_map/ppermute | solution.py:425
  39.3 0.3 convolution_convert_fusion
  39.6 7.6 %collective-permute-done.3.refs_2_ = bf16[8,144,128]{2,1,0:T(8,128)(2,1)S(1)} collective-permute-done((bf16[8,144,128]{2,1,0:T(8,128)(2,1)S(1)}, bf16[8,144,128]{2,1,0:T(8,128)(2,1)S(1)}, u32[]{:S(2)}, u32[]{:S(2)}) %collective-permute-start.3) | collective-permute-done | bytes 294944 | tf_op jit(solution)/shard_map/ppermute | solution.py:425
  47.2 2.8 %collective-permute-done.1.refs_1_ = bf16[4,128,128]{2,1,0:T(8,128)(2,1)S(1)} collective-permute-done((bf16[4,128,128]{2,1,0:T(8,128)(2,1)S(1)}, bf16[4,128,128]{2,1,0:T(8,128)(2,1)S(1)}, u32[]{:S(2)}, u32[]{:S(2)}) %collective-permute-start.1) | collective-permute-done | bytes 131104 | tf_op jit(solution)/shard_map/ppermute | solution.py:425
  50.0 2.8 %collective-permute-done.2.refs_2_ = bf16[4,128,128]{2,1,0:T(8,128)(2,1)S(1)} collective-permute-done((bf16[4,128,128]{2,1,0:T(8,128)(2,1)S(1)}, bf16[4,128,128]{2,1,0:T(8,128)(2,1)S(1)}, u32[]{:S(2)}, u32[]{:S(2)}) %collective-permute-start.2) | collective-permute-done | bytes 131104 | tf_op jit(solution)/shard_map/ppermute | solution.py:425
  52.8 0.9 shard_map.76
  53.7 5.0 %all-to-all-start.1 = ((bf16[8,1,144,128]{3,2,1,0:T(8,128)(2,1)}), bf16[8,1,144,128]{3,2,1,0:T(8,128)(2,1)S(1)}, u32[]{:S(2)}, u32[]{:S(2)}) async-start(bf16[8,1,144,128]{3,2,1,0:T(8,128)(2,1)} %shard_map.76), calls=%async_computation.1 | async-start | bytes 589824 | tf_op jit(solution)/shard_map/all_to_all | solution.py:261
  58.8 2.8 %collective-permute-start.4 = (bf16[4,128,128]{2,1,0:T(8,128)(2,1)S(1)}, bf16[4,128,128]{2,1,0:T(8,128)(2,1)S(1)}, u32[]{:S(2)}, u32[]{:S(2)}) collective-permute-start(bf16[4,128,128]{2,1,0:T(8,128)(2,1)S(1)} %get-tuple-element.36), channel_id=1, source_target_pairs={{0,24},{8,0},{16,8},{24,16},{1,25},{9,1},{17,9},{25,17},{2,26},{10... | collective-permute-start | bytes 393224 | tf_op jit(solution)/shard_map/ppermute | solution.py:425
  61.6 2.5 %collective-permute-done.4.refs_3_ = bf16[4,128,128]{2,1,0:T(8,128)(2,1)S(1)} collective-permute-done((bf16[4,128,128]{2,1,0:T(8,128)(2,1)S(1)}, bf16[4,128,128]{2,1,0:T(8,128)(2,1)S(1)}, u32[]{:S(2)}, u32[]{:S(2)}) %collective-permute-start.4) | collective-permute-done | bytes 131104 | tf_op jit(solution)/shard_map/ppermute | solution.py:425
  64.2 0.5 shard_map.77
  64.7 1.3 collective-permute-start.6
  66.0 1.0 collective-permute-done.6
  67.0 1.2 collective-permute-start.7
  68.3 1.4 collective-permute-start.10
  69.7 3.1 %collective-permute-start.11 = (bf16[16,48,128]{2,1,0:T(8,128)(2,1)S(1)}, bf16[16,48,128]{2,1,0:T(8,128)(2,1)S(1)}, u32[]{:S(2)}, u32[]{:S(2)}) collective-permute-start(bf16[16,48,128]{2,1,0:T(8,128)(2,1)S(1)} %pad_maximum_fusion.2), channel_id=1, source_target_pairs={{0,16},{8,24},{16,0},{24,8},{1,17},{9,25},{17,1},{25,9},{2,18},{10... | collective-permute-start | bytes 589832 | tf_op jit(solution)/shard_map/ppermute | solution.py:425
  72.7 1.4 collective-permute-start.12
  74.1 0.3 collective-permute-start.8
  74.4 1.2 collective-permute-start.9
  75.6 1.6 %collective-permute-done.8 = bf16[16,16,128]{2,1,0:T(8,128)(2,1)S(1)} collective-permute-done((bf16[16,16,128]{2,1,0:T(8,128)(2,1)S(1)}, bf16[16,16,128]{2,1,0:T(8,128)(2,1)S(1)}, u32[]{:S(2)}, u32[]{:S(2)}) %collective-permute-start.8) | collective-permute-done | bytes 65568 | tf_op jit(solution)/shard_map/ppermute | solution.py:437
  77.2 1.2 collective-permute-done.9
  78.5 7.4 %collective-permute-done.11 = bf16[16,48,128]{2,1,0:T(8,128)(2,1)S(1)} collective-permute-done((bf16[16,48,128]{2,1,0:T(8,128)(2,1)S(1)}, bf16[16,48,128]{2,1,0:T(8,128)(2,1)S(1)}, u32[]{:S(2)}, u32[]{:S(2)}) %collective-permute-start.11) | collective-permute-done | bytes 196640 | tf_op jit(solution)/shard_map/ppermute | solution.py:425
  85.9 4.7 %collective-permute-done.12 = bf16[16,48,128]{2,1,0:T(8,128)(2,1)S(1)} collective-permute-done((bf16[16,48,128]{2,1,0:T(8,128)(2,1)S(1)}, bf16[16,48,128]{2,1,0:T(8,128)(2,1)S(1)}, u32[]{:S(2)}, u32[]{:S(2)}) %collective-permute-start.12) | collective-permute-done | bytes 196640 | tf_op jit(solution)/shard_map/ppermute | solution.py:425
  90.8 0.5 collective-permute-start.14
  91.4 1.4 collective-permute-start.22
  92.8 5.6 %collective-permute-done.15.refs_1_ = bf16[64,16,128]{2,1,0:T(8,128)(2,1)S(1)} collective-permute-done((bf16[64,16,128]{2,1,0:T(8,128)(2,1)S(1)}, bf16[64,16,128]{2,1,0:T(8,128)(2,1)S(1)}, u32[]{:S(2)}, u32[]{:S(2)}) %collective-permute-start.15) | collective-permute-done | bytes 262176 | tf_op jit(solution)/shard_map/ppermute | solution.py:425
  98.4 2.8 %collective-permute-start.23 = (bf16[64,16,128]{2,1,0:T(8,128)(2,1)S(1)}, bf16[64,16,128]{2,1,0:T(8,128)(2,1)S(1)}, u32[]{:S(2)}, u32[]{:S(2)}) collective-permute-start(bf16[64,16,128]{2,1,0:T(8,128)(2,1)S(1)} %pad_maximum_fusion.1.refs_0_), channel_id=1, source_target_pairs={{0,1},{1,0},{2,3},{3,2},{4,5},{5,4},{6,7},{7,6},{8,9},{9,8},{10,11... | collective-permute-start | bytes 786440 | tf_op jit(solution)/shard_map/ppermute | solution.py:441
  101.3 0.8 multiply_add_fusion
  102.0 6.7 %collective-permute-done.14.refs_1_ = bf16[64,48,128]{2,1,0:T(8,128)(2,1)} collective-permute-done((bf16[64,48,128]{2,1,0:T(8,128)(2,1)S(1)}, bf16[64,48,128]{2,1,0:T(8,128)(2,1)}, u32[]{:S(2)}, u32[]{:S(2)}) %collective-permute-start.14) | collective-permute-done | bytes 786464 | tf_op jit(solution)/shard_map/ppermute | solution.py:433
  108.7 3.0 %collective-permute-start.19 = (bf16[64,48,128]{2,1,0:T(8,128)(2,1)}, bf16[64,48,128]{2,1,0:T(8,128)(2,1)}, u32[]{:S(2)}, u32[]{:S(2)}) collective-permute-start(bf16[64,48,128]{2,1,0:T(8,128)(2,1)} %collective-permute-done.14.refs_1_), channel_id=1, source_target_pairs={{0,4},{1,3},{2,6},{3,1},{4,0},{5,7},{6,2},{7,5},{8,12},{9,11},{10,... | collective-permute-start | bytes 2359304 | tf_op jit(solution)/shard_map/ppermute | solution.py:433
  111.8 0.7 constant_dynamic-slice_fusion.root_ref
  112.4 0.9 collective-permute-done.21.refs_2_
  113.3 1.3 collective-permute-start.25
  114.7 0.5 collective-permute-start.24
  115.3 0.5 collective-permute-done.25.refs_6_
  115.8 0.4 collective-permute-start.13
  116.2 0.4 collective-permute-start.16
  116.7 6.9 %shard_map.78.refs_4_ = bf16[512,128,128]{2,1,0:T(8,128)(2,1)} custom-call(s32[2]{0:T(128)S(1)} %pad_add_fusion.halves_ref, s32[4,512]{1,0:T(4,128)S(1)} %get-tuple-element.49.places_ref, f32[1,512]{1,0:T(1,128)S(1)} %constant_dynamic-slice_fusion.root_ref, f32[1,128]{1,0:T(1,128)S(1)} %bitcast.26, bf16[64,16,128]{2,1,0:T(8,128)(2,1)S(1)} %pad_maximum_fusion.1.refs_0_, ...), custom_call_target="tpu_custom_call" | custom-call | flops 4294967296 | bytes 4194304 | tf_op jit(solution)/shard_map/pallas_call | solution.py:400
  123.6 0.4 collective-permute-start.20
  124.1 8.5 %shard_map.79.refs_4_ = bf16[512,128,128]{2,1,0:T(8,128)(2,1)} custom-call(s32[1]{0:T(128)} %bitcast.6.halves_ref, s32[4,512]{1,0:T(4,128)S(1)} %get-tuple-element.56.places_ref, f32[1,512]{1,0:T(1,128)S(1)} %constant_dynamic-slice_fusion.root_ref, f32[1,128]{1,0:T(1,128)S(1)} %bitcast.27, ...), custom_call_target="tpu_custom_call", output_to_operand_aliasing={{}: (8, {})} | custom-call | flops 12884901888 | bytes 12582912 | tf_op jit(solution)/shard_map/pallas_call | solution.py:400
  132.7 7.1 %shard_map.80 = bf16[512,128,128]{2,1,0:T(8,128)(2,1)} custom-call(s32[1]{0:T(128)} %bitcast.halves_ref, s32[4,512]{1,0:T(4,128)S(1)} %get-tuple-element.57.places_ref, f32[1,512]{1,0:T(1,128)S(1)} %constant_dynamic-slice_fusion.root_ref, f32[1,128]{1,0:T(1,128)S(1)} %bitcast.28, ...), custom_call_target="tpu_custom_call", output_to_operand_aliasing={{}: (8, {})} | custom-call | flops 12884901888 | bytes 12582912 | tf_op jit(solution)/shard_map/pallas_call | solution.py:400
  (52 shorter events, 1.2 us)
Async XLA Ops:
  9.8 10.1 %collective-permute-start = (bf16[8,144,128]{2,1,0:T(8,128)(2,1)}, bf16[8,144,128]{2,1,0:T(8,128)(2,1)S(1)}, u32[]{:S(2)}, u32[]{:S(2)}) collective-permute-start(bf16[8,144,128]{2,1,0:T(8,128)(2,1)} %get-tuple-element.28), channel_id=1, source_target_pairs={{0,8},{8,16},{16,24},{24,0},{1,9},{9,17},{17,25},{25,1},{2,10},{10... | collective-permute-start | bytes 884744 | tf_op jit(solution)/shard_map/ppermute | solution.py:425
  11.1 13.6 %copy-start.6 = (bf16[8,144,128]{2,1,0:T(8,128)(2,1)S(1)}, bf16[8,144,128]{2,1,0:T(8,128)(2,1)}, u32[]{:S(2)}) copy-start(bf16[8,144,128]{2,1,0:T(8,128)(2,1)} %get-tuple-element.33) | copy-start | bytes 884740
  11.1 14.5 %copy-start.5 = (bf16[8,144,128]{2,1,0:T(8,128)(2,1)S(1)}, bf16[8,144,128]{2,1,0:T(8,128)(2,1)}, u32[]{:S(2)}) copy-start(bf16[8,144,128]{2,1,0:T(8,128)(2,1)} %get-tuple-element.40) | copy-start | bytes 884740
  11.1 16.1 %copy-start.3 = (s32[128,3]{0,1:T(4,128)S(1)}, s32[128,3]{0,1:T(4,128)}, u32[]{:S(2)}) copy-start(s32[128,3]{0,1:T(4,128)} %param.11) | copy-start | bytes 4612
  11.1 16.2 %copy-start.4 = (f32[128]{0:T(128)S(1)}, f32[128]{0:T(128)}, u32[]{:S(2)}) copy-start(f32[128]{0:T(128)} %param.12) | copy-start | bytes 1540
  11.1 41.7 %copy-start = (bf16[8,144,128]{2,1,0:T(8,128)(2,1)S(1)}, bf16[8,144,128]{2,1,0:T(8,128)(2,1)}, u32[]{:S(2)}) copy-start(bf16[8,144,128]{2,1,0:T(8,128)(2,1)} %get-tuple-element.37.refs_0_) | copy-start | bytes 884740
  11.1 47.6 %copy-start.7 = (f32[256]{0:T(256)S(1)}, f32[256]{0:T(256)}, u32[]{:S(2)}) copy-start(f32[256]{0:T(256)} %param.9) | copy-start | bytes 3076
  11.2 53.0 %copy-start.1 = (bf16[128,128]{1,0:T(8,128)(2,1)S(1)}, bf16[128,128]{1,0:T(8,128)(2,1)}, u32[]{:S(2)}) copy-start(bf16[128,128]{1,0:T(8,128)(2,1)} %mixing_ref.1) | copy-start | bytes 98308
  11.2 105.6 %copy-start.2 = (f32[128]{0:T(128)S(1)}, f32[128]{0:T(128)}, u32[]{:S(2)}) copy-start(f32[128]{0:T(128)} %param.13) | copy-start | bytes 1540
  19.9 16.5 %all-to-all-start = ((bf16[8,4,128,128]{3,2,1,0:T(8,128)(2,1)}), bf16[8,4,128,128]{3,2,1,0:T(8,128)(2,1)S(1)}, u32[]{:S(2)}, u32[]{:S(2)}) async-start(bf16[8,4,128,128]{3,2,1,0:T(8,128)(2,1)} %shard_map.74), calls=%async_computation | async-start | bytes 2097152 | tf_op jit(solution)/shard_map/all_to_all | solution.py:256
  24.7 22.5 %collective-permute-start.3 = (bf16[8,144,128]{2,1,0:T(8,128)(2,1)S(1)}, bf16[8,144,128]{2,1,0:T(8,128)(2,1)S(1)}, u32[]{:S(2)}, u32[]{:S(2)}) collective-permute-start(bf16[8,144,128]{2,1,0:T(8,128)(2,1)S(1)} %copy-done.6), channel_id=1, source_target_pairs={{0,16},{8,24},{16,0},{24,8},{1,17},{9,25},{17,1},{25,9},{2,18},{10... | collective-permute-start | bytes 884744 | tf_op jit(solution)/shard_map/ppermute | solution.py:425
  25.7 27.1 %collective-permute-start.5 = (bf16[8,144,128]{2,1,0:T(8,128)(2,1)S(1)}, bf16[8,144,128]{2,1,0:T(8,128)(2,1)S(1)}, u32[]{:S(2)}, u32[]{:S(2)}) collective-permute-start(bf16[8,144,128]{2,1,0:T(8,128)(2,1)S(1)} %copy-done.5), channel_id=1, source_target_pairs={{0,24},{8,0},{16,8},{24,16},{1,25},{9,1},{17,9},{25,17},{2,26},{10... | collective-permute-start | bytes 884744 | tf_op jit(solution)/shard_map/ppermute | solution.py:425
  36.5 13.5 %collective-permute-start.1 = (bf16[4,128,128]{2,1,0:T(8,128)(2,1)S(1)}, bf16[4,128,128]{2,1,0:T(8,128)(2,1)S(1)}, u32[]{:S(2)}, u32[]{:S(2)}) collective-permute-start(bf16[4,128,128]{2,1,0:T(8,128)(2,1)S(1)} %get-tuple-element.31), channel_id=1, source_target_pairs={{0,8},{8,16},{16,24},{24,0},{1,9},{9,17},{17,25},{25,1},{2,10},{10... | collective-permute-start | bytes 393224 | tf_op jit(solution)/shard_map/ppermute | solution.py:425
  37.8 15.0 %collective-permute-start.2 = (bf16[4,128,128]{2,1,0:T(8,128)(2,1)S(1)}, bf16[4,128,128]{2,1,0:T(8,128)(2,1)S(1)}, u32[]{:S(2)}, u32[]{:S(2)}) collective-permute-start(bf16[4,128,128]{2,1,0:T(8,128)(2,1)S(1)} %get-tuple-element.32), channel_id=1, source_target_pairs={{0,16},{8,24},{16,0},{24,8},{1,17},{9,25},{17,1},{25,9},{2,18},{10... | collective-permute-start | bytes 393224 | tf_op jit(solution)/shard_map/ppermute | solution.py:425
  53.7 10.4 %all-to-all-start.1 = ((bf16[8,1,144,128]{3,2,1,0:T(8,128)(2,1)}), bf16[8,1,144,128]{3,2,1,0:T(8,128)(2,1)S(1)}, u32[]{:S(2)}, u32[]{:S(2)}) async-start(bf16[8,1,144,128]{3,2,1,0:T(8,128)(2,1)} %shard_map.76), calls=%async_computation.1 | async-start | bytes 589824 | tf_op jit(solution)/shard_map/all_to_all | solution.py:261
  58.8 5.3 %collective-permute-start.4 = (bf16[4,128,128]{2,1,0:T(8,128)(2,1)S(1)}, bf16[4,128,128]{2,1,0:T(8,128)(2,1)S(1)}, u32[]{:S(2)}, u32[]{:S(2)}) collective-permute-start(bf16[4,128,128]{2,1,0:T(8,128)(2,1)S(1)} %get-tuple-element.36), channel_id=1, source_target_pairs={{0,24},{8,0},{16,8},{24,16},{1,25},{9,1},{17,9},{25,17},{2,26},{10... | collective-permute-start | bytes 393224 | tf_op jit(solution)/shard_map/ppermute | solution.py:425
  64.7 2.2 %collective-permute-start.6 = (bf16[8,64,128]{2,1,0:T(8,128)(2,1)S(1)}, bf16[8,64,128]{2,1,0:T(8,128)(2,1)S(1)}, u32[]{:S(2)}, u32[]{:S(2)}) collective-permute-start(bf16[8,64,128]{2,1,0:T(8,128)(2,1)S(1)} %get-tuple-element.42), channel_id=1, source_target_pairs={{0,1},{1,0},{2,3},{3,2},{4,5},{5,4},{6,7},{7,6},{8,9},{9,8},{10,11... | collective-permute-start | bytes 393224 | tf_op jit(solution)/shard_map/ppermute | solution.py:441
  67.0 7.4 %collective-permute-start.7 = (bf16[16,16,128]{2,1,0:T(8,128)(2,1)S(1)}, bf16[16,16,128]{2,1,0:T(8,128)(2,1)S(1)}, u32[]{:S(2)}, u32[]{:S(2)}) collective-permute-start(bf16[16,16,128]{2,1,0:T(8,128)(2,1)S(1)} %pad_maximum_fusion.3), channel_id=1, source_target_pairs={{0,2},{1,3},{2,0},{3,1},{4,6},{5,7},{6,4},{7,5},{8,10},{9,11},{10,... | collective-permute-start | bytes 196616 | tf_op jit(solution)/shard_map/ppermute | solution.py:437
  68.3 10.2 %collective-permute-start.10 = (bf16[16,48,128]{2,1,0:T(8,128)(2,1)S(1)}, bf16[16,48,128]{2,1,0:T(8,128)(2,1)S(1)}, u32[]{:S(2)}, u32[]{:S(2)}) collective-permute-start(bf16[16,48,128]{2,1,0:T(8,128)(2,1)S(1)} %pad_maximum_fusion.2), channel_id=1, source_target_pairs={{0,8},{8,16},{16,24},{24,0},{1,9},{9,17},{17,25},{25,1},{2,10},{10... | collective-permute-start | bytes 589832 | tf_op jit(solution)/shard_map/ppermute | solution.py:425
  69.7 16.2 %collective-permute-start.11 = (bf16[16,48,128]{2,1,0:T(8,128)(2,1)S(1)}, bf16[16,48,128]{2,1,0:T(8,128)(2,1)S(1)}, u32[]{:S(2)}, u32[]{:S(2)}) collective-permute-start(bf16[16,48,128]{2,1,0:T(8,128)(2,1)S(1)} %pad_maximum_fusion.2), channel_id=1, source_target_pairs={{0,16},{8,24},{16,0},{24,8},{1,17},{9,25},{17,1},{25,9},{2,18},{10... | collective-permute-start | bytes 589832 | tf_op jit(solution)/shard_map/ppermute | solution.py:425
  72.7 17.9 %collective-permute-start.12 = (bf16[16,48,128]{2,1,0:T(8,128)(2,1)S(1)}, bf16[16,48,128]{2,1,0:T(8,128)(2,1)S(1)}, u32[]{:S(2)}, u32[]{:S(2)}) collective-permute-start(bf16[16,48,128]{2,1,0:T(8,128)(2,1)S(1)} %pad_maximum_fusion.2), channel_id=1, source_target_pairs={{0,24},{8,0},{16,8},{24,16},{1,25},{9,1},{17,9},{25,17},{2,26},{10... | collective-permute-start | bytes 589832 | tf_op jit(solution)/shard_map/ppermute | solution.py:425
  74.1 3.1 %collective-permute-start.8 = (bf16[16,16,128]{2,1,0:T(8,128)(2,1)S(1)}, bf16[16,16,128]{2,1,0:T(8,128)(2,1)S(1)}, u32[]{:S(2)}, u32[]{:S(2)}) collective-permute-start(bf16[16,16,128]{2,1,0:T(8,128)(2,1)S(1)} %pad_maximum_fusion.3), channel_id=1, source_target_pairs={{0,4},{1,5},{2,6},{3,7},{4,0},{5,1},{6,2},{7,3},{8,12},{9,13},{10,... | collective-permute-start | bytes 196616 | tf_op jit(solution)/shard_map/ppermute | solution.py:437
  74.4 4.0 %collective-permute-start.9 = (bf16[16,16,128]{2,1,0:T(8,128)(2,1)S(1)}, bf16[16,16,128]{2,1,0:T(8,128)(2,1)S(1)}, u32[]{:S(2)}, u32[]{:S(2)}) collective-permute-start(bf16[16,16,128]{2,1,0:T(8,128)(2,1)S(1)} %pad_maximum_fusion.3), channel_id=1, source_target_pairs={{0,6},{1,7},{2,4},{3,5},{4,2},{5,3},{6,0},{7,1},{8,14},{9,15},{10,... | collective-permute-start | bytes 196616 | tf_op jit(solution)/shard_map/ppermute | solution.py:437
  90.8 18.0 %collective-permute-start.14 = (bf16[64,48,128]{2,1,0:T(8,128)(2,1)S(1)}, bf16[64,48,128]{2,1,0:T(8,128)(2,1)}, u32[]{:S(2)}, u32[]{:S(2)}) collective-permute-start(bf16[64,48,128]{2,1,0:T(8,128)(2,1)S(1)} %pad_maximum_fusion.refs_0_), channel_id=1, source_target_pairs={{0,2},{1,5},{2,0},{3,7},{4,6},{5,1},{6,4},{7,3},{8,10},{9,13},{10,... | collective-permute-start | bytes 2359304 | tf_op jit(solution)/shard_map/ppermute | solution.py:433
  91.3 7.2 %collective-permute-start.15 = (bf16[64,16,128]{2,1,0:T(8,128)(2,1)S(1)}, bf16[64,16,128]{2,1,0:T(8,128)(2,1)S(1)}, u32[]{:S(2)}, u32[]{:S(2)}) collective-permute-start(bf16[64,16,128]{2,1,0:T(8,128)(2,1)S(1)} %pad_maximum_fusion.1.refs_0_), channel_id=1, source_target_pairs={{0,8},{8,16},{16,24},{24,0},{1,9},{9,17},{17,25},{25,1},{2,10},{10... | collective-permute-start | bytes 786440 | tf_op jit(solution)/shard_map/ppermute | solution.py:425
  91.3 25.3 %collective-permute-start.17 = (bf16[64,48,128]{2,1,0:T(8,128)(2,1)S(1)}, bf16[64,48,128]{2,1,0:T(8,128)(2,1)}, u32[]{:S(2)}, u32[]{:S(2)}) collective-permute-start(bf16[64,48,128]{2,1,0:T(8,128)(2,1)S(1)} %pad_maximum_fusion.refs_0_), channel_id=1, source_target_pairs={{0,4},{1,3},{2,6},{3,1},{4,0},{5,7},{6,2},{7,5},{8,12},{9,11},{10,... | collective-permute-start | bytes 2359304 | tf_op jit(solution)/shard_map/ppermute | solution.py:433
  91.4 21.9 %collective-permute-start.21 = (bf16[64,16,128]{2,1,0:T(8,128)(2,1)S(1)}, bf16[64,16,128]{2,1,0:T(8,128)(2,1)S(1)}, u32[]{:S(2)}, u32[]{:S(2)}) collective-permute-start(bf16[64,16,128]{2,1,0:T(8,128)(2,1)S(1)} %pad_maximum_fusion.1.refs_0_), channel_id=1, source_target_pairs={{0,16},{8,24},{16,0},{24,8},{1,17},{9,25},{17,1},{25,9},{2,18},{10... | collective-permute-start | bytes 786440 | tf_op jit(solution)/shard_map/ppermute | solution.py:425
  91.4 23.2 %collective-permute-start.22 = (bf16[64,16,128]{2,1,0:T(8,128)(2,1)S(1)}, bf16[64,16,128]{2,1,0:T(8,128)(2,1)S(1)}, u32[]{:S(2)}, u32[]{:S(2)}) collective-permute-start(bf16[64,16,128]{2,1,0:T(8,128)(2,1)S(1)} %pad_maximum_fusion.1.refs_0_), channel_id=1, source_target_pairs={{0,24},{8,0},{16,8},{24,16},{1,25},{9,1},{17,9},{25,17},{2,26},{10... | collective-permute-start | bytes 786440 | tf_op jit(solution)/shard_map/ppermute | solution.py:425
  98.4 16.2 %collective-permute-start.23 = (bf16[64,16,128]{2,1,0:T(8,128)(2,1)S(1)}, bf16[64,16,128]{2,1,0:T(8,128)(2,1)S(1)}, u32[]{:S(2)}, u32[]{:S(2)}) collective-permute-start(bf16[64,16,128]{2,1,0:T(8,128)(2,1)S(1)} %pad_maximum_fusion.1.refs_0_), channel_id=1, source_target_pairs={{0,1},{1,0},{2,3},{3,2},{4,5},{5,4},{6,7},{7,6},{8,9},{9,8},{10,11... | collective-permute-start | bytes 786440 | tf_op jit(solution)/shard_map/ppermute | solution.py:441
  108.7 14.9 %collective-permute-start.19 = (bf16[64,48,128]{2,1,0:T(8,128)(2,1)}, bf16[64,48,128]{2,1,0:T(8,128)(2,1)}, u32[]{:S(2)}, u32[]{:S(2)}) collective-permute-start(bf16[64,48,128]{2,1,0:T(8,128)(2,1)} %collective-permute-done.14.refs_1_), channel_id=1, source_target_pairs={{0,4},{1,3},{2,6},{3,1},{4,0},{5,7},{6,2},{7,5},{8,12},{9,11},{10,... | collective-permute-start | bytes 2359304 | tf_op jit(solution)/shard_map/ppermute | solution.py:433
  113.3 2.5 %collective-permute-start.25 = (bf16[64,16,128]{2,1,0:T(8,128)(2,1)S(1)}, bf16[64,16,128]{2,1,0:T(8,128)(2,1)S(1)}, u32[]{:S(2)}, u32[]{:S(2)}) collective-permute-start(bf16[64,16,128]{2,1,0:T(8,128)(2,1)S(1)} %collective-permute-done.21.refs_2_), channel_id=1, source_target_pairs={{0,1},{1,0},{2,3},{3,2},{4,5},{5,4},{6,7},{7,6},{8,9},{9,8},{10,11... | collective-permute-start | bytes 786440 | tf_op jit(solution)/shard_map/ppermute | solution.py:441
  114.7 1.5 %collective-permute-start.26 = (bf16[64,16,128]{2,1,0:T(8,128)(2,1)S(1)}, bf16[64,16,128]{2,1,0:T(8,128)(2,1)S(1)}, u32[]{:S(2)}, u32[]{:S(2)}) collective-permute-start(bf16[64,16,128]{2,1,0:T(8,128)(2,1)S(1)} %collective-permute-done.22.refs_3_), channel_id=1, source_target_pairs={{0,1},{1,0},{2,3},{3,2},{4,5},{5,4},{6,7},{7,6},{8,9},{9,8},{10,11... | collective-permute-start | bytes 786440 | tf_op jit(solution)/shard_map/ppermute | solution.py:441
  114.7 2.0 %collective-permute-start.24 = (bf16[64,16,128]{2,1,0:T(8,128)(2,1)S(1)}, bf16[64,16,128]{2,1,0:T(8,128)(2,1)S(1)}, u32[]{:S(2)}, u32[]{:S(2)}) collective-permute-start(bf16[64,16,128]{2,1,0:T(8,128)(2,1)S(1)} %collective-permute-done.15.refs_1_), channel_id=1, source_target_pairs={{0,1},{1,0},{2,3},{3,2},{4,5},{5,4},{6,7},{7,6},{8,9},{9,8},{10,11... | collective-permute-start | bytes 786440 | tf_op jit(solution)/shard_map/ppermute | solution.py:441
  115.8 16.8 %collective-permute-start.13 = (bf16[64,48,128]{2,1,0:T(8,128)(2,1)S(1)}, bf16[64,48,128]{2,1,0:T(8,128)(2,1)S(1)}, u32[]{:S(2)}, u32[]{:S(2)}) collective-permute-start(bf16[64,48,128]{2,1,0:T(8,128)(2,1)S(1)} %pad_maximum_fusion.refs_0_), channel_id=1, source_target_pairs={{0,1},{1,0},{2,3},{3,2},{4,5},{5,4},{6,7},{7,6},{8,9},{9,8},{10,11... | collective-permute-start | bytes 2359304 | tf_op jit(solution)/shard_map/ppermute | solution.py:441
  116.2 16.4 %collective-permute-start.16 = (bf16[64,48,128]{2,1,0:T(8,128)(2,1)}, bf16[64,48,128]{2,1,0:T(8,128)(2,1)S(1)}, u32[]{:S(2)}, u32[]{:S(2)}) collective-permute-start(bf16[64,48,128]{2,1,0:T(8,128)(2,1)} %collective-permute-done.14.refs_1_), channel_id=1, source_target_pairs={{0,1},{1,0},{2,3},{3,2},{4,5},{5,4},{6,7},{7,6},{8,9},{9,8},{10,11... | collective-permute-start | bytes 2359304 | tf_op jit(solution)/shard_map/ppermute | solution.py:441
  116.6 16.1 %collective-permute-start.18 = (bf16[64,48,128]{2,1,0:T(8,128)(2,1)}, bf16[64,48,128]{2,1,0:T(8,128)(2,1)S(1)}, u32[]{:S(2)}, u32[]{:S(2)}) collective-permute-start(bf16[64,48,128]{2,1,0:T(8,128)(2,1)} %collective-permute-done.17.refs_2_), channel_id=1, source_target_pairs={{0,1},{1,0},{2,3},{3,2},{4,5},{5,4},{6,7},{7,6},{8,9},{9,8},{10,11... | collective-permute-start | bytes 2359304 | tf_op jit(solution)/shard_map/ppermute | solution.py:441
  123.6 9.0 %collective-permute-start.20 = (bf16[64,48,128]{2,1,0:T(8,128)(2,1)}, bf16[64,48,128]{2,1,0:T(8,128)(2,1)S(1)}, u32[]{:S(2)}, u32[]{:S(2)}) collective-permute-start(bf16[64,48,128]{2,1,0:T(8,128)(2,1)} %collective-permute-done.19.refs_3_), channel_id=1, source_target_pairs={{0,1},{1,0},{2,3},{3,2},{4,5},{5,4},{6,7},{7,6},{8,9},{9,8},{10,11... | collective-permute-start | bytes 2359304 | tf_op jit(solution)/shard_map/ppermute | solution.py:441

commit v17 on v16

--- a/solution.py
+++ b/solution.py
@@ -336,7 +336,7 @@
     bias = bias_ref[...]
     count = places_ref.shape[0]
     tile = 16
-    batch = min(8, rows)
+    batch = min(16, rows)
     tiles = zones // tile
 
     def leaving(step, slot, side):

time: 142 us -> 140 us (0.986)
  Pallas kernels: 42.6 us -> 41 us
    pallas_call x3, Pallas kernels: 22.6 us -> 21 us  [spread(): pl.pallas_call(functools.partial(spread_kernel, sides, count, stride, off...]
where the time goes in v17:
time: 140 us; the launch traced here: 138 us
  waiting for transfers between devices  54.3 us (39%)
  Pallas kernels  41 us (29%)
  starting transfers between devices  40.3 us (29%)
    ppermute x12, waiting for transfers between devices, shifted(): lax.ppermute(x, LINE, [(i, (i + amount) % size) for i in range(size)])  34.4 us
    pallas_call x3, Pallas kernels, spread(): pl.pallas_call(functools.partial(spread_kernel, sides, count, stride, off...  21 us
    pallas_call x2, Pallas kernels, half_sums(): pl.pallas_call(functools.partial(kernel, plan, begin, half, pitch), grid=...  18.5 us
    ppermute x12, starting transfers between devices, shifted(): lax.ppermute(x, LINE, [(i, (i + amount) % size) for i in range(size)])  16.6 us
    all_to_all x1, waiting for transfers between devices, org_sums(): lax.all_to_all(first, SQUARE, split_axis=0, concat_axis=0, tiled=True)  8.92 us
    ppermute x9, starting transfers between devices, swapped(): return lax.ppermute(x, 'core', [(0, 1), (1, 0)])  7.42 us
    ppermute x3, waiting for transfers between devices, crossed(): return lax.ppermute(x, SQUARE, pairs)  6.69 us
    all_to_all x1, starting transfers between devices, org_sums(): lax.all_to_all(second, SQUARE, split_axis=0, concat_axis=0, tiled=True)  5.03 us
  transfers between devices with their start and end apart: 29, of which 14 were waited for; matrix products, arithmetic and copies ran while one was open for 2% of the time, Pallas kernels for 17%

profile of v17, /device:TPU:13, one launch (start us, length us, event | category | flops | bytes accessed | tf_op | source)
XLA Modules:
  0.0 138.4 jit_solution(3718247275176445953)
XLA Ops:
  0.0 9.8 %shard_map.73 = (bf16[8,144,128]{2,1,0:T(8,128)(2,1)}, bf16[8,144,128]{2,1,0:T(8,128)(2,1)}, bf16[8,144,128]{2,1,0:T(8,128)(2,1)}, bf16[8,144,128]{2,1,0:T(8,128...) custom-call(s32[1]{0:T(128)} %bitcast.2.line_ref, s32[4,2048]{1,0:T(4,128)} %bitcast.29, f32[1,256]{1,0:T(1,128)} %bitcast.30, ...), custom_call_target="tpu_custom_call" | custom-call | flops 8589934592 | bytes 16777216 | tf_op jit(solution)/shard_map/pallas_call | solution.py:171
  9.8 1.3 collective-permute-start
  11.2 8.7 %shard_map.74 = bf16[8,4,128,128]{3,2,1,0:T(8,128)(2,1)} custom-call(s32[1]{0:T(128)} %bitcast.2.line_ref, bf16[256,2048]{1,0:T(8,128)(2,1)} %get-tuple-element.27.weighted_ref, bf16[2048,32,128]{2,1,0:T(8,128)(2,1)} %cells_ref.3), custom_call_target="tpu_custom_call" | custom-call | flops 8589934592 | bytes 16777216 | tf_op jit(solution)/shard_map/pallas_call | solution.py:171
  19.9 4.8 %all-to-all-start = ((bf16[8,4,128,128]{3,2,1,0:T(8,128)(2,1)}), bf16[8,4,128,128]{3,2,1,0:T(8,128)(2,1)S(1)}, u32[]{:S(2)}, u32[]{:S(2)}) async-start(bf16[8,4,128,128]{3,2,1,0:T(8,128)(2,1)} %shard_map.74), calls=%async_computation | async-start | bytes 2097152 | tf_op jit(solution)/shard_map/all_to_all | solution.py:256
  24.7 1.0 collective-permute-start.3
  25.7 1.5 %collective-permute-start.5 = (bf16[8,144,128]{2,1,0:T(8,128)(2,1)S(1)}, bf16[8,144,128]{2,1,0:T(8,128)(2,1)S(1)}, u32[]{:S(2)}, u32[]{:S(2)}) collective-permute-start(bf16[8,144,128]{2,1,0:T(8,128)(2,1)S(1)} %copy-done.5), channel_id=1, source_target_pairs={{0,24},{8,0},{16,8},{24,16},{1,25},{9,1},{17,9},{25,17},{2,26},{10... | collective-permute-start | bytes 884744 | tf_op jit(solution)/shard_map/ppermute | solution.py:425
  27.5 8.9 %all-to-all-done.part_ref = bf16[8,4,128,128]{3,2,1,0:T(8,128)(2,1)S(1)} async-done(((bf16[8,4,128,128]{3,2,1,0:T(8,128)(2,1)}), bf16[8,4,128,128]{3,2,1,0:T(8,128)(2,1)S(1)}, u32[]{:S(2)}, u32[]{:S(2)}) %all-to-all-start) | async-done | bytes 1048608 | tf_op jit(solution)/shard_map/all_to_all | solution.py:256
  36.5 1.3 collective-permute-start.1
  37.8 1.4 %collective-permute-start.2 = (bf16[4,128,128]{2,1,0:T(8,128)(2,1)S(1)}, bf16[4,128,128]{2,1,0:T(8,128)(2,1)S(1)}, u32[]{:S(2)}, u32[]{:S(2)}) collective-permute-start(bf16[4,128,128]{2,1,0:T(8,128)(2,1)S(1)} %get-tuple-element.32), channel_id=1, source_target_pairs={{0,16},{8,24},{16,0},{24,8},{1,17},{9,25},{17,1},{25,9},{2,18},{10... | collective-permute-start | bytes 393224 | tf_op jit(solution)/shard_map/ppermute | solution.py:425
  39.3 0.3 convolution_convert_fusion
  39.6 7.6 %collective-permute-done.3.refs_2_ = bf16[8,144,128]{2,1,0:T(8,128)(2,1)S(1)} collective-permute-done((bf16[8,144,128]{2,1,0:T(8,128)(2,1)S(1)}, bf16[8,144,128]{2,1,0:T(8,128)(2,1)S(1)}, u32[]{:S(2)}, u32[]{:S(2)}) %collective-permute-start.3) | collective-permute-done | bytes 294944 | tf_op jit(solution)/shard_map/ppermute | solution.py:425
  47.2 2.8 %collective-permute-done.1.refs_1_ = bf16[4,128,128]{2,1,0:T(8,128)(2,1)S(1)} collective-permute-done((bf16[4,128,128]{2,1,0:T(8,128)(2,1)S(1)}, bf16[4,128,128]{2,1,0:T(8,128)(2,1)S(1)}, u32[]{:S(2)}, u32[]{:S(2)}) %collective-permute-start.1) | collective-permute-done | bytes 131104 | tf_op jit(solution)/shard_map/ppermute | solution.py:425
  50.0 2.8 %collective-permute-done.2.refs_2_ = bf16[4,128,128]{2,1,0:T(8,128)(2,1)S(1)} collective-permute-done((bf16[4,128,128]{2,1,0:T(8,128)(2,1)S(1)}, bf16[4,128,128]{2,1,0:T(8,128)(2,1)S(1)}, u32[]{:S(2)}, u32[]{:S(2)}) %collective-permute-start.2) | collective-permute-done | bytes 131104 | tf_op jit(solution)/shard_map/ppermute | solution.py:425
  52.8 0.9 shard_map.76
  53.7 5.0 %all-to-all-start.1 = ((bf16[8,1,144,128]{3,2,1,0:T(8,128)(2,1)}), bf16[8,1,144,128]{3,2,1,0:T(8,128)(2,1)S(1)}, u32[]{:S(2)}, u32[]{:S(2)}) async-start(bf16[8,1,144,128]{3,2,1,0:T(8,128)(2,1)} %shard_map.76), calls=%async_computation.1 | async-start | bytes 589824 | tf_op jit(solution)/shard_map/all_to_all | solution.py:261
  58.8 2.8 %collective-permute-start.4 = (bf16[4,128,128]{2,1,0:T(8,128)(2,1)S(1)}, bf16[4,128,128]{2,1,0:T(8,128)(2,1)S(1)}, u32[]{:S(2)}, u32[]{:S(2)}) collective-permute-start(bf16[4,128,128]{2,1,0:T(8,128)(2,1)S(1)} %get-tuple-element.36), channel_id=1, source_target_pairs={{0,24},{8,0},{16,8},{24,16},{1,25},{9,1},{17,9},{25,17},{2,26},{10... | collective-permute-start | bytes 393224 | tf_op jit(solution)/shard_map/ppermute | solution.py:425
  61.6 2.5 %collective-permute-done.4.refs_3_ = bf16[4,128,128]{2,1,0:T(8,128)(2,1)S(1)} collective-permute-done((bf16[4,128,128]{2,1,0:T(8,128)(2,1)S(1)}, bf16[4,128,128]{2,1,0:T(8,128)(2,1)S(1)}, u32[]{:S(2)}, u32[]{:S(2)}) %collective-permute-start.4) | collective-permute-done | bytes 131104 | tf_op jit(solution)/shard_map/ppermute | solution.py:425
  64.2 0.5 shard_map.77
  64.7 1.3 collective-permute-start.6
  66.0 1.0 collective-permute-done.6
  67.0 1.2 collective-permute-start.7
  68.3 1.4 %collective-permute-start.10 = (bf16[16,48,128]{2,1,0:T(8,128)(2,1)S(1)}, bf16[16,48,128]{2,1,0:T(8,128)(2,1)S(1)}, u32[]{:S(2)}, u32[]{:S(2)}) collective-permute-start(bf16[16,48,128]{2,1,0:T(8,128)(2,1)S(1)} %pad_maximum_fusion.2), channel_id=1, source_target_pairs={{0,8},{8,16},{16,24},{24,0},{1,9},{9,17},{17,25},{25,1},{2,10},{10... | collective-permute-start | bytes 589832 | tf_op jit(solution)/shard_map/ppermute | solution.py:425
  69.7 3.1 %collective-permute-start.11 = (bf16[16,48,128]{2,1,0:T(8,128)(2,1)S(1)}, bf16[16,48,128]{2,1,0:T(8,128)(2,1)S(1)}, u32[]{:S(2)}, u32[]{:S(2)}) collective-permute-start(bf16[16,48,128]{2,1,0:T(8,128)(2,1)S(1)} %pad_maximum_fusion.2), channel_id=1, source_target_pairs={{0,16},{8,24},{16,0},{24,8},{1,17},{9,25},{17,1},{25,9},{2,18},{10... | collective-permute-start | bytes 589832 | tf_op jit(solution)/shard_map/ppermute | solution.py:425
  72.7 1.4 %collective-permute-start.12 = (bf16[16,48,128]{2,1,0:T(8,128)(2,1)S(1)}, bf16[16,48,128]{2,1,0:T(8,128)(2,1)S(1)}, u32[]{:S(2)}, u32[]{:S(2)}) collective-permute-start(bf16[16,48,128]{2,1,0:T(8,128)(2,1)S(1)} %pad_maximum_fusion.2), channel_id=1, source_target_pairs={{0,24},{8,0},{16,8},{24,16},{1,25},{9,1},{17,9},{25,17},{2,26},{10... | collective-permute-start | bytes 589832 | tf_op jit(solution)/shard_map/ppermute | solution.py:425
  74.1 0.3 collective-permute-start.8
  74.4 1.2 collective-permute-start.9
  75.6 1.6 %collective-permute-done.8 = bf16[16,16,128]{2,1,0:T(8,128)(2,1)S(1)} collective-permute-done((bf16[16,16,128]{2,1,0:T(8,128)(2,1)S(1)}, bf16[16,16,128]{2,1,0:T(8,128)(2,1)S(1)}, u32[]{:S(2)}, u32[]{:S(2)}) %collective-permute-start.8) | collective-permute-done | bytes 65568 | tf_op jit(solution)/shard_map/ppermute | solution.py:437
  77.2 1.2 collective-permute-done.9
  78.5 7.4 %collective-permute-done.11 = bf16[16,48,128]{2,1,0:T(8,128)(2,1)S(1)} collective-permute-done((bf16[16,48,128]{2,1,0:T(8,128)(2,1)S(1)}, bf16[16,48,128]{2,1,0:T(8,128)(2,1)S(1)}, u32[]{:S(2)}, u32[]{:S(2)}) %collective-permute-start.11) | collective-permute-done | bytes 196640 | tf_op jit(solution)/shard_map/ppermute | solution.py:425
  85.9 4.7 %collective-permute-done.12 = bf16[16,48,128]{2,1,0:T(8,128)(2,1)S(1)} collective-permute-done((bf16[16,48,128]{2,1,0:T(8,128)(2,1)S(1)}, bf16[16,48,128]{2,1,0:T(8,128)(2,1)S(1)}, u32[]{:S(2)}, u32[]{:S(2)}) %collective-permute-start.12) | collective-permute-done | bytes 196640 | tf_op jit(solution)/shard_map/ppermute | solution.py:425
  90.8 0.5 collective-permute-start.14
  91.4 1.4 %collective-permute-start.22 = (bf16[64,16,128]{2,1,0:T(8,128)(2,1)S(1)}, bf16[64,16,128]{2,1,0:T(8,128)(2,1)S(1)}, u32[]{:S(2)}, u32[]{:S(2)}) collective-permute-start(bf16[64,16,128]{2,1,0:T(8,128)(2,1)S(1)} %pad_maximum_fusion.1.refs_0_), channel_id=1, source_target_pairs={{0,24},{8,0},{16,8},{24,16},{1,25},{9,1},{17,9},{25,17},{2,26},{10... | collective-permute-start | bytes 786440 | tf_op jit(solution)/shard_map/ppermute | solution.py:425
  92.8 5.6 %collective-permute-done.15.refs_1_ = bf16[64,16,128]{2,1,0:T(8,128)(2,1)S(1)} collective-permute-done((bf16[64,16,128]{2,1,0:T(8,128)(2,1)S(1)}, bf16[64,16,128]{2,1,0:T(8,128)(2,1)S(1)}, u32[]{:S(2)}, u32[]{:S(2)}) %collective-permute-start.15) | collective-permute-done | bytes 262176 | tf_op jit(solution)/shard_map/ppermute | solution.py:425
  98.4 2.8 %collective-permute-start.23 = (bf16[64,16,128]{2,1,0:T(8,128)(2,1)S(1)}, bf16[64,16,128]{2,1,0:T(8,128)(2,1)S(1)}, u32[]{:S(2)}, u32[]{:S(2)}) collective-permute-start(bf16[64,16,128]{2,1,0:T(8,128)(2,1)S(1)} %pad_maximum_fusion.1.refs_0_), channel_id=1, source_target_pairs={{0,1},{1,0},{2,3},{3,2},{4,5},{5,4},{6,7},{7,6},{8,9},{9,8},{10,11... | collective-permute-start | bytes 786440 | tf_op jit(solution)/shard_map/ppermute | solution.py:441
  101.3 0.8 multiply_add_fusion
  102.0 6.7 %collective-permute-done.14.refs_1_ = bf16[64,48,128]{2,1,0:T(8,128)(2,1)} collective-permute-done((bf16[64,48,128]{2,1,0:T(8,128)(2,1)S(1)}, bf16[64,48,128]{2,1,0:T(8,128)(2,1)}, u32[]{:S(2)}, u32[]{:S(2)}) %collective-permute-start.14) | collective-permute-done | bytes 786464 | tf_op jit(solution)/shard_map/ppermute | solution.py:433
  108.7 3.0 %collective-permute-start.19 = (bf16[64,48,128]{2,1,0:T(8,128)(2,1)}, bf16[64,48,128]{2,1,0:T(8,128)(2,1)}, u32[]{:S(2)}, u32[]{:S(2)}) collective-permute-start(bf16[64,48,128]{2,1,0:T(8,128)(2,1)} %collective-permute-done.14.refs_1_), channel_id=1, source_target_pairs={{0,4},{1,3},{2,6},{3,1},{4,0},{5,7},{6,2},{7,5},{8,12},{9,11},{10,... | collective-permute-start | bytes 2359304 | tf_op jit(solution)/shard_map/ppermute | solution.py:433
  111.8 0.7 constant_dynamic-slice_fusion.root_ref
  112.4 0.9 collective-permute-done.21.refs_2_
  113.3 1.3 collective-permute-start.25
  114.7 0.5 collective-permute-start.24
  115.3 0.5 collective-permute-done.25.refs_6_
  115.8 0.4 collective-permute-start.13
  116.2 0.4 collective-permute-start.16
  116.7 6.3 %shard_map.78.refs_4_ = bf16[512,128,128]{2,1,0:T(8,128)(2,1)} custom-call(s32[2]{0:T(128)S(1)} %pad_add_fusion.halves_ref, s32[4,512]{1,0:T(4,128)S(1)} %get-tuple-element.49.places_ref, f32[1,512]{1,0:T(1,128)S(1)} %constant_dynamic-slice_fusion.root_ref, f32[1,128]{1,0:T(1,128)S(1)} %bitcast.26, bf16[64,16,128]{2,1,0:T(8,128)(2,1)S(1)} %pad_maximum_fusion.1.refs_0_, ...), custom_call_target="tpu_custom_call" | custom-call | flops 4294967296 | bytes 4194304 | tf_op jit(solution)/shard_map/pallas_call | solution.py:400
  123.1 0.6 collective-permute-start.20
  123.7 8.0 %shard_map.79.refs_4_ = bf16[512,128,128]{2,1,0:T(8,128)(2,1)} custom-call(s32[1]{0:T(128)} %bitcast.6.halves_ref, s32[4,512]{1,0:T(4,128)S(1)} %get-tuple-element.56.places_ref, f32[1,512]{1,0:T(1,128)S(1)} %constant_dynamic-slice_fusion.root_ref, f32[1,128]{1,0:T(1,128)S(1)} %bitcast.27, ...), custom_call_target="tpu_custom_call", output_to_operand_aliasing={{}: (8, {})} | custom-call | flops 12884901888 | bytes 12582912 | tf_op jit(solution)/shard_map/pallas_call | solution.py:400
  131.7 6.6 %shard_map.80 = bf16[512,128,128]{2,1,0:T(8,128)(2,1)} custom-call(s32[1]{0:T(128)} %bitcast.halves_ref, s32[4,512]{1,0:T(4,128)S(1)} %get-tuple-element.57.places_ref, f32[1,512]{1,0:T(1,128)S(1)} %constant_dynamic-slice_fusion.root_ref, f32[1,128]{1,0:T(1,128)S(1)} %bitcast.28, ...), custom_call_target="tpu_custom_call", output_to_operand_aliasing={{}: (8, {})} | custom-call | flops 12884901888 | bytes 12582912 | tf_op jit(solution)/shard_map/pallas_call | solution.py:400
  (52 shorter events, 1.2 us)
Async XLA Ops:
  9.8 10.1 %collective-permute-start = (bf16[8,144,128]{2,1,0:T(8,128)(2,1)}, bf16[8,144,128]{2,1,0:T(8,128)(2,1)S(1)}, u32[]{:S(2)}, u32[]{:S(2)}) collective-permute-start(bf16[8,144,128]{2,1,0:T(8,128)(2,1)} %get-tuple-element.28), channel_id=1, source_target_pairs={{0,8},{8,16},{16,24},{24,0},{1,9},{9,17},{17,25},{25,1},{2,10},{10... | collective-permute-start | bytes 884744 | tf_op jit(solution)/shard_map/ppermute | solution.py:425
  11.1 13.6 %copy-start.6 = (bf16[8,144,128]{2,1,0:T(8,128)(2,1)S(1)}, bf16[8,144,128]{2,1,0:T(8,128)(2,1)}, u32[]{:S(2)}) copy-start(bf16[8,144,128]{2,1,0:T(8,128)(2,1)} %get-tuple-element.33) | copy-start | bytes 884740
  11.1 14.5 %copy-start.5 = (bf16[8,144,128]{2,1,0:T(8,128)(2,1)S(1)}, bf16[8,144,128]{2,1,0:T(8,128)(2,1)}, u32[]{:S(2)}) copy-start(bf16[8,144,128]{2,1,0:T(8,128)(2,1)} %get-tuple-element.40) | copy-start | bytes 884740
  11.1 16.1 %copy-start.3 = (s32[128,3]{0,1:T(4,128)S(1)}, s32[128,3]{0,1:T(4,128)}, u32[]{:S(2)}) copy-start(s32[128,3]{0,1:T(4,128)} %param.11) | copy-start | bytes 4612
  11.1 16.2 %copy-start.4 = (f32[128]{0:T(128)S(1)}, f32[128]{0:T(128)}, u32[]{:S(2)}) copy-start(f32[128]{0:T(128)} %param.12) | copy-start | bytes 1540
  11.1 41.7 %copy-start = (bf16[8,144,128]{2,1,0:T(8,128)(2,1)S(1)}, bf16[8,144,128]{2,1,0:T(8,128)(2,1)}, u32[]{:S(2)}) copy-start(bf16[8,144,128]{2,1,0:T(8,128)(2,1)} %get-tuple-element.37.refs_0_) | copy-start | bytes 884740
  11.1 47.6 %copy-start.7 = (f32[256]{0:T(256)S(1)}, f32[256]{0:T(256)}, u32[]{:S(2)}) copy-start(f32[256]{0:T(256)} %param.9) | copy-start | bytes 3076
  11.2 53.0 %copy-start.1 = (bf16[128,128]{1,0:T(8,128)(2,1)S(1)}, bf16[128,128]{1,0:T(8,128)(2,1)}, u32[]{:S(2)}) copy-start(bf16[128,128]{1,0:T(8,128)(2,1)} %mixing_ref.1) | copy-start | bytes 98308
  11.2 105.6 %copy-start.2 = (f32[128]{0:T(128)S(1)}, f32[128]{0:T(128)}, u32[]{:S(2)}) copy-start(f32[128]{0:T(128)} %param.13) | copy-start | bytes 1540
  19.9 16.5 %all-to-all-start = ((bf16[8,4,128,128]{3,2,1,0:T(8,128)(2,1)}), bf16[8,4,128,128]{3,2,1,0:T(8,128)(2,1)S(1)}, u32[]{:S(2)}, u32[]{:S(2)}) async-start(bf16[8,4,128,128]{3,2,1,0:T(8,128)(2,1)} %shard_map.74), calls=%async_computation | async-start | bytes 2097152 | tf_op jit(solution)/shard_map/all_to_all | solution.py:256
  24.7 22.5 %collective-permute-start.3 = (bf16[8,144,128]{2,1,0:T(8,128)(2,1)S(1)}, bf16[8,144,128]{2,1,0:T(8,128)(2,1)S(1)}, u32[]{:S(2)}, u32[]{:S(2)}) collective-permute-start(bf16[8,144,128]{2,1,0:T(8,128)(2,1)S(1)} %copy-done.6), channel_id=1, source_target_pairs={{0,16},{8,24},{16,0},{24,8},{1,17},{9,25},{17,1},{25,9},{2,18},{10... | collective-permute-start | bytes 884744 | tf_op jit(solution)/shard_map/ppermute | solution.py:425
  25.7 27.1 %collective-permute-start.5 = (bf16[8,144,128]{2,1,0:T(8,128)(2,1)S(1)}, bf16[8,144,128]{2,1,0:T(8,128)(2,1)S(1)}, u32[]{:S(2)}, u32[]{:S(2)}) collective-permute-start(bf16[8,144,128]{2,1,0:T(8,128)(2,1)S(1)} %copy-done.5), channel_id=1, source_target_pairs={{0,24},{8,0},{16,8},{24,16},{1,25},{9,1},{17,9},{25,17},{2,26},{10... | collective-permute-start | bytes 884744 | tf_op jit(solution)/shard_map/ppermute | solution.py:425
  36.5 13.5 %collective-permute-start.1 = (bf16[4,128,128]{2,1,0:T(8,128)(2,1)S(1)}, bf16[4,128,128]{2,1,0:T(8,128)(2,1)S(1)}, u32[]{:S(2)}, u32[]{:S(2)}) collective-permute-start(bf16[4,128,128]{2,1,0:T(8,128)(2,1)S(1)} %get-tuple-element.31), channel_id=1, source_target_pairs={{0,8},{8,16},{16,24},{24,0},{1,9},{9,17},{17,25},{25,1},{2,10},{10... | collective-permute-start | bytes 393224 | tf_op jit(solution)/shard_map/ppermute | solution.py:425
  37.8 15.0 %collective-permute-start.2 = (bf16[4,128,128]{2,1,0:T(8,128)(2,1)S(1)}, bf16[4,128,128]{2,1,0:T(8,128)(2,1)S(1)}, u32[]{:S(2)}, u32[]{:S(2)}) collective-permute-start(bf16[4,128,128]{2,1,0:T(8,128)(2,1)S(1)} %get-tuple-element.32), channel_id=1, source_target_pairs={{0,16},{8,24},{16,0},{24,8},{1,17},{9,25},{17,1},{25,9},{2,18},{10... | collective-permute-start | bytes 393224 | tf_op jit(solution)/shard_map/ppermute | solution.py:425
  53.7 10.4 %all-to-all-start.1 = ((bf16[8,1,144,128]{3,2,1,0:T(8,128)(2,1)}), bf16[8,1,144,128]{3,2,1,0:T(8,128)(2,1)S(1)}, u32[]{:S(2)}, u32[]{:S(2)}) async-start(bf16[8,1,144,128]{3,2,1,0:T(8,128)(2,1)} %shard_map.76), calls=%async_computation.1 | async-start | bytes 589824 | tf_op jit(solution)/shard_map/all_to_all | solution.py:261
  58.8 5.3 %collective-permute-start.4 = (bf16[4,128,128]{2,1,0:T(8,128)(2,1)S(1)}, bf16[4,128,128]{2,1,0:T(8,128)(2,1)S(1)}, u32[]{:S(2)}, u32[]{:S(2)}) collective-permute-start(bf16[4,128,128]{2,1,0:T(8,128)(2,1)S(1)} %get-tuple-element.36), channel_id=1, source_target_pairs={{0,24},{8,0},{16,8},{24,16},{1,25},{9,1},{17,9},{25,17},{2,26},{10... | collective-permute-start | bytes 393224 | tf_op jit(solution)/shard_map/ppermute | solution.py:425
  64.7 2.2 %collective-permute-start.6 = (bf16[8,64,128]{2,1,0:T(8,128)(2,1)S(1)}, bf16[8,64,128]{2,1,0:T(8,128)(2,1)S(1)}, u32[]{:S(2)}, u32[]{:S(2)}) collective-permute-start(bf16[8,64,128]{2,1,0:T(8,128)(2,1)S(1)} %get-tuple-element.42), channel_id=1, source_target_pairs={{0,1},{1,0},{2,3},{3,2},{4,5},{5,4},{6,7},{7,6},{8,9},{9,8},{10,11... | collective-permute-start | bytes 393224 | tf_op jit(solution)/shard_map/ppermute | solution.py:441
  67.0 7.4 %collective-permute-start.7 = (bf16[16,16,128]{2,1,0:T(8,128)(2,1)S(1)}, bf16[16,16,128]{2,1,0:T(8,128)(2,1)S(1)}, u32[]{:S(2)}, u32[]{:S(2)}) collective-permute-start(bf16[16,16,128]{2,1,0:T(8,128)(2,1)S(1)} %pad_maximum_fusion.3), channel_id=1, source_target_pairs={{0,2},{1,3},{2,0},{3,1},{4,6},{5,7},{6,4},{7,5},{8,10},{9,11},{10,... | collective-permute-start | bytes 196616 | tf_op jit(solution)/shard_map/ppermute | solution.py:437
  68.3 10.2 %collective-permute-start.10 = (bf16[16,48,128]{2,1,0:T(8,128)(2,1)S(1)}, bf16[16,48,128]{2,1,0:T(8,128)(2,1)S(1)}, u32[]{:S(2)}, u32[]{:S(2)}) collective-permute-start(bf16[16,48,128]{2,1,0:T(8,128)(2,1)S(1)} %pad_maximum_fusion.2), channel_id=1, source_target_pairs={{0,8},{8,16},{16,24},{24,0},{1,9},{9,17},{17,25},{25,1},{2,10},{10... | collective-permute-start | bytes 589832 | tf_op jit(solution)/shard_map/ppermute | solution.py:425
  69.7 16.2 %collective-permute-start.11 = (bf16[16,48,128]{2,1,0:T(8,128)(2,1)S(1)}, bf16[16,48,128]{2,1,0:T(8,128)(2,1)S(1)}, u32[]{:S(2)}, u32[]{:S(2)}) collective-permute-start(bf16[16,48,128]{2,1,0:T(8,128)(2,1)S(1)} %pad_maximum_fusion.2), channel_id=1, source_target_pairs={{0,16},{8,24},{16,0},{24,8},{1,17},{9,25},{17,1},{25,9},{2,18},{10... | collective-permute-start | bytes 589832 | tf_op jit(solution)/shard_map/ppermute | solution.py:425
  72.7 17.9 %collective-permute-start.12 = (bf16[16,48,128]{2,1,0:T(8,128)(2,1)S(1)}, bf16[16,48,128]{2,1,0:T(8,128)(2,1)S(1)}, u32[]{:S(2)}, u32[]{:S(2)}) collective-permute-start(bf16[16,48,128]{2,1,0:T(8,128)(2,1)S(1)} %pad_maximum_fusion.2), channel_id=1, source_target_pairs={{0,24},{8,0},{16,8},{24,16},{1,25},{9,1},{17,9},{25,17},{2,26},{10... | collective-permute-start | bytes 589832 | tf_op jit(solution)/shard_map/ppermute | solution.py:425
  74.1 3.1 %collective-permute-start.8 = (bf16[16,16,128]{2,1,0:T(8,128)(2,1)S(1)}, bf16[16,16,128]{2,1,0:T(8,128)(2,1)S(1)}, u32[]{:S(2)}, u32[]{:S(2)}) collective-permute-start(bf16[16,16,128]{2,1,0:T(8,128)(2,1)S(1)} %pad_maximum_fusion.3), channel_id=1, source_target_pairs={{0,4},{1,5},{2,6},{3,7},{4,0},{5,1},{6,2},{7,3},{8,12},{9,13},{10,... | collective-permute-start | bytes 196616 | tf_op jit(solution)/shard_map/ppermute | solution.py:437
  74.4 4.0 %collective-permute-start.9 = (bf16[16,16,128]{2,1,0:T(8,128)(2,1)S(1)}, bf16[16,16,128]{2,1,0:T(8,128)(2,1)S(1)}, u32[]{:S(2)}, u32[]{:S(2)}) collective-permute-start(bf16[16,16,128]{2,1,0:T(8,128)(2,1)S(1)} %pad_maximum_fusion.3), channel_id=1, source_target_pairs={{0,6},{1,7},{2,4},{3,5},{4,2},{5,3},{6,0},{7,1},{8,14},{9,15},{10,... | collective-permute-start | bytes 196616 | tf_op jit(solution)/shard_map/ppermute | solution.py:437
  90.8 18.0 %collective-permute-start.14 = (bf16[64,48,128]{2,1,0:T(8,128)(2,1)S(1)}, bf16[64,48,128]{2,1,0:T(8,128)(2,1)}, u32[]{:S(2)}, u32[]{:S(2)}) collective-permute-start(bf16[64,48,128]{2,1,0:T(8,128)(2,1)S(1)} %pad_maximum_fusion.refs_0_), channel_id=1, source_target_pairs={{0,2},{1,5},{2,0},{3,7},{4,6},{5,1},{6,4},{7,3},{8,10},{9,13},{10,... | collective-permute-start | bytes 2359304 | tf_op jit(solution)/shard_map/ppermute | solution.py:433
  91.3 7.2 %collective-permute-start.15 = (bf16[64,16,128]{2,1,0:T(8,128)(2,1)S(1)}, bf16[64,16,128]{2,1,0:T(8,128)(2,1)S(1)}, u32[]{:S(2)}, u32[]{:S(2)}) collective-permute-start(bf16[64,16,128]{2,1,0:T(8,128)(2,1)S(1)} %pad_maximum_fusion.1.refs_0_), channel_id=1, source_target_pairs={{0,8},{8,16},{16,24},{24,0},{1,9},{9,17},{17,25},{25,1},{2,10},{10... | collective-permute-start | bytes 786440 | tf_op jit(solution)/shard_map/ppermute | solution.py:425
  91.3 25.3 %collective-permute-start.17 = (bf16[64,48,128]{2,1,0:T(8,128)(2,1)S(1)}, bf16[64,48,128]{2,1,0:T(8,128)(2,1)}, u32[]{:S(2)}, u32[]{:S(2)}) collective-permute-start(bf16[64,48,128]{2,1,0:T(8,128)(2,1)S(1)} %pad_maximum_fusion.refs_0_), channel_id=1, source_target_pairs={{0,4},{1,3},{2,6},{3,1},{4,0},{5,7},{6,2},{7,5},{8,12},{9,11},{10,... | collective-permute-start | bytes 2359304 | tf_op jit(solution)/shard_map/ppermute | solution.py:433
  91.4 21.9 %collective-permute-start.21 = (bf16[64,16,128]{2,1,0:T(8,128)(2,1)S(1)}, bf16[64,16,128]{2,1,0:T(8,128)(2,1)S(1)}, u32[]{:S(2)}, u32[]{:S(2)}) collective-permute-start(bf16[64,16,128]{2,1,0:T(8,128)(2,1)S(1)} %pad_maximum_fusion.1.refs_0_), channel_id=1, source_target_pairs={{0,16},{8,24},{16,0},{24,8},{1,17},{9,25},{17,1},{25,9},{2,18},{10... | collective-permute-start | bytes 786440 | tf_op jit(solution)/shard_map/ppermute | solution.py:425
  91.4 23.2 %collective-permute-start.22 = (bf16[64,16,128]{2,1,0:T(8,128)(2,1)S(1)}, bf16[64,16,128]{2,1,0:T(8,128)(2,1)S(1)}, u32[]{:S(2)}, u32[]{:S(2)}) collective-permute-start(bf16[64,16,128]{2,1,0:T(8,128)(2,1)S(1)} %pad_maximum_fusion.1.refs_0_), channel_id=1, source_target_pairs={{0,24},{8,0},{16,8},{24,16},{1,25},{9,1},{17,9},{25,17},{2,26},{10... | collective-permute-start | bytes 786440 | tf_op jit(solution)/shard_map/ppermute | solution.py:425
  98.4 16.2 %collective-permute-start.23 = (bf16[64,16,128]{2,1,0:T(8,128)(2,1)S(1)}, bf16[64,16,128]{2,1,0:T(8,128)(2,1)S(1)}, u32[]{:S(2)}, u32[]{:S(2)}) collective-permute-start(bf16[64,16,128]{2,1,0:T(8,128)(2,1)S(1)} %pad_maximum_fusion.1.refs_0_), channel_id=1, source_target_pairs={{0,1},{1,0},{2,3},{3,2},{4,5},{5,4},{6,7},{7,6},{8,9},{9,8},{10,11... | collective-permute-start | bytes 786440 | tf_op jit(solution)/shard_map/ppermute | solution.py:441
  108.7 14.3 %collective-permute-start.19 = (bf16[64,48,128]{2,1,0:T(8,128)(2,1)}, bf16[64,48,128]{2,1,0:T(8,128)(2,1)}, u32[]{:S(2)}, u32[]{:S(2)}) collective-permute-start(bf16[64,48,128]{2,1,0:T(8,128)(2,1)} %collective-permute-done.14.refs_1_), channel_id=1, source_target_pairs={{0,4},{1,3},{2,6},{3,1},{4,0},{5,7},{6,2},{7,5},{8,12},{9,11},{10,... | collective-permute-start | bytes 2359304 | tf_op jit(solution)/shard_map/ppermute | solution.py:433
  113.3 2.5 %collective-permute-start.25 = (bf16[64,16,128]{2,1,0:T(8,128)(2,1)S(1)}, bf16[64,16,128]{2,1,0:T(8,128)(2,1)S(1)}, u32[]{:S(2)}, u32[]{:S(2)}) collective-permute-start(bf16[64,16,128]{2,1,0:T(8,128)(2,1)S(1)} %collective-permute-done.21.refs_2_), channel_id=1, source_target_pairs={{0,1},{1,0},{2,3},{3,2},{4,5},{5,4},{6,7},{7,6},{8,9},{9,8},{10,11... | collective-permute-start | bytes 786440 | tf_op jit(solution)/shard_map/ppermute | solution.py:441
  114.7 1.5 %collective-permute-start.26 = (bf16[64,16,128]{2,1,0:T(8,128)(2,1)S(1)}, bf16[64,16,128]{2,1,0:T(8,128)(2,1)S(1)}, u32[]{:S(2)}, u32[]{:S(2)}) collective-permute-start(bf16[64,16,128]{2,1,0:T(8,128)(2,1)S(1)} %collective-permute-done.22.refs_3_), channel_id=1, source_target_pairs={{0,1},{1,0},{2,3},{3,2},{4,5},{5,4},{6,7},{7,6},{8,9},{9,8},{10,11... | collective-permute-start | bytes 786440 | tf_op jit(solution)/shard_map/ppermute | solution.py:441
  114.7 2.0 %collective-permute-start.24 = (bf16[64,16,128]{2,1,0:T(8,128)(2,1)S(1)}, bf16[64,16,128]{2,1,0:T(8,128)(2,1)S(1)}, u32[]{:S(2)}, u32[]{:S(2)}) collective-permute-start(bf16[64,16,128]{2,1,0:T(8,128)(2,1)S(1)} %collective-permute-done.15.refs_1_), channel_id=1, source_target_pairs={{0,1},{1,0},{2,3},{3,2},{4,5},{5,4},{6,7},{7,6},{8,9},{9,8},{10,11... | collective-permute-start | bytes 786440 | tf_op jit(solution)/shard_map/ppermute | solution.py:441
  115.8 15.9 %collective-permute-start.13 = (bf16[64,48,128]{2,1,0:T(8,128)(2,1)S(1)}, bf16[64,48,128]{2,1,0:T(8,128)(2,1)S(1)}, u32[]{:S(2)}, u32[]{:S(2)}) collective-permute-start(bf16[64,48,128]{2,1,0:T(8,128)(2,1)S(1)} %pad_maximum_fusion.refs_0_), channel_id=1, source_target_pairs={{0,1},{1,0},{2,3},{3,2},{4,5},{5,4},{6,7},{7,6},{8,9},{9,8},{10,11... | collective-permute-start | bytes 2359304 | tf_op jit(solution)/shard_map/ppermute | solution.py:441
  116.2 15.5 %collective-permute-start.16 = (bf16[64,48,128]{2,1,0:T(8,128)(2,1)}, bf16[64,48,128]{2,1,0:T(8,128)(2,1)S(1)}, u32[]{:S(2)}, u32[]{:S(2)}) collective-permute-start(bf16[64,48,128]{2,1,0:T(8,128)(2,1)} %collective-permute-done.14.refs_1_), channel_id=1, source_target_pairs={{0,1},{1,0},{2,3},{3,2},{4,5},{5,4},{6,7},{7,6},{8,9},{9,8},{10,11... | collective-permute-start | bytes 2359304 | tf_op jit(solution)/shard_map/ppermute | solution.py:441
  116.6 15.2 %collective-permute-start.18 = (bf16[64,48,128]{2,1,0:T(8,128)(2,1)}, bf16[64,48,128]{2,1,0:T(8,128)(2,1)S(1)}, u32[]{:S(2)}, u32[]{:S(2)}) collective-permute-start(bf16[64,48,128]{2,1,0:T(8,128)(2,1)} %collective-permute-done.17.refs_2_), channel_id=1, source_target_pairs={{0,1},{1,0},{2,3},{3,2},{4,5},{5,4},{6,7},{7,6},{8,9},{9,8},{10,11... | collective-permute-start | bytes 2359304 | tf_op jit(solution)/shard_map/ppermute | solution.py:441
  123.1 8.7 %collective-permute-start.20 = (bf16[64,48,128]{2,1,0:T(8,128)(2,1)}, bf16[64,48,128]{2,1,0:T(8,128)(2,1)S(1)}, u32[]{:S(2)}, u32[]{:S(2)}) collective-permute-start(bf16[64,48,128]{2,1,0:T(8,128)(2,1)} %collective-permute-done.19.refs_3_), channel_id=1, source_target_pairs={{0,1},{1,0},{2,3},{3,2},{4,5},{5,4},{6,7},{7,6},{8,9},{9,8},{10,11... | collective-permute-start | bytes 2359304 | tf_op jit(solution)/shard_map/ppermute | solution.py:441

commit v18 on v17

--- a/solution.py
+++ b/solution.py
@@ -256,7 +256,7 @@
     first = lax.all_to_all(first, SQUARE, split_axis=0, concat_axis=0, tiled=True)
     firsts = fold(fold_first_kernel, plan, [first], [(4, plan.first_rows, lanes)] * plan.line)
     firsts = [shifted(part, shift) if shift else part for shift, part in enumerate(firsts)]
-    *firsts[1:3], seconds[2] = lax.optimization_barrier((*firsts[1:3], seconds[2]))
+    *firsts[1:], seconds[2] = lax.optimization_barrier((*firsts[1:], seconds[2]))
     second = fold(fold_second_kernel, plan, seconds, [(8, plan.rest, plan.second_rows, lanes)])[0]
     second = lax.all_to_all(second, SQUARE, split_axis=0, concat_axis=0, tiled=True)
     return firsts, second, roots

time: 140 us -> 141 us (level)
  waiting for transfers between devices: 54.3 us -> 60.3 us
  starting transfers between devices: 40.3 us -> 35.7 us
    ppermute x12, starting transfers between devices: 16.6 us -> 11.2 us  [shifted(): lax.ppermute(x, LINE, [(i, (i + amount) % size) for i in range(size)])]
    all_to_all x1, waiting for transfers between devices: 0.01 us -> 4.58 us  [org_sums(): lax.all_to_all(second, SQUARE, split_axis=0, concat_axis=0, tiled=True)]
    ppermute x12, waiting for transfers between devices: 34.4 us -> 36.9 us  [shifted(): lax.ppermute(x, LINE, [(i, (i + amount) % size) for i in range(size)])]
    ppermute x3, waiting for transfers between devices: 6.69 us -> 5.23 us  [crossed(): return lax.ppermute(x, SQUARE, pairs)]
  transfers between devices with their start and end apart: 29 -> 29, of which waited for: 14 -> 16; matrix products, arithmetic and copies ran while one was open for 2% -> 2% of each run, Pallas kernels for 17% -> 17%
where the time goes in v18:
time: 141 us; the launch traced here: 140 us
  waiting for transfers between devices  60.3 us (43%)
  Pallas kernels  41 us (29%)
  starting transfers between devices  35.7 us (25%)
    ppermute x12, waiting for transfers between devices, shifted(): lax.ppermute(x, LINE, [(i, (i + amount) % size) for i in range(size)])  36.9 us
    pallas_call x3, Pallas kernels, spread(): pl.pallas_call(functools.partial(spread_kernel, sides, count, stride, off...  21 us
    pallas_call x2, Pallas kernels, half_sums(): pl.pallas_call(functools.partial(kernel, plan, begin, half, pitch), grid=...  18.5 us
    ppermute x12, starting transfers between devices, shifted(): lax.ppermute(x, LINE, [(i, (i + amount) % size) for i in range(size)])  11.2 us
    all_to_all x1, waiting for transfers between devices, org_sums(): lax.all_to_all(first, SQUARE, split_axis=0, concat_axis=0, tiled=True)  8.92 us
    ppermute x9, starting transfers between devices, swapped(): return lax.ppermute(x, 'core', [(0, 1), (1, 0)])  7.64 us
    ppermute x3, waiting for transfers between devices, crossed(): return lax.ppermute(x, SQUARE, pairs)  5.23 us
    all_to_all x1, starting transfers between devices, org_sums(): lax.all_to_all(second, SQUARE, split_axis=0, concat_axis=0, tiled=True)  4.84 us
  transfers between devices with their start and end apart: 29, of which 16 were waited for; matrix products, arithmetic and copies ran while one was open for 2% of the time, Pallas kernels for 17%

profile of v18, /device:TPU:13, one launch (start us, length us, event | category | flops | bytes accessed | tf_op | source)
XLA Modules:
  0.0 139.8 jit_solution(16620941461707759722)
XLA Ops:
  0.0 9.8 %shard_map.73 = (bf16[8,144,128]{2,1,0:T(8,128)(2,1)}, bf16[8,144,128]{2,1,0:T(8,128)(2,1)}, bf16[8,144,128]{2,1,0:T(8,128)(2,1)}, bf16[8,144,128]{2,1,0:T(8,128...) custom-call(s32[1]{0:T(128)} %bitcast.2.line_ref, s32[4,2048]{1,0:T(4,128)} %bitcast.29, f32[1,256]{1,0:T(1,128)} %bitcast.30, ...), custom_call_target="tpu_custom_call" | custom-call | flops 8589934592 | bytes 16777216 | tf_op jit(solution)/shard_map/pallas_call | solution.py:171
  9.8 1.3 collective-permute-start
  11.2 8.7 %shard_map.74 = bf16[8,4,128,128]{3,2,1,0:T(8,128)(2,1)} custom-call(s32[1]{0:T(128)} %bitcast.2.line_ref, bf16[256,2048]{1,0:T(8,128)(2,1)} %get-tuple-element.28.weighted_ref, bf16[2048,32,128]{2,1,0:T(8,128)(2,1)} %cells_ref.3), custom_call_target="tpu_custom_call" | custom-call | flops 8589934592 | bytes 16777216 | tf_op jit(solution)/shard_map/pallas_call | solution.py:171
  19.9 4.8 %all-to-all-start = ((bf16[8,4,128,128]{3,2,1,0:T(8,128)(2,1)}), bf16[8,4,128,128]{3,2,1,0:T(8,128)(2,1)S(1)}, u32[]{:S(2)}, u32[]{:S(2)}) async-start(bf16[8,4,128,128]{3,2,1,0:T(8,128)(2,1)} %shard_map.74), calls=%async_computation | async-start | bytes 2097152 | tf_op jit(solution)/shard_map/all_to_all | solution.py:256
  24.7 1.0 collective-permute-start.4
  25.7 1.5 %collective-permute-start.5 = (bf16[8,144,128]{2,1,0:T(8,128)(2,1)S(1)}, bf16[8,144,128]{2,1,0:T(8,128)(2,1)S(1)}, u32[]{:S(2)}, u32[]{:S(2)}) collective-permute-start(bf16[8,144,128]{2,1,0:T(8,128)(2,1)S(1)} %copy-done.5), channel_id=1, source_target_pairs={{0,24},{8,0},{16,8},{24,16},{1,25},{9,1},{17,9},{25,17},{2,26},{10... | collective-permute-start | bytes 884744 | tf_op jit(solution)/shard_map/ppermute | solution.py:425
  27.5 8.9 %all-to-all-done.part_ref = bf16[8,4,128,128]{3,2,1,0:T(8,128)(2,1)S(1)} async-done(((bf16[8,4,128,128]{3,2,1,0:T(8,128)(2,1)}), bf16[8,4,128,128]{3,2,1,0:T(8,128)(2,1)S(1)}, u32[]{:S(2)}, u32[]{:S(2)}) %all-to-all-start) | async-done | bytes 1048608 | tf_op jit(solution)/shard_map/all_to_all | solution.py:256
  36.5 1.3 collective-permute-start.1
  37.8 1.4 %collective-permute-start.2 = (bf16[4,128,128]{2,1,0:T(8,128)(2,1)S(1)}, bf16[4,128,128]{2,1,0:T(8,128)(2,1)S(1)}, u32[]{:S(2)}, u32[]{:S(2)}) collective-permute-start(bf16[4,128,128]{2,1,0:T(8,128)(2,1)S(1)} %get-tuple-element.33), channel_id=1, source_target_pairs={{0,16},{8,24},{16,0},{24,8},{1,17},{9,25},{17,1},{25,9},{2,18},{10... | collective-permute-start | bytes 393224 | tf_op jit(solution)/shard_map/ppermute | solution.py:425
  39.6 10.4 %collective-permute-done.4.refs_2_ = bf16[8,144,128]{2,1,0:T(8,128)(2,1)S(1)} collective-permute-done((bf16[8,144,128]{2,1,0:T(8,128)(2,1)S(1)}, bf16[8,144,128]{2,1,0:T(8,128)(2,1)S(1)}, u32[]{:S(2)}, u32[]{:S(2)}) %collective-permute-start.4) | collective-permute-done | bytes 294944 | tf_op jit(solution)/shard_map/ppermute | solution.py:425
  50.0 2.8 %collective-permute-done.1.refs_1_ = bf16[4,128,128]{2,1,0:T(8,128)(2,1)S(1)} collective-permute-done((bf16[4,128,128]{2,1,0:T(8,128)(2,1)S(1)}, bf16[4,128,128]{2,1,0:T(8,128)(2,1)S(1)}, u32[]{:S(2)}, u32[]{:S(2)}) %collective-permute-start.1) | collective-permute-done | bytes 131104 | tf_op jit(solution)/shard_map/ppermute | solution.py:425
  52.8 2.8 %collective-permute-done.2.refs_2_ = bf16[4,128,128]{2,1,0:T(8,128)(2,1)S(1)} collective-permute-done((bf16[4,128,128]{2,1,0:T(8,128)(2,1)S(1)}, bf16[4,128,128]{2,1,0:T(8,128)(2,1)S(1)}, u32[]{:S(2)}, u32[]{:S(2)}) %collective-permute-start.2) | collective-permute-done | bytes 131104 | tf_op jit(solution)/shard_map/ppermute | solution.py:425
  55.6 1.8 %collective-permute-done.3.refs_3_ = bf16[4,128,128]{2,1,0:T(8,128)(2,1)S(1)} collective-permute-done((bf16[4,128,128]{2,1,0:T(8,128)(2,1)S(1)}, bf16[4,128,128]{2,1,0:T(8,128)(2,1)S(1)}, u32[]{:S(2)}, u32[]{:S(2)}) %collective-permute-start.3) | collective-permute-done | bytes 131104 | tf_op jit(solution)/shard_map/ppermute | solution.py:425
  57.4 0.9 shard_map.76
  58.3 4.8 %all-to-all-start.1 = ((bf16[8,1,144,128]{3,2,1,0:T(8,128)(2,1)}), bf16[8,1,144,128]{3,2,1,0:T(8,128)(2,1)S(1)}, u32[]{:S(2)}, u32[]{:S(2)}) async-start(bf16[8,1,144,128]{3,2,1,0:T(8,128)(2,1)} %shard_map.76), calls=%async_computation.1 | async-start | bytes 589824 | tf_op jit(solution)/shard_map/all_to_all | solution.py:261
  63.2 4.6 %all-to-all-done.1.refs_4_ = bf16[8,1,144,128]{3,2,1,0:T(8,128)(2,1)S(1)} async-done(((bf16[8,1,144,128]{3,2,1,0:T(8,128)(2,1)}), bf16[8,1,144,128]{3,2,1,0:T(8,128)(2,1)S(1)}, u32[]{:S(2)}, u32[]{:S(2)}) %all-to-all-start.1) | async-done | bytes 294944 | tf_op jit(solution)/shard_map/all_to_all | solution.py:261
  67.9 0.5 shard_map.77
  68.4 1.6 %collective-permute-start.6 = (bf16[8,64,128]{2,1,0:T(8,128)(2,1)S(1)}, bf16[8,64,128]{2,1,0:T(8,128)(2,1)S(1)}, u32[]{:S(2)}, u32[]{:S(2)}) collective-permute-start(bf16[8,64,128]{2,1,0:T(8,128)(2,1)S(1)} %get-tuple-element.44), channel_id=1, source_target_pairs={{0,1},{1,0},{2,3},{3,2},{4,5},{5,4},{6,7},{7,6},{8,9},{9,8},{10,11... | collective-permute-start | bytes 393224 | tf_op jit(solution)/shard_map/ppermute | solution.py:441
  70.0 1.0 collective-permute-done.6
  71.0 0.3 collective-permute-start.7
  71.5 1.6 %collective-permute-start.11 = (bf16[16,48,128]{2,1,0:T(8,128)(2,1)S(1)}, bf16[16,48,128]{2,1,0:T(8,128)(2,1)S(1)}, u32[]{:S(2)}, u32[]{:S(2)}) collective-permute-start(bf16[16,48,128]{2,1,0:T(8,128)(2,1)S(1)} %pad_maximum_fusion.2), channel_id=1, source_target_pairs={{0,16},{8,24},{16,0},{24,8},{1,17},{9,25},{17,1},{25,9},{2,18},{10... | collective-permute-start | bytes 589832 | tf_op jit(solution)/shard_map/ppermute | solution.py:425
  73.0 1.4 collective-permute-start.12
  74.4 1.2 collective-permute-start.8
  75.6 1.2 collective-permute-start.9
  76.8 1.0 collective-permute-done.8
  77.8 2.1 %collective-permute-done.9 = bf16[16,16,128]{2,1,0:T(8,128)(2,1)S(1)} collective-permute-done((bf16[16,16,128]{2,1,0:T(8,128)(2,1)S(1)}, bf16[16,16,128]{2,1,0:T(8,128)(2,1)S(1)}, u32[]{:S(2)}, u32[]{:S(2)}) %collective-permute-start.9) | collective-permute-done | bytes 65568 | tf_op jit(solution)/shard_map/ppermute | solution.py:437
  80.0 8.1 %collective-permute-done.11 = bf16[16,48,128]{2,1,0:T(8,128)(2,1)S(1)} collective-permute-done((bf16[16,48,128]{2,1,0:T(8,128)(2,1)S(1)}, bf16[16,48,128]{2,1,0:T(8,128)(2,1)S(1)}, u32[]{:S(2)}, u32[]{:S(2)}) %collective-permute-start.11) | collective-permute-done | bytes 196640 | tf_op jit(solution)/shard_map/ppermute | solution.py:425
  88.0 3.0 %collective-permute-done.12 = bf16[16,48,128]{2,1,0:T(8,128)(2,1)S(1)} collective-permute-done((bf16[16,48,128]{2,1,0:T(8,128)(2,1)S(1)}, bf16[16,48,128]{2,1,0:T(8,128)(2,1)S(1)}, u32[]{:S(2)}, u32[]{:S(2)}) %collective-permute-start.12) | collective-permute-done | bytes 196640 | tf_op jit(solution)/shard_map/ppermute | solution.py:425
  91.1 1.3 collective-permute-start.14
  92.4 1.2 collective-permute-start.17
  93.7 1.5 %collective-permute-start.22 = (bf16[64,16,128]{2,1,0:T(8,128)(2,1)S(1)}, bf16[64,16,128]{2,1,0:T(8,128)(2,1)S(1)}, u32[]{:S(2)}, u32[]{:S(2)}) collective-permute-start(bf16[64,16,128]{2,1,0:T(8,128)(2,1)S(1)} %pad_maximum_fusion.1.refs_0_), channel_id=1, source_target_pairs={{0,24},{8,0},{16,8},{24,16},{1,25},{9,1},{17,9},{25,17},{2,26},{10... | collective-permute-start | bytes 786440 | tf_op jit(solution)/shard_map/ppermute | solution.py:425
  95.1 4.4 %collective-permute-done.15.refs_1_ = bf16[64,16,128]{2,1,0:T(8,128)(2,1)S(1)} collective-permute-done((bf16[64,16,128]{2,1,0:T(8,128)(2,1)S(1)}, bf16[64,16,128]{2,1,0:T(8,128)(2,1)S(1)}, u32[]{:S(2)}, u32[]{:S(2)}) %collective-permute-start.15) | collective-permute-done | bytes 262176 | tf_op jit(solution)/shard_map/ppermute | solution.py:425
  99.5 2.8 %collective-permute-start.23 = (bf16[64,16,128]{2,1,0:T(8,128)(2,1)S(1)}, bf16[64,16,128]{2,1,0:T(8,128)(2,1)S(1)}, u32[]{:S(2)}, u32[]{:S(2)}) collective-permute-start(bf16[64,16,128]{2,1,0:T(8,128)(2,1)S(1)} %pad_maximum_fusion.1.refs_0_), channel_id=1, source_target_pairs={{0,1},{1,0},{2,3},{3,2},{4,5},{5,4},{6,7},{7,6},{8,9},{9,8},{10,11... | collective-permute-start | bytes 786440 | tf_op jit(solution)/shard_map/ppermute | solution.py:441
  102.3 0.8 multiply_add_fusion
  103.1 5.2 %collective-permute-done.14.refs_1_ = bf16[64,48,128]{2,1,0:T(8,128)(2,1)} collective-permute-done((bf16[64,48,128]{2,1,0:T(8,128)(2,1)S(1)}, bf16[64,48,128]{2,1,0:T(8,128)(2,1)}, u32[]{:S(2)}, u32[]{:S(2)}) %collective-permute-start.14) | collective-permute-done | bytes 786464 | tf_op jit(solution)/shard_map/ppermute | solution.py:433
  108.3 2.1 %collective-permute-start.19 = (bf16[64,48,128]{2,1,0:T(8,128)(2,1)}, bf16[64,48,128]{2,1,0:T(8,128)(2,1)}, u32[]{:S(2)}, u32[]{:S(2)}) collective-permute-start(bf16[64,48,128]{2,1,0:T(8,128)(2,1)} %collective-permute-done.14.refs_1_), channel_id=1, source_target_pairs={{0,4},{1,3},{2,6},{3,1},{4,0},{5,7},{6,2},{7,5},{8,12},{9,11},{10,... | collective-permute-start | bytes 2359304 | tf_op jit(solution)/shard_map/ppermute | solution.py:433
  110.4 0.7 constant_dynamic-slice_fusion.root_ref
  111.1 3.3 %collective-permute-done.21.refs_2_ = bf16[64,16,128]{2,1,0:T(8,128)(2,1)S(1)} collective-permute-done((bf16[64,16,128]{2,1,0:T(8,128)(2,1)S(1)}, bf16[64,16,128]{2,1,0:T(8,128)(2,1)S(1)}, u32[]{:S(2)}, u32[]{:S(2)}) %collective-permute-start.21) | collective-permute-done | bytes 262176 | tf_op jit(solution)/shard_map/ppermute | solution.py:425
  114.4 1.3 collective-permute-start.25
  115.7 0.5 collective-permute-done.22.refs_3_
  116.2 0.4 collective-permute-start.26
  116.9 0.4 collective-permute-start.13
  117.3 0.4 collective-permute-done.26.refs_7_
  117.8 0.4 collective-permute-start.16
  118.3 6.3 %shard_map.78.refs_4_ = bf16[512,128,128]{2,1,0:T(8,128)(2,1)} custom-call(s32[2]{0:T(128)S(1)} %pad_add_fusion.halves_ref, s32[4,512]{1,0:T(4,128)S(1)} %get-tuple-element.51.places_ref, f32[1,512]{1,0:T(1,128)S(1)} %constant_dynamic-slice_fusion.root_ref, f32[1,128]{1,0:T(1,128)S(1)} %bitcast.26, bf16[64,16,128]{2,1,0:T(8,128)(2,1)S(1)} %pad_maximum_fusion.1.refs_0_, ...), custom_call_target="tpu_custom_call" | custom-call | flops 4294967296 | bytes 4194304 | tf_op jit(solution)/shard_map/pallas_call | solution.py:400
  124.6 0.4 collective-permute-start.20
  125.1 8.0 %shard_map.79.refs_4_ = bf16[512,128,128]{2,1,0:T(8,128)(2,1)} custom-call(s32[1]{0:T(128)} %bitcast.6.halves_ref, s32[4,512]{1,0:T(4,128)S(1)} %get-tuple-element.58.places_ref, f32[1,512]{1,0:T(1,128)S(1)} %constant_dynamic-slice_fusion.root_ref, f32[1,128]{1,0:T(1,128)S(1)} %bitcast.27, ...), custom_call_target="tpu_custom_call", output_to_operand_aliasing={{}: (8, {})} | custom-call | flops 12884901888 | bytes 12582912 | tf_op jit(solution)/shard_map/pallas_call | solution.py:400
  133.1 6.6 %shard_map.80 = bf16[512,128,128]{2,1,0:T(8,128)(2,1)} custom-call(s32[1]{0:T(128)} %bitcast.halves_ref, s32[4,512]{1,0:T(4,128)S(1)} %get-tuple-element.59.places_ref, f32[1,512]{1,0:T(1,128)S(1)} %constant_dynamic-slice_fusion.root_ref, f32[1,128]{1,0:T(1,128)S(1)} %bitcast.28, ...), custom_call_target="tpu_custom_call", output_to_operand_aliasing={{}: (8, {})} | custom-call | flops 12884901888 | bytes 12582912 | tf_op jit(solution)/shard_map/pallas_call | solution.py:400
  (52 shorter events, 1.8 us)
Async XLA Ops:
  9.8 10.1 %collective-permute-start = (bf16[8,144,128]{2,1,0:T(8,128)(2,1)}, bf16[8,144,128]{2,1,0:T(8,128)(2,1)S(1)}, u32[]{:S(2)}, u32[]{:S(2)}) collective-permute-start(bf16[8,144,128]{2,1,0:T(8,128)(2,1)} %get-tuple-element.29), channel_id=1, source_target_pairs={{0,8},{8,16},{16,24},{24,0},{1,9},{9,17},{17,25},{25,1},{2,10},{10... | collective-permute-start | bytes 884744 | tf_op jit(solution)/shard_map/ppermute | solution.py:425
  11.1 13.6 %copy-start.6 = (bf16[8,144,128]{2,1,0:T(8,128)(2,1)S(1)}, bf16[8,144,128]{2,1,0:T(8,128)(2,1)}, u32[]{:S(2)}) copy-start(bf16[8,144,128]{2,1,0:T(8,128)(2,1)} %get-tuple-element.35) | copy-start | bytes 884740
  11.1 14.5 %copy-start.5 = (bf16[8,144,128]{2,1,0:T(8,128)(2,1)S(1)}, bf16[8,144,128]{2,1,0:T(8,128)(2,1)}, u32[]{:S(2)}) copy-start(bf16[8,144,128]{2,1,0:T(8,128)(2,1)} %get-tuple-element.42) | copy-start | bytes 884740
  11.1 16.1 %copy-start.3 = (s32[128,3]{0,1:T(4,128)S(1)}, s32[128,3]{0,1:T(4,128)}, u32[]{:S(2)}) copy-start(s32[128,3]{0,1:T(4,128)} %param.11) | copy-start | bytes 4612
  11.1 16.2 %copy-start.4 = (f32[128]{0:T(128)S(1)}, f32[128]{0:T(128)}, u32[]{:S(2)}) copy-start(f32[128]{0:T(128)} %param.12) | copy-start | bytes 1540
  11.1 46.3 %copy-start = (bf16[8,144,128]{2,1,0:T(8,128)(2,1)S(1)}, bf16[8,144,128]{2,1,0:T(8,128)(2,1)}, u32[]{:S(2)}) copy-start(bf16[8,144,128]{2,1,0:T(8,128)(2,1)} %get-tuple-element.39.refs_0_) | copy-start | bytes 884740
  11.1 52.0 %copy-start.7 = (f32[256]{0:T(256)S(1)}, f32[256]{0:T(256)}, u32[]{:S(2)}) copy-start(f32[256]{0:T(256)} %param.9) | copy-start | bytes 3076
  11.2 56.7 %copy-start.1 = (bf16[128,128]{1,0:T(8,128)(2,1)S(1)}, bf16[128,128]{1,0:T(8,128)(2,1)}, u32[]{:S(2)}) copy-start(bf16[128,128]{1,0:T(8,128)(2,1)} %mixing_ref.1) | copy-start | bytes 98308
  11.2 107.1 %copy-start.2 = (f32[128]{0:T(128)S(1)}, f32[128]{0:T(128)}, u32[]{:S(2)}) copy-start(f32[128]{0:T(128)} %param.13) | copy-start | bytes 1540
  19.9 16.5 %all-to-all-start = ((bf16[8,4,128,128]{3,2,1,0:T(8,128)(2,1)}), bf16[8,4,128,128]{3,2,1,0:T(8,128)(2,1)S(1)}, u32[]{:S(2)}, u32[]{:S(2)}) async-start(bf16[8,4,128,128]{3,2,1,0:T(8,128)(2,1)} %shard_map.74), calls=%async_computation | async-start | bytes 2097152 | tf_op jit(solution)/shard_map/all_to_all | solution.py:256
  24.7 25.3 %collective-permute-start.4 = (bf16[8,144,128]{2,1,0:T(8,128)(2,1)S(1)}, bf16[8,144,128]{2,1,0:T(8,128)(2,1)S(1)}, u32[]{:S(2)}, u32[]{:S(2)}) collective-permute-start(bf16[8,144,128]{2,1,0:T(8,128)(2,1)S(1)} %copy-done.6), channel_id=1, source_target_pairs={{0,16},{8,24},{16,0},{24,8},{1,17},{9,25},{17,1},{25,9},{2,18},{10... | collective-permute-start | bytes 884744 | tf_op jit(solution)/shard_map/ppermute | solution.py:425
  25.7 31.7 %collective-permute-start.5 = (bf16[8,144,128]{2,1,0:T(8,128)(2,1)S(1)}, bf16[8,144,128]{2,1,0:T(8,128)(2,1)S(1)}, u32[]{:S(2)}, u32[]{:S(2)}) collective-permute-start(bf16[8,144,128]{2,1,0:T(8,128)(2,1)S(1)} %copy-done.5), channel_id=1, source_target_pairs={{0,24},{8,0},{16,8},{24,16},{1,25},{9,1},{17,9},{25,17},{2,26},{10... | collective-permute-start | bytes 884744 | tf_op jit(solution)/shard_map/ppermute | solution.py:425
  36.5 16.3 %collective-permute-start.1 = (bf16[4,128,128]{2,1,0:T(8,128)(2,1)S(1)}, bf16[4,128,128]{2,1,0:T(8,128)(2,1)S(1)}, u32[]{:S(2)}, u32[]{:S(2)}) collective-permute-start(bf16[4,128,128]{2,1,0:T(8,128)(2,1)S(1)} %get-tuple-element.32), channel_id=1, source_target_pairs={{0,8},{8,16},{16,24},{24,0},{1,9},{9,17},{17,25},{25,1},{2,10},{10... | collective-permute-start | bytes 393224 | tf_op jit(solution)/shard_map/ppermute | solution.py:425
  37.8 17.8 %collective-permute-start.2 = (bf16[4,128,128]{2,1,0:T(8,128)(2,1)S(1)}, bf16[4,128,128]{2,1,0:T(8,128)(2,1)S(1)}, u32[]{:S(2)}, u32[]{:S(2)}) collective-permute-start(bf16[4,128,128]{2,1,0:T(8,128)(2,1)S(1)} %get-tuple-element.33), channel_id=1, source_target_pairs={{0,16},{8,24},{16,0},{24,8},{1,17},{9,25},{17,1},{25,9},{2,18},{10... | collective-permute-start | bytes 393224 | tf_op jit(solution)/shard_map/ppermute | solution.py:425
  39.3 18.1 %collective-permute-start.3 = (bf16[4,128,128]{2,1,0:T(8,128)(2,1)S(1)}, bf16[4,128,128]{2,1,0:T(8,128)(2,1)S(1)}, u32[]{:S(2)}, u32[]{:S(2)}) collective-permute-start(bf16[4,128,128]{2,1,0:T(8,128)(2,1)S(1)} %get-tuple-element.34), channel_id=1, source_target_pairs={{0,24},{8,0},{16,8},{24,16},{1,25},{9,1},{17,9},{25,17},{2,26},{10... | collective-permute-start | bytes 393224 | tf_op jit(solution)/shard_map/ppermute | solution.py:425
  58.3 9.5 %all-to-all-start.1 = ((bf16[8,1,144,128]{3,2,1,0:T(8,128)(2,1)}), bf16[8,1,144,128]{3,2,1,0:T(8,128)(2,1)S(1)}, u32[]{:S(2)}, u32[]{:S(2)}) async-start(bf16[8,1,144,128]{3,2,1,0:T(8,128)(2,1)} %shard_map.76), calls=%async_computation.1 | async-start | bytes 589824 | tf_op jit(solution)/shard_map/all_to_all | solution.py:261
  68.4 2.6 %collective-permute-start.6 = (bf16[8,64,128]{2,1,0:T(8,128)(2,1)S(1)}, bf16[8,64,128]{2,1,0:T(8,128)(2,1)S(1)}, u32[]{:S(2)}, u32[]{:S(2)}) collective-permute-start(bf16[8,64,128]{2,1,0:T(8,128)(2,1)S(1)} %get-tuple-element.44), channel_id=1, source_target_pairs={{0,1},{1,0},{2,3},{3,2},{4,5},{5,4},{6,7},{7,6},{8,9},{9,8},{10,11... | collective-permute-start | bytes 393224 | tf_op jit(solution)/shard_map/ppermute | solution.py:441
  71.0 4.6 %collective-permute-start.7 = (bf16[16,16,128]{2,1,0:T(8,128)(2,1)S(1)}, bf16[16,16,128]{2,1,0:T(8,128)(2,1)S(1)}, u32[]{:S(2)}, u32[]{:S(2)}) collective-permute-start(bf16[16,16,128]{2,1,0:T(8,128)(2,1)S(1)} %pad_maximum_fusion.3), channel_id=1, source_target_pairs={{0,2},{1,3},{2,0},{3,1},{4,6},{5,7},{6,4},{7,5},{8,10},{9,11},{10,... | collective-permute-start | bytes 196616 | tf_op jit(solution)/shard_map/ppermute | solution.py:437
  71.4 8.6 %collective-permute-start.10 = (bf16[16,48,128]{2,1,0:T(8,128)(2,1)S(1)}, bf16[16,48,128]{2,1,0:T(8,128)(2,1)S(1)}, u32[]{:S(2)}, u32[]{:S(2)}) collective-permute-start(bf16[16,48,128]{2,1,0:T(8,128)(2,1)S(1)} %pad_maximum_fusion.2), channel_id=1, source_target_pairs={{0,8},{8,16},{16,24},{24,0},{1,9},{9,17},{17,25},{25,1},{2,10},{10... | collective-permute-start | bytes 589832 | tf_op jit(solution)/shard_map/ppermute | solution.py:425
  71.5 16.6 %collective-permute-start.11 = (bf16[16,48,128]{2,1,0:T(8,128)(2,1)S(1)}, bf16[16,48,128]{2,1,0:T(8,128)(2,1)S(1)}, u32[]{:S(2)}, u32[]{:S(2)}) collective-permute-start(bf16[16,48,128]{2,1,0:T(8,128)(2,1)S(1)} %pad_maximum_fusion.2), channel_id=1, source_target_pairs={{0,16},{8,24},{16,0},{24,8},{1,17},{9,25},{17,1},{25,9},{2,18},{10... | collective-permute-start | bytes 589832 | tf_op jit(solution)/shard_map/ppermute | solution.py:425
  73.0 18.0 %collective-permute-start.12 = (bf16[16,48,128]{2,1,0:T(8,128)(2,1)S(1)}, bf16[16,48,128]{2,1,0:T(8,128)(2,1)S(1)}, u32[]{:S(2)}, u32[]{:S(2)}) collective-permute-start(bf16[16,48,128]{2,1,0:T(8,128)(2,1)S(1)} %pad_maximum_fusion.2), channel_id=1, source_target_pairs={{0,24},{8,0},{16,8},{24,16},{1,25},{9,1},{17,9},{25,17},{2,26},{10... | collective-permute-start | bytes 589832 | tf_op jit(solution)/shard_map/ppermute | solution.py:425
  74.4 3.4 %collective-permute-start.8 = (bf16[16,16,128]{2,1,0:T(8,128)(2,1)S(1)}, bf16[16,16,128]{2,1,0:T(8,128)(2,1)S(1)}, u32[]{:S(2)}, u32[]{:S(2)}) collective-permute-start(bf16[16,16,128]{2,1,0:T(8,128)(2,1)S(1)} %pad_maximum_fusion.3), channel_id=1, source_target_pairs={{0,4},{1,5},{2,6},{3,7},{4,0},{5,1},{6,2},{7,3},{8,12},{9,13},{10,... | collective-permute-start | bytes 196616 | tf_op jit(solution)/shard_map/ppermute | solution.py:437
  75.6 4.3 %collective-permute-start.9 = (bf16[16,16,128]{2,1,0:T(8,128)(2,1)S(1)}, bf16[16,16,128]{2,1,0:T(8,128)(2,1)S(1)}, u32[]{:S(2)}, u32[]{:S(2)}) collective-permute-start(bf16[16,16,128]{2,1,0:T(8,128)(2,1)S(1)} %pad_maximum_fusion.3), channel_id=1, source_target_pairs={{0,6},{1,7},{2,4},{3,5},{4,2},{5,3},{6,0},{7,1},{8,14},{9,15},{10,... | collective-permute-start | bytes 196616 | tf_op jit(solution)/shard_map/ppermute | solution.py:437
  91.1 17.2 %collective-permute-start.14 = (bf16[64,48,128]{2,1,0:T(8,128)(2,1)S(1)}, bf16[64,48,128]{2,1,0:T(8,128)(2,1)}, u32[]{:S(2)}, u32[]{:S(2)}) collective-permute-start(bf16[64,48,128]{2,1,0:T(8,128)(2,1)S(1)} %pad_maximum_fusion.refs_0_), channel_id=1, source_target_pairs={{0,2},{1,5},{2,0},{3,7},{4,6},{5,1},{6,4},{7,3},{8,10},{9,13},{10,... | collective-permute-start | bytes 2359304 | tf_op jit(solution)/shard_map/ppermute | solution.py:433
  92.3 7.2 %collective-permute-start.15 = (bf16[64,16,128]{2,1,0:T(8,128)(2,1)S(1)}, bf16[64,16,128]{2,1,0:T(8,128)(2,1)S(1)}, u32[]{:S(2)}, u32[]{:S(2)}) collective-permute-start(bf16[64,16,128]{2,1,0:T(8,128)(2,1)S(1)} %pad_maximum_fusion.1.refs_0_), channel_id=1, source_target_pairs={{0,8},{8,16},{16,24},{24,0},{1,9},{9,17},{17,25},{25,1},{2,10},{10... | collective-permute-start | bytes 786440 | tf_op jit(solution)/shard_map/ppermute | solution.py:425
  92.4 25.8 %collective-permute-start.17 = (bf16[64,48,128]{2,1,0:T(8,128)(2,1)S(1)}, bf16[64,48,128]{2,1,0:T(8,128)(2,1)}, u32[]{:S(2)}, u32[]{:S(2)}) collective-permute-start(bf16[64,48,128]{2,1,0:T(8,128)(2,1)S(1)} %pad_maximum_fusion.refs_0_), channel_id=1, source_target_pairs={{0,4},{1,3},{2,6},{3,1},{4,0},{5,7},{6,2},{7,5},{8,12},{9,11},{10,... | collective-permute-start | bytes 2359304 | tf_op jit(solution)/shard_map/ppermute | solution.py:433
  93.5 20.8 %collective-permute-start.21 = (bf16[64,16,128]{2,1,0:T(8,128)(2,1)S(1)}, bf16[64,16,128]{2,1,0:T(8,128)(2,1)S(1)}, u32[]{:S(2)}, u32[]{:S(2)}) collective-permute-start(bf16[64,16,128]{2,1,0:T(8,128)(2,1)S(1)} %pad_maximum_fusion.1.refs_0_), channel_id=1, source_target_pairs={{0,16},{8,24},{16,0},{24,8},{1,17},{9,25},{17,1},{25,9},{2,18},{10... | collective-permute-start | bytes 786440 | tf_op jit(solution)/shard_map/ppermute | solution.py:425
  93.7 22.5 %collective-permute-start.22 = (bf16[64,16,128]{2,1,0:T(8,128)(2,1)S(1)}, bf16[64,16,128]{2,1,0:T(8,128)(2,1)S(1)}, u32[]{:S(2)}, u32[]{:S(2)}) collective-permute-start(bf16[64,16,128]{2,1,0:T(8,128)(2,1)S(1)} %pad_maximum_fusion.1.refs_0_), channel_id=1, source_target_pairs={{0,24},{8,0},{16,8},{24,16},{1,25},{9,1},{17,9},{25,17},{2,26},{10... | collective-permute-start | bytes 786440 | tf_op jit(solution)/shard_map/ppermute | solution.py:425
  99.5 17.1 %collective-permute-start.23 = (bf16[64,16,128]{2,1,0:T(8,128)(2,1)S(1)}, bf16[64,16,128]{2,1,0:T(8,128)(2,1)S(1)}, u32[]{:S(2)}, u32[]{:S(2)}) collective-permute-start(bf16[64,16,128]{2,1,0:T(8,128)(2,1)S(1)} %pad_maximum_fusion.1.refs_0_), channel_id=1, source_target_pairs={{0,1},{1,0},{2,3},{3,2},{4,5},{5,4},{6,7},{7,6},{8,9},{9,8},{10,11... | collective-permute-start | bytes 786440 | tf_op jit(solution)/shard_map/ppermute | solution.py:441
  108.3 16.3 %collective-permute-start.19 = (bf16[64,48,128]{2,1,0:T(8,128)(2,1)}, bf16[64,48,128]{2,1,0:T(8,128)(2,1)}, u32[]{:S(2)}, u32[]{:S(2)}) collective-permute-start(bf16[64,48,128]{2,1,0:T(8,128)(2,1)} %collective-permute-done.14.refs_1_), channel_id=1, source_target_pairs={{0,4},{1,3},{2,6},{3,1},{4,0},{5,7},{6,2},{7,5},{8,12},{9,11},{10,... | collective-permute-start | bytes 2359304 | tf_op jit(solution)/shard_map/ppermute | solution.py:433
  114.4 2.5 %collective-permute-start.25 = (bf16[64,16,128]{2,1,0:T(8,128)(2,1)S(1)}, bf16[64,16,128]{2,1,0:T(8,128)(2,1)S(1)}, u32[]{:S(2)}, u32[]{:S(2)}) collective-permute-start(bf16[64,16,128]{2,1,0:T(8,128)(2,1)S(1)} %collective-permute-done.21.refs_2_), channel_id=1, source_target_pairs={{0,1},{1,0},{2,3},{3,2},{4,5},{5,4},{6,7},{7,6},{8,9},{9,8},{10,11... | collective-permute-start | bytes 786440 | tf_op jit(solution)/shard_map/ppermute | solution.py:441
  116.2 1.6 %collective-permute-start.26 = (bf16[64,16,128]{2,1,0:T(8,128)(2,1)S(1)}, bf16[64,16,128]{2,1,0:T(8,128)(2,1)S(1)}, u32[]{:S(2)}, u32[]{:S(2)}) collective-permute-start(bf16[64,16,128]{2,1,0:T(8,128)(2,1)S(1)} %collective-permute-done.22.refs_3_), channel_id=1, source_target_pairs={{0,1},{1,0},{2,3},{3,2},{4,5},{5,4},{6,7},{7,6},{8,9},{9,8},{10,11... | collective-permute-start | bytes 786440 | tf_op jit(solution)/shard_map/ppermute | solution.py:441
  116.6 1.7 %collective-permute-start.24 = (bf16[64,16,128]{2,1,0:T(8,128)(2,1)S(1)}, bf16[64,16,128]{2,1,0:T(8,128)(2,1)S(1)}, u32[]{:S(2)}, u32[]{:S(2)}) collective-permute-start(bf16[64,16,128]{2,1,0:T(8,128)(2,1)S(1)} %collective-permute-done.15.refs_1_), channel_id=1, source_target_pairs={{0,1},{1,0},{2,3},{3,2},{4,5},{5,4},{6,7},{7,6},{8,9},{9,8},{10,11... | collective-permute-start | bytes 786440 | tf_op jit(solution)/shard_map/ppermute | solution.py:441
  116.9 16.2 %collective-permute-start.13 = (bf16[64,48,128]{2,1,0:T(8,128)(2,1)S(1)}, bf16[64,48,128]{2,1,0:T(8,128)(2,1)S(1)}, u32[]{:S(2)}, u32[]{:S(2)}) collective-permute-start(bf16[64,48,128]{2,1,0:T(8,128)(2,1)S(1)} %pad_maximum_fusion.refs_0_), channel_id=1, source_target_pairs={{0,1},{1,0},{2,3},{3,2},{4,5},{5,4},{6,7},{7,6},{8,9},{9,8},{10,11... | collective-permute-start | bytes 2359304 | tf_op jit(solution)/shard_map/ppermute | solution.py:441
  117.8 15.4 %collective-permute-start.16 = (bf16[64,48,128]{2,1,0:T(8,128)(2,1)}, bf16[64,48,128]{2,1,0:T(8,128)(2,1)S(1)}, u32[]{:S(2)}, u32[]{:S(2)}) collective-permute-start(bf16[64,48,128]{2,1,0:T(8,128)(2,1)} %collective-permute-done.14.refs_1_), channel_id=1, source_target_pairs={{0,1},{1,0},{2,3},{3,2},{4,5},{5,4},{6,7},{7,6},{8,9},{9,8},{10,11... | collective-permute-start | bytes 2359304 | tf_op jit(solution)/shard_map/ppermute | solution.py:441
  118.1 15.0 %collective-permute-start.18 = (bf16[64,48,128]{2,1,0:T(8,128)(2,1)}, bf16[64,48,128]{2,1,0:T(8,128)(2,1)S(1)}, u32[]{:S(2)}, u32[]{:S(2)}) collective-permute-start(bf16[64,48,128]{2,1,0:T(8,128)(2,1)} %collective-permute-done.17.refs_2_), channel_id=1, source_target_pairs={{0,1},{1,0},{2,3},{3,2},{4,5},{5,4},{6,7},{7,6},{8,9},{9,8},{10,11... | collective-permute-start | bytes 2359304 | tf_op jit(solution)/shard_map/ppermute | solution.py:441
  124.6 8.5 %collective-permute-start.20 = (bf16[64,48,128]{2,1,0:T(8,128)(2,1)}, bf16[64,48,128]{2,1,0:T(8,128)(2,1)S(1)}, u32[]{:S(2)}, u32[]{:S(2)}) collective-permute-start(bf16[64,48,128]{2,1,0:T(8,128)(2,1)} %collective-permute-done.19.refs_3_), channel_id=1, source_target_pairs={{0,1},{1,0},{2,3},{3,2},{4,5},{5,4},{6,7},{7,6},{8,9},{9,8},{10,11... | collective-permute-start | bytes 2359304 | tf_op jit(solution)/shard_map/ppermute | solution.py:441
